TPU v7x, 32 devices: a whole 2x2x4 slice. The times are simulated.
32 devices in a mesh: owner: 4 (over y, core), dp: 8 (over z, x).
Axes of the slice: x: 2, y: 2, z: 4, core: 2. Of those that a mesh axis runs over, the one named last changes fastest.
Arguments:
- activations: bfloat16 [64, 8, 8, 512], P(('owner', 'dp')), may hold values from -8 to 8
- out_grad: bfloat16 [64, 8, 8, 512], P(('owner', 'dp')), may hold values from -6 to 6
- group_weight: bfloat16 [16, 288, 32], replicated, may hold values from -0.375 to 0.375
- proj_weight: bfloat16 [512, 512], replicated, may hold values from -0.25 to 0.25
- bn_gain: float32 [512], replicated, may hold values from 0.1 to 1.9
- bn_shift: float32 [512], replicated, may hold values from -3 to 3
- slot_block: int32 [4, 24], replicated, may hold values from -1 to 47, as said below
Outputs:
- group_grad: float32 [16, 288, 32], replicated
- proj_grad: float32 [512, 512], replicated
- out_factor: float32 [16, 32, 32], replicated
- factor_owned: float32 [96, 96, 288], P('owner', 'dp')
Inputs may be any that keep to these rules, and one draw needn't show every extreme that they name: `slot_block`: each of the 48 blocks stands in exactly one slot; an owner's blocks fill its slots from the first, the rest hold -1; some owner's 24 slots are all used.
All inputs are finite; a program needn't handle non-finite values.
Results may differ from a plain program's by a relative error of at most 0.0065.
Values sent between devices are 32-bit elements; how exact they have to be, the bound alone decides.
No kernel may reach another device: no remote copies, remote signals or barrier semaphores. Data moves between devices by JAX's collectives and lax.ppermute only.
A program may use at most 64 MiB of HBM per device.

v0:
```python
import math

import jax
import jax.numpy as jnp
from jax import lax
from jax.sharding import PartitionSpec as P


def pick_slots(factor_blocks, slot_block):
    flat_slots = slot_block.reshape(-1)
    picked = jnp.take(factor_blocks, jnp.clip(flat_slots, 0, factor_blocks.shape[0] - 1), axis=0)
    return picked * (flat_slots >= 0).astype(jnp.float32)[:, None, None]


def per_device(activations, out_grad, group_weight, proj_weight, bn_gain, bn_shift, slot_block):
    img_count, side_len = (activations.shape[0], activations.shape[1])
    in_width = activations.shape[3]
    groups, patch_len, group_width = group_weight.shape
    out_width = out_grad.shape[3]
    row_count = img_count * side_len * side_len
    padded = jnp.pad(activations, ((0, 0), (1, 1), (1, 1), (0, 0)))
    padded = padded.reshape(img_count, side_len + 2, side_len + 2, groups, group_width)
    shifted = [
        padded[:, row_shift : row_shift + side_len, col_shift : col_shift + side_len]
        for row_shift in range(3)
        for col_shift in range(3)
    ]
    patches = jnp.stack(shifted, axis=4).reshape(row_count, groups, patch_len)
    conv_out = jnp.einsum(
        "rgp,gpo->rgo", patches, group_weight, preferred_element_type=jnp.float32
    ).reshape(row_count, in_width)
    preact = conv_out * bn_gain + bn_shift
    hidden = jnp.maximum(preact, 0.0).astype(jnp.bfloat16)
    upstream = out_grad.reshape(row_count, out_width)
    back_grad = jnp.einsum("ro,co->rc", upstream, proj_weight, preferred_element_type=jnp.float32)
    grad_pre = (
        jnp.where(preact > 0.0, back_grad * bn_gain, 0.0)
        .astype(jnp.bfloat16)
        .reshape(row_count, groups, group_width)
    )
    proj_part = jnp.einsum("rc,ro->co", hidden, upstream, preferred_element_type=jnp.float32)
    group_part = jnp.einsum("rgp,rgo->gpo", patches, grad_pre, preferred_element_type=jnp.float32)
    out_part = jnp.einsum("rga,rgb->gab", grad_pre, grad_pre, preferred_element_type=jnp.float32)
    in_part = jnp.einsum("rgp,rgq->gpq", patches, patches, preferred_element_type=jnp.float32)
    total_rows = row_count * lax.axis_size("owner") * lax.axis_size("dp")
    grad_scale = 1.0 / math.sqrt(total_rows)
    mean_scale = 1.0 / total_rows
    group_sum, proj_sum, out_sum = lax.psum((group_part, proj_part, out_part), ("owner", "dp"))
    factor_blocks = in_part.reshape(groups * 3, patch_len // 3, patch_len)
    block_part = lax.psum_scatter(factor_blocks, "dp", scatter_dimension=1, tiled=True)
    slotted = pick_slots(block_part, slot_block)
    owned = lax.psum_scatter(slotted, "owner", scatter_dimension=0, tiled=True)
    return (group_sum * grad_scale, proj_sum * grad_scale, out_sum * mean_scale, owned * mean_scale)


def solution(mesh):
    placed = (
        P(("owner", "dp"), None, None, None),
        P(("owner", "dp"), None, None, None),
        P(),
        P(),
        P(),
        P(),
        P(),
    )
    return jax.shard_map(
        per_device,
        mesh=mesh,
        in_specs=placed,
        out_specs=(P(), P(), P(), P("owner", "dp", None)),
        check_vma=False,
    )
```

profile of v0, /device:TPU:0, one launch (start us, length us, event | category | flops | bytes accessed | tf_op | source)
XLA Modules:
  0.0 275.3 jit_solution(1473913675037735070)
XLA Ops:
  8.0 0.0 copy-start
  8.0 0.0 reduce-scatter.3.cloned.1.call-start
  8.1 1.0 pad.4
  9.1 0.5 reshape.79
  9.6 0.1 fusion.9
  9.7 0.1 fusion.8
  9.8 0.1 fusion.7
  9.9 0.1 fusion.6
  10.0 0.1 fusion.5
  10.1 0.1 fusion.4
  10.2 0.1 fusion.3
  10.3 0.1 fusion.2
  10.4 11.1 %copy.47 = bf16[2,8,8,16,9,32]{5,4,3,2,1,0:T(8,128)(2,1)} copy(bf16[2,8,8,16,9,32]{5,3,2,1,0,4:T(8,128)(2,1)S(1)} %fusion.2) | data formatting | bytes 2359296 | tf_op jit(solution)/shard_map/stack | solution.py:28
  21.5 8.8 %reshape.80 = bf16[128,16,288]{2,1,0:T(8,128)(2,1)S(1)} reshape(bf16[2,8,8,16,9,32]{5,4,3,2,1,0:T(8,128)(2,1)} %copy.47) | data formatting | bytes 2359296 | tf_op jit(solution)/shard_map/reshape | solution.py:28
  30.3 1.1 copy.51
  31.4 1.1 fusion.18
  32.5 7.0 %copy.54 = f32[48,96,288]{2,0,1:T(8,128)} copy(f32[48,96,288]{2,1,0:T(8,128)S(1)} %bitcast.64) | data formatting | bytes 10616832 | tf_op jit(solution)/shard_map/reshape | solution.py:49
  39.5 0.0 copy-start.3
  39.5 0.0 copy-start.4
  39.5 0.0 copy-start.2
  39.5 0.0 copy-start.1
  39.5 0.0 reduce-scatter.3.cloned.1.call-update
  39.5 0.0 all-reduce.4.cloned.1.call-start
  39.6 0.6 copy-done.3
  40.2 0.1 add.50
  40.2 0.0 copy-done.4
  40.2 0.1 mul.58
  40.3 0.2 copy-done.2
  40.5 0.0 copy-start.5
  40.5 0.4 fusion.13
  40.9 0.1 copy.49
  41.0 0.0 copy-done
  41.0 0.0 copy-done.1
  41.0 0.3 fusion.1
  41.4 0.1 copy.50
  41.5 0.9 fusion.17
  42.4 1.3 fusion.16
  43.6 1.4 fusion.15
  45.0 0.0 all-reduce.4.cloned.1.call-update
  45.0 0.0 reduce-scatter.5.cloned.1.call-start
  45.1 0.0 copy-done.5
  45.1 0.1 min.18
  45.2 0.1 min.16
  45.3 0.1 reshape.85
  45.4 134.8 %reduce-scatter.3.cloned.1.call-done = f32[48,12,288]{2,0,1:T(8,128)} async-done(((f32[48,96,288]{2,0,1:T(8,128)}), f32[48,12,288]{2,0,1:T(8,128)}) %reduce-scatter.3.cloned.1.call-update) | async-done | bytes 663568 | tf_op jit(solution)/shard_map/reduce_scatter | solution.py:50
  180.2 1.5 copy.55
  181.7 2.2 gather_fusion
  183.9 3.4 %select_multiply_fusion = f32[96,12,288]{2,1,0:T(8,128)} fusion(f32[96,12,288]{2,1,0:T(8,128)} %gather_fusion, f32[96]{0:T(128)S(1)} %reshape.85, pred[96]{0:T(512)(128)(4,1)S(1)} %compare_and_fusion), kind=kLoop, calls=%fused_computation.1 | loop fusion | flops 663552 | bytes 2654688 | tf_op jit(solution)/shard_map/mul | solution.py:12
  187.2 0.0 reduce-scatter.5.cloned.1.call-update
  187.2 72.6 %all-reduce.4.cloned.1.call-done = (f32[16,288,32]{1,2,0:T(8,128)}, f32[512,512]{1,0:T(8,128)}, f32[16,32,32]{2,1,0:T(8,128)}) async-done(((f32[16,288,32]{1,2,0:T(8,128)}, f32[512,512]{1,0:T(8,128)}, f32[16,32,32]{2,1,0:T(8,128)}), (f32[16,288,32]{1,2,0:T(8,128)}, f32[512,512]{1,0:T(8,128)}, f32[16,32,32]{2,1,0:T(8,128)})) %all-reduce.4.cloned.1.call-update) | async-done | bytes 1703952 | tf_op jit(solution)/shard_map/psum | solution.py:48
  259.8 1.7 broadcast_multiply_fusion.3
  261.5 2.1 broadcast_multiply_fusion.1
  263.6 2.3 broadcast_multiply_fusion
  265.9 0.0 reduce-scatter.5.cloned.1.call-done
  265.9 1.1 broadcast_multiply_fusion.2
  267.0 0.9 copy.56
  (6 shorter events, 0.1 us)
Async XLA Ops:
  8.0 33.0 %copy-start = (bf16[512,512]{1,0:T(8,128)(2,1)S(1)}, bf16[512,512]{1,0:T(8,128)(2,1)}, u32[]{:S(2)}) copy-start(bf16[512,512]{1,0:T(8,128)(2,1)} %param.10) | copy-start | bytes 1572868
  8.0 172.2 %reduce-scatter.3.cloned.1.call-start = ((), (), s32[]{:S(2)}) async-start(), calls=%async_computation.2 | async-start | bytes 7962624 | tf_op jit(solution)/shard_map/reduce_scatter | solution.py:50
  39.5 0.7 copy-start.3
  39.5 0.8 copy-start.4
  39.5 1.0 copy-start.2
  39.5 1.5 copy-start.1
  39.5 220.3 %all-reduce.4.cloned.1.call-start = ((), (), s32[]{:S(2)}) async-start(), calls=%async_computation.4 | async-start | bytes 4194304 | tf_op jit(solution)/shard_map/psum | solution.py:48
  40.5 4.6 %copy-start.5 = (s32[4,24]{1,0:T(4,128)S(1)}, s32[4,24]{1,0:T(4,128)}, u32[]{:S(2)}) copy-start(s32[4,24]{1,0:T(4,128)} %param.13) | copy-start | bytes 1156
  45.0 220.8 %reduce-scatter.5.cloned.1.call-start = ((), (), s32[]{:S(2)}) async-start(), calls=%async_computation.3 | async-start | bytes 2949120 | tf_op jit(solution)/shard_map/reduce_scatter | solution.py:52
Sparse Core Ops, SparseCore 0:
  39.6 140.5 reduce-scatter.2
  187.4 32.3 reduce-scatter.4
Sparse Core Ops, SparseCore 1:
  46.2 213.6 all-reduce.3
where the time goes:
time: 276 us; the launch traced here: 275 us
  waiting for transfers between devices  207 us (75%)
  local copies, waits for them, and re-layouts  36.2 us (13%)
  between operations  15.7 us (6%)
  other arithmetic  10.5 us (4%)
  matrix products  5.27 us (2%)
    reduce_scatter x1, waiting for transfers between devices, per_device(): lax.psum_scatter(factor_blocks, 'dp', scatter_dimension=1, tiled=True)  135 us
    psum x1, waiting for transfers between devices, per_device(): lax.psum((group_part, proj_part, out_part), ('owner', 'dp'))  72.6 us
    another operation x2, local copies, waits for them, and re-layouts, per_device(): patches = jnp.stack(shifted, axis=4).reshape(row_count, groups, patch_len)  11.2 us
    reshape x2, local copies, waits for them, and re-layouts, per_device(): patches = jnp.stack(shifted, axis=4).reshape(row_count, groups, patch_len)  9.86 us
    reshape x1, local copies, waits for them, and re-layouts, per_device(): factor_blocks = in_part.reshape(groups * 3, patch_len // 3, patch_len)  7.02 us
  transfers between devices with their start and end apart: 3, of which 2 were waited for; matrix products, arithmetic and copies ran while one was open for 7% of the time, Pallas kernels for 0%

commit v1 on v0

v1 whole, which is shorter than its diff:
```python
import functools
import math

import jax
import jax.numpy as jnp
from jax import lax
from jax.experimental import pallas as pl
from jax.experimental.pallas import tpu as pltpu
from jax.sharding import PartitionSpec as P

AXES = ("owner", "dp")
F32 = jnp.float32
BF16 = jnp.bfloat16
VMEM_LIMIT = 48 * 1024 * 1024
PAIRS = ((0, 0), (0, 1), (0, 2), (1, 0), (1, 1), (2, 0), (2, 2))
SAME = {(1, 2): (0, 1), (2, 1): (1, 0)}


def whole_vmem():
    return pl.BlockSpec(memory_space=pltpu.VMEM)


def call(body, outs, scratch, *args):
    return pl.pallas_call(
        body,
        out_shape=[jax.ShapeDtypeStruct(shape, kind) for shape, kind in outs],
        in_specs=[whole_vmem() if a.dtype != jnp.int32 else pl.BlockSpec(memory_space=pltpu.SMEM) for a in args],
        out_specs=[whole_vmem() for _ in outs],
        scratch_shapes=scratch,
        compiler_params=pltpu.CompilerParams(vmem_limit_bytes=VMEM_LIMIT),
    )(*args)


def plane_id():
    owner, dp = lax.axis_index("owner"), lax.axis_index("dp")
    return (owner & 1) * 4 + ((owner >> 1) & 1) * 2 + (dp & 1)


def cell_id():
    return plane_id() * 4 + ((lax.axis_index("dp") >> 1) & 3)


def send_kernel(x_ref, *refs):
    out_refs, held = refs[:-1], refs[-1]
    me = plane_id()
    x_t = x_ref[...].astype(F32).reshape(128, 512).T
    for block in range(8):
        held[block ^ me] = x_t[64 * block : 64 * block + 64]
    for place, out in enumerate(out_refs):
        out[...] = held[place]


def shift_rows(value, row_step, col_step):
    images, side, _, width = value.shape
    if col_step != 0:
        flat = value.reshape(images * side, side, width)
        flat = pltpu.roll(flat, (-col_step) % side, 1)
        column = lax.broadcasted_iota(jnp.int32, flat.shape, 1) + col_step
        value = jnp.where((column >= 0) & (column < side), flat, 0.0).reshape(value.shape)
    if row_step != 0:
        edge = jnp.zeros((images, 1, side, width), F32)
        if row_step < 0:
            value = jnp.concatenate([edge, value[:, :-1]], axis=1)
        else:
            value = jnp.concatenate([value[:, 1:], edge], axis=1)
    return value


def diagonal(square):
    lane = lax.broadcasted_iota(jnp.int32, (32, 128), 1)
    out = square[96:128]
    for g in (2, 1, 0):
        out = jnp.where(lane < 32 * (g + 1), square[32 * g : 32 * g + 32], out)
    return out


def local_kernel(x_ref, og_ref, gw_ref, pw_ref, gain_ref, shift_ref, mine_ref, other_ref, block_w, hid_t, sums):
    me = cell_id()
    images = x_ref.shape[0]
    rows = images * 64
    spot_row = lax.broadcasted_iota(jnp.int32, (32, 128), 0)
    spot_lane = lax.broadcasted_iota(jnp.int32, (32, 128), 1)
    for g in range(16):
        place = (spot_lane == spot_row + 32 * (g % 4)).astype(F32).astype(BF16)
        spread = jnp.dot(gw_ref[g], place, preferred_element_type=F32).astype(BF16)
        for s in range(9):
            at = s * 128 + 32 * (g % 4)
            block_w[g // 4, at : at + 32, :] = spread[32 * s : 32 * s + 32]
    x = x_ref[...].astype(F32)
    moved = [
        shift_rows(x, a - 1, b - 1).reshape(rows, 512).astype(BF16) for a in range(3) for b in range(3)
    ]
    conv = []
    for q in range(4):
        lhs = jnp.concatenate([m[:, 128 * q : 128 * q + 128] for m in moved], axis=1)
        conv.append(jnp.dot(lhs, block_w[q], preferred_element_type=F32))
    conv = jnp.concatenate(conv, axis=1)
    gain = gain_ref[...]
    preact = conv * gain + shift_ref[...]
    hidden = jnp.maximum(preact, 0.0)
    og = og_ref[...].reshape(rows, 512)
    back = lax.dot_general(og, pw_ref[...], (((1,), (1,)), ((), ())), preferred_element_type=F32)
    grad = jnp.where(preact > 0.0, back * gain, 0.0).astype(BF16).astype(F32)
    h_t = hidden.T.astype(BF16)
    for j in range(32):
        hid_t[j ^ me] = h_t[16 * j : 16 * j + 16]
    for half, out in enumerate((mine_ref, other_ref)):
        lhs = hid_t[16 * half : 16 * half + 16].reshape(256, rows)
        part = jnp.dot(lhs, og, preferred_element_type=F32)
        for k in range(16):
            for w in range(4):
                out[k, 16 * w : 16 * w + 16, :] = part[16 * k : 16 * k + 16, 128 * w : 128 * w + 128]
    x_t = x.reshape(rows, 512).T.astype(BF16)
    g_t = grad.reshape(rows, 512).T.astype(BF16)
    grad4 = grad.reshape(images, 8, 8, 512)
    back_moved = [
        shift_rows(grad4, 1 - a, 1 - b).reshape(rows, 512).astype(BF16) for a in range(3) for b in range(3)
    ]
    for q in range(4):
        cut = slice(128 * q, 128 * q + 128)
        rhs = jnp.concatenate([m[:, cut] for m in back_moved], axis=1)
        part = jnp.dot(x_t[cut], rhs, preferred_element_type=F32)
        for s in range(9):
            at = 320 * q + 32 * s
            sums[at : at + 32, :] = diagonal(part[:, 128 * s : 128 * s + 128])
        part = jnp.dot(g_t[cut], back_moved[4][:, cut], preferred_element_type=F32)
        sums[320 * q + 288 : 320 * q + 320, :] = diagonal(part)
    for half, out in enumerate((mine_ref, other_ref)):
        for k in range(16):
            j = (16 * half + k) ^ me
            out[k, 64:104, :] = sums[pl.ds(pl.multiple_of(40 * j, 8), 40), :]


def factor_kernel(steps, *refs):
    parts, outs, (patches, held) = refs[:8], refs[8 : 8 + steps], refs[8 + steps :]
    me = lax.axis_index("dp") >> 1
    lane = lax.broadcasted_iota(jnp.int32, (64, 128), 1)
    row, col = (lane >> 3) & 7, lane & 7
    for src, ref in enumerate(parts):
        x_t = ref[...]
        for a in range(3):
            for b in range(3):
                step = (a - 1) * 8 + b - 1
                value = x_t if step == 0 else pltpu.roll(x_t, (-step) % 128, 1)
                keep = (row + a >= 1) & (row + a <= 8) & (col + b >= 1) & (col + b <= 8)
                value = jnp.where(keep, value, 0.0).astype(BF16)
                at = (3 * a + b) * 32
                patches[0, at : at + 32, 128 * src : 128 * src + 128] = value[:32]
                patches[1, at : at + 32, 128 * src : 128 * src + 128] = value[32:]
    pieces = []
    for g in range(2):
        for a, width in ((0, 288), (1, 192), (2, 288)):
            part = lax.dot_general(
                patches[g, 96 * a : 96 * a + 96, :],
                patches[g, :width, :],
                (((1,), (1,)), ((), ())),
                preferred_element_type=F32,
            )
            for pair in PAIRS:
                if pair[0] == a:
                    pieces.append(part[:, 96 * pair[1] : 96 * pair[1] + 96])
    full = jnp.concatenate(pieces, axis=1)
    size = 96 // steps
    for t in range(steps):
        held[t ^ me] = full[size * t : size * t + size]
    for t, out in enumerate(outs):
        out[...] = held[t]


def slots_kernel(scale, groups_of, slot_ref, *refs):
    parts, out_ref, held = refs[:8], refs[8], refs[9]
    me = plane_id()
    for place, ref in enumerate(parts):
        value = ref[...] * scale
        for g in range(2):
            for a in range(3):
                pieces = []
                for b in range(3):
                    at = 672 * g + 96 * PAIRS.index(SAME.get((a, b), (a, b)))
                    pieces.append(value[:, at : at + 96])
                held[6 * (place ^ me) + 3 * g + a] = jnp.concatenate(pieces, axis=1)
    owner = lax.axis_index("owner")
    for s in range(out_ref.shape[0]):
        block = slot_ref[owner, s]
        value = held[jnp.maximum(block, 0)]
        out_ref[s] = jnp.where(block >= 0, value, 0.0)


def unpack_kernel(grad_scale, mean_scale, *refs):
    parts, (group_ref, proj_ref, out_ref), sums = refs[:8], refs[8:11], refs[11]
    me = cell_id()
    for place, ref in enumerate(parts):
        for z in range(4):
            j = (4 * place + z) ^ me
            for w in range(4):
                at = pl.multiple_of(16 * j, 16)
                proj_ref[pl.ds(at, 16), 128 * w : 128 * w + 128] = ref[z, 16 * w : 16 * w + 16, :] * grad_scale
            sums[pl.ds(pl.multiple_of(40 * j, 8), 40), :] = ref[z, 64:104, :]
    for g in range(16):
        base, lanes = 320 * (g // 4), slice(32 * (g % 4), 32 * (g % 4) + 32)
        group_ref[g] = sums[base : base + 288, lanes] * grad_scale
        out_ref[g] = sums[base + 288 : base + 320, lanes] * mean_scale


def per_device(n_owner, n_dp, activations, out_grad, group_weight, proj_weight, bn_gain, bn_shift, slot_block):
    def swap(value, owner_mask, dp_mask):
        pairs = [
            (o * n_dp + d, (o ^ owner_mask) * n_dp + (d ^ dp_mask)) for o in range(n_owner) for d in range(n_dp)
        ]
        return lax.ppermute(value, AXES, pairs)

    def add_over(value, owner_bits, dp_bits):
        for bit in owner_bits:
            value = value + swap(value, 1 << bit, 0)
        for bit in dp_bits:
            value = value + swap(value, 0, 1 << bit)
        return value

    far_owner = range(2, n_owner.bit_length() - 1)
    far_dp = range(3, n_dp.bit_length() - 1)
    steps = n_dp // 2
    images = activations.shape[0]
    rows = images * 64
    total_rows = rows * n_owner * n_dp
    grad_scale = 1.0 / math.sqrt(total_rows)
    mean_scale = 1.0 / total_rows

    sent = call(send_kernel, [((64, 128), F32)] * 8, [pltpu.VMEM((8, 64, 128), F32)], activations)
    owner_of = lambda p: ((p >> 2) & 1) | (p & 2)
    got = [sent[0]] + [swap(sent[p], owner_of(p), p & 1) for p in range(1, 8)]

    mine, other = call(
        local_kernel,
        [((16, 104, 128), F32)] * 2,
        [
            pltpu.VMEM((4, 1152, 128), BF16),
            pltpu.VMEM((32, 16, rows), BF16),
            pltpu.VMEM((1280, 128), F32),
        ],
        activations,
        out_grad,
        group_weight,
        proj_weight,
        bn_gain.reshape(1, -1),
        bn_shift.reshape(1, -1),
    )
    total = mine + swap(other, 1, 0)
    total = total[0:4] + swap(total[4:8], 0, 1) + swap(total[8:12], 2, 0) + swap(total[12:16], 2, 1)
    total = total[0] + swap(total[1], 0, 2) + swap(total[2], 0, 4) + swap(total[3], 0, 6)
    total = add_over(total, far_owner, far_dp)
    total = jnp.stack([total] + [swap(total, 0, 2 * z) for z in range(1, 4)])
    near = [total] + [swap(total, 2 * (p >> 1), p & 1) for p in range(1, 4)]
    parts = near + [swap(v, 1, 0) for v in near]
    group_grad, proj_grad, out_factor = call(
        functools.partial(unpack_kernel, grad_scale, mean_scale),
        [((16, 288, 32), F32), ((512, 512), F32), ((16, 32, 32), F32)],
        [pltpu.VMEM((1280, 128), F32)],
        *parts,
    )

    size = 96 // steps
    pieces = call(
        functools.partial(factor_kernel, steps),
        [((size, 1344), F32)] * steps,
        [pltpu.VMEM((2, 288, 1024), BF16), pltpu.VMEM((steps, size, 1344), F32)],
        *got,
    )
    piece = pieces[0]
    for t in range(1, steps):
        piece = piece + swap(pieces[t], 0, 2 * t)
    piece = add_over(piece, far_owner, ())
    half = size // 2
    at = (lax.axis_index("dp") & 1) * half
    own = lax.dynamic_slice_in_dim(piece, at, half, 0)
    peer = lax.dynamic_slice_in_dim(piece, half - at, half, 0)
    near = [own, swap(peer, 0, 1), swap(own, 2, 0), swap(peer, 2, 1)]
    parts = near + [swap(v, 1, 0) for v in near]
    slots = slot_block.shape[1]
    (factor_owned,) = call(
        functools.partial(slots_kernel, mean_scale, 2),
        [((slots, half, 288), F32)],
        [pltpu.VMEM((48, half, 288), F32)],
        slot_block,
        *parts,
    )
    return group_grad, proj_grad, out_factor, factor_owned


def solution(mesh):
    placed = (P(AXES, None, None, None), P(AXES, None, None, None), P(), P(), P(), P(), P())
    return jax.shard_map(
        functools.partial(per_device, mesh.shape["owner"], mesh.shape["dp"]),
        mesh=mesh,
        in_specs=placed,
        out_specs=(P(), P(), P(), P("owner", "dp", None)),
        check_vma=False,
    )
```

time: 276 us -> 87.5 us (0.32)
  waiting for transfers between devices: 207 us -> 32 us
  starting transfers between devices: 0.12 us -> 40 us
  local copies, waits for them, and re-layouts: 36.2 us -> 8.44 us
  between operations: 15.7 us -> 0.78 us
  other arithmetic: 10.5 us -> 0.23 us
  Pallas kernels: 0 us -> 5.77 us
  matrix products: 5.27 us -> 0 us
    reduce_scatter x2 -> x0, waiting for transfers between devices: 135 us -> none  [the longest x1 135 us: per_device(): lax.psum_scatter(factor_blocks, 'dp', scatter_dimension=1, tiled=True)]
    psum x1 -> x0, waiting for transfers between devices: 72.6 us -> none  [per_device(): lax.psum((group_part, proj_part, out_part), ('owner', 'dp'))]
    ppermute x0 -> x34, starting transfers between devices: none -> 40 us  [swap(): return lax.ppermute(value, AXES, pairs)]
    ppermute x0 -> x34, waiting for transfers between devices: none -> 32 us  [swap(): return lax.ppermute(value, AXES, pairs)]
    reshape x5 -> x0, local copies, waits for them, and re-layouts: 17.5 us -> none  [the longest x2 9.86 us: per_device(): patches = jnp.stack(shifted, axis=4).reshape(row_count, groups, patch_len)]
    another operation x2 -> x0, local copies, waits for them, and re-layouts: 11.2 us -> none  [per_device(): patches = jnp.stack(shifted, axis=4).reshape(row_count, groups, patch_len)]
    mul x5 -> x0, other arithmetic: 10.5 us -> none  [the longest x1 3.36 us: pick_slots(): return picked * (flat_slots >= 0).astype(jnp.float32)[:, None, None]]
    unnamed x21 -> x15, local copies, waits for them, and re-layouts: 2.36 us -> 8.36 us
  transfers between devices with their start and end apart: 3 -> 34, of which waited for: 2 -> 14; matrix products, arithmetic and copies ran while one was open for 7% -> 1% of each run, Pallas kernels for 0% -> 3%
where the time goes in v1:
time: 87.5 us; the launch traced here: 87.2 us
  starting transfers between devices  40 us (46%)
  waiting for transfers between devices  32 us (37%)
  local copies, waits for them, and re-layouts  8.44 us (10%)
  Pallas kernels  5.77 us (7%)
    ppermute x34, starting transfers between devices, swap(): return lax.ppermute(value, AXES, pairs)  40 us
    ppermute x34, waiting for transfers between devices, swap(): return lax.ppermute(value, AXES, pairs)  32 us
    unnamed x15, local copies, waits for them, and re-layouts  8.36 us
    pallas_call x5, Pallas kernels, call(): pl.pallas_call(body, out_shape=[jax.ShapeDtypeStruct(shape, kind) for sha...  5.77 us
  transfers between devices with their start and end apart: 34, of which 14 were waited for; matrix products, arithmetic and copies ran while one was open for 1% of the time, Pallas kernels for 3%

profile of v1, /device:TPU:0, one launch (start us, length us, event | category | flops | bytes accessed | tf_op | source)
XLA Modules:
  0.0 87.2 jit_solution(11659152407281736432)
XLA Ops:
  0.6 1.5 %copy.11.gw_ref = bf16[16,288,32]{2,1,0:T(8,128)(2,1)S(1)} copy(bf16[16,288,32]{1,2,0:T(8,128)(2,1)} %param.9) | data formatting | bytes 589824 | tf_op args[2]
  2.2 0.0 copy-start
  2.2 1.0 %copy-done = bf16[512,512]{1,0:T(8,128)(2,1)S(1)} copy-done((bf16[512,512]{1,0:T(8,128)(2,1)S(1)}, bf16[512,512]{1,0:T(8,128)(2,1)}, u32[]{:S(2)}) %copy-start) | copy-done | bytes 524312
  3.2 0.9 %copy-done.1 = bf16[2,8,8,512]{3,2,1,0:T(8,128)(2,1)S(1)} copy-done((bf16[2,8,8,512]{3,2,1,0:T(8,128)(2,1)S(1)}, bf16[2,8,8,512]{3,2,1,0:T(8,128)(2,1)}, u32[]{:S(2)}) %copy-start.1) | copy-done | bytes 131096
  4.1 0.9 %copy-done.2 = bf16[2,8,8,512]{3,2,1,0:T(8,128)(2,1)S(1)} copy-done((bf16[2,8,8,512]{3,2,1,0:T(8,128)(2,1)S(1)}, bf16[2,8,8,512]{3,2,1,0:T(8,128)(2,1)}, u32[]{:S(2)}) %copy-start.2) | copy-done | bytes 131096
  5.0 0.7 copy-done.4
  5.7 0.7 copy-done.5
  6.4 1.6 %shard_map.102 = (f32[16,104,128]{2,1,0:T(8,128)S(1)}, f32[16,104,128]{2,1,0:T(8,128)S(1)}) custom-call(bf16[2,8,8,512]{3,2,1,0:T(8,128)(2,1)S(1)} %copy-done.1, bf16[2,8,8,512]{3,2,1,0:T(8,128)(2,1)S(1)} %copy-done.2, bf16[16,288,32]{2,1,0:T(8,128)(2,1)S(1)} %copy.11.gw_ref, bf16[512,512]{1,0:T(8,128)(2,1)S(1)} %copy-done, f32[1,512]{1,0:T(1,128)S(1)} %bitcast.20, ...), custom_call_target="tpu_custom_call" | custom-call | tf_op jit(solution)/shard_map/pallas_call | solution.py:24
  7.9 0.5 collective-permute-start
  8.5 2.0 %collective-permute-done = f32[16,104,128]{2,1,0:T(8,128)S(1)} collective-permute-done((f32[16,104,128]{2,1,0:T(8,128)S(1)}, f32[16,104,128]{2,1,0:T(8,128)S(1)}, u32[]{:S(2)}, u32[]{:S(2)}) %collective-permute-start) | collective-permute-done | bytes 852000 | tf_op jit(solution)/shard_map/ppermute | solution.py:210
  10.5 0.1 add.37
  10.6 0.0 copy-start.3
  10.7 3.9 %collective-permute-start.3 = (f32[4,104,128]{2,1,0:T(8,128)S(1)}, f32[4,104,128]{2,1,0:T(8,128)S(1)}, u32[]{:S(2)}, u32[]{:S(2)}) collective-permute-start(f32[4,104,128]{2,1,0:T(8,128)S(1)} %get-tuple-element.43), channel_id=1, source_target_pairs={{0,17},{1,16},{2,19},{3,18},{4,21},{5,20},{6,23},{7,22},{8,25},{9,... | collective-permute-start | bytes 638984 | tf_op jit(solution)/shard_map/ppermute | solution.py:210
  14.5 0.5 collective-permute-start.2
  15.0 0.1 collective-permute-start.1
  15.2 0.1 shard_map.104
  15.3 2.0 %collective-permute-start.17 = (f32[64,128]{1,0:T(8,128)S(1)}, f32[64,128]{1,0:T(8,128)S(1)}, u32[]{:S(2)}, u32[]{:S(2)}) collective-permute-start(f32[64,128]{1,0:T(8,128)S(1)} %get-tuple-element.27), channel_id=1, source_target_pairs={{0,1},{1,0},{2,3},{3,2},{4,5},{5,4},{6,7},{7,6},{8,9},{9,8},{10,11... | collective-permute-start | bytes 98312 | tf_op jit(solution)/shard_map/ppermute | solution.py:210
  17.3 1.5 %collective-permute-start.18 = (f32[64,128]{1,0:T(8,128)S(1)}, f32[64,128]{1,0:T(8,128)S(1)}, u32[]{:S(2)}, u32[]{:S(2)}) collective-permute-start(f32[64,128]{1,0:T(8,128)S(1)} %get-tuple-element.28), channel_id=1, source_target_pairs={{0,16},{1,17},{2,18},{3,19},{4,20},{5,21},{6,22},{7,23},{8,24},{9,... | collective-permute-start | bytes 98312 | tf_op jit(solution)/shard_map/ppermute | solution.py:210
  18.8 1.8 %collective-permute-done.3 = f32[4,104,128]{2,1,0:T(8,128)S(1)} collective-permute-done((f32[4,104,128]{2,1,0:T(8,128)S(1)}, f32[4,104,128]{2,1,0:T(8,128)S(1)}, u32[]{:S(2)}, u32[]{:S(2)}) %collective-permute-start.3) | collective-permute-done | bytes 213024 | tf_op jit(solution)/shard_map/ppermute | solution.py:210
  20.6 3.0 %collective-permute-start.19 = (f32[64,128]{1,0:T(8,128)S(1)}, f32[64,128]{1,0:T(8,128)S(1)}, u32[]{:S(2)}, u32[]{:S(2)}) collective-permute-start(f32[64,128]{1,0:T(8,128)S(1)} %get-tuple-element.29), channel_id=1, source_target_pairs={{0,17},{1,16},{2,19},{3,18},{4,21},{5,20},{6,23},{7,22},{8,25},{9,... | collective-permute-start | bytes 98312 | tf_op jit(solution)/shard_map/ppermute | solution.py:210
  23.6 1.2 %collective-permute-done.2 = f32[4,104,128]{2,1,0:T(8,128)S(1)} collective-permute-done((f32[4,104,128]{2,1,0:T(8,128)S(1)}, f32[4,104,128]{2,1,0:T(8,128)S(1)}, u32[]{:S(2)}, u32[]{:S(2)}) %collective-permute-start.2) | collective-permute-done | bytes 213024 | tf_op jit(solution)/shard_map/ppermute | solution.py:210
  24.7 0.0 collective-permute-start.20
  24.7 0.9 %collective-permute-done.1 = f32[4,104,128]{2,1,0:T(8,128)S(1)} collective-permute-done((f32[4,104,128]{2,1,0:T(8,128)S(1)}, f32[4,104,128]{2,1,0:T(8,128)S(1)}, u32[]{:S(2)}, u32[]{:S(2)}) %collective-permute-start.1) | collective-permute-done | bytes 213024 | tf_op jit(solution)/shard_map/ppermute | solution.py:210
  25.6 1.1 %collective-permute-start.21 = (f32[64,128]{1,0:T(8,128)S(1)}, f32[64,128]{1,0:T(8,128)S(1)}, u32[]{:S(2)}, u32[]{:S(2)}) collective-permute-start(f32[64,128]{1,0:T(8,128)S(1)} %get-tuple-element.31), channel_id=1, source_target_pairs={{0,9},{1,8},{2,11},{3,10},{4,13},{5,12},{6,15},{7,14},{8,1},{9,0},... | collective-permute-start | bytes 98312 | tf_op jit(solution)/shard_map/ppermute | solution.py:210
  26.8 3.7 %collective-permute-start.6 = (f32[104,128]{1,0:T(8,128)S(1)}, f32[104,128]{1,0:T(8,128)S(1)}, u32[]{:S(2)}, u32[]{:S(2)}) collective-permute-start(f32[104,128]{1,0:T(8,128)S(1)} %get-tuple-element.46), channel_id=1, source_target_pairs={{0,6},{1,7},{2,4},{3,5},{4,2},{5,3},{6,0},{7,1},{8,14},{9,15},{10,... | collective-permute-start | bytes 159752 | tf_op jit(solution)/shard_map/ppermute | solution.py:210
  30.4 0.0 collective-permute-start.5
  30.4 0.0 collective-permute-done.19.refs_3_
  30.5 0.8 collective-permute-start.4
  31.2 0.0 collective-permute-done.20.refs_4_
  31.2 1.8 %collective-permute-start.23 = (f32[64,128]{1,0:T(8,128)S(1)}, f32[64,128]{1,0:T(8,128)S(1)}, u32[]{:S(2)}, u32[]{:S(2)}) collective-permute-start(f32[64,128]{1,0:T(8,128)S(1)} %get-tuple-element.33), channel_id=1, source_target_pairs={{0,25},{1,24},{2,27},{3,26},{4,29},{5,28},{6,31},{7,30},{8,17},{9,... | collective-permute-start | bytes 98312 | tf_op jit(solution)/shard_map/ppermute | solution.py:210
  33.1 1.8 %collective-permute-done.22.refs_6_ = f32[64,128]{1,0:T(8,128)S(1)} collective-permute-done((f32[64,128]{1,0:T(8,128)S(1)}, f32[64,128]{1,0:T(8,128)S(1)}, u32[]{:S(2)}, u32[]{:S(2)}) %collective-permute-start.22) | collective-permute-done | bytes 32800 | tf_op jit(solution)/shard_map/ppermute | solution.py:210
  34.9 0.7 collective-permute-done.23.refs_7_
  35.5 1.4 %shard_map.105 = (f32[24,1344]{1,0:T(8,128)S(1)}, f32[24,1344]{1,0:T(8,128)S(1)}, f32[24,1344]{1,0:T(8,128)S(1)}, f32[24,1344]{1,0:T(8,128)S(1)}) custom-call(f32[64,128]{1,0:T(8,128)S(1)} %get-tuple-element.26.refs_0_, f32[64,128]{1,0:T(8,128)S(1)} %collective-permute-done.17.refs_1_, f32[64,128]{1,0:T(8,128)S(1)} %collective-permute-done.18.refs_2_, ...), custom_call_target="tpu_custom_call" | custom-call | tf_op jit(solution)/shard_map/pallas_call | solution.py:24
  36.9 3.7 %collective-permute-start.26 = (f32[24,1344]{1,0:T(8,128)S(1)}, f32[24,1344]{1,0:T(8,128)S(1)}, u32[]{:S(2)}, u32[]{:S(2)}) collective-permute-start(f32[24,1344]{1,0:T(8,128)S(1)} %get-tuple-element.37), channel_id=1, source_target_pairs={{0,6},{1,7},{2,4},{3,5},{4,2},{5,3},{6,0},{7,1},{8,14},{9,15},{10,... | collective-permute-start | bytes 387080 | tf_op jit(solution)/shard_map/ppermute | solution.py:210
  40.6 0.0 collective-permute-done.6
  40.6 0.8 collective-permute-start.24
  41.4 0.0 collective-permute-done.5
  41.4 0.0 collective-permute-done.4
  41.4 3.7 %collective-permute-start.9 = (f32[104,128]{1,0:T(8,128)S(1)}, f32[104,128]{1,0:T(8,128)S(1)}, u32[]{:S(2)}, u32[]{:S(2)}) collective-permute-start(f32[104,128]{1,0:T(8,128)S(1)} %fusion.4), channel_id=1, source_target_pairs={{0,6},{1,7},{2,4},{3,5},{4,2},{5,3},{6,0},{7,1},{8,14},{9,15},{10,... | collective-permute-start | bytes 159752 | tf_op jit(solution)/shard_map/ppermute | solution.py:210
  45.1 0.3 collective-permute-done.26
  45.4 5.2 %collective-permute-start.7 = (f32[104,128]{1,0:T(8,128)S(1)}, f32[104,128]{1,0:T(8,128)S(1)}, u32[]{:S(2)}, u32[]{:S(2)}) collective-permute-start(f32[104,128]{1,0:T(8,128)S(1)} %fusion.4), channel_id=1, source_target_pairs={{0,2},{1,3},{2,0},{3,1},{4,6},{5,7},{6,4},{7,5},{8,10},{9,11},{10,... | collective-permute-start | bytes 159752 | tf_op jit(solution)/shard_map/ppermute | solution.py:210
  50.6 4.6 %collective-permute-done.25 = f32[24,1344]{1,0:T(8,128)S(1)} collective-permute-done((f32[24,1344]{1,0:T(8,128)S(1)}, f32[24,1344]{1,0:T(8,128)S(1)}, u32[]{:S(2)}, u32[]{:S(2)}) %collective-permute-start.25) | collective-permute-done | bytes 129056 | tf_op jit(solution)/shard_map/ppermute | solution.py:210
  55.3 2.2 %collective-permute-done.8 = f32[104,128]{1,0:T(8,128)S(1)} collective-permute-done((f32[104,128]{1,0:T(8,128)S(1)}, f32[104,128]{1,0:T(8,128)S(1)}, u32[]{:S(2)}, u32[]{:S(2)}) %collective-permute-start.8) | collective-permute-done | bytes 53280 | tf_op jit(solution)/shard_map/ppermute | solution.py:210
  57.5 1.0 %collective-permute-start.10 = (f32[4,104,128]{2,1,0:T(8,128)S(1)}, f32[4,104,128]{2,1,0:T(8,128)S(1)}, u32[]{:S(2)}, u32[]{:S(2)}) collective-permute-start(f32[4,104,128]{2,1,0:T(8,128)S(1)} %pad_maximum_fusion.refs_0_), channel_id=1, source_target_pairs={{0,1},{1,0},{2,3},{3,2},{4,5},{5,4},{6,7},{7,6},{8,9},{9,8},{10,11... | collective-permute-start | bytes 638984 | tf_op jit(solution)/shard_map/ppermute | solution.py:210
  58.5 0.8 collective-permute-start.11
  59.3 1.7 %collective-permute-start.12 = (f32[4,104,128]{2,1,0:T(8,128)S(1)}, f32[4,104,128]{2,1,0:T(8,128)S(1)}, u32[]{:S(2)}, u32[]{:S(2)}) collective-permute-start(f32[4,104,128]{2,1,0:T(8,128)S(1)} %pad_maximum_fusion.refs_0_), channel_id=1, source_target_pairs={{0,17},{1,16},{2,19},{3,18},{4,21},{5,20},{6,23},{7,22},{8,25},{9,... | collective-permute-start | bytes 638984 | tf_op jit(solution)/shard_map/ppermute | solution.py:210
  61.1 1.0 %collective-permute-start.27 = (f32[12,1344]{1,0:T(8,128)S(1)}, f32[12,1344]{1,0:T(8,128)S(1)}, u32[]{:S(2)}, u32[]{:S(2)}) collective-permute-start(f32[12,1344]{1,0:T(8,128)S(1)} %get-tuple-element.48), channel_id=1, source_target_pairs={{0,1},{1,0},{2,3},{3,2},{4,5},{5,4},{6,7},{7,6},{8,9},{9,8},{10,11... | collective-permute-start | bytes 193544 | tf_op jit(solution)/shard_map/ppermute | solution.py:210
  62.1 0.8 collective-permute-start.28
  62.9 8.4 %collective-permute-done.27.refs_1_ = f32[12,1344]{1,0:T(8,128)S(1)} collective-permute-done((f32[12,1344]{1,0:T(8,128)S(1)}, f32[12,1344]{1,0:T(8,128)S(1)}, u32[]{:S(2)}, u32[]{:S(2)}) %collective-permute-start.27) | collective-permute-done | bytes 64544 | tf_op jit(solution)/shard_map/ppermute | solution.py:210
  71.3 0.9 %collective-permute-start.29 = (f32[12,1344]{1,0:T(8,128)S(1)}, f32[12,1344]{1,0:T(8,128)S(1)}, u32[]{:S(2)}, u32[]{:S(2)}) collective-permute-start(f32[12,1344]{1,0:T(8,128)S(1)} %get-tuple-element.48), channel_id=1, source_target_pairs={{0,17},{1,16},{2,19},{3,18},{4,21},{5,20},{6,23},{7,22},{8,25},{9,... | collective-permute-start | bytes 193544 | tf_op jit(solution)/shard_map/ppermute | solution.py:210
  72.2 4.5 %collective-permute-done.29.refs_3_ = f32[12,1344]{1,0:T(8,128)S(1)} collective-permute-done((f32[12,1344]{1,0:T(8,128)S(1)}, f32[12,1344]{1,0:T(8,128)S(1)}, u32[]{:S(2)}, u32[]{:S(2)}) %collective-permute-start.29) | collective-permute-done | bytes 64544 | tf_op jit(solution)/shard_map/ppermute | solution.py:210
  76.7 0.5 collective-permute-start.14
  77.2 0.1 collective-permute-start.15
  77.3 0.4 collective-permute-start.16
  77.8 0.1 collective-permute-start.31
  77.8 1.4 %collective-permute-done.31.refs_5_ = f32[12,1344]{1,0:T(8,128)S(1)} collective-permute-done((f32[12,1344]{1,0:T(8,128)S(1)}, f32[12,1344]{1,0:T(8,128)S(1)}, u32[]{:S(2)}, u32[]{:S(2)}) %collective-permute-start.31) | collective-permute-done | bytes 64544 | tf_op jit(solution)/shard_map/ppermute | solution.py:210
  79.2 0.2 collective-permute-start.32
  79.4 1.1 %collective-permute-done.32.refs_6_ = f32[12,1344]{1,0:T(8,128)S(1)} collective-permute-done((f32[12,1344]{1,0:T(8,128)S(1)}, f32[12,1344]{1,0:T(8,128)S(1)}, u32[]{:S(2)}, u32[]{:S(2)}) %collective-permute-start.32) | collective-permute-done | bytes 64544 | tf_op jit(solution)/shard_map/ppermute | solution.py:210
  80.5 0.2 collective-permute-start.33
  80.7 1.1 %collective-permute-done.33.refs_7_ = f32[12,1344]{1,0:T(8,128)S(1)} collective-permute-done((f32[12,1344]{1,0:T(8,128)S(1)}, f32[12,1344]{1,0:T(8,128)S(1)}, u32[]{:S(2)}, u32[]{:S(2)}) %collective-permute-start.33) | collective-permute-done | bytes 64544 | tf_op jit(solution)/shard_map/ppermute | solution.py:210
  81.8 1.0 %shard_map.106 = f32[24,12,288]{2,1,0:T(8,128)S(1)} custom-call(s32[4,24]{1,0:T(4,128)S(1)} %copy-done.3, f32[12,1344]{1,0:T(8,128)S(1)} %get-tuple-element.49.refs_0_, f32[12,1344]{1,0:T(8,128)S(1)} %collective-permute-done.27.refs_1_, f32[12,1344]{1,0:T(8,128)S(1)} %collective-permute-done.28.refs_2_, f32[12,1344]{1,0:T(8,128)S(1)} %collective-permute-done.29.refs_3_, ...), custom_call_target="tpu_custom_call" | custom-call | tf_op jit(solution)/shard_map/pallas_call | solution.py:24
  82.8 0.9 %copy.13 = f32[24,12,288]{2,0,1:T(8,128)} copy(f32[24,12,288]{2,1,0:T(8,128)S(1)} %shard_map.106) | data formatting | bytes 663552
  83.7 1.7 %shard_map.103 = (f32[16,288,32]{2,1,0:T(8,128)S(1)}, f32[512,512]{1,0:T(8,128)}, f32[16,32,32]{2,1,0:T(8,128)}) custom-call(f32[4,104,128]{2,1,0:T(8,128)S(1)} %pad_maximum_fusion.refs_0_, f32[4,104,128]{2,1,0:T(8,128)S(1)} %collective-permute-done.10.refs_1_, f32[4,104,128]{2,1,0:T(8,128)S(1)} %collective-permute-done.11.refs_2_, ...), custom_call_target="tpu_custom_call" | custom-call | tf_op jit(solution)/shard_map/pallas_call | solution.py:24
  85.5 1.7 %copy.12 = f32[16,288,32]{1,2,0:T(8,128)} copy(f32[16,288,32]{2,1,0:T(8,128)S(1)} %get-tuple-element.38) | data formatting | bytes 1179648
  (32 shorter events, 0.3 us)
Async XLA Ops:
  2.2 1.0 %copy-start = (bf16[512,512]{1,0:T(8,128)(2,1)S(1)}, bf16[512,512]{1,0:T(8,128)(2,1)}, u32[]{:S(2)}) copy-start(bf16[512,512]{1,0:T(8,128)(2,1)} %pw_ref.1) | copy-start | bytes 1572868
  3.2 0.9 %copy-start.1 = (bf16[2,8,8,512]{3,2,1,0:T(8,128)(2,1)S(1)}, bf16[2,8,8,512]{3,2,1,0:T(8,128)(2,1)}, u32[]{:S(2)}) copy-start(bf16[2,8,8,512]{3,2,1,0:T(8,128)(2,1)} %x_ref.3) | copy-start | bytes 393220
  4.1 0.9 %copy-start.2 = (bf16[2,8,8,512]{3,2,1,0:T(8,128)(2,1)S(1)}, bf16[2,8,8,512]{3,2,1,0:T(8,128)(2,1)}, u32[]{:S(2)}) copy-start(bf16[2,8,8,512]{3,2,1,0:T(8,128)(2,1)} %og_ref.1) | copy-start | bytes 393220
  5.0 0.7 copy-start.4
  5.7 0.7 copy-start.5
  7.9 2.5 %collective-permute-start = (f32[16,104,128]{2,1,0:T(8,128)S(1)}, f32[16,104,128]{2,1,0:T(8,128)S(1)}, u32[]{:S(2)}, u32[]{:S(2)}) collective-permute-start(f32[16,104,128]{2,1,0:T(8,128)S(1)} %get-tuple-element.22), channel_id=1, source_target_pairs={{0,8},{1,9},{2,10},{3,11},{4,12},{5,13},{6,14},{7,15},{8,0},{9,1},... | collective-permute-start | bytes 2555912 | tf_op jit(solution)/shard_map/ppermute | solution.py:210
  10.6 71.2 %copy-start.3 = (s32[4,24]{1,0:T(4,128)S(1)}, s32[4,24]{1,0:T(4,128)}, u32[]{:S(2)}) copy-start(s32[4,24]{1,0:T(4,128)} %slot_ref.1) | copy-start | bytes 1156
  10.7 10.0 %collective-permute-start.3 = (f32[4,104,128]{2,1,0:T(8,128)S(1)}, f32[4,104,128]{2,1,0:T(8,128)S(1)}, u32[]{:S(2)}, u32[]{:S(2)}) collective-permute-start(f32[4,104,128]{2,1,0:T(8,128)S(1)} %get-tuple-element.43), channel_id=1, source_target_pairs={{0,17},{1,16},{2,19},{3,18},{4,21},{5,20},{6,23},{7,22},{8,25},{9,... | collective-permute-start | bytes 638984 | tf_op jit(solution)/shard_map/ppermute | solution.py:210
  14.5 10.2 %collective-permute-start.2 = (f32[4,104,128]{2,1,0:T(8,128)S(1)}, f32[4,104,128]{2,1,0:T(8,128)S(1)}, u32[]{:S(2)}, u32[]{:S(2)}) collective-permute-start(f32[4,104,128]{2,1,0:T(8,128)S(1)} %get-tuple-element.44), channel_id=1, source_target_pairs={{0,16},{1,17},{2,18},{3,19},{4,20},{5,21},{6,22},{7,23},{8,24},{9,... | collective-permute-start | bytes 638984 | tf_op jit(solution)/shard_map/ppermute | solution.py:210
  15.0 10.6 %collective-permute-start.1 = (f32[4,104,128]{2,1,0:T(8,128)S(1)}, f32[4,104,128]{2,1,0:T(8,128)S(1)}, u32[]{:S(2)}, u32[]{:S(2)}) collective-permute-start(f32[4,104,128]{2,1,0:T(8,128)S(1)} %get-tuple-element.42), channel_id=1, source_target_pairs={{0,1},{1,0},{2,3},{3,2},{4,5},{5,4},{6,7},{7,6},{8,9},{9,8},{10,11... | collective-permute-start | bytes 638984 | tf_op jit(solution)/shard_map/ppermute | solution.py:210
  15.3 11.5 %collective-permute-start.17 = (f32[64,128]{1,0:T(8,128)S(1)}, f32[64,128]{1,0:T(8,128)S(1)}, u32[]{:S(2)}, u32[]{:S(2)}) collective-permute-start(f32[64,128]{1,0:T(8,128)S(1)} %get-tuple-element.27), channel_id=1, source_target_pairs={{0,1},{1,0},{2,3},{3,2},{4,5},{5,4},{6,7},{7,6},{8,9},{9,8},{10,11... | collective-permute-start | bytes 98312 | tf_op jit(solution)/shard_map/ppermute | solution.py:210
  17.3 13.2 %collective-permute-start.18 = (f32[64,128]{1,0:T(8,128)S(1)}, f32[64,128]{1,0:T(8,128)S(1)}, u32[]{:S(2)}, u32[]{:S(2)}) collective-permute-start(f32[64,128]{1,0:T(8,128)S(1)} %get-tuple-element.28), channel_id=1, source_target_pairs={{0,16},{1,17},{2,18},{3,19},{4,20},{5,21},{6,22},{7,23},{8,24},{9,... | collective-permute-start | bytes 98312 | tf_op jit(solution)/shard_map/ppermute | solution.py:210
  20.6 9.8 %collective-permute-start.19 = (f32[64,128]{1,0:T(8,128)S(1)}, f32[64,128]{1,0:T(8,128)S(1)}, u32[]{:S(2)}, u32[]{:S(2)}) collective-permute-start(f32[64,128]{1,0:T(8,128)S(1)} %get-tuple-element.29), channel_id=1, source_target_pairs={{0,17},{1,16},{2,19},{3,18},{4,21},{5,20},{6,23},{7,22},{8,25},{9,... | collective-permute-start | bytes 98312 | tf_op jit(solution)/shard_map/ppermute | solution.py:210
  24.7 6.5 %collective-permute-start.20 = (f32[64,128]{1,0:T(8,128)S(1)}, f32[64,128]{1,0:T(8,128)S(1)}, u32[]{:S(2)}, u32[]{:S(2)}) collective-permute-start(f32[64,128]{1,0:T(8,128)S(1)} %get-tuple-element.30), channel_id=1, source_target_pairs={{0,8},{1,9},{2,10},{3,11},{4,12},{5,13},{6,14},{7,15},{8,0},{9,1},... | collective-permute-start | bytes 98312 | tf_op jit(solution)/shard_map/ppermute | solution.py:210
  25.6 5.6 %collective-permute-start.21 = (f32[64,128]{1,0:T(8,128)S(1)}, f32[64,128]{1,0:T(8,128)S(1)}, u32[]{:S(2)}, u32[]{:S(2)}) collective-permute-start(f32[64,128]{1,0:T(8,128)S(1)} %get-tuple-element.31), channel_id=1, source_target_pairs={{0,9},{1,8},{2,11},{3,10},{4,13},{5,12},{6,15},{7,14},{8,1},{9,0},... | collective-permute-start | bytes 98312 | tf_op jit(solution)/shard_map/ppermute | solution.py:210
  26.8 13.8 %collective-permute-start.6 = (f32[104,128]{1,0:T(8,128)S(1)}, f32[104,128]{1,0:T(8,128)S(1)}, u32[]{:S(2)}, u32[]{:S(2)}) collective-permute-start(f32[104,128]{1,0:T(8,128)S(1)} %get-tuple-element.46), channel_id=1, source_target_pairs={{0,6},{1,7},{2,4},{3,5},{4,2},{5,3},{6,0},{7,1},{8,14},{9,15},{10,... | collective-permute-start | bytes 159752 | tf_op jit(solution)/shard_map/ppermute | solution.py:210
  30.4 10.9 %collective-permute-start.5 = (f32[104,128]{1,0:T(8,128)S(1)}, f32[104,128]{1,0:T(8,128)S(1)}, u32[]{:S(2)}, u32[]{:S(2)}) collective-permute-start(f32[104,128]{1,0:T(8,128)S(1)} %get-tuple-element.47), channel_id=1, source_target_pairs={{0,4},{1,5},{2,6},{3,7},{4,0},{5,1},{6,2},{7,3},{8,12},{9,13},{10,... | collective-permute-start | bytes 159752 | tf_op jit(solution)/shard_map/ppermute | solution.py:210
  30.5 10.9 %collective-permute-start.4 = (f32[104,128]{1,0:T(8,128)S(1)}, f32[104,128]{1,0:T(8,128)S(1)}, u32[]{:S(2)}, u32[]{:S(2)}) collective-permute-start(f32[104,128]{1,0:T(8,128)S(1)} %get-tuple-element.45), channel_id=1, source_target_pairs={{0,2},{1,3},{2,0},{3,1},{4,6},{5,7},{6,4},{7,5},{8,10},{9,11},{10,... | collective-permute-start | bytes 159752 | tf_op jit(solution)/shard_map/ppermute | solution.py:210
  31.2 3.6 %collective-permute-start.22 = (f32[64,128]{1,0:T(8,128)S(1)}, f32[64,128]{1,0:T(8,128)S(1)}, u32[]{:S(2)}, u32[]{:S(2)}) collective-permute-start(f32[64,128]{1,0:T(8,128)S(1)} %get-tuple-element.32), channel_id=1, source_target_pairs={{0,24},{1,25},{2,26},{3,27},{4,28},{5,29},{6,30},{7,31},{8,16},{9,... | collective-permute-start | bytes 98312 | tf_op jit(solution)/shard_map/ppermute | solution.py:210
  31.2 4.3 %collective-permute-start.23 = (f32[64,128]{1,0:T(8,128)S(1)}, f32[64,128]{1,0:T(8,128)S(1)}, u32[]{:S(2)}, u32[]{:S(2)}) collective-permute-start(f32[64,128]{1,0:T(8,128)S(1)} %get-tuple-element.33), channel_id=1, source_target_pairs={{0,25},{1,24},{2,27},{3,26},{4,29},{5,28},{6,31},{7,30},{8,17},{9,... | collective-permute-start | bytes 98312 | tf_op jit(solution)/shard_map/ppermute | solution.py:210
  36.9 8.5 %collective-permute-start.26 = (f32[24,1344]{1,0:T(8,128)S(1)}, f32[24,1344]{1,0:T(8,128)S(1)}, u32[]{:S(2)}, u32[]{:S(2)}) collective-permute-start(f32[24,1344]{1,0:T(8,128)S(1)} %get-tuple-element.37), channel_id=1, source_target_pairs={{0,6},{1,7},{2,4},{3,5},{4,2},{5,3},{6,0},{7,1},{8,14},{9,15},{10,... | collective-permute-start | bytes 387080 | tf_op jit(solution)/shard_map/ppermute | solution.py:210
  40.6 14.6 %collective-permute-start.25 = (f32[24,1344]{1,0:T(8,128)S(1)}, f32[24,1344]{1,0:T(8,128)S(1)}, u32[]{:S(2)}, u32[]{:S(2)}) collective-permute-start(f32[24,1344]{1,0:T(8,128)S(1)} %get-tuple-element.36), channel_id=1, source_target_pairs={{0,4},{1,5},{2,6},{3,7},{4,0},{5,1},{6,2},{7,3},{8,12},{9,13},{10,... | collective-permute-start | bytes 387080 | tf_op jit(solution)/shard_map/ppermute | solution.py:210
  40.6 14.6 %collective-permute-start.24 = (f32[24,1344]{1,0:T(8,128)S(1)}, f32[24,1344]{1,0:T(8,128)S(1)}, u32[]{:S(2)}, u32[]{:S(2)}) collective-permute-start(f32[24,1344]{1,0:T(8,128)S(1)} %get-tuple-element.35), channel_id=1, source_target_pairs={{0,2},{1,3},{2,0},{3,1},{4,6},{5,7},{6,4},{7,5},{8,10},{9,11},{10,... | collective-permute-start | bytes 387080 | tf_op jit(solution)/shard_map/ppermute | solution.py:210
  41.4 13.9 %collective-permute-start.9 = (f32[104,128]{1,0:T(8,128)S(1)}, f32[104,128]{1,0:T(8,128)S(1)}, u32[]{:S(2)}, u32[]{:S(2)}) collective-permute-start(f32[104,128]{1,0:T(8,128)S(1)} %fusion.4), channel_id=1, source_target_pairs={{0,6},{1,7},{2,4},{3,5},{4,2},{5,3},{6,0},{7,1},{8,14},{9,15},{10,... | collective-permute-start | bytes 159752 | tf_op jit(solution)/shard_map/ppermute | solution.py:210
  45.1 12.4 %collective-permute-start.8 = (f32[104,128]{1,0:T(8,128)S(1)}, f32[104,128]{1,0:T(8,128)S(1)}, u32[]{:S(2)}, u32[]{:S(2)}) collective-permute-start(f32[104,128]{1,0:T(8,128)S(1)} %fusion.4), channel_id=1, source_target_pairs={{0,4},{1,5},{2,6},{3,7},{4,0},{5,1},{6,2},{7,3},{8,12},{9,13},{10,... | collective-permute-start | bytes 159752 | tf_op jit(solution)/shard_map/ppermute | solution.py:210
  45.4 12.1 %collective-permute-start.7 = (f32[104,128]{1,0:T(8,128)S(1)}, f32[104,128]{1,0:T(8,128)S(1)}, u32[]{:S(2)}, u32[]{:S(2)}) collective-permute-start(f32[104,128]{1,0:T(8,128)S(1)} %fusion.4), channel_id=1, source_target_pairs={{0,2},{1,3},{2,0},{3,1},{4,6},{5,7},{6,4},{7,5},{8,10},{9,11},{10,... | collective-permute-start | bytes 159752 | tf_op jit(solution)/shard_map/ppermute | solution.py:210
  57.5 19.3 %collective-permute-start.10 = (f32[4,104,128]{2,1,0:T(8,128)S(1)}, f32[4,104,128]{2,1,0:T(8,128)S(1)}, u32[]{:S(2)}, u32[]{:S(2)}) collective-permute-start(f32[4,104,128]{2,1,0:T(8,128)S(1)} %pad_maximum_fusion.refs_0_), channel_id=1, source_target_pairs={{0,1},{1,0},{2,3},{3,2},{4,5},{5,4},{6,7},{7,6},{8,9},{9,8},{10,11... | collective-permute-start | bytes 638984 | tf_op jit(solution)/shard_map/ppermute | solution.py:210
  58.5 18.8 %collective-permute-start.11 = (f32[4,104,128]{2,1,0:T(8,128)S(1)}, f32[4,104,128]{2,1,0:T(8,128)S(1)}, u32[]{:S(2)}, u32[]{:S(2)}) collective-permute-start(f32[4,104,128]{2,1,0:T(8,128)S(1)} %pad_maximum_fusion.refs_0_), channel_id=1, source_target_pairs={{0,16},{1,17},{2,18},{3,19},{4,20},{5,21},{6,22},{7,23},{8,24},{9,... | collective-permute-start | bytes 638984 | tf_op jit(solution)/shard_map/ppermute | solution.py:210
  59.3 18.0 %collective-permute-start.12 = (f32[4,104,128]{2,1,0:T(8,128)S(1)}, f32[4,104,128]{2,1,0:T(8,128)S(1)}, u32[]{:S(2)}, u32[]{:S(2)}) collective-permute-start(f32[4,104,128]{2,1,0:T(8,128)S(1)} %pad_maximum_fusion.refs_0_), channel_id=1, source_target_pairs={{0,17},{1,16},{2,19},{3,18},{4,21},{5,20},{6,23},{7,22},{8,25},{9,... | collective-permute-start | bytes 638984 | tf_op jit(solution)/shard_map/ppermute | solution.py:210
  61.1 10.2 %collective-permute-start.27 = (f32[12,1344]{1,0:T(8,128)S(1)}, f32[12,1344]{1,0:T(8,128)S(1)}, u32[]{:S(2)}, u32[]{:S(2)}) collective-permute-start(f32[12,1344]{1,0:T(8,128)S(1)} %get-tuple-element.48), channel_id=1, source_target_pairs={{0,1},{1,0},{2,3},{3,2},{4,5},{5,4},{6,7},{7,6},{8,9},{9,8},{10,11... | collective-permute-start | bytes 193544 | tf_op jit(solution)/shard_map/ppermute | solution.py:210
  62.1 10.2 %collective-permute-start.28 = (f32[12,1344]{1,0:T(8,128)S(1)}, f32[12,1344]{1,0:T(8,128)S(1)}, u32[]{:S(2)}, u32[]{:S(2)}) collective-permute-start(f32[12,1344]{1,0:T(8,128)S(1)} %get-tuple-element.49.refs_0_), channel_id=1, source_target_pairs={{0,16},{1,17},{2,18},{3,19},{4,20},{5,21},{6,22},{7,23},{8,24},{9,... | collective-permute-start | bytes 193544 | tf_op jit(solution)/shard_map/ppermute | solution.py:210
  71.3 5.4 %collective-permute-start.29 = (f32[12,1344]{1,0:T(8,128)S(1)}, f32[12,1344]{1,0:T(8,128)S(1)}, u32[]{:S(2)}, u32[]{:S(2)}) collective-permute-start(f32[12,1344]{1,0:T(8,128)S(1)} %get-tuple-element.48), channel_id=1, source_target_pairs={{0,17},{1,16},{2,19},{3,18},{4,21},{5,20},{6,23},{7,22},{8,25},{9,... | collective-permute-start | bytes 193544 | tf_op jit(solution)/shard_map/ppermute | solution.py:210
  72.2 5.5 %collective-permute-start.30 = (f32[12,1344]{1,0:T(8,128)S(1)}, f32[12,1344]{1,0:T(8,128)S(1)}, u32[]{:S(2)}, u32[]{:S(2)}) collective-permute-start(f32[12,1344]{1,0:T(8,128)S(1)} %get-tuple-element.49.refs_0_), channel_id=1, source_target_pairs={{0,8},{1,9},{2,10},{3,11},{4,12},{5,13},{6,14},{7,15},{8,0},{9,1},... | collective-permute-start | bytes 193544 | tf_op jit(solution)/shard_map/ppermute | solution.py:210
  76.7 7.0 %collective-permute-start.13 = (f32[4,104,128]{2,1,0:T(8,128)S(1)}, f32[4,104,128]{2,1,0:T(8,128)S(1)}, u32[]{:S(2)}, u32[]{:S(2)}) collective-permute-start(f32[4,104,128]{2,1,0:T(8,128)S(1)} %pad_maximum_fusion.refs_0_), channel_id=1, source_target_pairs={{0,8},{1,9},{2,10},{3,11},{4,12},{5,13},{6,14},{7,15},{8,0},{9,1},... | collective-permute-start | bytes 638984 | tf_op jit(solution)/shard_map/ppermute | solution.py:210
  76.7 7.0 %collective-permute-start.14 = (f32[4,104,128]{2,1,0:T(8,128)S(1)}, f32[4,104,128]{2,1,0:T(8,128)S(1)}, u32[]{:S(2)}, u32[]{:S(2)}) collective-permute-start(f32[4,104,128]{2,1,0:T(8,128)S(1)} %collective-permute-done.10.refs_1_), channel_id=1, source_target_pairs={{0,8},{1,9},{2,10},{3,11},{4,12},{5,13},{6,14},{7,15},{8,0},{9,1},... | collective-permute-start | bytes 638984 | tf_op jit(solution)/shard_map/ppermute | solution.py:210
  77.2 6.5 %collective-permute-start.15 = (f32[4,104,128]{2,1,0:T(8,128)S(1)}, f32[4,104,128]{2,1,0:T(8,128)S(1)}, u32[]{:S(2)}, u32[]{:S(2)}) collective-permute-start(f32[4,104,128]{2,1,0:T(8,128)S(1)} %collective-permute-done.11.refs_2_), channel_id=1, source_target_pairs={{0,8},{1,9},{2,10},{3,11},{4,12},{5,13},{6,14},{7,15},{8,0},{9,1},... | collective-permute-start | bytes 638984 | tf_op jit(solution)/shard_map/ppermute | solution.py:210
  77.3 6.4 %collective-permute-start.16 = (f32[4,104,128]{2,1,0:T(8,128)S(1)}, f32[4,104,128]{2,1,0:T(8,128)S(1)}, u32[]{:S(2)}, u32[]{:S(2)}) collective-permute-start(f32[4,104,128]{2,1,0:T(8,128)S(1)} %collective-permute-done.12.refs_3_), channel_id=1, source_target_pairs={{0,8},{1,9},{2,10},{3,11},{4,12},{5,13},{6,14},{7,15},{8,0},{9,1},... | collective-permute-start | bytes 638984 | tf_op jit(solution)/shard_map/ppermute | solution.py:210
  77.8 1.5 %collective-permute-start.31 = (f32[12,1344]{1,0:T(8,128)S(1)}, f32[12,1344]{1,0:T(8,128)S(1)}, u32[]{:S(2)}, u32[]{:S(2)}) collective-permute-start(f32[12,1344]{1,0:T(8,128)S(1)} %collective-permute-done.27.refs_1_), channel_id=1, source_target_pairs={{0,8},{1,9},{2,10},{3,11},{4,12},{5,13},{6,14},{7,15},{8,0},{9,1},... | collective-permute-start | bytes 193544 | tf_op jit(solution)/shard_map/ppermute | solution.py:210
  79.2 1.3 %collective-permute-start.32 = (f32[12,1344]{1,0:T(8,128)S(1)}, f32[12,1344]{1,0:T(8,128)S(1)}, u32[]{:S(2)}, u32[]{:S(2)}) collective-permute-start(f32[12,1344]{1,0:T(8,128)S(1)} %collective-permute-done.28.refs_2_), channel_id=1, source_target_pairs={{0,8},{1,9},{2,10},{3,11},{4,12},{5,13},{6,14},{7,15},{8,0},{9,1},... | collective-permute-start | bytes 193544 | tf_op jit(solution)/shard_map/ppermute | solution.py:210
  80.5 1.3 %collective-permute-start.33 = (f32[12,1344]{1,0:T(8,128)S(1)}, f32[12,1344]{1,0:T(8,128)S(1)}, u32[]{:S(2)}, u32[]{:S(2)}) collective-permute-start(f32[12,1344]{1,0:T(8,128)S(1)} %collective-permute-done.29.refs_3_), channel_id=1, source_target_pairs={{0,8},{1,9},{2,10},{3,11},{4,12},{5,13},{6,14},{7,15},{8,0},{9,1},... | collective-permute-start | bytes 193544 | tf_op jit(solution)/shard_map/ppermute | solution.py:210

commit v2 on v1

--- a/solution.py
+++ b/solution.py
@@ -20,11 +20,16 @@
     return pl.BlockSpec(memory_space=pltpu.VMEM)
 
 
-def call(body, outs, scratch, *args):
+def call(body, outs, scratch, *args, in_hbm=False):
+    def place(arg):
+        if arg.dtype == jnp.int32:
+            return pl.BlockSpec(memory_space=pltpu.SMEM)
+        return pl.BlockSpec(memory_space=pltpu.HBM) if in_hbm else whole_vmem()
+
     return pl.pallas_call(
         body,
         out_shape=[jax.ShapeDtypeStruct(shape, kind) for shape, kind in outs],
-        in_specs=[whole_vmem() if a.dtype != jnp.int32 else pl.BlockSpec(memory_space=pltpu.SMEM) for a in args],
+        in_specs=[place(a) for a in args],
         out_specs=[whole_vmem() for _ in outs],
         scratch_shapes=scratch,
         compiler_params=pltpu.CompilerParams(vmem_limit_bytes=VMEM_LIMIT),
@@ -40,14 +45,16 @@
     return plane_id() * 4 + ((lax.axis_index("dp") >> 1) & 3)
 
 
-def send_kernel(x_ref, *refs):
-    out_refs, held = refs[:-1], refs[-1]
+def send_kernel(x_hbm, keep_ref, give_ref, x_ref, held, sem):
+    copy = pltpu.make_async_copy(x_hbm, x_ref, sem)
+    copy.start()
     me = plane_id()
+    copy.wait()
     x_t = x_ref[...].astype(F32).reshape(128, 512).T
     for block in range(8):
         held[block ^ me] = x_t[64 * block : 64 * block + 64]
-    for place, out in enumerate(out_refs):
-        out[...] = held[place]
+    keep_ref[...] = held[0:4]
+    give_ref[...] = held[4:8]
 
 
 def shift_rows(value, row_step, col_step):
@@ -74,18 +81,25 @@
     return out
 
 
-def local_kernel(x_ref, og_ref, gw_ref, pw_ref, gain_ref, shift_ref, mine_ref, other_ref, block_w, hid_t, sums):
+def local_kernel(*refs):
+    sources, (mine_ref, other_ref), held, sems = refs[:6], refs[6:8], refs[8:14], refs[14]
+    block_w, hid_t, sums = refs[15:]
+    copies = [pltpu.make_async_copy(src, dst, sems.at[i]) for i, (src, dst) in enumerate(zip(sources, held))]
+    for copy in copies:
+        copy.start()
+    x_ref, og_ref, gw_ref, pw_ref, gain_ref, shift_ref = held
     me = cell_id()
     images = x_ref.shape[0]
     rows = images * 64
-    spot_row = lax.broadcasted_iota(jnp.int32, (32, 128), 0)
-    spot_lane = lax.broadcasted_iota(jnp.int32, (32, 128), 1)
-    for g in range(16):
-        place = (spot_lane == spot_row + 32 * (g % 4)).astype(F32).astype(BF16)
-        spread = jnp.dot(gw_ref[g], place, preferred_element_type=F32).astype(BF16)
+    for copy in copies:
+        copy.wait()
+    group_at = lax.broadcasted_iota(jnp.int32, (32, 128), 1) // 32
+    for q in range(4):
+        stacked = gw_ref[4 * q : 4 * q + 4].astype(F32).reshape(128, 288).T
         for s in range(9):
-            at = s * 128 + 32 * (g % 4)
-            block_w[g // 4, at : at + 32, :] = spread[32 * s : 32 * s + 32]
+            for g in range(4):
+                at = s * 128 + 32 * g
+                block_w[q, at : at + 32, :] = jnp.where(group_at == g, stacked[32 * s : 32 * s + 32], 0.0).astype(BF16)
     x = x_ref[...].astype(F32)
     moved = [
         shift_rows(x, a - 1, b - 1).reshape(rows, 512).astype(BF16) for a in range(3) for b in range(3)
@@ -132,12 +146,12 @@
 
 
 def factor_kernel(steps, *refs):
-    parts, outs, (patches, held) = refs[:8], refs[8 : 8 + steps], refs[8 + steps :]
-    me = lax.axis_index("dp") >> 1
+    parts, outs, (patches, held) = refs[:5], refs[5 : 5 + steps], refs[5 + steps :]
+    dp = lax.axis_index("dp")
     lane = lax.broadcasted_iota(jnp.int32, (64, 128), 1)
     row, col = (lane >> 3) & 7, lane & 7
-    for src, ref in enumerate(parts):
-        x_t = ref[...]
+    sources = [parts[0][0], parts[1][0]] + [ref[i] for ref in parts[2:] for i in range(2)]
+    for src, x_t in enumerate(sources):
         for a in range(3):
             for b in range(3):
                 step = (a - 1) * 8 + b - 1
@@ -159,47 +173,50 @@
             for pair in PAIRS:
                 if pair[0] == a:
                     pieces.append(part[:, 96 * pair[1] : 96 * pair[1] + 96])
+    pieces.append(jnp.zeros((96, 64), F32))
     full = jnp.concatenate(pieces, axis=1)
-    size = 96 // steps
-    for t in range(steps):
-        held[t ^ me] = full[size * t : size * t + size]
+    half = 96 // (2 * steps)
+    for t in range(2 * steps):
+        for tile in range(11):
+            held[t ^ dp, half * tile : half * tile + half, :] = full[
+                half * t : half * t + half, 128 * tile : 128 * tile + 128
+            ]
+        if 11 * half < held.shape[1]:
+            held[t ^ dp, 11 * half :, :] = jnp.zeros((held.shape[1] - 11 * half, 128), F32)
     for t, out in enumerate(outs):
-        out[...] = held[t]
-
-
-def slots_kernel(scale, groups_of, slot_ref, *refs):
-    parts, out_ref, held = refs[:8], refs[8], refs[9]
-    me = plane_id()
+        out[...] = held[2 * t : 2 * t + 2]
+
+
+def finish_kernel(grad_scale, mean_scale, slot_ref, *refs):
+    parts, (group_ref, proj_ref, out_ref, owned_ref), (sums, blocks) = refs[:8], refs[8:12], refs[12:]
+    me, plane = cell_id(), plane_id()
+    half = owned_ref.shape[0]
     for place, ref in enumerate(parts):
-        value = ref[...] * scale
+        for z in range(4):
+            j = (4 * place + z) ^ me
+            for w in range(4):
+                at = pl.multiple_of(16 * j, 16)
+                row = 104 * z + 16 * w
+                proj_ref[pl.ds(at, 16), 128 * w : 128 * w + 128] = ref[row : row + 16, :] * grad_scale
+            sums[pl.ds(pl.multiple_of(40 * j, 8), 40), :] = ref[104 * z + 64 : 104 * z + 104, :]
+        tiles = [ref[416 + half * t : 416 + half * t + half, :] for t in range(11)]
+        value = jnp.concatenate(tiles, axis=1) * mean_scale
         for g in range(2):
             for a in range(3):
                 pieces = []
                 for b in range(3):
                     at = 672 * g + 96 * PAIRS.index(SAME.get((a, b), (a, b)))
                     pieces.append(value[:, at : at + 96])
-                held[6 * (place ^ me) + 3 * g + a] = jnp.concatenate(pieces, axis=1)
+                blocks[6 * (place ^ plane) + 3 * g + a] = jnp.concatenate(pieces, axis=1)
+    for q in range(4):
+        group_ref[4 * q : 4 * q + 4] = (sums[320 * q : 320 * q + 288, :].T * grad_scale).reshape(4, 32, 288)
+        for g in range(4):
+            out_ref[4 * q + g] = sums[320 * q + 288 : 320 * q + 320, 32 * g : 32 * g + 32] * mean_scale
     owner = lax.axis_index("owner")
-    for s in range(out_ref.shape[0]):
+    for s in range(owned_ref.shape[1]):
         block = slot_ref[owner, s]
-        value = held[jnp.maximum(block, 0)]
-        out_ref[s] = jnp.where(block >= 0, value, 0.0)
-
-
-def unpack_kernel(grad_scale, mean_scale, *refs):
-    parts, (group_ref, proj_ref, out_ref), sums = refs[:8], refs[8:11], refs[11]
-    me = cell_id()
-    for place, ref in enumerate(parts):
-        for z in range(4):
-            j = (4 * place + z) ^ me
-            for w in range(4):
-                at = pl.multiple_of(16 * j, 16)
-                proj_ref[pl.ds(at, 16), 128 * w : 128 * w + 128] = ref[z, 16 * w : 16 * w + 16, :] * grad_scale
-            sums[pl.ds(pl.multiple_of(40 * j, 8), 40), :] = ref[z, 64:104, :]
-    for g in range(16):
-        base, lanes = 320 * (g // 4), slice(32 * (g % 4), 32 * (g % 4) + 32)
-        group_ref[g] = sums[base : base + 288, lanes] * grad_scale
-        out_ref[g] = sums[base + 288 : base + 320, lanes] * mean_scale
+        value = blocks[jnp.maximum(block, 0)]
+        owned_ref[:, s, :] = jnp.where(block >= 0, value, 0.0)
 
 
 def per_device(n_owner, n_dp, activations, out_grad, group_weight, proj_weight, bn_gain, bn_shift, slot_block):
@@ -225,65 +242,69 @@
     grad_scale = 1.0 / math.sqrt(total_rows)
     mean_scale = 1.0 / total_rows
 
-    sent = call(send_kernel, [((64, 128), F32)] * 8, [pltpu.VMEM((8, 64, 128), F32)], activations)
-    owner_of = lambda p: ((p >> 2) & 1) | (p & 2)
-    got = [sent[0]] + [swap(sent[p], owner_of(p), p & 1) for p in range(1, 8)]
-
+    keep, give = call(
+        send_kernel,
+        [((4, 64, 128), F32)] * 2,
+        [pltpu.VMEM(activations.shape, BF16), pltpu.VMEM((8, 64, 128), F32), pltpu.SemaphoreType.DMA],
+        activations,
+        in_hbm=True,
+    )
+    taken = swap(give, 1, 0)
+    got = [keep, taken]
+    for p in range(1, 4):
+        got.append(swap(jnp.stack([keep[p], taken[p]]), p & 2, p & 1))
+
+    inputs = [
+        activations,
+        out_grad,
+        group_weight.transpose(0, 2, 1),
+        proj_weight,
+        bn_gain.reshape(1, -1),
+        bn_shift.reshape(1, -1),
+    ]
     mine, other = call(
         local_kernel,
         [((16, 104, 128), F32)] * 2,
-        [
+        [pltpu.VMEM(a.shape, a.dtype) for a in inputs]
+        + [
+            pltpu.SemaphoreType.DMA((len(inputs),)),
             pltpu.VMEM((4, 1152, 128), BF16),
             pltpu.VMEM((32, 16, rows), BF16),
             pltpu.VMEM((1280, 128), F32),
         ],
-        activations,
-        out_grad,
-        group_weight,
-        proj_weight,
-        bn_gain.reshape(1, -1),
-        bn_shift.reshape(1, -1),
+        *inputs,
+        in_hbm=True,
     )
     total = mine + swap(other, 1, 0)
     total = total[0:4] + swap(total[4:8], 0, 1) + swap(total[8:12], 2, 0) + swap(total[12:16], 2, 1)
     total = total[0] + swap(total[1], 0, 2) + swap(total[2], 0, 4) + swap(total[3], 0, 6)
     total = add_over(total, far_owner, far_dp)
-    total = jnp.stack([total] + [swap(total, 0, 2 * z) for z in range(1, 4)])
-    near = [total] + [swap(total, 2 * (p >> 1), p & 1) for p in range(1, 4)]
-    parts = near + [swap(v, 1, 0) for v in near]
-    group_grad, proj_grad, out_factor = call(
-        functools.partial(unpack_kernel, grad_scale, mean_scale),
-        [((16, 288, 32), F32), ((512, 512), F32), ((16, 32, 32), F32)],
-        [pltpu.VMEM((1280, 128), F32)],
-        *parts,
-    )
-
-    size = 96 // steps
+
+    half = 96 // n_dp
+    padded = -(-11 * half // 8) * 8
     pieces = call(
         functools.partial(factor_kernel, steps),
-        [((size, 1344), F32)] * steps,
-        [pltpu.VMEM((2, 288, 1024), BF16), pltpu.VMEM((steps, size, 1344), F32)],
+        [((2, padded, 128), F32)] * steps,
+        [pltpu.VMEM((2, 288, 1024), BF16), pltpu.VMEM((2 * steps, padded, 128), F32)],
         *got,
     )
     piece = pieces[0]
     for t in range(1, steps):
         piece = piece + swap(pieces[t], 0, 2 * t)
     piece = add_over(piece, far_owner, ())
-    half = size // 2
-    at = (lax.axis_index("dp") & 1) * half
-    own = lax.dynamic_slice_in_dim(piece, at, half, 0)
-    peer = lax.dynamic_slice_in_dim(piece, half - at, half, 0)
+
+    total = jnp.concatenate([total] + [swap(total, 0, 2 * z) for z in range(1, 4)])
+    own, peer = (jnp.concatenate([total, piece[i]]) for i in range(2))
     near = [own, swap(peer, 0, 1), swap(own, 2, 0), swap(peer, 2, 1)]
     parts = near + [swap(v, 1, 0) for v in near]
-    slots = slot_block.shape[1]
-    (factor_owned,) = call(
-        functools.partial(slots_kernel, mean_scale, 2),
-        [((slots, half, 288), F32)],
-        [pltpu.VMEM((48, half, 288), F32)],
+    group_grad, proj_grad, out_factor, factor_owned = call(
+        functools.partial(finish_kernel, grad_scale, mean_scale),
+        [((16, 32, 288), F32), ((512, 512), F32), ((16, 32, 32), F32), ((half, slot_block.shape[1], 288), F32)],
+        [pltpu.VMEM((1280, 128), F32), pltpu.VMEM((48, half, 288), F32)],
         slot_block,
         *parts,
     )
-    return group_grad, proj_grad, out_factor, factor_owned
+    return group_grad.transpose(0, 2, 1), proj_grad, out_factor, factor_owned.transpose(1, 0, 2)
 
 
 def solution(mesh):

time: 87.5 us -> 71.7 us (0.82)
  starting transfers between devices: 40 us -> 26.6 us
  local copies, waits for them, and re-layouts: 8.44 us -> 4.65 us
    ppermute x34 -> x24, starting transfers between devices: 40 us -> 26.6 us  [swap(): return lax.ppermute(value, AXES, pairs)]
    unnamed x15 -> x18, local copies, waits for them, and re-layouts: 8.36 us -> 4.57 us
    ppermute x34 -> x24, waiting for transfers between devices: 32 us -> 32.6 us  [swap(): return lax.ppermute(value, AXES, pairs)]
    pallas_call x5 -> x4, Pallas kernels: 5.77 us -> 6.37 us  [call(): pl.pallas_call(body, out_shape=[jax.ShapeDtypeStruct(shape, kind) for sha...]
  transfers between devices with their start and end apart: 34 -> 24, of which waited for: 14 -> 12; matrix products, arithmetic and copies ran while one was open for 1% -> 0% of each run, Pallas kernels for 3% -> 2%
where the time goes in v2:
time: 71.7 us; the launch traced here: 71.2 us
  waiting for transfers between devices  32.6 us (45%)
  starting transfers between devices  26.6 us (37%)
  Pallas kernels  6.37 us (9%)
  local copies, waits for them, and re-layouts  4.65 us (6%)
  between operations  0.79 us (1%)
    ppermute x24, waiting for transfers between devices, swap(): return lax.ppermute(value, AXES, pairs)  32.6 us
    ppermute x24, starting transfers between devices, swap(): return lax.ppermute(value, AXES, pairs)  26.6 us
    pallas_call x4, Pallas kernels, call(): pl.pallas_call(body, out_shape=[jax.ShapeDtypeStruct(shape, kind) for sha...  6.37 us
    unnamed x18, local copies, waits for them, and re-layouts  4.57 us
  transfers between devices with their start and end apart: 24, of which 12 were waited for; matrix products, arithmetic and copies ran while one was open for 0% of the time, Pallas kernels for 2%

profile of v2, /device:TPU:0, one launch (start us, length us, event | category | flops | bytes accessed | tf_op | source)
XLA Modules:
  0.0 71.2 jit_solution(7495288675853101761)
XLA Ops:
  0.6 0.0 copy-start.5
  0.6 0.0 copy-start.4
  0.7 0.7 copy-done.5
  1.3 0.0 copy-done.4
  1.3 0.9 %copy-done = bf16[2,8,8,512]{3,2,1,0:T(8,128)(2,1)S(1)} copy-done((bf16[2,8,8,512]{3,2,1,0:T(8,128)(2,1)S(1)}, bf16[2,8,8,512]{3,2,1,0:T(8,128)(2,1)}, u32[]{:S(2)}) %copy-start) | copy-done | bytes 131096
  2.2 1.0 %copy-done.1 = bf16[512,512]{1,0:T(8,128)(2,1)S(1)} copy-done((bf16[512,512]{1,0:T(8,128)(2,1)S(1)}, bf16[512,512]{1,0:T(8,128)(2,1)}, u32[]{:S(2)}) %copy-start.1) | copy-done | bytes 524312
  3.3 1.0 %copy-done.2 = bf16[16,288,32]{1,2,0:T(8,128)(2,1)S(1)} copy-done((bf16[16,288,32]{1,2,0:T(8,128)(2,1)S(1)}, bf16[16,288,32]{1,2,0:T(8,128)(2,1)}, u32[]{:S(2)}) %copy-start.2) | copy-done | bytes 294936
  4.3 0.9 %copy-done.3 = bf16[2,8,8,512]{3,2,1,0:T(8,128)(2,1)S(1)} copy-done((bf16[2,8,8,512]{3,2,1,0:T(8,128)(2,1)S(1)}, bf16[2,8,8,512]{3,2,1,0:T(8,128)(2,1)}, u32[]{:S(2)}) %copy-start.3) | copy-done | bytes 131096
  5.2 2.0 %shard_map.102 = (f32[16,104,128]{2,1,0:T(8,128)S(1)}, f32[16,104,128]{2,1,0:T(8,128)S(1)}) custom-call(bf16[2,8,8,512]{3,2,1,0:T(8,128)(2,1)S(1)} %copy-done, bf16[2,8,8,512]{3,2,1,0:T(8,128)(2,1)S(1)} %copy-done.3, bf16[16,32,288]{2,1,0:T(8,128)(2,1)S(1)} %bitcast.28, bf16[512,512]{1,0:T(8,128)(2,1)S(1)} %copy-done.1, f32[1,512]{1,0:T(1,128)S(1)} %bitcast.29, ...), custom_call_target="tpu_custom_call" | custom-call | tf_op jit(solution)/shard_map/pallas_call | solution.py:29
  7.2 0.5 collective-permute-start
  7.7 0.3 shard_map.103
  8.0 0.1 collective-permute-start.10
  8.1 1.8 %collective-permute-done.10.refs_1_ = f32[4,64,128]{2,1,0:T(8,128)S(1)} collective-permute-done((f32[4,64,128]{2,1,0:T(8,128)S(1)}, f32[4,64,128]{2,1,0:T(8,128)S(1)}, u32[]{:S(2)}, u32[]{:S(2)}) %collective-permute-start.10) | collective-permute-done | bytes 131104 | tf_op jit(solution)/shard_map/ppermute | solution.py:227
  9.9 3.0 %collective-permute-start.11 = (f32[2,64,128]{2,1,0:T(8,128)S(1)}, f32[2,64,128]{2,1,0:T(8,128)S(1)}, u32[]{:S(2)}, u32[]{:S(2)}) collective-permute-start(f32[2,64,128]{2,1,0:T(8,128)S(1)} %pad_maximum_fusion), channel_id=1, source_target_pairs={{0,1},{1,0},{2,3},{3,2},{4,5},{5,4},{6,7},{7,6},{8,9},{9,8},{10,11... | collective-permute-start | bytes 196616 | tf_op jit(solution)/shard_map/ppermute | solution.py:227
  12.8 0.0 collective-permute-done
  12.8 0.1 add.30
  13.0 0.1 collective-permute-start.1
  13.1 3.0 %collective-permute-start.3 = (f32[4,104,128]{2,1,0:T(8,128)S(1)}, f32[4,104,128]{2,1,0:T(8,128)S(1)}, u32[]{:S(2)}, u32[]{:S(2)}) collective-permute-start(f32[4,104,128]{2,1,0:T(8,128)S(1)} %get-tuple-element.31), channel_id=1, source_target_pairs={{0,17},{1,16},{2,19},{3,18},{4,21},{5,20},{6,23},{7,22},{8,25},{9,... | collective-permute-start | bytes 638984 | tf_op jit(solution)/shard_map/ppermute | solution.py:227
  16.0 0.5 collective-permute-start.2
  16.6 1.5 %collective-permute-start.12 = (f32[2,64,128]{2,1,0:T(8,128)S(1)}, f32[2,64,128]{2,1,0:T(8,128)S(1)}, u32[]{:S(2)}, u32[]{:S(2)}) collective-permute-start(f32[2,64,128]{2,1,0:T(8,128)S(1)} %pad_maximum_fusion.1), channel_id=1, source_target_pairs={{0,16},{1,17},{2,18},{3,19},{4,20},{5,21},{6,22},{7,23},{8,24},{9,... | collective-permute-start | bytes 196616 | tf_op jit(solution)/shard_map/ppermute | solution.py:227
  18.1 3.1 %collective-permute-done.1 = f32[4,104,128]{2,1,0:T(8,128)S(1)} collective-permute-done((f32[4,104,128]{2,1,0:T(8,128)S(1)}, f32[4,104,128]{2,1,0:T(8,128)S(1)}, u32[]{:S(2)}, u32[]{:S(2)}) %collective-permute-start.1) | collective-permute-done | bytes 213024 | tf_op jit(solution)/shard_map/ppermute | solution.py:227
  21.2 2.1 %collective-permute-start.13 = (f32[2,64,128]{2,1,0:T(8,128)S(1)}, f32[2,64,128]{2,1,0:T(8,128)S(1)}, u32[]{:S(2)}, u32[]{:S(2)}) collective-permute-start(f32[2,64,128]{2,1,0:T(8,128)S(1)} %pad_maximum_fusion.2), channel_id=1, source_target_pairs={{0,17},{1,16},{2,19},{3,18},{4,21},{5,20},{6,23},{7,22},{8,25},{9,... | collective-permute-start | bytes 196616 | tf_op jit(solution)/shard_map/ppermute | solution.py:227
  23.3 3.2 %collective-permute-done.3 = f32[4,104,128]{2,1,0:T(8,128)S(1)} collective-permute-done((f32[4,104,128]{2,1,0:T(8,128)S(1)}, f32[4,104,128]{2,1,0:T(8,128)S(1)}, u32[]{:S(2)}, u32[]{:S(2)}) %collective-permute-start.3) | collective-permute-done | bytes 213024 | tf_op jit(solution)/shard_map/ppermute | solution.py:227
  26.5 2.7 %collective-permute-done.2 = f32[4,104,128]{2,1,0:T(8,128)S(1)} collective-permute-done((f32[4,104,128]{2,1,0:T(8,128)S(1)}, f32[4,104,128]{2,1,0:T(8,128)S(1)}, u32[]{:S(2)}, u32[]{:S(2)}) %collective-permute-start.2) | collective-permute-done | bytes 213024 | tf_op jit(solution)/shard_map/ppermute | solution.py:227
  29.2 0.1 fusion.1
  29.2 1.6 %collective-permute-start.4 = (f32[104,128]{1,0:T(8,128)S(1)}, f32[104,128]{1,0:T(8,128)S(1)}, u32[]{:S(2)}, u32[]{:S(2)}) collective-permute-start(f32[104,128]{1,0:T(8,128)S(1)} %get-tuple-element.33), channel_id=1, source_target_pairs={{0,2},{1,3},{2,0},{3,1},{4,6},{5,7},{6,4},{7,5},{8,10},{9,11},{10,... | collective-permute-start | bytes 159752 | tf_op jit(solution)/shard_map/ppermute | solution.py:227
  30.9 2.5 %collective-permute-start.6 = (f32[104,128]{1,0:T(8,128)S(1)}, f32[104,128]{1,0:T(8,128)S(1)}, u32[]{:S(2)}, u32[]{:S(2)}) collective-permute-start(f32[104,128]{1,0:T(8,128)S(1)} %get-tuple-element.34), channel_id=1, source_target_pairs={{0,6},{1,7},{2,4},{3,5},{4,2},{5,3},{6,0},{7,1},{8,14},{9,15},{10,... | collective-permute-start | bytes 159752 | tf_op jit(solution)/shard_map/ppermute | solution.py:227
  33.3 0.0 collective-permute-done.11.refs_2_
  33.3 0.2 collective-permute-start.5
  33.5 0.0 collective-permute-done.12.refs_3_
  33.5 0.0 collective-permute-done.13.refs_4_
  33.5 1.4 %shard_map.104 = (f32[2,136,128]{2,1,0:T(8,128)S(1)}, f32[2,136,128]{2,1,0:T(8,128)S(1)}, f32[2,136,128]{2,1,0:T(8,128)S(1)}, f32[2,136,128]{2,1,0:T(8,128)S(1)}) custom-call(f32[4,64,128]{2,1,0:T(8,128)S(1)} %get-tuple-element.18.refs_0_, f32[4,64,128]{2,1,0:T(8,128)S(1)} %collective-permute-done.10.refs_1_, ...), custom_call_target="tpu_custom_call" | custom-call | tf_op jit(solution)/shard_map/pallas_call | solution.py:29
  34.9 1.8 %collective-permute-start.14 = (f32[2,136,128]{2,1,0:T(8,128)S(1)}, f32[2,136,128]{2,1,0:T(8,128)S(1)}, u32[]{:S(2)}, u32[]{:S(2)}) collective-permute-start(f32[2,136,128]{2,1,0:T(8,128)S(1)} %get-tuple-element.21), channel_id=1, source_target_pairs={{0,2},{1,3},{2,0},{3,1},{4,6},{5,7},{6,4},{7,5},{8,10},{9,11},{10,... | collective-permute-start | bytes 417800 | tf_op jit(solution)/shard_map/ppermute | solution.py:227
  36.7 1.7 %collective-permute-start.15 = (f32[2,136,128]{2,1,0:T(8,128)S(1)}, f32[2,136,128]{2,1,0:T(8,128)S(1)}, u32[]{:S(2)}, u32[]{:S(2)}) collective-permute-start(f32[2,136,128]{2,1,0:T(8,128)S(1)} %get-tuple-element.22), channel_id=1, source_target_pairs={{0,4},{1,5},{2,6},{3,7},{4,0},{5,1},{6,2},{7,3},{8,12},{9,13},{10,... | collective-permute-start | bytes 417800 | tf_op jit(solution)/shard_map/ppermute | solution.py:227
  38.5 0.0 collective-permute-done.4
  38.5 0.9 %collective-permute-start.16 = (f32[2,136,128]{2,1,0:T(8,128)S(1)}, f32[2,136,128]{2,1,0:T(8,128)S(1)}, u32[]{:S(2)}, u32[]{:S(2)}) collective-permute-start(f32[2,136,128]{2,1,0:T(8,128)S(1)} %get-tuple-element.23), channel_id=1, source_target_pairs={{0,6},{1,7},{2,4},{3,5},{4,2},{5,3},{6,0},{7,1},{8,14},{9,15},{10,... | collective-permute-start | bytes 417800 | tf_op jit(solution)/shard_map/ppermute | solution.py:227
  39.4 0.0 collective-permute-done.6
  39.4 2.8 %collective-permute-done.5 = f32[104,128]{1,0:T(8,128)S(1)} collective-permute-done((f32[104,128]{1,0:T(8,128)S(1)}, f32[104,128]{1,0:T(8,128)S(1)}, u32[]{:S(2)}, u32[]{:S(2)}) %collective-permute-start.5) | collective-permute-done | bytes 53280 | tf_op jit(solution)/shard_map/ppermute | solution.py:227
  42.2 0.1 collective-permute-start.7
  42.3 0.0 collective-permute-done.14
  42.3 5.9 %collective-permute-done.15 = f32[2,136,128]{2,1,0:T(8,128)S(1)} collective-permute-done((f32[2,136,128]{2,1,0:T(8,128)S(1)}, f32[2,136,128]{2,1,0:T(8,128)S(1)}, u32[]{:S(2)}, u32[]{:S(2)}) %collective-permute-start.15) | collective-permute-done | bytes 139296 | tf_op jit(solution)/shard_map/ppermute | solution.py:227
  48.2 0.0 collective-permute-done.16
  48.2 2.5 %collective-permute-start.9 = (f32[104,128]{1,0:T(8,128)S(1)}, f32[104,128]{1,0:T(8,128)S(1)}, u32[]{:S(2)}, u32[]{:S(2)}) collective-permute-start(f32[104,128]{1,0:T(8,128)S(1)} %get-tuple-element.29), channel_id=1, source_target_pairs={{0,6},{1,7},{2,4},{3,5},{4,2},{5,3},{6,0},{7,1},{8,14},{9,15},{10,... | collective-permute-start | bytes 159752 | tf_op jit(solution)/shard_map/ppermute | solution.py:227
  50.7 1.1 %collective-permute-start.8 = (f32[104,128]{1,0:T(8,128)S(1)}, f32[104,128]{1,0:T(8,128)S(1)}, u32[]{:S(2)}, u32[]{:S(2)}) collective-permute-start(f32[104,128]{1,0:T(8,128)S(1)} %get-tuple-element.29), channel_id=1, source_target_pairs={{0,4},{1,5},{2,6},{3,7},{4,0},{5,1},{6,2},{7,3},{8,12},{9,13},{10,... | collective-permute-start | bytes 159752 | tf_op jit(solution)/shard_map/ppermute | solution.py:227
  51.8 0.0 collective-permute-done.7
  51.8 4.0 %collective-permute-done.8 = f32[104,128]{1,0:T(8,128)S(1)} collective-permute-done((f32[104,128]{1,0:T(8,128)S(1)}, f32[104,128]{1,0:T(8,128)S(1)}, u32[]{:S(2)}, u32[]{:S(2)}) %collective-permute-start.8) | collective-permute-done | bytes 53280 | tf_op jit(solution)/shard_map/ppermute | solution.py:227
  55.7 0.0 collective-permute-done.9
  55.8 0.0 copy-start.6
  55.8 0.3 collective-permute-start.19
  56.1 1.8 %collective-permute-start.17 = (f32[552,128]{1,0:T(8,128)S(1)}, f32[552,128]{1,0:T(8,128)S(1)}, u32[]{:S(2)}, u32[]{:S(2)}) collective-permute-start(f32[552,128]{1,0:T(8,128)S(1)} %fusion.2), channel_id=1, source_target_pairs={{0,1},{1,0},{2,3},{3,2},{4,5},{5,4},{6,7},{7,6},{8,9},{9,8},{10,11... | collective-permute-start | bytes 847880 | tf_op jit(solution)/shard_map/ppermute | solution.py:227
  57.8 1.5 %collective-permute-start.18 = (f32[552,128]{1,0:T(8,128)S(1)}, f32[552,128]{1,0:T(8,128)S(1)}, u32[]{:S(2)}, u32[]{:S(2)}) collective-permute-start(f32[552,128]{1,0:T(8,128)S(1)} %fusion.3.refs_0_), channel_id=1, source_target_pairs={{0,16},{1,17},{2,18},{3,19},{4,20},{5,21},{6,22},{7,23},{8,24},{9,... | collective-permute-start | bytes 847880 | tf_op jit(solution)/shard_map/ppermute | solution.py:227
  59.4 0.0 collective-permute-start.20
  59.4 4.7 %collective-permute-done.19.refs_3_ = f32[552,128]{1,0:T(8,128)S(1)} collective-permute-done((f32[552,128]{1,0:T(8,128)S(1)}, f32[552,128]{1,0:T(8,128)S(1)}, u32[]{:S(2)}, u32[]{:S(2)}) %collective-permute-start.19) | collective-permute-done | bytes 282656 | tf_op jit(solution)/shard_map/ppermute | solution.py:227
  64.0 0.0 collective-permute-start.23
  64.1 2.1 %collective-permute-done.17.refs_1_ = f32[552,128]{1,0:T(8,128)S(1)} collective-permute-done((f32[552,128]{1,0:T(8,128)S(1)}, f32[552,128]{1,0:T(8,128)S(1)}, u32[]{:S(2)}, u32[]{:S(2)}) %collective-permute-start.17) | collective-permute-done | bytes 282656 | tf_op jit(solution)/shard_map/ppermute | solution.py:227
  66.2 0.0 collective-permute-start.21
  66.2 0.8 %collective-permute-done.18.refs_2_ = f32[552,128]{1,0:T(8,128)S(1)} collective-permute-done((f32[552,128]{1,0:T(8,128)S(1)}, f32[552,128]{1,0:T(8,128)S(1)}, u32[]{:S(2)}, u32[]{:S(2)}) %collective-permute-start.18) | collective-permute-done | bytes 282656 | tf_op jit(solution)/shard_map/ppermute | solution.py:227
  67.0 0.0 collective-permute-start.22
  67.0 0.0 collective-permute-done.20.refs_4_
  67.0 0.0 collective-permute-done.23.refs_7_
  67.0 0.7 %collective-permute-done.21.refs_5_ = f32[552,128]{1,0:T(8,128)S(1)} collective-permute-done((f32[552,128]{1,0:T(8,128)S(1)}, f32[552,128]{1,0:T(8,128)S(1)}, u32[]{:S(2)}, u32[]{:S(2)}) %collective-permute-start.21) | collective-permute-done | bytes 282656 | tf_op jit(solution)/shard_map/ppermute | solution.py:227
  67.7 0.8 %collective-permute-done.22.refs_6_ = f32[552,128]{1,0:T(8,128)S(1)} collective-permute-done((f32[552,128]{1,0:T(8,128)S(1)}, f32[552,128]{1,0:T(8,128)S(1)}, u32[]{:S(2)}, u32[]{:S(2)}) %collective-permute-start.22) | collective-permute-done | bytes 282656 | tf_op jit(solution)/shard_map/ppermute | solution.py:227
  68.5 0.0 copy-done.6
  68.5 2.7 %shard_map.105 = (f32[16,32,288]{2,1,0:T(8,128)}, f32[512,512]{1,0:T(8,128)}, f32[16,32,32]{2,1,0:T(8,128)}, f32[12,24,288]{2,1,0:T(8,128)}) custom-call(s32[4,24]{1,0:T(4,128)S(1)} %copy-done.6, f32[552,128]{1,0:T(8,128)S(1)} %fusion.3.refs_0_, f32[552,128]{1,0:T(8,128)S(1)} %collective-permute-done.17.refs_1_, ...), custom_call_target="tpu_custom_call" | custom-call | tf_op jit(solution)/shard_map/pallas_call | solution.py:29
  (19 shorter events, 0.2 us)
Async XLA Ops:
  0.6 0.7 copy-start.5
  0.6 0.7 copy-start.4
  1.3 0.9 %copy-start = (bf16[2,8,8,512]{3,2,1,0:T(8,128)(2,1)S(1)}, bf16[2,8,8,512]{3,2,1,0:T(8,128)(2,1)}, u32[]{:S(2)}) copy-start(bf16[2,8,8,512]{3,2,1,0:T(8,128)(2,1)} %x_hbm.1) | copy-start | bytes 393220
  2.2 1.0 %copy-start.1 = (bf16[512,512]{1,0:T(8,128)(2,1)S(1)}, bf16[512,512]{1,0:T(8,128)(2,1)}, u32[]{:S(2)}) copy-start(bf16[512,512]{1,0:T(8,128)(2,1)} %refs_3_.1) | copy-start | bytes 1572868
  3.3 1.0 %copy-start.2 = (bf16[16,288,32]{1,2,0:T(8,128)(2,1)S(1)}, bf16[16,288,32]{1,2,0:T(8,128)(2,1)}, u32[]{:S(2)}) copy-start(bf16[16,288,32]{1,2,0:T(8,128)(2,1)} %param.9) | copy-start | bytes 884740
  4.3 0.9 %copy-start.3 = (bf16[2,8,8,512]{3,2,1,0:T(8,128)(2,1)S(1)}, bf16[2,8,8,512]{3,2,1,0:T(8,128)(2,1)}, u32[]{:S(2)}) copy-start(bf16[2,8,8,512]{3,2,1,0:T(8,128)(2,1)} %refs_1_.1) | copy-start | bytes 393220
  7.2 5.7 %collective-permute-start = (f32[16,104,128]{2,1,0:T(8,128)S(1)}, f32[16,104,128]{2,1,0:T(8,128)S(1)}, u32[]{:S(2)}, u32[]{:S(2)}) collective-permute-start(f32[16,104,128]{2,1,0:T(8,128)S(1)} %get-tuple-element.17), channel_id=1, source_target_pairs={{0,8},{1,9},{2,10},{3,11},{4,12},{5,13},{6,14},{7,15},{8,0},{9,1},... | collective-permute-start | bytes 2555912 | tf_op jit(solution)/shard_map/ppermute | solution.py:227
  8.0 1.9 %collective-permute-start.10 = (f32[4,64,128]{2,1,0:T(8,128)S(1)}, f32[4,64,128]{2,1,0:T(8,128)S(1)}, u32[]{:S(2)}, u32[]{:S(2)}) collective-permute-start(f32[4,64,128]{2,1,0:T(8,128)S(1)} %get-tuple-element.19), channel_id=1, source_target_pairs={{0,8},{1,9},{2,10},{3,11},{4,12},{5,13},{6,14},{7,15},{8,0},{9,1},... | collective-permute-start | bytes 393224 | tf_op jit(solution)/shard_map/ppermute | solution.py:227
  9.9 23.4 %collective-permute-start.11 = (f32[2,64,128]{2,1,0:T(8,128)S(1)}, f32[2,64,128]{2,1,0:T(8,128)S(1)}, u32[]{:S(2)}, u32[]{:S(2)}) collective-permute-start(f32[2,64,128]{2,1,0:T(8,128)S(1)} %pad_maximum_fusion), channel_id=1, source_target_pairs={{0,1},{1,0},{2,3},{3,2},{4,5},{5,4},{6,7},{7,6},{8,9},{9,8},{10,11... | collective-permute-start | bytes 196616 | tf_op jit(solution)/shard_map/ppermute | solution.py:227
  13.0 8.2 %collective-permute-start.1 = (f32[4,104,128]{2,1,0:T(8,128)S(1)}, f32[4,104,128]{2,1,0:T(8,128)S(1)}, u32[]{:S(2)}, u32[]{:S(2)}) collective-permute-start(f32[4,104,128]{2,1,0:T(8,128)S(1)} %get-tuple-element.30), channel_id=1, source_target_pairs={{0,1},{1,0},{2,3},{3,2},{4,5},{5,4},{6,7},{7,6},{8,9},{9,8},{10,11... | collective-permute-start | bytes 638984 | tf_op jit(solution)/shard_map/ppermute | solution.py:227
  13.1 13.4 %collective-permute-start.3 = (f32[4,104,128]{2,1,0:T(8,128)S(1)}, f32[4,104,128]{2,1,0:T(8,128)S(1)}, u32[]{:S(2)}, u32[]{:S(2)}) collective-permute-start(f32[4,104,128]{2,1,0:T(8,128)S(1)} %get-tuple-element.31), channel_id=1, source_target_pairs={{0,17},{1,16},{2,19},{3,18},{4,21},{5,20},{6,23},{7,22},{8,25},{9,... | collective-permute-start | bytes 638984 | tf_op jit(solution)/shard_map/ppermute | solution.py:227
  16.0 13.1 %collective-permute-start.2 = (f32[4,104,128]{2,1,0:T(8,128)S(1)}, f32[4,104,128]{2,1,0:T(8,128)S(1)}, u32[]{:S(2)}, u32[]{:S(2)}) collective-permute-start(f32[4,104,128]{2,1,0:T(8,128)S(1)} %get-tuple-element.32), channel_id=1, source_target_pairs={{0,16},{1,17},{2,18},{3,19},{4,20},{5,21},{6,22},{7,23},{8,24},{9,... | collective-permute-start | bytes 638984 | tf_op jit(solution)/shard_map/ppermute | solution.py:227
  16.6 16.9 %collective-permute-start.12 = (f32[2,64,128]{2,1,0:T(8,128)S(1)}, f32[2,64,128]{2,1,0:T(8,128)S(1)}, u32[]{:S(2)}, u32[]{:S(2)}) collective-permute-start(f32[2,64,128]{2,1,0:T(8,128)S(1)} %pad_maximum_fusion.1), channel_id=1, source_target_pairs={{0,16},{1,17},{2,18},{3,19},{4,20},{5,21},{6,22},{7,23},{8,24},{9,... | collective-permute-start | bytes 196616 | tf_op jit(solution)/shard_map/ppermute | solution.py:227
  21.2 12.3 %collective-permute-start.13 = (f32[2,64,128]{2,1,0:T(8,128)S(1)}, f32[2,64,128]{2,1,0:T(8,128)S(1)}, u32[]{:S(2)}, u32[]{:S(2)}) collective-permute-start(f32[2,64,128]{2,1,0:T(8,128)S(1)} %pad_maximum_fusion.2), channel_id=1, source_target_pairs={{0,17},{1,16},{2,19},{3,18},{4,21},{5,20},{6,23},{7,22},{8,25},{9,... | collective-permute-start | bytes 196616 | tf_op jit(solution)/shard_map/ppermute | solution.py:227
  29.2 9.2 %collective-permute-start.4 = (f32[104,128]{1,0:T(8,128)S(1)}, f32[104,128]{1,0:T(8,128)S(1)}, u32[]{:S(2)}, u32[]{:S(2)}) collective-permute-start(f32[104,128]{1,0:T(8,128)S(1)} %get-tuple-element.33), channel_id=1, source_target_pairs={{0,2},{1,3},{2,0},{3,1},{4,6},{5,7},{6,4},{7,5},{8,10},{9,11},{10,... | collective-permute-start | bytes 159752 | tf_op jit(solution)/shard_map/ppermute | solution.py:227
  30.9 8.5 %collective-permute-start.6 = (f32[104,128]{1,0:T(8,128)S(1)}, f32[104,128]{1,0:T(8,128)S(1)}, u32[]{:S(2)}, u32[]{:S(2)}) collective-permute-start(f32[104,128]{1,0:T(8,128)S(1)} %get-tuple-element.34), channel_id=1, source_target_pairs={{0,6},{1,7},{2,4},{3,5},{4,2},{5,3},{6,0},{7,1},{8,14},{9,15},{10,... | collective-permute-start | bytes 159752 | tf_op jit(solution)/shard_map/ppermute | solution.py:227
  33.3 8.8 %collective-permute-start.5 = (f32[104,128]{1,0:T(8,128)S(1)}, f32[104,128]{1,0:T(8,128)S(1)}, u32[]{:S(2)}, u32[]{:S(2)}) collective-permute-start(f32[104,128]{1,0:T(8,128)S(1)} %get-tuple-element.35), channel_id=1, source_target_pairs={{0,4},{1,5},{2,6},{3,7},{4,0},{5,1},{6,2},{7,3},{8,12},{9,13},{10,... | collective-permute-start | bytes 159752 | tf_op jit(solution)/shard_map/ppermute | solution.py:227
  34.9 7.4 %collective-permute-start.14 = (f32[2,136,128]{2,1,0:T(8,128)S(1)}, f32[2,136,128]{2,1,0:T(8,128)S(1)}, u32[]{:S(2)}, u32[]{:S(2)}) collective-permute-start(f32[2,136,128]{2,1,0:T(8,128)S(1)} %get-tuple-element.21), channel_id=1, source_target_pairs={{0,2},{1,3},{2,0},{3,1},{4,6},{5,7},{6,4},{7,5},{8,10},{9,11},{10,... | collective-permute-start | bytes 417800 | tf_op jit(solution)/shard_map/ppermute | solution.py:227
  36.7 11.5 %collective-permute-start.15 = (f32[2,136,128]{2,1,0:T(8,128)S(1)}, f32[2,136,128]{2,1,0:T(8,128)S(1)}, u32[]{:S(2)}, u32[]{:S(2)}) collective-permute-start(f32[2,136,128]{2,1,0:T(8,128)S(1)} %get-tuple-element.22), channel_id=1, source_target_pairs={{0,4},{1,5},{2,6},{3,7},{4,0},{5,1},{6,2},{7,3},{8,12},{9,13},{10,... | collective-permute-start | bytes 417800 | tf_op jit(solution)/shard_map/ppermute | solution.py:227
  38.5 9.8 %collective-permute-start.16 = (f32[2,136,128]{2,1,0:T(8,128)S(1)}, f32[2,136,128]{2,1,0:T(8,128)S(1)}, u32[]{:S(2)}, u32[]{:S(2)}) collective-permute-start(f32[2,136,128]{2,1,0:T(8,128)S(1)} %get-tuple-element.23), channel_id=1, source_target_pairs={{0,6},{1,7},{2,4},{3,5},{4,2},{5,3},{6,0},{7,1},{8,14},{9,15},{10,... | collective-permute-start | bytes 417800 | tf_op jit(solution)/shard_map/ppermute | solution.py:227
  42.2 9.6 %collective-permute-start.7 = (f32[104,128]{1,0:T(8,128)S(1)}, f32[104,128]{1,0:T(8,128)S(1)}, u32[]{:S(2)}, u32[]{:S(2)}) collective-permute-start(f32[104,128]{1,0:T(8,128)S(1)} %get-tuple-element.29), channel_id=1, source_target_pairs={{0,2},{1,3},{2,0},{3,1},{4,6},{5,7},{6,4},{7,5},{8,10},{9,11},{10,... | collective-permute-start | bytes 159752 | tf_op jit(solution)/shard_map/ppermute | solution.py:227
  48.2 7.5 %collective-permute-start.9 = (f32[104,128]{1,0:T(8,128)S(1)}, f32[104,128]{1,0:T(8,128)S(1)}, u32[]{:S(2)}, u32[]{:S(2)}) collective-permute-start(f32[104,128]{1,0:T(8,128)S(1)} %get-tuple-element.29), channel_id=1, source_target_pairs={{0,6},{1,7},{2,4},{3,5},{4,2},{5,3},{6,0},{7,1},{8,14},{9,15},{10,... | collective-permute-start | bytes 159752 | tf_op jit(solution)/shard_map/ppermute | solution.py:227
  50.7 5.0 %collective-permute-start.8 = (f32[104,128]{1,0:T(8,128)S(1)}, f32[104,128]{1,0:T(8,128)S(1)}, u32[]{:S(2)}, u32[]{:S(2)}) collective-permute-start(f32[104,128]{1,0:T(8,128)S(1)} %get-tuple-element.29), channel_id=1, source_target_pairs={{0,4},{1,5},{2,6},{3,7},{4,0},{5,1},{6,2},{7,3},{8,12},{9,13},{10,... | collective-permute-start | bytes 159752 | tf_op jit(solution)/shard_map/ppermute | solution.py:227
  55.8 12.7 %copy-start.6 = (s32[4,24]{1,0:T(4,128)S(1)}, s32[4,24]{1,0:T(4,128)}, u32[]{:S(2)}) copy-start(s32[4,24]{1,0:T(4,128)} %slot_ref.1) | copy-start | bytes 1156
  55.8 8.2 %collective-permute-start.19 = (f32[552,128]{1,0:T(8,128)S(1)}, f32[552,128]{1,0:T(8,128)S(1)}, u32[]{:S(2)}, u32[]{:S(2)}) collective-permute-start(f32[552,128]{1,0:T(8,128)S(1)} %fusion.2), channel_id=1, source_target_pairs={{0,17},{1,16},{2,19},{3,18},{4,21},{5,20},{6,23},{7,22},{8,25},{9,... | collective-permute-start | bytes 847880 | tf_op jit(solution)/shard_map/ppermute | solution.py:227
  56.1 10.1 %collective-permute-start.17 = (f32[552,128]{1,0:T(8,128)S(1)}, f32[552,128]{1,0:T(8,128)S(1)}, u32[]{:S(2)}, u32[]{:S(2)}) collective-permute-start(f32[552,128]{1,0:T(8,128)S(1)} %fusion.2), channel_id=1, source_target_pairs={{0,1},{1,0},{2,3},{3,2},{4,5},{5,4},{6,7},{7,6},{8,9},{9,8},{10,11... | collective-permute-start | bytes 847880 | tf_op jit(solution)/shard_map/ppermute | solution.py:227
  57.8 9.1 %collective-permute-start.18 = (f32[552,128]{1,0:T(8,128)S(1)}, f32[552,128]{1,0:T(8,128)S(1)}, u32[]{:S(2)}, u32[]{:S(2)}) collective-permute-start(f32[552,128]{1,0:T(8,128)S(1)} %fusion.3.refs_0_), channel_id=1, source_target_pairs={{0,16},{1,17},{2,18},{3,19},{4,20},{5,21},{6,22},{7,23},{8,24},{9,... | collective-permute-start | bytes 847880 | tf_op jit(solution)/shard_map/ppermute | solution.py:227
  59.4 7.6 %collective-permute-start.20 = (f32[552,128]{1,0:T(8,128)S(1)}, f32[552,128]{1,0:T(8,128)S(1)}, u32[]{:S(2)}, u32[]{:S(2)}) collective-permute-start(f32[552,128]{1,0:T(8,128)S(1)} %fusion.3.refs_0_), channel_id=1, source_target_pairs={{0,8},{1,9},{2,10},{3,11},{4,12},{5,13},{6,14},{7,15},{8,0},{9,1},... | collective-permute-start | bytes 847880 | tf_op jit(solution)/shard_map/ppermute | solution.py:227
  64.0 2.9 %collective-permute-start.23 = (f32[552,128]{1,0:T(8,128)S(1)}, f32[552,128]{1,0:T(8,128)S(1)}, u32[]{:S(2)}, u32[]{:S(2)}) collective-permute-start(f32[552,128]{1,0:T(8,128)S(1)} %collective-permute-done.19.refs_3_), channel_id=1, source_target_pairs={{0,8},{1,9},{2,10},{3,11},{4,12},{5,13},{6,14},{7,15},{8,0},{9,1},... | collective-permute-start | bytes 847880 | tf_op jit(solution)/shard_map/ppermute | solution.py:227
  66.2 1.6 %collective-permute-start.21 = (f32[552,128]{1,0:T(8,128)S(1)}, f32[552,128]{1,0:T(8,128)S(1)}, u32[]{:S(2)}, u32[]{:S(2)}) collective-permute-start(f32[552,128]{1,0:T(8,128)S(1)} %collective-permute-done.17.refs_1_), channel_id=1, source_target_pairs={{0,8},{1,9},{2,10},{3,11},{4,12},{5,13},{6,14},{7,15},{8,0},{9,1},... | collective-permute-start | bytes 847880 | tf_op jit(solution)/shard_map/ppermute | solution.py:227
  67.0 1.6 %collective-permute-start.22 = (f32[552,128]{1,0:T(8,128)S(1)}, f32[552,128]{1,0:T(8,128)S(1)}, u32[]{:S(2)}, u32[]{:S(2)}) collective-permute-start(f32[552,128]{1,0:T(8,128)S(1)} %collective-permute-done.18.refs_2_), channel_id=1, source_target_pairs={{0,8},{1,9},{2,10},{3,11},{4,12},{5,13},{6,14},{7,15},{8,0},{9,1},... | collective-permute-start | bytes 847880 | tf_op jit(solution)/shard_map/ppermute | solution.py:227

commit v3 on v2

--- a/solution.py
+++ b/solution.py
@@ -11,6 +11,7 @@
 AXES = ("owner", "dp")
 F32 = jnp.float32
 BF16 = jnp.bfloat16
+LOCAL_FLOPS = 4000000000
 VMEM_LIMIT = 48 * 1024 * 1024
 PAIRS = ((0, 0), (0, 1), (0, 2), (1, 0), (1, 1), (2, 0), (2, 2))
 SAME = {(1, 2): (0, 1), (2, 1): (1, 0)}
@@ -20,7 +21,7 @@
     return pl.BlockSpec(memory_space=pltpu.VMEM)
 
 
-def call(body, outs, scratch, *args, in_hbm=False):
+def call(body, outs, scratch, *args, in_hbm=False, flops=0):
     def place(arg):
         if arg.dtype == jnp.int32:
             return pl.BlockSpec(memory_space=pltpu.SMEM)
@@ -33,6 +34,7 @@
         out_specs=[whole_vmem() for _ in outs],
         scratch_shapes=scratch,
         compiler_params=pltpu.CompilerParams(vmem_limit_bytes=VMEM_LIMIT),
+        cost_estimate=pl.CostEstimate(flops=flops, bytes_accessed=0, transcendentals=0) if flops else None,
     )(*args)
 
 
@@ -45,16 +47,17 @@
     return plane_id() * 4 + ((lax.axis_index("dp") >> 1) & 3)
 
 
-def send_kernel(x_hbm, keep_ref, give_ref, x_ref, held, sem):
+def send_kernel(x_hbm, *refs):
+    out_refs, (x_ref, held, sem) = refs[:4], refs[4:]
     copy = pltpu.make_async_copy(x_hbm, x_ref, sem)
     copy.start()
-    me = plane_id()
+    me = cell_id()
     copy.wait()
     x_t = x_ref[...].astype(F32).reshape(128, 512).T
-    for block in range(8):
-        held[block ^ me] = x_t[64 * block : 64 * block + 64]
-    keep_ref[...] = held[0:4]
-    give_ref[...] = held[4:8]
+    for group in range(16):
+        held[group ^ (me & 15)] = x_t[32 * group : 32 * group + 32]
+    for place, out in enumerate(out_refs):
+        out[...] = held[4 * place : 4 * place + 4]
 
 
 def shift_rows(value, row_step, col_step):
@@ -145,69 +148,77 @@
             out[k, 64:104, :] = sums[pl.ds(pl.multiple_of(40 * j, 8), 40), :]
 
 
-def factor_kernel(steps, *refs):
-    parts, outs, (patches, held) = refs[:5], refs[5 : 5 + steps], refs[5 + steps :]
-    dp = lax.axis_index("dp")
-    lane = lax.broadcasted_iota(jnp.int32, (64, 128), 1)
+def packed_rows(count):
+    return 5 * count + -(-count // 4)
+
+
+def factor_kernel(n_dp, *refs):
+    parts, (keep_ref, give_ref), (patches, held) = refs[:7], refs[7:9], refs[9:]
+    dp, core = lax.axis_index("dp"), lax.axis_index("owner") & 1
+    lane = lax.broadcasted_iota(jnp.int32, (32, 128), 1)
     row, col = (lane >> 3) & 7, lane & 7
-    sources = [parts[0][0], parts[1][0]] + [ref[i] for ref in parts[2:] for i in range(2)]
+    sources = [ref[0] for ref in parts[:4]] + [ref[i] for ref in parts[4:] for i in range(4)]
     for src, x_t in enumerate(sources):
         for a in range(3):
             for b in range(3):
                 step = (a - 1) * 8 + b - 1
                 value = x_t if step == 0 else pltpu.roll(x_t, (-step) % 128, 1)
                 keep = (row + a >= 1) & (row + a <= 8) & (col + b >= 1) & (col + b <= 8)
-                value = jnp.where(keep, value, 0.0).astype(BF16)
                 at = (3 * a + b) * 32
-                patches[0, at : at + 32, 128 * src : 128 * src + 128] = value[:32]
-                patches[1, at : at + 32, 128 * src : 128 * src + 128] = value[32:]
+                patches[at : at + 32, 128 * src : 128 * src + 128] = jnp.where(keep, value, 0.0).astype(BF16)
     pieces = []
-    for g in range(2):
-        for a, width in ((0, 288), (1, 192), (2, 288)):
-            part = lax.dot_general(
-                patches[g, 96 * a : 96 * a + 96, :],
-                patches[g, :width, :],
-                (((1,), (1,)), ((), ())),
-                preferred_element_type=F32,
-            )
-            for pair in PAIRS:
-                if pair[0] == a:
-                    pieces.append(part[:, 96 * pair[1] : 96 * pair[1] + 96])
-    pieces.append(jnp.zeros((96, 64), F32))
+    for a, width in ((0, 288), (1, 192), (2, 288)):
+        part = lax.dot_general(
+            patches[96 * a : 96 * a + 96, :],
+            patches[:width, :],
+            (((1,), (1,)), ((), ())),
+            preferred_element_type=F32,
+        )
+        for pair in PAIRS:
+            if pair[0] == a:
+                pieces.append(part[:, 96 * pair[1] : 96 * pair[1] + 96])
     full = jnp.concatenate(pieces, axis=1)
-    half = 96 // (2 * steps)
-    for t in range(2 * steps):
-        for tile in range(11):
-            held[t ^ dp, half * tile : half * tile + half, :] = full[
-                half * t : half * t + half, 128 * tile : 128 * tile + 128
-            ]
-        if 11 * half < held.shape[1]:
-            held[t ^ dp, 11 * half :, :] = jnp.zeros((held.shape[1] - 11 * half, 128), F32)
-    for t, out in enumerate(outs):
-        out[...] = held[2 * t : 2 * t + 2]
+    count = 96 // n_dp // 2
+    held[...] = jnp.zeros(held.shape, F32)
+    for block in range(2 * n_dp):
+        at = (block & 1) ^ core, (block >> 1) ^ dp
+        rows = full[count * block : count * block + count]
+        for tile in range(5):
+            held[at[0], at[1], count * tile : count * tile + count, :] = rows[:, 128 * tile : 128 * tile + 128]
+        for i in range(count):
+            spot = 5 * count + i // 4
+            held[at[0], at[1], spot : spot + 1, 32 * (i % 4) : 32 * (i % 4) + 32] = rows[i : i + 1, 640:672]
+    keep_ref[...] = held[0]
+    give_ref[...] = held[1]
 
 
 def finish_kernel(grad_scale, mean_scale, slot_ref, *refs):
     parts, (group_ref, proj_ref, out_ref, owned_ref), (sums, blocks) = refs[:8], refs[8:12], refs[12:]
-    me, plane = cell_id(), plane_id()
-    half = owned_ref.shape[0]
+    me = cell_id()
+    count = owned_ref.shape[0] // 2
+    step = 104 + packed_rows(count)
     for place, ref in enumerate(parts):
         for z in range(4):
             j = (4 * place + z) ^ me
+            base = step * z
             for w in range(4):
                 at = pl.multiple_of(16 * j, 16)
-                row = 104 * z + 16 * w
+                row = base + 16 * w
                 proj_ref[pl.ds(at, 16), 128 * w : 128 * w + 128] = ref[row : row + 16, :] * grad_scale
-            sums[pl.ds(pl.multiple_of(40 * j, 8), 40), :] = ref[104 * z + 64 : 104 * z + 104, :]
-        tiles = [ref[416 + half * t : 416 + half * t + half, :] for t in range(11)]
-        value = jnp.concatenate(tiles, axis=1) * mean_scale
-        for g in range(2):
+            sums[pl.ds(pl.multiple_of(40 * j, 8), 40), :] = ref[base + 64 : base + 104, :]
+            base += 104
+            tiles = [ref[base + count * t : base + count * t + count, :] for t in range(5)]
+            last = []
+            for i in range(count):
+                spot = base + 5 * count + i // 4
+                last.append(ref[spot : spot + 1, 32 * (i % 4) : 32 * (i % 4) + 32])
+            value = jnp.concatenate(tiles + [jnp.concatenate(last, axis=0)], axis=1) * mean_scale
             for a in range(3):
                 pieces = []
                 for b in range(3):
-                    at = 672 * g + 96 * PAIRS.index(SAME.get((a, b), (a, b)))
+                    at = 96 * PAIRS.index(SAME.get((a, b), (a, b)))
                     pieces.append(value[:, at : at + 96])
-                blocks[6 * (place ^ plane) + 3 * g + a] = jnp.concatenate(pieces, axis=1)
+                blocks[j >> 4, 3 * (j & 15) + a] = jnp.concatenate(pieces, axis=1)
     for q in range(4):
         group_ref[4 * q : 4 * q + 4] = (sums[320 * q : 320 * q + 288, :].T * grad_scale).reshape(4, 32, 288)
         for g in range(4):
@@ -215,8 +226,9 @@
     owner = lax.axis_index("owner")
     for s in range(owned_ref.shape[1]):
         block = slot_ref[owner, s]
-        value = blocks[jnp.maximum(block, 0)]
-        owned_ref[:, s, :] = jnp.where(block >= 0, value, 0.0)
+        for core in range(2):
+            value = blocks[core, jnp.maximum(block, 0)]
+            owned_ref[count * core : count * core + count, s, :] = jnp.where(block >= 0, value, 0.0)
 
 
 def per_device(n_owner, n_dp, activations, out_grad, group_weight, proj_weight, bn_gain, bn_shift, slot_block):
@@ -235,24 +247,20 @@
 
     far_owner = range(2, n_owner.bit_length() - 1)
     far_dp = range(3, n_dp.bit_length() - 1)
-    steps = n_dp // 2
     images = activations.shape[0]
     rows = images * 64
     total_rows = rows * n_owner * n_dp
     grad_scale = 1.0 / math.sqrt(total_rows)
     mean_scale = 1.0 / total_rows
 
-    keep, give = call(
+    sent = call(
         send_kernel,
-        [((4, 64, 128), F32)] * 2,
-        [pltpu.VMEM(activations.shape, BF16), pltpu.VMEM((8, 64, 128), F32), pltpu.SemaphoreType.DMA],
+        [((4, 32, 128), F32)] * 4,
+        [pltpu.VMEM(activations.shape, BF16), pltpu.VMEM((16, 32, 128), F32), pltpu.SemaphoreType.DMA],
         activations,
         in_hbm=True,
     )
-    taken = swap(give, 1, 0)
-    got = [keep, taken]
-    for p in range(1, 4):
-        got.append(swap(jnp.stack([keep[p], taken[p]]), p & 2, p & 1))
+    got = [sent[0], swap(sent[1], 0, 1), swap(sent[2], 2, 0), swap(sent[3], 2, 1)]
 
     inputs = [
         activations,
@@ -274,33 +282,40 @@
         ],
         *inputs,
         in_hbm=True,
+        flops=LOCAL_FLOPS,
     )
     total = mine + swap(other, 1, 0)
+    far = [swap(jnp.stack([v[z] for v in got]), 0, 2 * z) for z in range(1, 4)]
     total = total[0:4] + swap(total[4:8], 0, 1) + swap(total[8:12], 2, 0) + swap(total[12:16], 2, 1)
     total = total[0] + swap(total[1], 0, 2) + swap(total[2], 0, 4) + swap(total[3], 0, 6)
     total = add_over(total, far_owner, far_dp)
 
     half = 96 // n_dp
-    padded = -(-11 * half // 8) * 8
-    pieces = call(
-        functools.partial(factor_kernel, steps),
-        [((2, padded, 128), F32)] * steps,
-        [pltpu.VMEM((2, 288, 1024), BF16), pltpu.VMEM((2 * steps, padded, 128), F32)],
+    packed = packed_rows(half // 2)
+    keep, give = call(
+        functools.partial(factor_kernel, n_dp),
+        [((n_dp, packed, 128), F32)] * 2,
+        [pltpu.VMEM((288, 2048), BF16), pltpu.VMEM((2, n_dp, packed, 128), F32)],
         *got,
-    )
-    piece = pieces[0]
-    for t in range(1, steps):
-        piece = piece + swap(pieces[t], 0, 2 * t)
-    piece = add_over(piece, far_owner, ())
-
-    total = jnp.concatenate([total] + [swap(total, 0, 2 * z) for z in range(1, 4)])
-    own, peer = (jnp.concatenate([total, piece[i]]) for i in range(2))
+        *far,
+    )
+    piece = add_over(keep + swap(give, 1, 0), far_owner, ())
+    for bit in reversed(far_dp):
+        near = piece.shape[0] // 2
+        piece = piece[:near] + swap(piece[near:], 0, 1 << bit)
+    piece = piece.reshape(4, 2 * packed, 128)
+
+    line = [jnp.concatenate([total, piece[z]]) for z in range(4)]
+    line = [line[0]] + [swap(line[z], 0, 2 * z) for z in range(1, 4)]
+    own = jnp.concatenate([v[: 104 + packed] for v in line])
+    peer = jnp.concatenate([w for v in line for w in (v[:104], v[104 + packed :])])
     near = [own, swap(peer, 0, 1), swap(own, 2, 0), swap(peer, 2, 1)]
     parts = near + [swap(v, 1, 0) for v in near]
+    slots = slot_block.shape[1]
     group_grad, proj_grad, out_factor, factor_owned = call(
         functools.partial(finish_kernel, grad_scale, mean_scale),
-        [((16, 32, 288), F32), ((512, 512), F32), ((16, 32, 32), F32), ((half, slot_block.shape[1], 288), F32)],
-        [pltpu.VMEM((1280, 128), F32), pltpu.VMEM((48, half, 288), F32)],
+        [((16, 32, 288), F32), ((512, 512), F32), ((16, 32, 32), F32), ((half, slots, 288), F32)],
+        [pltpu.VMEM((1280, 128), F32), pltpu.VMEM((2, 48, half // 2, 288), F32)],
         slot_block,
         *parts,
     )

time: 71.7 us -> 66.7 us (0.930)
  waiting for transfers between devices: 32.6 us -> 26.9 us
    ppermute x24, waiting for transfers between devices: 32.6 us -> 26.9 us  [swap(): return lax.ppermute(value, AXES, pairs)]
    slice x2 -> x9, local copies, waits for them, and re-layouts: 0.01 us -> 0.92 us  [the longest x4 0.89 us: per_device(): own = jnp.concatenate([v[:104 + packed] for v in line])]
    unnamed x18 -> x24, local copies, waits for them, and re-layouts: 4.57 us -> 4.29 us
  transfers between devices with their start and end apart: 24 -> 24, of which waited for: 12 -> 13; matrix products, arithmetic and copies ran while one was open for 0% -> 0% of each run, Pallas kernels for 2% -> 5%
where the time goes in v3:
time: 66.7 us; the launch traced here: 66.4 us
  waiting for transfers between devices  26.9 us (40%)
  starting transfers between devices  26.5 us (40%)
  Pallas kernels  6.55 us (10%)
  local copies, waits for them, and re-layouts  5.27 us (8%)
  between operations  0.87 us (1%)
    ppermute x24, waiting for transfers between devices, swap(): return lax.ppermute(value, AXES, pairs)  26.9 us
    ppermute x24, starting transfers between devices, swap(): return lax.ppermute(value, AXES, pairs)  26.5 us
    pallas_call x4, Pallas kernels, call(): pl.pallas_call(body, out_shape=[jax.ShapeDtypeStruct(shape, kind) for sha...  6.55 us
    unnamed x24, local copies, waits for them, and re-layouts  4.29 us
  transfers between devices with their start and end apart: 24, of which 13 were waited for; matrix products, arithmetic and copies ran while one was open for 0% of the time, Pallas kernels for 5%

profile of v3, /device:TPU:0, one launch (start us, length us, event | category | flops | bytes accessed | tf_op | source)
XLA Modules:
  0.0 66.4 jit_solution(10220574511936353243)
XLA Ops:
  0.6 0.0 copy-start
  0.6 0.9 %copy-done = bf16[2,8,8,512]{3,2,1,0:T(8,128)(2,1)S(1)} copy-done((bf16[2,8,8,512]{3,2,1,0:T(8,128)(2,1)S(1)}, bf16[2,8,8,512]{3,2,1,0:T(8,128)(2,1)}, u32[]{:S(2)}) %copy-start) | copy-done | bytes 131096
  1.5 0.3 shard_map.103
  1.8 3.0 %collective-permute-start.7 = (f32[4,32,128]{2,1,0:T(8,128)S(1)}, f32[4,32,128]{2,1,0:T(8,128)S(1)}, u32[]{:S(2)}, u32[]{:S(2)}) collective-permute-start(f32[4,32,128]{2,1,0:T(8,128)S(1)} %get-tuple-element.19), channel_id=1, source_target_pairs={{0,1},{1,0},{2,3},{3,2},{4,5},{5,4},{6,7},{7,6},{8,9},{9,8},{10,11... | collective-permute-start | bytes 196616 | tf_op jit(solution)/shard_map/ppermute | solution.py:239
  4.8 1.5 %collective-permute-start.8 = (f32[4,32,128]{2,1,0:T(8,128)S(1)}, f32[4,32,128]{2,1,0:T(8,128)S(1)}, u32[]{:S(2)}, u32[]{:S(2)}) collective-permute-start(f32[4,32,128]{2,1,0:T(8,128)S(1)} %get-tuple-element.20), channel_id=1, source_target_pairs={{0,16},{1,17},{2,18},{3,19},{4,20},{5,21},{6,22},{7,23},{8,24},{9,... | collective-permute-start | bytes 196616 | tf_op jit(solution)/shard_map/ppermute | solution.py:239
  6.4 0.0 collective-permute-start.9
  6.4 0.7 %copy-done.6 = f32[512]{0:T(512)S(1)} copy-done((f32[512]{0:T(512)S(1)}, f32[512]{0:T(512)}, u32[]{:S(2)}) %copy-start.6) | copy-done | bytes 2072
  7.1 0.0 copy-done.5
  7.1 1.0 %copy-done.2 = bf16[512,512]{1,0:T(8,128)(2,1)S(1)} copy-done((bf16[512,512]{1,0:T(8,128)(2,1)S(1)}, bf16[512,512]{1,0:T(8,128)(2,1)}, u32[]{:S(2)}) %copy-start.2) | copy-done | bytes 524312
  8.1 1.0 %copy-done.3 = bf16[16,288,32]{1,2,0:T(8,128)(2,1)S(1)} copy-done((bf16[16,288,32]{1,2,0:T(8,128)(2,1)S(1)}, bf16[16,288,32]{1,2,0:T(8,128)(2,1)}, u32[]{:S(2)}) %copy-start.3) | copy-done | bytes 294936
  9.1 2.0 %shard_map.102 = (f32[16,104,128]{2,1,0:T(8,128)S(1)}, f32[16,104,128]{2,1,0:T(8,128)S(1)}) custom-call(bf16[2,8,8,512]{3,2,1,0:T(8,128)(2,1)S(1)} %copy-done, bf16[2,8,8,512]{3,2,1,0:T(8,128)(2,1)S(1)} %copy-done.4, bf16[16,32,288]{2,1,0:T(8,128)(2,1)S(1)} %bitcast.28, bf16[512,512]{1,0:T(8,128)(2,1)S(1)} %copy-done.2, f32[1,512]{1,0:T(1,128)S(1)} %bitcast.29, ...), custom_call_target="tpu_custom_call" | custom-call | flops 4000000000 | tf_op jit(solution)/shard_map/pallas_call | solution.py:30
  11.1 0.1 collective-permute-start
  11.2 0.0 collective-permute-done.7.refs_1_
  11.2 0.0 collective-permute-done.8.refs_2_
  11.3 0.3 collective-permute-done.9.refs_3_
  11.5 1.9 %collective-permute-start.10 = (f32[4,32,128]{2,1,0:T(8,128)S(1)}, f32[4,32,128]{2,1,0:T(8,128)S(1)}, u32[]{:S(2)}, u32[]{:S(2)}) collective-permute-start(f32[4,32,128]{2,1,0:T(8,128)S(1)} %pad_maximum_fusion.3), channel_id=1, source_target_pairs={{0,2},{1,3},{2,0},{3,1},{4,6},{5,7},{6,4},{7,5},{8,10},{9,11},{10,... | collective-permute-start | bytes 196616 | tf_op jit(solution)/shard_map/ppermute | solution.py:239
  13.4 2.6 %collective-permute-start.11 = (f32[4,32,128]{2,1,0:T(8,128)S(1)}, f32[4,32,128]{2,1,0:T(8,128)S(1)}, u32[]{:S(2)}, u32[]{:S(2)}) collective-permute-start(f32[4,32,128]{2,1,0:T(8,128)S(1)} %pad_maximum_fusion.4), channel_id=1, source_target_pairs={{0,4},{1,5},{2,6},{3,7},{4,0},{5,1},{6,2},{7,3},{8,12},{9,13},{10,... | collective-permute-start | bytes 196616 | tf_op jit(solution)/shard_map/ppermute | solution.py:239
  16.0 0.0 collective-permute-done
  16.0 0.1 add.24
  16.2 1.5 %collective-permute-start.1 = (f32[4,104,128]{2,1,0:T(8,128)S(1)}, f32[4,104,128]{2,1,0:T(8,128)S(1)}, u32[]{:S(2)}, u32[]{:S(2)}) collective-permute-start(f32[4,104,128]{2,1,0:T(8,128)S(1)} %get-tuple-element.30), channel_id=1, source_target_pairs={{0,1},{1,0},{2,3},{3,2},{4,5},{5,4},{6,7},{7,6},{8,9},{9,8},{10,11... | collective-permute-start | bytes 638984 | tf_op jit(solution)/shard_map/ppermute | solution.py:239
  17.7 1.5 %collective-permute-start.3 = (f32[4,104,128]{2,1,0:T(8,128)S(1)}, f32[4,104,128]{2,1,0:T(8,128)S(1)}, u32[]{:S(2)}, u32[]{:S(2)}) collective-permute-start(f32[4,104,128]{2,1,0:T(8,128)S(1)} %get-tuple-element.31), channel_id=1, source_target_pairs={{0,17},{1,16},{2,19},{3,18},{4,21},{5,20},{6,23},{7,22},{8,25},{9,... | collective-permute-start | bytes 638984 | tf_op jit(solution)/shard_map/ppermute | solution.py:239
  19.2 0.5 collective-permute-start.2
  19.7 0.0 collective-permute-done.10.refs_4_
  19.7 1.7 %collective-permute-start.12 = (f32[4,32,128]{2,1,0:T(8,128)S(1)}, f32[4,32,128]{2,1,0:T(8,128)S(1)}, u32[]{:S(2)}, u32[]{:S(2)}) collective-permute-start(f32[4,32,128]{2,1,0:T(8,128)S(1)} %pad_maximum_fusion.5), channel_id=1, source_target_pairs={{0,6},{1,7},{2,4},{3,5},{4,2},{5,3},{6,0},{7,1},{8,14},{9,15},{10,... | collective-permute-start | bytes 196616 | tf_op jit(solution)/shard_map/ppermute | solution.py:239
  21.4 0.0 collective-permute-done.11.refs_5_
  21.4 4.4 %collective-permute-done.12.refs_6_ = f32[4,32,128]{2,1,0:T(8,128)S(1)} collective-permute-done((f32[4,32,128]{2,1,0:T(8,128)S(1)}, f32[4,32,128]{2,1,0:T(8,128)S(1)}, u32[]{:S(2)}, u32[]{:S(2)}) %collective-permute-start.12) | collective-permute-done | bytes 65568 | tf_op jit(solution)/shard_map/ppermute | solution.py:239
  25.9 1.4 %shard_map.104 = (f32[8,32,128]{2,1,0:T(8,128)S(1)}, f32[8,32,128]{2,1,0:T(8,128)S(1)}) custom-call(f32[4,32,128]{2,1,0:T(8,128)S(1)} %get-tuple-element.18.refs_0_, f32[4,32,128]{2,1,0:T(8,128)S(1)} %collective-permute-done.7.refs_1_, f32[4,32,128]{2,1,0:T(8,128)S(1)} %collective-permute-done.8.refs_2_, f32[4,32,128]{2,1,0:T(8,128)S(1)} %collective-permute-done.9.refs_3_, ...), custom_call_target="tpu_custom_call" | custom-call | tf_op jit(solution)/shard_map/pallas_call | solution.py:30
  27.3 0.1 collective-permute-start.13
  27.4 1.3 %collective-permute-done.13 = f32[8,32,128]{2,1,0:T(8,128)S(1)} collective-permute-done((f32[8,32,128]{2,1,0:T(8,128)S(1)}, f32[8,32,128]{2,1,0:T(8,128)S(1)}, u32[]{:S(2)}, u32[]{:S(2)}) %collective-permute-start.13) | collective-permute-done | bytes 131104 | tf_op jit(solution)/shard_map/ppermute | solution.py:239
  28.7 0.0 collective-permute-done.1
  28.8 0.2 collective-permute-done.3
  28.9 1.4 %collective-permute-done.2 = f32[4,104,128]{2,1,0:T(8,128)S(1)} collective-permute-done((f32[4,104,128]{2,1,0:T(8,128)S(1)}, f32[4,104,128]{2,1,0:T(8,128)S(1)}, u32[]{:S(2)}, u32[]{:S(2)}) %collective-permute-start.2) | collective-permute-done | bytes 213024 | tf_op jit(solution)/shard_map/ppermute | solution.py:239
  30.3 0.1 fusion.4
  30.4 0.5 collective-permute-start.4
  30.9 1.8 %collective-permute-start.6 = (f32[104,128]{1,0:T(8,128)S(1)}, f32[104,128]{1,0:T(8,128)S(1)}, u32[]{:S(2)}, u32[]{:S(2)}) collective-permute-start(f32[104,128]{1,0:T(8,128)S(1)} %get-tuple-element.34), channel_id=1, source_target_pairs={{0,6},{1,7},{2,4},{3,5},{4,2},{5,3},{6,0},{7,1},{8,14},{9,15},{10,... | collective-permute-start | bytes 159752 | tf_op jit(solution)/shard_map/ppermute | solution.py:239
  32.7 1.2 %collective-permute-start.5 = (f32[104,128]{1,0:T(8,128)S(1)}, f32[104,128]{1,0:T(8,128)S(1)}, u32[]{:S(2)}, u32[]{:S(2)}) collective-permute-start(f32[104,128]{1,0:T(8,128)S(1)} %get-tuple-element.35), channel_id=1, source_target_pairs={{0,4},{1,5},{2,6},{3,7},{4,0},{5,1},{6,2},{7,3},{8,12},{9,13},{10,... | collective-permute-start | bytes 159752 | tf_op jit(solution)/shard_map/ppermute | solution.py:239
  34.0 1.3 %collective-permute-done.4 = f32[104,128]{1,0:T(8,128)S(1)} collective-permute-done((f32[104,128]{1,0:T(8,128)S(1)}, f32[104,128]{1,0:T(8,128)S(1)}, u32[]{:S(2)}, u32[]{:S(2)}) %collective-permute-start.4) | collective-permute-done | bytes 53280 | tf_op jit(solution)/shard_map/ppermute | solution.py:239
  35.3 1.6 %collective-permute-done.6 = f32[104,128]{1,0:T(8,128)S(1)} collective-permute-done((f32[104,128]{1,0:T(8,128)S(1)}, f32[104,128]{1,0:T(8,128)S(1)}, u32[]{:S(2)}, u32[]{:S(2)}) %collective-permute-start.6) | collective-permute-done | bytes 53280 | tf_op jit(solution)/shard_map/ppermute | solution.py:239
  36.8 1.6 %collective-permute-done.5 = f32[104,128]{1,0:T(8,128)S(1)} collective-permute-done((f32[104,128]{1,0:T(8,128)S(1)}, f32[104,128]{1,0:T(8,128)S(1)}, u32[]{:S(2)}, u32[]{:S(2)}) %collective-permute-start.5) | collective-permute-done | bytes 53280 | tf_op jit(solution)/shard_map/ppermute | solution.py:239
  38.5 0.2 collective-permute-start.14
  38.7 2.4 %collective-permute-start.15 = (f32[168,128]{1,0:T(8,128)S(1)}, f32[168,128]{1,0:T(8,128)S(1)}, u32[]{:S(2)}, u32[]{:S(2)}) collective-permute-start(f32[168,128]{1,0:T(8,128)S(1)} %get-tuple-element.53), channel_id=1, source_target_pairs={{0,4},{1,5},{2,6},{3,7},{4,0},{5,1},{6,2},{7,3},{8,12},{9,13},{10,... | collective-permute-start | bytes 258056 | tf_op jit(solution)/shard_map/ppermute | solution.py:239
  41.1 1.8 %collective-permute-start.16 = (f32[168,128]{1,0:T(8,128)S(1)}, f32[168,128]{1,0:T(8,128)S(1)}, u32[]{:S(2)}, u32[]{:S(2)}) collective-permute-start(f32[168,128]{1,0:T(8,128)S(1)} %get-tuple-element.54), channel_id=1, source_target_pairs={{0,6},{1,7},{2,4},{3,5},{4,2},{5,3},{6,0},{7,1},{8,14},{9,15},{10,... | collective-permute-start | bytes 258056 | tf_op jit(solution)/shard_map/ppermute | solution.py:239
  42.9 1.4 %collective-permute-done.14 = f32[168,128]{1,0:T(8,128)S(1)} collective-permute-done((f32[168,128]{1,0:T(8,128)S(1)}, f32[168,128]{1,0:T(8,128)S(1)}, u32[]{:S(2)}, u32[]{:S(2)}) %collective-permute-start.14) | collective-permute-done | bytes 86048 | tf_op jit(solution)/shard_map/ppermute | solution.py:239
  44.3 0.0 collective-permute-done.15
  44.3 0.6 copy-done.7
  45.0 2.4 %collective-permute-done.16 = f32[168,128]{1,0:T(8,128)S(1)} collective-permute-done((f32[168,128]{1,0:T(8,128)S(1)}, f32[168,128]{1,0:T(8,128)S(1)}, u32[]{:S(2)}, u32[]{:S(2)}) %collective-permute-start.16) | collective-permute-done | bytes 86048 | tf_op jit(solution)/shard_map/ppermute | solution.py:239
  47.4 0.9 %slice-done = f32[136,128]{1,0:T(8,128)S(1)} async-done(((f32[168,128]{1,0:T(8,128)}), f32[136,128]{1,0:T(8,128)S(1)}, s32[]{:S(2)}) %slice-start) | async-done | bytes 69656 | tf_op jit(solution)/shard_map/slice | solution.py:310
  48.3 1.2 %collective-permute-start.18 = (f32[544,128]{1,0:T(8,128)S(1)}, f32[544,128]{1,0:T(8,128)S(1)}, u32[]{:S(2)}, u32[]{:S(2)}) collective-permute-start(f32[544,128]{1,0:T(8,128)S(1)} %fusion.2.refs_0_), channel_id=1, source_target_pairs={{0,16},{1,17},{2,18},{3,19},{4,20},{5,21},{6,22},{7,23},{8,24},{9,... | collective-permute-start | bytes 835592 | tf_op jit(solution)/shard_map/ppermute | solution.py:239
  49.5 0.0 copy-done.8
  49.6 0.0 copy-start.1
  49.6 1.9 %collective-permute-start.19 = (f32[544,128]{1,0:T(8,128)S(1)}, f32[544,128]{1,0:T(8,128)S(1)}, u32[]{:S(2)}, u32[]{:S(2)}) collective-permute-start(f32[544,128]{1,0:T(8,128)S(1)} %constant_dynamic-update-slice_fusion), channel_id=1, source_target_pairs={{0,17},{1,16},{2,19},{3,18},{4,21},{5,20},{6,23},{7,22},{8,25},{9,... | collective-permute-start | bytes 835592 | tf_op jit(solution)/shard_map/ppermute | solution.py:239
  51.5 0.5 collective-permute-start.17
  52.0 0.0 collective-permute-start.20
  52.0 7.9 %collective-permute-done.18.refs_2_ = f32[544,128]{1,0:T(8,128)S(1)} collective-permute-done((f32[544,128]{1,0:T(8,128)S(1)}, f32[544,128]{1,0:T(8,128)S(1)}, u32[]{:S(2)}, u32[]{:S(2)}) %collective-permute-start.18) | collective-permute-done | bytes 278560 | tf_op jit(solution)/shard_map/ppermute | solution.py:239
  59.9 0.0 collective-permute-start.22
  59.9 0.0 collective-permute-done.19.refs_3_
  59.9 0.5 collective-permute-start.23
  60.4 1.6 %collective-permute-done.17.refs_1_ = f32[544,128]{1,0:T(8,128)S(1)} collective-permute-done((f32[544,128]{1,0:T(8,128)S(1)}, f32[544,128]{1,0:T(8,128)S(1)}, u32[]{:S(2)}, u32[]{:S(2)}) %collective-permute-start.17) | collective-permute-done | bytes 278560 | tf_op jit(solution)/shard_map/ppermute | solution.py:239
  62.0 0.0 collective-permute-start.21
  62.0 0.0 collective-permute-done.20.refs_4_
  62.0 0.0 collective-permute-done.22.refs_6_
  62.0 0.0 collective-permute-done.23.refs_7_
  62.0 1.5 %collective-permute-done.21.refs_5_ = f32[544,128]{1,0:T(8,128)S(1)} collective-permute-done((f32[544,128]{1,0:T(8,128)S(1)}, f32[544,128]{1,0:T(8,128)S(1)}, u32[]{:S(2)}, u32[]{:S(2)}) %collective-permute-start.21) | collective-permute-done | bytes 278560 | tf_op jit(solution)/shard_map/ppermute | solution.py:239
  63.6 2.8 %shard_map.105 = (f32[16,32,288]{2,1,0:T(8,128)}, f32[512,512]{1,0:T(8,128)}, f32[16,32,32]{2,1,0:T(8,128)}, f32[12,24,288]{2,1,0:T(8,128)}) custom-call(s32[4,24]{1,0:T(4,128)S(1)} %copy-done.1, f32[544,128]{1,0:T(8,128)S(1)} %fusion.2.refs_0_, f32[544,128]{1,0:T(8,128)S(1)} %collective-permute-done.17.refs_1_, ...), custom_call_target="tpu_custom_call" | custom-call | tf_op jit(solution)/shard_map/pallas_call | solution.py:30
  (33 shorter events, 0.2 us)
Async XLA Ops:
  0.6 0.9 %copy-start = (bf16[2,8,8,512]{3,2,1,0:T(8,128)(2,1)S(1)}, bf16[2,8,8,512]{3,2,1,0:T(8,128)(2,1)}, u32[]{:S(2)}) copy-start(bf16[2,8,8,512]{3,2,1,0:T(8,128)(2,1)} %x_hbm.1) | copy-start | bytes 393220
  1.5 4.9 %copy-start.4 = (bf16[2,8,8,512]{3,2,1,0:T(8,128)(2,1)S(1)}, bf16[2,8,8,512]{3,2,1,0:T(8,128)(2,1)}, u32[]{:S(2)}) copy-start(bf16[2,8,8,512]{3,2,1,0:T(8,128)(2,1)} %refs_1_.1) | copy-start | bytes 393220
  1.8 9.4 %collective-permute-start.7 = (f32[4,32,128]{2,1,0:T(8,128)S(1)}, f32[4,32,128]{2,1,0:T(8,128)S(1)}, u32[]{:S(2)}, u32[]{:S(2)}) collective-permute-start(f32[4,32,128]{2,1,0:T(8,128)S(1)} %get-tuple-element.19), channel_id=1, source_target_pairs={{0,1},{1,0},{2,3},{3,2},{4,5},{5,4},{6,7},{7,6},{8,9},{9,8},{10,11... | collective-permute-start | bytes 196616 | tf_op jit(solution)/shard_map/ppermute | solution.py:239
  4.8 6.4 %collective-permute-start.8 = (f32[4,32,128]{2,1,0:T(8,128)S(1)}, f32[4,32,128]{2,1,0:T(8,128)S(1)}, u32[]{:S(2)}, u32[]{:S(2)}) collective-permute-start(f32[4,32,128]{2,1,0:T(8,128)S(1)} %get-tuple-element.20), channel_id=1, source_target_pairs={{0,16},{1,17},{2,18},{3,19},{4,20},{5,21},{6,22},{7,23},{8,24},{9,... | collective-permute-start | bytes 196616 | tf_op jit(solution)/shard_map/ppermute | solution.py:239
  6.4 5.2 %collective-permute-start.9 = (f32[4,32,128]{2,1,0:T(8,128)S(1)}, f32[4,32,128]{2,1,0:T(8,128)S(1)}, u32[]{:S(2)}, u32[]{:S(2)}) collective-permute-start(f32[4,32,128]{2,1,0:T(8,128)S(1)} %get-tuple-element.21), channel_id=1, source_target_pairs={{0,17},{1,16},{2,19},{3,18},{4,21},{5,20},{6,23},{7,22},{8,25},{9,... | collective-permute-start | bytes 196616 | tf_op jit(solution)/shard_map/ppermute | solution.py:239
  6.4 0.7 %copy-start.6 = (f32[512]{0:T(512)S(1)}, f32[512]{0:T(512)}, u32[]{:S(2)}) copy-start(f32[512]{0:T(512)} %param.12) | copy-start | bytes 6148
  6.4 0.7 %copy-start.5 = (f32[512]{0:T(512)S(1)}, f32[512]{0:T(512)}, u32[]{:S(2)}) copy-start(f32[512]{0:T(512)} %param.11) | copy-start | bytes 6148
  7.1 1.0 %copy-start.2 = (bf16[512,512]{1,0:T(8,128)(2,1)S(1)}, bf16[512,512]{1,0:T(8,128)(2,1)}, u32[]{:S(2)}) copy-start(bf16[512,512]{1,0:T(8,128)(2,1)} %refs_3_.1) | copy-start | bytes 1572868
  8.1 1.0 %copy-start.3 = (bf16[16,288,32]{1,2,0:T(8,128)(2,1)S(1)}, bf16[16,288,32]{1,2,0:T(8,128)(2,1)}, u32[]{:S(2)}) copy-start(bf16[16,288,32]{1,2,0:T(8,128)(2,1)} %param.9) | copy-start | bytes 884740
  11.1 4.9 %collective-permute-start = (f32[16,104,128]{2,1,0:T(8,128)S(1)}, f32[16,104,128]{2,1,0:T(8,128)S(1)}, u32[]{:S(2)}, u32[]{:S(2)}) collective-permute-start(f32[16,104,128]{2,1,0:T(8,128)S(1)} %get-tuple-element.17), channel_id=1, source_target_pairs={{0,8},{1,9},{2,10},{3,11},{4,12},{5,13},{6,14},{7,15},{8,0},{9,1},... | collective-permute-start | bytes 2555912 | tf_op jit(solution)/shard_map/ppermute | solution.py:239
  11.5 8.2 %collective-permute-start.10 = (f32[4,32,128]{2,1,0:T(8,128)S(1)}, f32[4,32,128]{2,1,0:T(8,128)S(1)}, u32[]{:S(2)}, u32[]{:S(2)}) collective-permute-start(f32[4,32,128]{2,1,0:T(8,128)S(1)} %pad_maximum_fusion.3), channel_id=1, source_target_pairs={{0,2},{1,3},{2,0},{3,1},{4,6},{5,7},{6,4},{7,5},{8,10},{9,11},{10,... | collective-permute-start | bytes 196616 | tf_op jit(solution)/shard_map/ppermute | solution.py:239
  13.4 8.0 %collective-permute-start.11 = (f32[4,32,128]{2,1,0:T(8,128)S(1)}, f32[4,32,128]{2,1,0:T(8,128)S(1)}, u32[]{:S(2)}, u32[]{:S(2)}) collective-permute-start(f32[4,32,128]{2,1,0:T(8,128)S(1)} %pad_maximum_fusion.4), channel_id=1, source_target_pairs={{0,4},{1,5},{2,6},{3,7},{4,0},{5,1},{6,2},{7,3},{8,12},{9,13},{10,... | collective-permute-start | bytes 196616 | tf_op jit(solution)/shard_map/ppermute | solution.py:239
  16.2 12.6 %collective-permute-start.1 = (f32[4,104,128]{2,1,0:T(8,128)S(1)}, f32[4,104,128]{2,1,0:T(8,128)S(1)}, u32[]{:S(2)}, u32[]{:S(2)}) collective-permute-start(f32[4,104,128]{2,1,0:T(8,128)S(1)} %get-tuple-element.30), channel_id=1, source_target_pairs={{0,1},{1,0},{2,3},{3,2},{4,5},{5,4},{6,7},{7,6},{8,9},{9,8},{10,11... | collective-permute-start | bytes 638984 | tf_op jit(solution)/shard_map/ppermute | solution.py:239
  17.7 11.2 %collective-permute-start.3 = (f32[4,104,128]{2,1,0:T(8,128)S(1)}, f32[4,104,128]{2,1,0:T(8,128)S(1)}, u32[]{:S(2)}, u32[]{:S(2)}) collective-permute-start(f32[4,104,128]{2,1,0:T(8,128)S(1)} %get-tuple-element.31), channel_id=1, source_target_pairs={{0,17},{1,16},{2,19},{3,18},{4,21},{5,20},{6,23},{7,22},{8,25},{9,... | collective-permute-start | bytes 638984 | tf_op jit(solution)/shard_map/ppermute | solution.py:239
  19.2 11.1 %collective-permute-start.2 = (f32[4,104,128]{2,1,0:T(8,128)S(1)}, f32[4,104,128]{2,1,0:T(8,128)S(1)}, u32[]{:S(2)}, u32[]{:S(2)}) collective-permute-start(f32[4,104,128]{2,1,0:T(8,128)S(1)} %get-tuple-element.32), channel_id=1, source_target_pairs={{0,16},{1,17},{2,18},{3,19},{4,20},{5,21},{6,22},{7,23},{8,24},{9,... | collective-permute-start | bytes 638984 | tf_op jit(solution)/shard_map/ppermute | solution.py:239
  19.7 6.1 %collective-permute-start.12 = (f32[4,32,128]{2,1,0:T(8,128)S(1)}, f32[4,32,128]{2,1,0:T(8,128)S(1)}, u32[]{:S(2)}, u32[]{:S(2)}) collective-permute-start(f32[4,32,128]{2,1,0:T(8,128)S(1)} %pad_maximum_fusion.5), channel_id=1, source_target_pairs={{0,6},{1,7},{2,4},{3,5},{4,2},{5,3},{6,0},{7,1},{8,14},{9,15},{10,... | collective-permute-start | bytes 196616 | tf_op jit(solution)/shard_map/ppermute | solution.py:239
  27.3 1.4 %collective-permute-start.13 = (f32[8,32,128]{2,1,0:T(8,128)S(1)}, f32[8,32,128]{2,1,0:T(8,128)S(1)}, u32[]{:S(2)}, u32[]{:S(2)}) collective-permute-start(f32[8,32,128]{2,1,0:T(8,128)S(1)} %get-tuple-element.23), channel_id=1, source_target_pairs={{0,8},{1,9},{2,10},{3,11},{4,12},{5,13},{6,14},{7,15},{8,0},{9,1},... | collective-permute-start | bytes 393224 | tf_op jit(solution)/shard_map/ppermute | solution.py:239
  30.4 4.9 %collective-permute-start.4 = (f32[104,128]{1,0:T(8,128)S(1)}, f32[104,128]{1,0:T(8,128)S(1)}, u32[]{:S(2)}, u32[]{:S(2)}) collective-permute-start(f32[104,128]{1,0:T(8,128)S(1)} %get-tuple-element.33), channel_id=1, source_target_pairs={{0,2},{1,3},{2,0},{3,1},{4,6},{5,7},{6,4},{7,5},{8,10},{9,11},{10,... | collective-permute-start | bytes 159752 | tf_op jit(solution)/shard_map/ppermute | solution.py:239
  30.9 5.9 %collective-permute-start.6 = (f32[104,128]{1,0:T(8,128)S(1)}, f32[104,128]{1,0:T(8,128)S(1)}, u32[]{:S(2)}, u32[]{:S(2)}) collective-permute-start(f32[104,128]{1,0:T(8,128)S(1)} %get-tuple-element.34), channel_id=1, source_target_pairs={{0,6},{1,7},{2,4},{3,5},{4,2},{5,3},{6,0},{7,1},{8,14},{9,15},{10,... | collective-permute-start | bytes 159752 | tf_op jit(solution)/shard_map/ppermute | solution.py:239
  32.7 5.7 %collective-permute-start.5 = (f32[104,128]{1,0:T(8,128)S(1)}, f32[104,128]{1,0:T(8,128)S(1)}, u32[]{:S(2)}, u32[]{:S(2)}) collective-permute-start(f32[104,128]{1,0:T(8,128)S(1)} %get-tuple-element.35), channel_id=1, source_target_pairs={{0,4},{1,5},{2,6},{3,7},{4,0},{5,1},{6,2},{7,3},{8,12},{9,13},{10,... | collective-permute-start | bytes 159752 | tf_op jit(solution)/shard_map/ppermute | solution.py:239
  38.5 5.8 %collective-permute-start.14 = (f32[168,128]{1,0:T(8,128)S(1)}, f32[168,128]{1,0:T(8,128)S(1)}, u32[]{:S(2)}, u32[]{:S(2)}) collective-permute-start(f32[168,128]{1,0:T(8,128)S(1)} %get-tuple-element.52), channel_id=1, source_target_pairs={{0,2},{1,3},{2,0},{3,1},{4,6},{5,7},{6,4},{7,5},{8,10},{9,11},{10,... | collective-permute-start | bytes 258056 | tf_op jit(solution)/shard_map/ppermute | solution.py:239
  38.7 5.7 %collective-permute-start.15 = (f32[168,128]{1,0:T(8,128)S(1)}, f32[168,128]{1,0:T(8,128)S(1)}, u32[]{:S(2)}, u32[]{:S(2)}) collective-permute-start(f32[168,128]{1,0:T(8,128)S(1)} %get-tuple-element.53), channel_id=1, source_target_pairs={{0,4},{1,5},{2,6},{3,7},{4,0},{5,1},{6,2},{7,3},{8,12},{9,13},{10,... | collective-permute-start | bytes 258056 | tf_op jit(solution)/shard_map/ppermute | solution.py:239
  41.1 6.3 %collective-permute-start.16 = (f32[168,128]{1,0:T(8,128)S(1)}, f32[168,128]{1,0:T(8,128)S(1)}, u32[]{:S(2)}, u32[]{:S(2)}) collective-permute-start(f32[168,128]{1,0:T(8,128)S(1)} %get-tuple-element.54), channel_id=1, source_target_pairs={{0,6},{1,7},{2,4},{3,5},{4,2},{5,3},{6,0},{7,1},{8,14},{9,15},{10,... | collective-permute-start | bytes 258056 | tf_op jit(solution)/shard_map/ppermute | solution.py:239
  44.3 0.6 copy-start.7
  47.4 0.9 %slice-start = ((f32[168,128]{1,0:T(8,128)}), f32[136,128]{1,0:T(8,128)S(1)}, s32[]{:S(2)}) async-start(f32[168,128]{1,0:T(8,128)} %copy-done.7), calls=%async_computation | async-start | bytes 139264 | tf_op jit(solution)/shard_map/slice | solution.py:310
  48.3 1.3 %copy-start.8 = (f32[168,128]{1,0:T(8,128)S(1)}, f32[168,128]{1,0:T(8,128)}, u32[]{:S(2)}) copy-start(f32[168,128]{1,0:T(8,128)} %copy-done.7) | copy-start | bytes 258052
  48.3 11.6 %collective-permute-start.18 = (f32[544,128]{1,0:T(8,128)S(1)}, f32[544,128]{1,0:T(8,128)S(1)}, u32[]{:S(2)}, u32[]{:S(2)}) collective-permute-start(f32[544,128]{1,0:T(8,128)S(1)} %fusion.2.refs_0_), channel_id=1, source_target_pairs={{0,16},{1,17},{2,18},{3,19},{4,20},{5,21},{6,22},{7,23},{8,24},{9,... | collective-permute-start | bytes 835592 | tf_op jit(solution)/shard_map/ppermute | solution.py:239
  49.6 14.0 %copy-start.1 = (s32[4,24]{1,0:T(4,128)S(1)}, s32[4,24]{1,0:T(4,128)}, u32[]{:S(2)}) copy-start(s32[4,24]{1,0:T(4,128)} %slot_ref.1) | copy-start | bytes 1156
  49.6 10.3 %collective-permute-start.19 = (f32[544,128]{1,0:T(8,128)S(1)}, f32[544,128]{1,0:T(8,128)S(1)}, u32[]{:S(2)}, u32[]{:S(2)}) collective-permute-start(f32[544,128]{1,0:T(8,128)S(1)} %constant_dynamic-update-slice_fusion), channel_id=1, source_target_pairs={{0,17},{1,16},{2,19},{3,18},{4,21},{5,20},{6,23},{7,22},{8,25},{9,... | collective-permute-start | bytes 835592 | tf_op jit(solution)/shard_map/ppermute | solution.py:239
  51.5 10.5 %collective-permute-start.17 = (f32[544,128]{1,0:T(8,128)S(1)}, f32[544,128]{1,0:T(8,128)S(1)}, u32[]{:S(2)}, u32[]{:S(2)}) collective-permute-start(f32[544,128]{1,0:T(8,128)S(1)} %constant_dynamic-update-slice_fusion), channel_id=1, source_target_pairs={{0,1},{1,0},{2,3},{3,2},{4,5},{5,4},{6,7},{7,6},{8,9},{9,8},{10,11... | collective-permute-start | bytes 835592 | tf_op jit(solution)/shard_map/ppermute | solution.py:239
  52.0 10.0 %collective-permute-start.20 = (f32[544,128]{1,0:T(8,128)S(1)}, f32[544,128]{1,0:T(8,128)S(1)}, u32[]{:S(2)}, u32[]{:S(2)}) collective-permute-start(f32[544,128]{1,0:T(8,128)S(1)} %fusion.2.refs_0_), channel_id=1, source_target_pairs={{0,8},{1,9},{2,10},{3,11},{4,12},{5,13},{6,14},{7,15},{8,0},{9,1},... | collective-permute-start | bytes 835592 | tf_op jit(solution)/shard_map/ppermute | solution.py:239
  59.9 2.2 %collective-permute-start.22 = (f32[544,128]{1,0:T(8,128)S(1)}, f32[544,128]{1,0:T(8,128)S(1)}, u32[]{:S(2)}, u32[]{:S(2)}) collective-permute-start(f32[544,128]{1,0:T(8,128)S(1)} %collective-permute-done.18.refs_2_), channel_id=1, source_target_pairs={{0,8},{1,9},{2,10},{3,11},{4,12},{5,13},{6,14},{7,15},{8,0},{9,1},... | collective-permute-start | bytes 835592 | tf_op jit(solution)/shard_map/ppermute | solution.py:239
  59.9 2.2 %collective-permute-start.23 = (f32[544,128]{1,0:T(8,128)S(1)}, f32[544,128]{1,0:T(8,128)S(1)}, u32[]{:S(2)}, u32[]{:S(2)}) collective-permute-start(f32[544,128]{1,0:T(8,128)S(1)} %collective-permute-done.19.refs_3_), channel_id=1, source_target_pairs={{0,8},{1,9},{2,10},{3,11},{4,12},{5,13},{6,14},{7,15},{8,0},{9,1},... | collective-permute-start | bytes 835592 | tf_op jit(solution)/shard_map/ppermute | solution.py:239
  62.0 1.6 %collective-permute-start.21 = (f32[544,128]{1,0:T(8,128)S(1)}, f32[544,128]{1,0:T(8,128)S(1)}, u32[]{:S(2)}, u32[]{:S(2)}) collective-permute-start(f32[544,128]{1,0:T(8,128)S(1)} %collective-permute-done.17.refs_1_), channel_id=1, source_target_pairs={{0,8},{1,9},{2,10},{3,11},{4,12},{5,13},{6,14},{7,15},{8,0},{9,1},... | collective-permute-start | bytes 835592 | tf_op jit(solution)/shard_map/ppermute | solution.py:239

commit v4 on v3

--- a/solution.py
+++ b/solution.py
@@ -11,6 +11,7 @@
 AXES = ("owner", "dp")
 F32 = jnp.float32
 BF16 = jnp.bfloat16
+SEND_FLOPS = 6000000000
 LOCAL_FLOPS = 4000000000
 VMEM_LIMIT = 48 * 1024 * 1024
 PAIRS = ((0, 0), (0, 1), (0, 2), (1, 0), (1, 1), (2, 0), (2, 2))
@@ -192,15 +193,42 @@
     give_ref[...] = held[1]
 
 
+def line_kernel(total_ref, piece_ref, first_ref, first_peer_ref, *line_refs):
+    total = total_ref[...]
+    size = first_ref.shape[0]
+    first_ref[:104, :] = total
+    first_ref[104:, :] = piece_ref[0, : size - 104, :]
+    first_peer_ref[:104, :] = total
+    first_peer_ref[104:, :] = piece_ref[0, size - 104 :, :]
+    for z, ref in enumerate(line_refs):
+        ref[:104, :] = total
+        ref[104:, :] = piece_ref[z + 1]
+
+
+def merge_kernel(*refs):
+    parts, (own_ref, peer_ref) = refs[:3], refs[3:]
+    size = own_ref.shape[0] // 3
+    for z, ref in enumerate(parts):
+        at = size * z
+        own_ref[at : at + size, :] = ref[:size, :]
+        peer_ref[at : at + 104, :] = ref[:104, :]
+        peer_ref[at + 104 : at + size, :] = ref[size:, :]
+
+
 def finish_kernel(grad_scale, mean_scale, slot_ref, *refs):
-    parts, (group_ref, proj_ref, out_ref, owned_ref), (sums, blocks) = refs[:8], refs[8:12], refs[12:]
+    parts, (group_ref, proj_ref, out_ref, owned_ref), (sums, blocks) = refs[:13], refs[13:17], refs[17:]
     me = cell_id()
     count = owned_ref.shape[0] // 2
     step = 104 + packed_rows(count)
-    for place, ref in enumerate(parts):
+    for place in range(8):
         for z in range(4):
             j = (4 * place + z) ^ me
-            base = step * z
+            if z > 0:
+                ref, base = parts[5 + place], step * (z - 1)
+            elif place < 4:
+                ref, base = parts[place], 0
+            else:
+                ref, base = parts[4].at[place - 4], 0
             for w in range(4):
                 at = pl.multiple_of(16 * j, 16)
                 row = base + 16 * w
@@ -259,9 +287,8 @@
         [pltpu.VMEM(activations.shape, BF16), pltpu.VMEM((16, 32, 128), F32), pltpu.SemaphoreType.DMA],
         activations,
         in_hbm=True,
-    )
-    got = [sent[0], swap(sent[1], 0, 1), swap(sent[2], 2, 0), swap(sent[3], 2, 1)]
-
+        flops=SEND_FLOPS,
+    )
     inputs = [
         activations,
         out_grad,
@@ -284,12 +311,12 @@
         in_hbm=True,
         flops=LOCAL_FLOPS,
     )
+    sent, other = lax.optimization_barrier((sent, other))
+    got = [sent[0], swap(sent[1], 0, 1), swap(sent[2], 2, 0), swap(sent[3], 2, 1)]
     total = mine + swap(other, 1, 0)
+    total, got = lax.optimization_barrier((total, got))
     far = [swap(jnp.stack([v[z] for v in got]), 0, 2 * z) for z in range(1, 4)]
     total = total[0:4] + swap(total[4:8], 0, 1) + swap(total[8:12], 2, 0) + swap(total[12:16], 2, 1)
-    total = total[0] + swap(total[1], 0, 2) + swap(total[2], 0, 4) + swap(total[3], 0, 6)
-    total = add_over(total, far_owner, far_dp)
-
     half = 96 // n_dp
     packed = packed_rows(half // 2)
     keep, give = call(
@@ -299,18 +326,28 @@
         *got,
         *far,
     )
+    give, total = lax.optimization_barrier((give, total))
+    total = total[0] + swap(total[1], 0, 2) + swap(total[2], 0, 4) + swap(total[3], 0, 6)
+    total = add_over(total, far_owner, far_dp)
+
     piece = add_over(keep + swap(give, 1, 0), far_owner, ())
     for bit in reversed(far_dp):
         near = piece.shape[0] // 2
         piece = piece[:near] + swap(piece[near:], 0, 1 << bit)
     piece = piece.reshape(4, 2 * packed, 128)
 
-    line = [jnp.concatenate([total, piece[z]]) for z in range(4)]
-    line = [line[0]] + [swap(line[z], 0, 2 * z) for z in range(1, 4)]
-    own = jnp.concatenate([v[: 104 + packed] for v in line])
-    peer = jnp.concatenate([w for v in line for w in (v[:104], v[104 + packed :])])
-    near = [own, swap(peer, 0, 1), swap(own, 2, 0), swap(peer, 2, 1)]
-    parts = near + [swap(v, 1, 0) for v in near]
+    first, first_peer, *line = call(
+        line_kernel,
+        [((104 + packed, 128), F32)] * 2 + [((104 + 2 * packed, 128), F32)] * 3,
+        [],
+        total,
+        piece,
+    )
+    line = [swap(line[z - 1], 0, 2 * z) for z in range(1, 4)]
+    early = [first, swap(first_peer, 0, 1), swap(first, 2, 0), swap(first_peer, 2, 1)]
+    own, peer = call(merge_kernel, [((3 * (104 + packed), 128), F32)] * 2, [], *line)
+    late = [own, swap(peer, 0, 1), swap(own, 2, 0), swap(peer, 2, 1)]
+    parts = early + [swap(jnp.stack(early), 1, 0)] + late + [swap(v, 1, 0) for v in late]
     slots = slot_block.shape[1]
     group_grad, proj_grad, out_factor, factor_owned = call(
         functools.partial(finish_kernel, grad_scale, mean_scale),

time: 66.7 us -> 61.2 us (0.918)
  waiting for transfers between devices: 26.9 us -> 22.8 us
  local copies, waits for them, and re-layouts: 5.27 us -> 1.73 us
  starting transfers between devices: 26.5 us -> 28.8 us
    ppermute x24 -> x28, waiting for transfers between devices: 26.9 us -> 22.8 us  [swap(): return lax.ppermute(value, AXES, pairs)]
    unnamed x24 -> x14, local copies, waits for them, and re-layouts: 4.29 us -> 1.66 us
    ppermute x24 -> x28, starting transfers between devices: 26.5 us -> 28.8 us  [swap(): return lax.ppermute(value, AXES, pairs)]
    slice x5 -> x0, local copies, waits for them, and re-layouts: 0.89 us -> none  [the longest x4 0.89 us: per_device(): own = jnp.concatenate([v[:104 + packed] for v in line])]
    pallas_call x4 -> x6, Pallas kernels: 6.55 us -> 6.62 us  [call(): pl.pallas_call(body, out_shape=[jax.ShapeDtypeStruct(shape, kind) for sha...]
  transfers between devices with their start and end apart: 24 -> 28, of which waited for: 13 -> 14; matrix products, arithmetic and copies ran while one was open for 0% -> 0% of each run, Pallas kernels for 5% -> 2%
where the time goes in v4:
time: 61.2 us; the launch traced here: 61 us
  starting transfers between devices  28.8 us (47%)
  waiting for transfers between devices  22.8 us (37%)
  Pallas kernels  6.62 us (11%)
  local copies, waits for them, and re-layouts  1.73 us (3%)
  between operations  0.85 us (1%)
    ppermute x28, starting transfers between devices, swap(): return lax.ppermute(value, AXES, pairs)  28.8 us
    ppermute x28, waiting for transfers between devices, swap(): return lax.ppermute(value, AXES, pairs)  22.8 us
    pallas_call x6, Pallas kernels, call(): pl.pallas_call(body, out_shape=[jax.ShapeDtypeStruct(shape, kind) for sha...  6.62 us
    unnamed x14, local copies, waits for them, and re-layouts  1.66 us
  transfers between devices with their start and end apart: 28, of which 14 were waited for; matrix products, arithmetic and copies ran while one was open for 0% of the time, Pallas kernels for 2%

profile of v4, /device:TPU:0, one launch (start us, length us, event | category | flops | bytes accessed | tf_op | source)
XLA Modules:
  0.0 61.0 jit_solution(13110022459158592077)
XLA Ops:
  0.7 1.0 %copy-done.3 = bf16[2,8,8,512]{3,2,1,0:T(8,128)(2,1)S(1)} copy-done((bf16[2,8,8,512]{3,2,1,0:T(8,128)(2,1)S(1)}, bf16[2,8,8,512]{3,2,1,0:T(8,128)(2,1)}, u32[]{:S(2)}) %copy-start.3) | copy-done | bytes 131096
  1.6 0.3 shard_map.103
  2.0 0.0 copy-start.5
  2.0 0.6 copy-done.4
  2.6 0.1 copy-done.5
  2.6 2.0 %shard_map.102 = (f32[16,104,128]{2,1,0:T(8,128)S(1)}, f32[16,104,128]{2,1,0:T(8,128)S(1)}) custom-call(bf16[2,8,8,512]{3,2,1,0:T(8,128)(2,1)S(1)} %copy-done.3, bf16[2,8,8,512]{3,2,1,0:T(8,128)(2,1)S(1)} %copy-done.4, bf16[16,32,288]{2,1,0:T(8,128)(2,1)S(1)} %bitcast.27, bf16[512,512]{1,0:T(8,128)(2,1)S(1)} %copy-done.1, f32[1,512]{1,0:T(1,128)S(1)} %bitcast.28, ...), custom_call_target="tpu_custom_call" | custom-call | flops 4000000000 | tf_op jit(solution)/shard_map/pallas_call | solution.py:31
  4.7 0.5 collective-permute-start
  5.2 2.6 %collective-permute-start.1 = (f32[4,32,128]{2,1,0:T(8,128)S(1)}, f32[4,32,128]{2,1,0:T(8,128)S(1)}, u32[]{:S(2)}, u32[]{:S(2)}) collective-permute-start(f32[4,32,128]{2,1,0:T(8,128)S(1)} %get-tuple-element.43), channel_id=1, source_target_pairs={{0,1},{1,0},{2,3},{3,2},{4,5},{5,4},{6,7},{7,6},{8,9},{9,8},{10,11... | collective-permute-start | bytes 196616 | tf_op jit(solution)/shard_map/ppermute | solution.py:267
  7.7 1.5 %collective-permute-start.2 = (f32[4,32,128]{2,1,0:T(8,128)S(1)}, f32[4,32,128]{2,1,0:T(8,128)S(1)}, u32[]{:S(2)}, u32[]{:S(2)}) collective-permute-start(f32[4,32,128]{2,1,0:T(8,128)S(1)} %get-tuple-element.44), channel_id=1, source_target_pairs={{0,16},{1,17},{2,18},{3,19},{4,20},{5,21},{6,22},{7,23},{8,24},{9,... | collective-permute-start | bytes 196616 | tf_op jit(solution)/shard_map/ppermute | solution.py:267
  9.2 0.0 collective-permute-start.3
  9.3 0.0 collective-permute-done
  9.3 0.1 add.24
  9.4 1.0 %collective-permute-done.1.refs_1_ = f32[4,32,128]{2,1,0:T(8,128)S(1)} collective-permute-done((f32[4,32,128]{2,1,0:T(8,128)S(1)}, f32[4,32,128]{2,1,0:T(8,128)S(1)}, u32[]{:S(2)}, u32[]{:S(2)}) %collective-permute-start.1) | collective-permute-done | bytes 65568 | tf_op jit(solution)/shard_map/ppermute | solution.py:267
  10.4 1.6 %collective-permute-done.2.refs_2_ = f32[4,32,128]{2,1,0:T(8,128)S(1)} collective-permute-done((f32[4,32,128]{2,1,0:T(8,128)S(1)}, f32[4,32,128]{2,1,0:T(8,128)S(1)}, u32[]{:S(2)}, u32[]{:S(2)}) %collective-permute-start.2) | collective-permute-done | bytes 65568 | tf_op jit(solution)/shard_map/ppermute | solution.py:267
  12.0 2.4 %collective-permute-done.3.refs_3_ = f32[4,32,128]{2,1,0:T(8,128)S(1)} collective-permute-done((f32[4,32,128]{2,1,0:T(8,128)S(1)}, f32[4,32,128]{2,1,0:T(8,128)S(1)}, u32[]{:S(2)}, u32[]{:S(2)}) %collective-permute-start.3) | collective-permute-done | bytes 65568 | tf_op jit(solution)/shard_map/ppermute | solution.py:267
  14.5 1.7 %collective-permute-start.4 = (f32[4,32,128]{2,1,0:T(8,128)S(1)}, f32[4,32,128]{2,1,0:T(8,128)S(1)}, u32[]{:S(2)}, u32[]{:S(2)}) collective-permute-start(f32[4,32,128]{2,1,0:T(8,128)S(1)} %pad_maximum_fusion.1), channel_id=1, source_target_pairs={{0,2},{1,3},{2,0},{3,1},{4,6},{5,7},{6,4},{7,5},{8,10},{9,11},{10,... | collective-permute-start | bytes 196616 | tf_op jit(solution)/shard_map/ppermute | solution.py:267
  16.2 0.6 collective-permute-start.7
  16.8 1.4 %collective-permute-start.9 = (f32[4,104,128]{2,1,0:T(8,128)S(1)}, f32[4,104,128]{2,1,0:T(8,128)S(1)}, u32[]{:S(2)}, u32[]{:S(2)}) collective-permute-start(f32[4,104,128]{2,1,0:T(8,128)S(1)} %get-tuple-element.67), channel_id=1, source_target_pairs={{0,17},{1,16},{2,19},{3,18},{4,21},{5,20},{6,23},{7,22},{8,25},{9,... | collective-permute-start | bytes 638984 | tf_op jit(solution)/shard_map/ppermute | solution.py:267
  18.2 1.5 %collective-permute-start.8 = (f32[4,104,128]{2,1,0:T(8,128)S(1)}, f32[4,104,128]{2,1,0:T(8,128)S(1)}, u32[]{:S(2)}, u32[]{:S(2)}) collective-permute-start(f32[4,104,128]{2,1,0:T(8,128)S(1)} %get-tuple-element.68), channel_id=1, source_target_pairs={{0,16},{1,17},{2,18},{3,19},{4,20},{5,21},{6,22},{7,23},{8,24},{9,... | collective-permute-start | bytes 638984 | tf_op jit(solution)/shard_map/ppermute | solution.py:267
  19.7 2.6 %collective-permute-start.5 = (f32[4,32,128]{2,1,0:T(8,128)S(1)}, f32[4,32,128]{2,1,0:T(8,128)S(1)}, u32[]{:S(2)}, u32[]{:S(2)}) collective-permute-start(f32[4,32,128]{2,1,0:T(8,128)S(1)} %pad_maximum_fusion.2), channel_id=1, source_target_pairs={{0,4},{1,5},{2,6},{3,7},{4,0},{5,1},{6,2},{7,3},{8,12},{9,13},{10,... | collective-permute-start | bytes 196616 | tf_op jit(solution)/shard_map/ppermute | solution.py:267
  22.3 0.0 collective-permute-done.4.refs_4_
  22.3 0.3 collective-permute-start.6
  22.6 3.6 %collective-permute-done.5.refs_5_ = f32[4,32,128]{2,1,0:T(8,128)S(1)} collective-permute-done((f32[4,32,128]{2,1,0:T(8,128)S(1)}, f32[4,32,128]{2,1,0:T(8,128)S(1)}, u32[]{:S(2)}, u32[]{:S(2)}) %collective-permute-start.5) | collective-permute-done | bytes 65568 | tf_op jit(solution)/shard_map/ppermute | solution.py:267
  26.2 2.3 %collective-permute-done.6.refs_6_ = f32[4,32,128]{2,1,0:T(8,128)S(1)} collective-permute-done((f32[4,32,128]{2,1,0:T(8,128)S(1)}, f32[4,32,128]{2,1,0:T(8,128)S(1)}, u32[]{:S(2)}, u32[]{:S(2)}) %collective-permute-start.6) | collective-permute-done | bytes 65568 | tf_op jit(solution)/shard_map/ppermute | solution.py:267
  28.4 1.4 %shard_map.104 = (f32[8,32,128]{2,1,0:T(8,128)S(1)}, f32[8,32,128]{2,1,0:T(8,128)S(1)}) custom-call(f32[4,32,128]{2,1,0:T(8,128)S(1)} %get-tuple-element.46.refs_0_, f32[4,32,128]{2,1,0:T(8,128)S(1)} %collective-permute-done.1.refs_1_, f32[4,32,128]{2,1,0:T(8,128)S(1)} %collective-permute-done.2.refs_2_, f32[4,32,128]{2,1,0:T(8,128)S(1)} %collective-permute-done.3.refs_3_, ...), custom_call_target="tpu_custom_call" | custom-call | tf_op jit(solution)/shard_map/pallas_call | solution.py:31
  29.9 0.0 collective-permute-done.7
  29.9 0.0 collective-permute-done.9
  29.9 0.0 collective-permute-done.8
  29.9 0.1 add_add_fusion
  30.0 0.1 collective-permute-start.10
  30.1 2.0 %collective-permute-start.12 = (f32[104,128]{1,0:T(8,128)S(1)}, f32[104,128]{1,0:T(8,128)S(1)}, u32[]{:S(2)}, u32[]{:S(2)}) collective-permute-start(f32[104,128]{1,0:T(8,128)S(1)} %get-tuple-element.70), channel_id=1, source_target_pairs={{0,6},{1,7},{2,4},{3,5},{4,2},{5,3},{6,0},{7,1},{8,14},{9,15},{10,... | collective-permute-start | bytes 159752 | tf_op jit(solution)/shard_map/ppermute | solution.py:267
  32.1 1.4 %collective-permute-start.11 = (f32[104,128]{1,0:T(8,128)S(1)}, f32[104,128]{1,0:T(8,128)S(1)}, u32[]{:S(2)}, u32[]{:S(2)}) collective-permute-start(f32[104,128]{1,0:T(8,128)S(1)} %get-tuple-element.71), channel_id=1, source_target_pairs={{0,4},{1,5},{2,6},{3,7},{4,0},{5,1},{6,2},{7,3},{8,12},{9,13},{10,... | collective-permute-start | bytes 159752 | tf_op jit(solution)/shard_map/ppermute | solution.py:267
  33.5 0.0 collective-permute-start.13
  33.5 0.6 %collective-permute-done.10 = f32[104,128]{1,0:T(8,128)S(1)} collective-permute-done((f32[104,128]{1,0:T(8,128)S(1)}, f32[104,128]{1,0:T(8,128)S(1)}, u32[]{:S(2)}, u32[]{:S(2)}) %collective-permute-start.10) | collective-permute-done | bytes 53280 | tf_op jit(solution)/shard_map/ppermute | solution.py:267
  34.2 2.0 %collective-permute-done.12 = f32[104,128]{1,0:T(8,128)S(1)} collective-permute-done((f32[104,128]{1,0:T(8,128)S(1)}, f32[104,128]{1,0:T(8,128)S(1)}, u32[]{:S(2)}, u32[]{:S(2)}) %collective-permute-start.12) | collective-permute-done | bytes 53280 | tf_op jit(solution)/shard_map/ppermute | solution.py:267
  36.2 1.2 %collective-permute-done.11 = f32[104,128]{1,0:T(8,128)S(1)} collective-permute-done((f32[104,128]{1,0:T(8,128)S(1)}, f32[104,128]{1,0:T(8,128)S(1)}, u32[]{:S(2)}, u32[]{:S(2)}) %collective-permute-start.11) | collective-permute-done | bytes 53280 | tf_op jit(solution)/shard_map/ppermute | solution.py:267
  37.4 0.0 collective-permute-done.13
  37.5 0.1 collective-permute-start.18
  37.5 2.2 %collective-permute-start.19 = (f32[168,128]{1,0:T(8,128)S(1)}, f32[168,128]{1,0:T(8,128)S(1)}, u32[]{:S(2)}, u32[]{:S(2)}) collective-permute-start(f32[168,128]{1,0:T(8,128)S(1)} %get-tuple-element.58), channel_id=1, source_target_pairs={{0,4},{1,5},{2,6},{3,7},{4,0},{5,1},{6,2},{7,3},{8,12},{9,13},{10,... | collective-permute-start | bytes 258056 | tf_op jit(solution)/shard_map/ppermute | solution.py:267
  39.7 2.2 %collective-permute-start.20 = (f32[168,128]{1,0:T(8,128)S(1)}, f32[168,128]{1,0:T(8,128)S(1)}, u32[]{:S(2)}, u32[]{:S(2)}) collective-permute-start(f32[168,128]{1,0:T(8,128)S(1)} %get-tuple-element.59), channel_id=1, source_target_pairs={{0,6},{1,7},{2,4},{3,5},{4,2},{5,3},{6,0},{7,1},{8,14},{9,15},{10,... | collective-permute-start | bytes 258056 | tf_op jit(solution)/shard_map/ppermute | solution.py:267
  41.9 1.2 %collective-permute-start.16 = (f32[136,128]{1,0:T(8,128)S(1)}, f32[136,128]{1,0:T(8,128)S(1)}, u32[]{:S(2)}, u32[]{:S(2)}) collective-permute-start(f32[136,128]{1,0:T(8,128)S(1)} %get-tuple-element.56), channel_id=1, source_target_pairs={{0,17},{1,16},{2,19},{3,18},{4,21},{5,20},{6,23},{7,22},{8,25},{9,... | collective-permute-start | bytes 208904 | tf_op jit(solution)/shard_map/ppermute | solution.py:267
  43.1 1.5 %collective-permute-start.14 = (f32[136,128]{1,0:T(8,128)S(1)}, f32[136,128]{1,0:T(8,128)S(1)}, u32[]{:S(2)}, u32[]{:S(2)}) collective-permute-start(f32[136,128]{1,0:T(8,128)S(1)} %get-tuple-element.56), channel_id=1, source_target_pairs={{0,1},{1,0},{2,3},{3,2},{4,5},{5,4},{6,7},{7,6},{8,9},{9,8},{10,11... | collective-permute-start | bytes 208904 | tf_op jit(solution)/shard_map/ppermute | solution.py:267
  44.6 0.0 collective-permute-done.18.refs_0_
  44.6 0.8 %collective-permute-start.15 = (f32[136,128]{1,0:T(8,128)S(1)}, f32[136,128]{1,0:T(8,128)S(1)}, u32[]{:S(2)}, u32[]{:S(2)}) collective-permute-start(f32[136,128]{1,0:T(8,128)S(1)} %get-tuple-element.55.refs_0_), channel_id=1, source_target_pairs={{0,16},{1,17},{2,18},{3,19},{4,20},{5,21},{6,22},{7,23},{8,24},{9,... | collective-permute-start | bytes 208904 | tf_op jit(solution)/shard_map/ppermute | solution.py:267
  45.4 0.0 collective-permute-done.19.refs_1_
  45.4 0.7 %collective-permute-done.20.refs_2_ = f32[168,128]{1,0:T(8,128)S(1)} collective-permute-done((f32[168,128]{1,0:T(8,128)S(1)}, f32[168,128]{1,0:T(8,128)S(1)}, u32[]{:S(2)}, u32[]{:S(2)}) %collective-permute-start.20) | collective-permute-done | bytes 86048 | tf_op jit(solution)/shard_map/ppermute | solution.py:267
  46.1 1.6 %collective-permute-start.23 = (f32[408,128]{1,0:T(8,128)S(1)}, f32[408,128]{1,0:T(8,128)S(1)}, u32[]{:S(2)}, u32[]{:S(2)}) collective-permute-start(f32[408,128]{1,0:T(8,128)S(1)} %get-tuple-element.61), channel_id=1, source_target_pairs={{0,17},{1,16},{2,19},{3,18},{4,21},{5,20},{6,23},{7,22},{8,25},{9,... | collective-permute-start | bytes 626696 | tf_op jit(solution)/shard_map/ppermute | solution.py:267
  47.7 1.5 %collective-permute-start.21 = (f32[408,128]{1,0:T(8,128)S(1)}, f32[408,128]{1,0:T(8,128)S(1)}, u32[]{:S(2)}, u32[]{:S(2)}) collective-permute-start(f32[408,128]{1,0:T(8,128)S(1)} %get-tuple-element.61), channel_id=1, source_target_pairs={{0,1},{1,0},{2,3},{3,2},{4,5},{5,4},{6,7},{7,6},{8,9},{9,8},{10,11... | collective-permute-start | bytes 626696 | tf_op jit(solution)/shard_map/ppermute | solution.py:267
  49.2 0.0 collective-permute-done.16.refs_3_
  49.2 0.5 collective-permute-start.22
  49.7 0.0 collective-permute-done.14.refs_1_
  49.7 0.6 collective-permute-done.15.refs_2_
  50.3 0.1 collective-permute-start.17
  50.4 0.5 collective-permute-start.24
  50.9 3.1 %collective-permute-done.23.refs_8_ = f32[408,128]{1,0:T(8,128)S(1)} collective-permute-done((f32[408,128]{1,0:T(8,128)S(1)}, f32[408,128]{1,0:T(8,128)S(1)}, u32[]{:S(2)}, u32[]{:S(2)}) %collective-permute-start.23) | collective-permute-done | bytes 208928 | tf_op jit(solution)/shard_map/ppermute | solution.py:267
  53.9 0.0 collective-permute-start.27
  54.0 2.5 %collective-permute-done.21.refs_6_ = f32[408,128]{1,0:T(8,128)S(1)} collective-permute-done((f32[408,128]{1,0:T(8,128)S(1)}, f32[408,128]{1,0:T(8,128)S(1)}, u32[]{:S(2)}, u32[]{:S(2)}) %collective-permute-start.21) | collective-permute-done | bytes 208928 | tf_op jit(solution)/shard_map/ppermute | solution.py:267
  56.4 0.0 collective-permute-start.25
  56.4 0.0 collective-permute-done.22.refs_7_
  56.4 0.5 collective-permute-start.26
  57.0 0.0 collective-permute-done.24.refs_9_
  57.0 0.9 %collective-permute-done.25.refs_10_ = f32[408,128]{1,0:T(8,128)S(1)} collective-permute-done((f32[408,128]{1,0:T(8,128)S(1)}, f32[408,128]{1,0:T(8,128)S(1)}, u32[]{:S(2)}, u32[]{:S(2)}) %collective-permute-start.25) | collective-permute-done | bytes 208928 | tf_op jit(solution)/shard_map/ppermute | solution.py:267
  57.9 0.3 collective-permute-done.26.refs_11_
  58.2 2.8 %shard_map.107 = (f32[16,32,288]{2,1,0:T(8,128)}, f32[512,512]{1,0:T(8,128)}, f32[16,32,32]{2,1,0:T(8,128)}, f32[12,24,288]{2,1,0:T(8,128)}) custom-call(s32[4,24]{1,0:T(4,128)S(1)} %copy-done, f32[136,128]{1,0:T(8,128)S(1)} %get-tuple-element.55.refs_0_, f32[136,128]{1,0:T(8,128)S(1)} %collective-permute-done.14.refs_1_, ...), custom_call_target="tpu_custom_call" | custom-call | tf_op jit(solution)/shard_map/pallas_call | solution.py:31
  (24 shorter events, 0.2 us)
Async XLA Ops:
  0.6 1.3 %copy-start.1 = (bf16[512,512]{1,0:T(8,128)(2,1)S(1)}, bf16[512,512]{1,0:T(8,128)(2,1)}, u32[]{:S(2)}) copy-start(bf16[512,512]{1,0:T(8,128)(2,1)} %refs_3_.1) | copy-start | bytes 1572868
  0.6 1.3 %copy-start.2 = (bf16[16,288,32]{1,2,0:T(8,128)(2,1)S(1)}, bf16[16,288,32]{1,2,0:T(8,128)(2,1)}, u32[]{:S(2)}) copy-start(bf16[16,288,32]{1,2,0:T(8,128)(2,1)} %param.9) | copy-start | bytes 884740
  0.7 1.0 %copy-start.3 = (bf16[2,8,8,512]{3,2,1,0:T(8,128)(2,1)S(1)}, bf16[2,8,8,512]{3,2,1,0:T(8,128)(2,1)}, u32[]{:S(2)}) copy-start(bf16[2,8,8,512]{3,2,1,0:T(8,128)(2,1)} %x_hbm.1) | copy-start | bytes 393220
  1.6 1.0 %copy-start.4 = (bf16[2,8,8,512]{3,2,1,0:T(8,128)(2,1)S(1)}, bf16[2,8,8,512]{3,2,1,0:T(8,128)(2,1)}, u32[]{:S(2)}) copy-start(bf16[2,8,8,512]{3,2,1,0:T(8,128)(2,1)} %refs_1_.1) | copy-start | bytes 393220
  1.6 1.0 %copy-start.6 = (f32[512]{0:T(512)S(1)}, f32[512]{0:T(512)}, u32[]{:S(2)}) copy-start(f32[512]{0:T(512)} %param.12) | copy-start | bytes 6148
  2.0 0.7 %copy-start.5 = (f32[512]{0:T(512)S(1)}, f32[512]{0:T(512)}, u32[]{:S(2)}) copy-start(f32[512]{0:T(512)} %param.11) | copy-start | bytes 6148
  4.7 4.6 %collective-permute-start = (f32[16,104,128]{2,1,0:T(8,128)S(1)}, f32[16,104,128]{2,1,0:T(8,128)S(1)}, u32[]{:S(2)}, u32[]{:S(2)}) collective-permute-start(f32[16,104,128]{2,1,0:T(8,128)S(1)} %get-tuple-element.41), channel_id=1, source_target_pairs={{0,8},{1,9},{2,10},{3,11},{4,12},{5,13},{6,14},{7,15},{8,0},{9,1},... | collective-permute-start | bytes 2555912 | tf_op jit(solution)/shard_map/ppermute | solution.py:267
  5.2 5.2 %collective-permute-start.1 = (f32[4,32,128]{2,1,0:T(8,128)S(1)}, f32[4,32,128]{2,1,0:T(8,128)S(1)}, u32[]{:S(2)}, u32[]{:S(2)}) collective-permute-start(f32[4,32,128]{2,1,0:T(8,128)S(1)} %get-tuple-element.43), channel_id=1, source_target_pairs={{0,1},{1,0},{2,3},{3,2},{4,5},{5,4},{6,7},{7,6},{8,9},{9,8},{10,11... | collective-permute-start | bytes 196616 | tf_op jit(solution)/shard_map/ppermute | solution.py:267
  7.7 4.3 %collective-permute-start.2 = (f32[4,32,128]{2,1,0:T(8,128)S(1)}, f32[4,32,128]{2,1,0:T(8,128)S(1)}, u32[]{:S(2)}, u32[]{:S(2)}) collective-permute-start(f32[4,32,128]{2,1,0:T(8,128)S(1)} %get-tuple-element.44), channel_id=1, source_target_pairs={{0,16},{1,17},{2,18},{3,19},{4,20},{5,21},{6,22},{7,23},{8,24},{9,... | collective-permute-start | bytes 196616 | tf_op jit(solution)/shard_map/ppermute | solution.py:267
  9.2 5.2 %collective-permute-start.3 = (f32[4,32,128]{2,1,0:T(8,128)S(1)}, f32[4,32,128]{2,1,0:T(8,128)S(1)}, u32[]{:S(2)}, u32[]{:S(2)}) collective-permute-start(f32[4,32,128]{2,1,0:T(8,128)S(1)} %get-tuple-element.45), channel_id=1, source_target_pairs={{0,17},{1,16},{2,19},{3,18},{4,21},{5,20},{6,23},{7,22},{8,25},{9,... | collective-permute-start | bytes 196616 | tf_op jit(solution)/shard_map/ppermute | solution.py:267
  14.5 7.9 %collective-permute-start.4 = (f32[4,32,128]{2,1,0:T(8,128)S(1)}, f32[4,32,128]{2,1,0:T(8,128)S(1)}, u32[]{:S(2)}, u32[]{:S(2)}) collective-permute-start(f32[4,32,128]{2,1,0:T(8,128)S(1)} %pad_maximum_fusion.1), channel_id=1, source_target_pairs={{0,2},{1,3},{2,0},{3,1},{4,6},{5,7},{6,4},{7,5},{8,10},{9,11},{10,... | collective-permute-start | bytes 196616 | tf_op jit(solution)/shard_map/ppermute | solution.py:267
  16.2 13.7 %collective-permute-start.7 = (f32[4,104,128]{2,1,0:T(8,128)S(1)}, f32[4,104,128]{2,1,0:T(8,128)S(1)}, u32[]{:S(2)}, u32[]{:S(2)}) collective-permute-start(f32[4,104,128]{2,1,0:T(8,128)S(1)} %get-tuple-element.66), channel_id=1, source_target_pairs={{0,1},{1,0},{2,3},{3,2},{4,5},{5,4},{6,7},{7,6},{8,9},{9,8},{10,11... | collective-permute-start | bytes 638984 | tf_op jit(solution)/shard_map/ppermute | solution.py:267
  16.8 13.1 %collective-permute-start.9 = (f32[4,104,128]{2,1,0:T(8,128)S(1)}, f32[4,104,128]{2,1,0:T(8,128)S(1)}, u32[]{:S(2)}, u32[]{:S(2)}) collective-permute-start(f32[4,104,128]{2,1,0:T(8,128)S(1)} %get-tuple-element.67), channel_id=1, source_target_pairs={{0,17},{1,16},{2,19},{3,18},{4,21},{5,20},{6,23},{7,22},{8,25},{9,... | collective-permute-start | bytes 638984 | tf_op jit(solution)/shard_map/ppermute | solution.py:267
  18.2 11.7 %collective-permute-start.8 = (f32[4,104,128]{2,1,0:T(8,128)S(1)}, f32[4,104,128]{2,1,0:T(8,128)S(1)}, u32[]{:S(2)}, u32[]{:S(2)}) collective-permute-start(f32[4,104,128]{2,1,0:T(8,128)S(1)} %get-tuple-element.68), channel_id=1, source_target_pairs={{0,16},{1,17},{2,18},{3,19},{4,20},{5,21},{6,22},{7,23},{8,24},{9,... | collective-permute-start | bytes 638984 | tf_op jit(solution)/shard_map/ppermute | solution.py:267
  19.7 6.4 %collective-permute-start.5 = (f32[4,32,128]{2,1,0:T(8,128)S(1)}, f32[4,32,128]{2,1,0:T(8,128)S(1)}, u32[]{:S(2)}, u32[]{:S(2)}) collective-permute-start(f32[4,32,128]{2,1,0:T(8,128)S(1)} %pad_maximum_fusion.2), channel_id=1, source_target_pairs={{0,4},{1,5},{2,6},{3,7},{4,0},{5,1},{6,2},{7,3},{8,12},{9,13},{10,... | collective-permute-start | bytes 196616 | tf_op jit(solution)/shard_map/ppermute | solution.py:267
  22.3 6.1 %collective-permute-start.6 = (f32[4,32,128]{2,1,0:T(8,128)S(1)}, f32[4,32,128]{2,1,0:T(8,128)S(1)}, u32[]{:S(2)}, u32[]{:S(2)}) collective-permute-start(f32[4,32,128]{2,1,0:T(8,128)S(1)} %pad_maximum_fusion.3), channel_id=1, source_target_pairs={{0,6},{1,7},{2,4},{3,5},{4,2},{5,3},{6,0},{7,1},{8,14},{9,15},{10,... | collective-permute-start | bytes 196616 | tf_op jit(solution)/shard_map/ppermute | solution.py:267
  30.0 4.2 %collective-permute-start.10 = (f32[104,128]{1,0:T(8,128)S(1)}, f32[104,128]{1,0:T(8,128)S(1)}, u32[]{:S(2)}, u32[]{:S(2)}) collective-permute-start(f32[104,128]{1,0:T(8,128)S(1)} %get-tuple-element.69), channel_id=1, source_target_pairs={{0,2},{1,3},{2,0},{3,1},{4,6},{5,7},{6,4},{7,5},{8,10},{9,11},{10,... | collective-permute-start | bytes 159752 | tf_op jit(solution)/shard_map/ppermute | solution.py:267
  30.1 6.1 %collective-permute-start.12 = (f32[104,128]{1,0:T(8,128)S(1)}, f32[104,128]{1,0:T(8,128)S(1)}, u32[]{:S(2)}, u32[]{:S(2)}) collective-permute-start(f32[104,128]{1,0:T(8,128)S(1)} %get-tuple-element.70), channel_id=1, source_target_pairs={{0,6},{1,7},{2,4},{3,5},{4,2},{5,3},{6,0},{7,1},{8,14},{9,15},{10,... | collective-permute-start | bytes 159752 | tf_op jit(solution)/shard_map/ppermute | solution.py:267
  32.1 5.3 %collective-permute-start.11 = (f32[104,128]{1,0:T(8,128)S(1)}, f32[104,128]{1,0:T(8,128)S(1)}, u32[]{:S(2)}, u32[]{:S(2)}) collective-permute-start(f32[104,128]{1,0:T(8,128)S(1)} %get-tuple-element.71), channel_id=1, source_target_pairs={{0,4},{1,5},{2,6},{3,7},{4,0},{5,1},{6,2},{7,3},{8,12},{9,13},{10,... | collective-permute-start | bytes 159752 | tf_op jit(solution)/shard_map/ppermute | solution.py:267
  33.5 3.8 %collective-permute-start.13 = (f32[8,32,128]{2,1,0:T(8,128)S(1)}, f32[8,32,128]{2,1,0:T(8,128)S(1)}, u32[]{:S(2)}, u32[]{:S(2)}) collective-permute-start(f32[8,32,128]{2,1,0:T(8,128)S(1)} %get-tuple-element.54), channel_id=1, source_target_pairs={{0,8},{1,9},{2,10},{3,11},{4,12},{5,13},{6,14},{7,15},{8,0},{9,1},... | collective-permute-start | bytes 393224 | tf_op jit(solution)/shard_map/ppermute | solution.py:267
  37.5 7.1 %collective-permute-start.18 = (f32[168,128]{1,0:T(8,128)S(1)}, f32[168,128]{1,0:T(8,128)S(1)}, u32[]{:S(2)}, u32[]{:S(2)}) collective-permute-start(f32[168,128]{1,0:T(8,128)S(1)} %get-tuple-element.57), channel_id=1, source_target_pairs={{0,2},{1,3},{2,0},{3,1},{4,6},{5,7},{6,4},{7,5},{8,10},{9,11},{10,... | collective-permute-start | bytes 258056 | tf_op jit(solution)/shard_map/ppermute | solution.py:267
  37.5 7.9 %collective-permute-start.19 = (f32[168,128]{1,0:T(8,128)S(1)}, f32[168,128]{1,0:T(8,128)S(1)}, u32[]{:S(2)}, u32[]{:S(2)}) collective-permute-start(f32[168,128]{1,0:T(8,128)S(1)} %get-tuple-element.58), channel_id=1, source_target_pairs={{0,4},{1,5},{2,6},{3,7},{4,0},{5,1},{6,2},{7,3},{8,12},{9,13},{10,... | collective-permute-start | bytes 258056 | tf_op jit(solution)/shard_map/ppermute | solution.py:267
  39.7 6.4 %collective-permute-start.20 = (f32[168,128]{1,0:T(8,128)S(1)}, f32[168,128]{1,0:T(8,128)S(1)}, u32[]{:S(2)}, u32[]{:S(2)}) collective-permute-start(f32[168,128]{1,0:T(8,128)S(1)} %get-tuple-element.59), channel_id=1, source_target_pairs={{0,6},{1,7},{2,4},{3,5},{4,2},{5,3},{6,0},{7,1},{8,14},{9,15},{10,... | collective-permute-start | bytes 258056 | tf_op jit(solution)/shard_map/ppermute | solution.py:267
  41.9 7.3 %collective-permute-start.16 = (f32[136,128]{1,0:T(8,128)S(1)}, f32[136,128]{1,0:T(8,128)S(1)}, u32[]{:S(2)}, u32[]{:S(2)}) collective-permute-start(f32[136,128]{1,0:T(8,128)S(1)} %get-tuple-element.56), channel_id=1, source_target_pairs={{0,17},{1,16},{2,19},{3,18},{4,21},{5,20},{6,23},{7,22},{8,25},{9,... | collective-permute-start | bytes 208904 | tf_op jit(solution)/shard_map/ppermute | solution.py:267
  43.1 6.6 %collective-permute-start.14 = (f32[136,128]{1,0:T(8,128)S(1)}, f32[136,128]{1,0:T(8,128)S(1)}, u32[]{:S(2)}, u32[]{:S(2)}) collective-permute-start(f32[136,128]{1,0:T(8,128)S(1)} %get-tuple-element.56), channel_id=1, source_target_pairs={{0,1},{1,0},{2,3},{3,2},{4,5},{5,4},{6,7},{7,6},{8,9},{9,8},{10,11... | collective-permute-start | bytes 208904 | tf_op jit(solution)/shard_map/ppermute | solution.py:267
  44.6 5.7 %collective-permute-start.15 = (f32[136,128]{1,0:T(8,128)S(1)}, f32[136,128]{1,0:T(8,128)S(1)}, u32[]{:S(2)}, u32[]{:S(2)}) collective-permute-start(f32[136,128]{1,0:T(8,128)S(1)} %get-tuple-element.55.refs_0_), channel_id=1, source_target_pairs={{0,16},{1,17},{2,18},{3,19},{4,20},{5,21},{6,22},{7,23},{8,24},{9,... | collective-permute-start | bytes 208904 | tf_op jit(solution)/shard_map/ppermute | solution.py:267
  46.1 7.8 %collective-permute-start.23 = (f32[408,128]{1,0:T(8,128)S(1)}, f32[408,128]{1,0:T(8,128)S(1)}, u32[]{:S(2)}, u32[]{:S(2)}) collective-permute-start(f32[408,128]{1,0:T(8,128)S(1)} %get-tuple-element.61), channel_id=1, source_target_pairs={{0,17},{1,16},{2,19},{3,18},{4,21},{5,20},{6,23},{7,22},{8,25},{9,... | collective-permute-start | bytes 626696 | tf_op jit(solution)/shard_map/ppermute | solution.py:267
  47.7 8.7 %collective-permute-start.21 = (f32[408,128]{1,0:T(8,128)S(1)}, f32[408,128]{1,0:T(8,128)S(1)}, u32[]{:S(2)}, u32[]{:S(2)}) collective-permute-start(f32[408,128]{1,0:T(8,128)S(1)} %get-tuple-element.61), channel_id=1, source_target_pairs={{0,1},{1,0},{2,3},{3,2},{4,5},{5,4},{6,7},{7,6},{8,9},{9,8},{10,11... | collective-permute-start | bytes 626696 | tf_op jit(solution)/shard_map/ppermute | solution.py:267
  49.2 7.3 %collective-permute-start.22 = (f32[408,128]{1,0:T(8,128)S(1)}, f32[408,128]{1,0:T(8,128)S(1)}, u32[]{:S(2)}, u32[]{:S(2)}) collective-permute-start(f32[408,128]{1,0:T(8,128)S(1)} %get-tuple-element.60.refs_5_), channel_id=1, source_target_pairs={{0,16},{1,17},{2,18},{3,19},{4,20},{5,21},{6,22},{7,23},{8,24},{9,... | collective-permute-start | bytes 626696 | tf_op jit(solution)/shard_map/ppermute | solution.py:267
  50.3 7.9 %copy-start = (s32[4,24]{1,0:T(4,128)S(1)}, s32[4,24]{1,0:T(4,128)}, u32[]{:S(2)}) copy-start(s32[4,24]{1,0:T(4,128)} %slot_ref.1) | copy-start | bytes 1156
  50.3 6.7 %collective-permute-start.17 = (f32[4,136,128]{2,1,0:T(8,128)S(1)}, f32[4,136,128]{2,1,0:T(8,128)S(1)}, u32[]{:S(2)}, u32[]{:S(2)}) collective-permute-start(f32[4,136,128]{2,1,0:T(8,128)S(1)} %pad_maximum_fusion), channel_id=1, source_target_pairs={{0,8},{1,9},{2,10},{3,11},{4,12},{5,13},{6,14},{7,15},{8,0},{9,1},... | collective-permute-start | bytes 835592 | tf_op jit(solution)/shard_map/ppermute | solution.py:267
  50.4 6.6 %collective-permute-start.24 = (f32[408,128]{1,0:T(8,128)S(1)}, f32[408,128]{1,0:T(8,128)S(1)}, u32[]{:S(2)}, u32[]{:S(2)}) collective-permute-start(f32[408,128]{1,0:T(8,128)S(1)} %get-tuple-element.60.refs_5_), channel_id=1, source_target_pairs={{0,8},{1,9},{2,10},{3,11},{4,12},{5,13},{6,14},{7,15},{8,0},{9,1},... | collective-permute-start | bytes 626696 | tf_op jit(solution)/shard_map/ppermute | solution.py:267
  53.9 3.0 %collective-permute-start.27 = (f32[408,128]{1,0:T(8,128)S(1)}, f32[408,128]{1,0:T(8,128)S(1)}, u32[]{:S(2)}, u32[]{:S(2)}) collective-permute-start(f32[408,128]{1,0:T(8,128)S(1)} %collective-permute-done.23.refs_8_), channel_id=1, source_target_pairs={{0,8},{1,9},{2,10},{3,11},{4,12},{5,13},{6,14},{7,15},{8,0},{9,1},... | collective-permute-start | bytes 626696 | tf_op jit(solution)/shard_map/ppermute | solution.py:267
  56.4 1.5 %collective-permute-start.25 = (f32[408,128]{1,0:T(8,128)S(1)}, f32[408,128]{1,0:T(8,128)S(1)}, u32[]{:S(2)}, u32[]{:S(2)}) collective-permute-start(f32[408,128]{1,0:T(8,128)S(1)} %collective-permute-done.21.refs_6_), channel_id=1, source_target_pairs={{0,8},{1,9},{2,10},{3,11},{4,12},{5,13},{6,14},{7,15},{8,0},{9,1},... | collective-permute-start | bytes 626696 | tf_op jit(solution)/shard_map/ppermute | solution.py:267
  56.4 1.8 %collective-permute-start.26 = (f32[408,128]{1,0:T(8,128)S(1)}, f32[408,128]{1,0:T(8,128)S(1)}, u32[]{:S(2)}, u32[]{:S(2)}) collective-permute-start(f32[408,128]{1,0:T(8,128)S(1)} %collective-permute-done.22.refs_7_), channel_id=1, source_target_pairs={{0,8},{1,9},{2,10},{3,11},{4,12},{5,13},{6,14},{7,15},{8,0},{9,1},... | collective-permute-start | bytes 626696 | tf_op jit(solution)/shard_map/ppermute | solution.py:267

commit v5 on v4

--- a/solution.py
+++ b/solution.py
@@ -11,6 +11,10 @@
 AXES = ("owner", "dp")
 F32 = jnp.float32
 BF16 = jnp.bfloat16
+STACK_FLOPS = 4000000000
+FACTOR_FLOPS = 4000000000
+FIRST_FLOPS = 4000000000
+AFTER_CORE = AFTER_PLANE = AFTER_LINE = True
 SEND_FLOPS = 6000000000
 LOCAL_FLOPS = 4000000000
 VMEM_LIMIT = 48 * 1024 * 1024
@@ -22,21 +26,26 @@
     return pl.BlockSpec(memory_space=pltpu.VMEM)
 
 
-def call(body, outs, scratch, *args, in_hbm=False, flops=0):
+def call(body, outs, scratch, *args, in_hbm=False, flops=0, after=()):
+    count = len(args)
+
+    def run(*refs):
+        body(*refs[:count], *refs[count + len(after) :])
+
     def place(arg):
         if arg.dtype == jnp.int32:
             return pl.BlockSpec(memory_space=pltpu.SMEM)
         return pl.BlockSpec(memory_space=pltpu.HBM) if in_hbm else whole_vmem()
 
     return pl.pallas_call(
-        body,
+        run,
         out_shape=[jax.ShapeDtypeStruct(shape, kind) for shape, kind in outs],
-        in_specs=[place(a) for a in args],
+        in_specs=[place(a) for a in args] + [pl.BlockSpec(memory_space=pl.ANY) for _ in after],
         out_specs=[whole_vmem() for _ in outs],
         scratch_shapes=scratch,
         compiler_params=pltpu.CompilerParams(vmem_limit_bytes=VMEM_LIMIT),
         cost_estimate=pl.CostEstimate(flops=flops, bytes_accessed=0, transcendentals=0) if flops else None,
-    )(*args)
+    )(*args, *after)
 
 
 def plane_id():
@@ -193,16 +202,27 @@
     give_ref[...] = held[1]
 
 
-def line_kernel(total_ref, piece_ref, first_ref, first_peer_ref, *line_refs):
-    total = total_ref[...]
+def stack_kernel(*refs):
+    for z, out in enumerate(refs[4:]):
+        for i, ref in enumerate(refs[:4]):
+            out[i] = ref[z + 1]
+
+
+def copy_kernel(src_ref, out_ref):
+    out_ref[...] = src_ref[...]
+
+
+def line_kernel(total_ref, piece_ref, *line_refs):
+    for z, ref in enumerate(line_refs):
+        ref[:104, :] = total_ref[...]
+        ref[104:, :] = piece_ref[z + 1]
+
+
+def first_kernel(total_ref, piece_ref, first_ref, peer_ref):
     size = first_ref.shape[0]
-    first_ref[:104, :] = total
-    first_ref[104:, :] = piece_ref[0, : size - 104, :]
-    first_peer_ref[:104, :] = total
-    first_peer_ref[104:, :] = piece_ref[0, size - 104 :, :]
-    for z, ref in enumerate(line_refs):
-        ref[:104, :] = total
-        ref[104:, :] = piece_ref[z + 1]
+    for ref, at in ((first_ref, 0), (peer_ref, size - 104)):
+        ref[:104, :] = total_ref[...]
+        ref[104:, :] = piece_ref[0, at : at + size - 104, :]
 
 
 def merge_kernel(*refs):
@@ -314,9 +334,17 @@
     sent, other = lax.optimization_barrier((sent, other))
     got = [sent[0], swap(sent[1], 0, 1), swap(sent[2], 2, 0), swap(sent[3], 2, 1)]
     total = mine + swap(other, 1, 0)
-    total, got = lax.optimization_barrier((total, got))
-    far = [swap(jnp.stack([v[z] for v in got]), 0, 2 * z) for z in range(1, 4)]
+    blocks = call(
+        stack_kernel, [((4, 32, 128), F32)] * 3, [], *got, flops=STACK_FLOPS, after=(total,) if AFTER_CORE else ()
+    )
+    far = [swap(blocks[z - 1], 0, 2 * z) for z in range(1, 4)]
     total = total[0:4] + swap(total[4:8], 0, 1) + swap(total[8:12], 2, 0) + swap(total[12:16], 2, 1)
+    plane_sum = total
+    z2, z3 = swap(total[2], 0, 4), swap(total[3], 0, 6)
+    (last,) = call(copy_kernel, [((104, 128), F32)], [], total[1], flops=4000000000, after=(total[2], total[3]))
+    z1 = swap(last, 0, 2)
+    total = total[0] + z1 + z2 + z3
+    total = add_over(total, far_owner, far_dp)
     half = 96 // n_dp
     packed = packed_rows(half // 2)
     keep, give = call(
@@ -325,23 +353,18 @@
         [pltpu.VMEM((288, 2048), BF16), pltpu.VMEM((2, n_dp, packed, 128), F32)],
         *got,
         *far,
-    )
-    give, total = lax.optimization_barrier((give, total))
-    total = total[0] + swap(total[1], 0, 2) + swap(total[2], 0, 4) + swap(total[3], 0, 6)
-    total = add_over(total, far_owner, far_dp)
-
+        flops=FACTOR_FLOPS,
+        after=(plane_sum,) if AFTER_PLANE else (),
+    )
     piece = add_over(keep + swap(give, 1, 0), far_owner, ())
     for bit in reversed(far_dp):
         near = piece.shape[0] // 2
         piece = piece[:near] + swap(piece[near:], 0, 1 << bit)
     piece = piece.reshape(4, 2 * packed, 128)
 
-    first, first_peer, *line = call(
-        line_kernel,
-        [((104 + packed, 128), F32)] * 2 + [((104 + 2 * packed, 128), F32)] * 3,
-        [],
-        total,
-        piece,
+    line = call(line_kernel, [((104 + 2 * packed, 128), F32)] * 3, [], total, piece)
+    first, first_peer = call(
+        first_kernel, [((104 + packed, 128), F32)] * 2, [], total, piece, flops=FIRST_FLOPS, after=line if AFTER_LINE else ()
     )
     line = [swap(line[z - 1], 0, 2 * z) for z in range(1, 4)]
     early = [first, swap(first_peer, 0, 1), swap(first, 2, 0), swap(first_peer, 2, 1)]

time: 61.2 us -> 58.1 us (0.949)
  waiting for transfers between devices: 22.8 us -> 16.1 us
  starting transfers between devices: 28.8 us -> 32.1 us
    ppermute x28, waiting for transfers between devices: 22.8 us -> 16.1 us  [swap(): return lax.ppermute(value, AXES, pairs)]
    ppermute x28, starting transfers between devices: 28.8 us -> 32.1 us  [swap(): return lax.ppermute(value, AXES, pairs)]
    pallas_call x6 -> x9, Pallas kernels: 6.62 us -> 6.64 us  [call(): pl.pallas_call(run, out_shape=[jax.ShapeDtypeStruct(shape, kind) for shap...]
  transfers between devices with their start and end apart: 28 -> 28, of which waited for: 14 -> 11; matrix products, arithmetic and copies ran while one was open for 0% -> 0% of each run, Pallas kernels for 2% -> 3%
where the time goes in v5:
time: 58.1 us; the launch traced here: 57.6 us
  starting transfers between devices  32.1 us (55%)
  waiting for transfers between devices  16.1 us (28%)
  Pallas kernels  6.64 us (11%)
  local copies, waits for them, and re-layouts  1.71 us (3%)
  between operations  0.83 us (1%)
    ppermute x28, starting transfers between devices, swap(): return lax.ppermute(value, AXES, pairs)  32.1 us
    ppermute x28, waiting for transfers between devices, swap(): return lax.ppermute(value, AXES, pairs)  16.1 us
    pallas_call x9, Pallas kernels, call(): pl.pallas_call(run, out_shape=[jax.ShapeDtypeStruct(shape, kind) for shap...  6.64 us
    unnamed x14, local copies, waits for them, and re-layouts  1.66 us
  transfers between devices with their start and end apart: 28, of which 11 were waited for; matrix products, arithmetic and copies ran while one was open for 0% of the time, Pallas kernels for 3%

profile of v5, /device:TPU:0, one launch (start us, length us, event | category | flops | bytes accessed | tf_op | source)
XLA Modules:
  0.0 57.6 jit_solution(12560085925522375234)
XLA Ops:
  0.7 1.0 %copy-done.3 = bf16[2,8,8,512]{3,2,1,0:T(8,128)(2,1)S(1)} copy-done((bf16[2,8,8,512]{3,2,1,0:T(8,128)(2,1)S(1)}, bf16[2,8,8,512]{3,2,1,0:T(8,128)(2,1)}, u32[]{:S(2)}) %copy-start.3) | copy-done | bytes 131096
  1.6 0.3 shard_map.103
  2.0 0.0 copy-start.5
  2.0 0.6 %copy-done.4 = bf16[2,8,8,512]{3,2,1,0:T(8,128)(2,1)S(1)} copy-done((bf16[2,8,8,512]{3,2,1,0:T(8,128)(2,1)S(1)}, bf16[2,8,8,512]{3,2,1,0:T(8,128)(2,1)}, u32[]{:S(2)}) %copy-start.4) | copy-done | bytes 131096
  2.6 0.1 copy-done.5
  2.6 2.0 %shard_map.102 = (f32[16,104,128]{2,1,0:T(8,128)S(1)}, f32[16,104,128]{2,1,0:T(8,128)S(1)}) custom-call(bf16[2,8,8,512]{3,2,1,0:T(8,128)(2,1)S(1)} %copy-done.3, bf16[2,8,8,512]{3,2,1,0:T(8,128)(2,1)S(1)} %copy-done.4, bf16[16,32,288]{2,1,0:T(8,128)(2,1)S(1)} %bitcast.30, bf16[512,512]{1,0:T(8,128)(2,1)S(1)} %copy-done.1, f32[1,512]{1,0:T(1,128)S(1)} %bitcast.31, ...), custom_call_target="tpu_custom_call" | custom-call | flops 4000000000 | tf_op jit(solution)/shard_map/pallas_call | solution.py:40
  4.7 0.5 collective-permute-start
  5.2 2.6 %collective-permute-start.7 = (f32[4,32,128]{2,1,0:T(8,128)S(1)}, f32[4,32,128]{2,1,0:T(8,128)S(1)}, u32[]{:S(2)}, u32[]{:S(2)}) collective-permute-start(f32[4,32,128]{2,1,0:T(8,128)S(1)} %get-tuple-element.39), channel_id=1, source_target_pairs={{0,1},{1,0},{2,3},{3,2},{4,5},{5,4},{6,7},{7,6},{8,9},{9,8},{10,11... | collective-permute-start | bytes 196616 | tf_op jit(solution)/shard_map/ppermute | solution.py:287
  7.7 1.5 %collective-permute-start.8 = (f32[4,32,128]{2,1,0:T(8,128)S(1)}, f32[4,32,128]{2,1,0:T(8,128)S(1)}, u32[]{:S(2)}, u32[]{:S(2)}) collective-permute-start(f32[4,32,128]{2,1,0:T(8,128)S(1)} %get-tuple-element.40), channel_id=1, source_target_pairs={{0,16},{1,17},{2,18},{3,19},{4,20},{5,21},{6,22},{7,23},{8,24},{9,... | collective-permute-start | bytes 196616 | tf_op jit(solution)/shard_map/ppermute | solution.py:287
  9.2 0.0 collective-permute-start.9
  9.3 0.0 collective-permute-done
  9.3 0.1 add.24.refs_4_
  9.4 2.0 %collective-permute-start.1 = (f32[4,104,128]{2,1,0:T(8,128)S(1)}, f32[4,104,128]{2,1,0:T(8,128)S(1)}, u32[]{:S(2)}, u32[]{:S(2)}) collective-permute-start(f32[4,104,128]{2,1,0:T(8,128)S(1)} %get-tuple-element.58), channel_id=1, source_target_pairs={{0,1},{1,0},{2,3},{3,2},{4,5},{5,4},{6,7},{7,6},{8,9},{9,8},{10,11... | collective-permute-start | bytes 638984 | tf_op jit(solution)/shard_map/ppermute | solution.py:287
  11.5 1.5 %collective-permute-start.3 = (f32[4,104,128]{2,1,0:T(8,128)S(1)}, f32[4,104,128]{2,1,0:T(8,128)S(1)}, u32[]{:S(2)}, u32[]{:S(2)}) collective-permute-start(f32[4,104,128]{2,1,0:T(8,128)S(1)} %get-tuple-element.59), channel_id=1, source_target_pairs={{0,17},{1,16},{2,19},{3,18},{4,21},{5,20},{6,23},{7,22},{8,25},{9,... | collective-permute-start | bytes 638984 | tf_op jit(solution)/shard_map/ppermute | solution.py:287
  12.9 0.0 collective-permute-done.7.refs_1_
  12.9 0.0 collective-permute-start.2
  13.0 0.0 collective-permute-done.8.refs_2_
  13.0 2.1 %collective-permute-done.9.refs_3_ = f32[4,32,128]{2,1,0:T(8,128)S(1)} collective-permute-done((f32[4,32,128]{2,1,0:T(8,128)S(1)}, f32[4,32,128]{2,1,0:T(8,128)S(1)}, u32[]{:S(2)}, u32[]{:S(2)}) %collective-permute-start.9) | collective-permute-done | bytes 65568 | tf_op jit(solution)/shard_map/ppermute | solution.py:287
  15.1 1.7 %collective-permute-start.10 = (f32[4,32,128]{2,1,0:T(8,128)S(1)}, f32[4,32,128]{2,1,0:T(8,128)S(1)}, u32[]{:S(2)}, u32[]{:S(2)}) collective-permute-start(f32[4,32,128]{2,1,0:T(8,128)S(1)} %get-tuple-element.42), channel_id=1, source_target_pairs={{0,2},{1,3},{2,0},{3,1},{4,6},{5,7},{6,4},{7,5},{8,10},{9,11},{10,... | collective-permute-start | bytes 196616 | tf_op jit(solution)/shard_map/ppermute | solution.py:287
  16.8 2.6 %collective-permute-start.11 = (f32[4,32,128]{2,1,0:T(8,128)S(1)}, f32[4,32,128]{2,1,0:T(8,128)S(1)}, u32[]{:S(2)}, u32[]{:S(2)}) collective-permute-start(f32[4,32,128]{2,1,0:T(8,128)S(1)} %get-tuple-element.43), channel_id=1, source_target_pairs={{0,4},{1,5},{2,6},{3,7},{4,0},{5,1},{6,2},{7,3},{8,12},{9,13},{10,... | collective-permute-start | bytes 196616 | tf_op jit(solution)/shard_map/ppermute | solution.py:287
  19.4 0.0 collective-permute-done.1
  19.4 3.0 %collective-permute-start.12 = (f32[4,32,128]{2,1,0:T(8,128)S(1)}, f32[4,32,128]{2,1,0:T(8,128)S(1)}, u32[]{:S(2)}, u32[]{:S(2)}) collective-permute-start(f32[4,32,128]{2,1,0:T(8,128)S(1)} %get-tuple-element.44), channel_id=1, source_target_pairs={{0,6},{1,7},{2,4},{3,5},{4,2},{5,3},{6,0},{7,1},{8,14},{9,15},{10,... | collective-permute-start | bytes 196616 | tf_op jit(solution)/shard_map/ppermute | solution.py:287
  22.3 0.9 %collective-permute-done.3 = f32[4,104,128]{2,1,0:T(8,128)S(1)} collective-permute-done((f32[4,104,128]{2,1,0:T(8,128)S(1)}, f32[4,104,128]{2,1,0:T(8,128)S(1)}, u32[]{:S(2)}, u32[]{:S(2)}) %collective-permute-start.3) | collective-permute-done | bytes 213024 | tf_op jit(solution)/shard_map/ppermute | solution.py:287
  23.3 0.7 %collective-permute-done.2 = f32[4,104,128]{2,1,0:T(8,128)S(1)} collective-permute-done((f32[4,104,128]{2,1,0:T(8,128)S(1)}, f32[4,104,128]{2,1,0:T(8,128)S(1)}, u32[]{:S(2)}, u32[]{:S(2)}) %collective-permute-start.2) | collective-permute-done | bytes 213024 | tf_op jit(solution)/shard_map/ppermute | solution.py:287
  24.0 0.1 fusion.1.refs_7_
  24.1 3.7 %collective-permute-start.6 = (f32[104,128]{1,0:T(8,128)S(1)}, f32[104,128]{1,0:T(8,128)S(1)}, u32[]{:S(2)}, u32[]{:S(2)}) collective-permute-start(f32[104,128]{1,0:T(8,128)S(1)} %get-tuple-element.62.refs_2_), channel_id=1, source_target_pairs={{0,6},{1,7},{2,4},{3,5},{4,2},{5,3},{6,0},{7,1},{8,14},{9,15},{10,... | collective-permute-start | bytes 159752 | tf_op jit(solution)/shard_map/ppermute | solution.py:287
  27.7 0.0 collective-permute-start.5
  27.8 0.0 collective-permute-done.10.refs_4_
  27.8 0.8 %collective-permute-start.4 = (f32[104,128]{1,0:T(8,128)S(1)}, f32[104,128]{1,0:T(8,128)S(1)}, u32[]{:S(2)}, u32[]{:S(2)}) collective-permute-start(f32[104,128]{1,0:T(8,128)S(1)} %shard_map.104), channel_id=1, source_target_pairs={{0,2},{1,3},{2,0},{3,1},{4,6},{5,7},{6,4},{7,5},{8,10},{9,11},{10,... | collective-permute-start | bytes 159752 | tf_op jit(solution)/shard_map/ppermute | solution.py:287
  28.6 0.0 collective-permute-done.11.refs_5_
  28.6 0.0 collective-permute-done.12.refs_6_
  28.6 1.4 %shard_map.106 = (f32[8,32,128]{2,1,0:T(8,128)S(1)}, f32[8,32,128]{2,1,0:T(8,128)S(1)}) custom-call(f32[4,32,128]{2,1,0:T(8,128)S(1)} %get-tuple-element.38.refs_0_, f32[4,32,128]{2,1,0:T(8,128)S(1)} %collective-permute-done.7.refs_1_, f32[4,32,128]{2,1,0:T(8,128)S(1)} %collective-permute-done.8.refs_2_, f32[4,32,128]{2,1,0:T(8,128)S(1)} %collective-permute-done.9.refs_3_, ...), custom_call_target="tpu_custom_call" | custom-call | flops 4000000000 | tf_op jit(solution)/shard_map/pallas_call | solution.py:40
  30.0 0.1 collective-permute-start.13
  30.1 1.8 %collective-permute-done.4 = f32[104,128]{1,0:T(8,128)S(1)} collective-permute-done((f32[104,128]{1,0:T(8,128)S(1)}, f32[104,128]{1,0:T(8,128)S(1)}, u32[]{:S(2)}, u32[]{:S(2)}) %collective-permute-start.4) | collective-permute-done | bytes 53280 | tf_op jit(solution)/shard_map/ppermute | solution.py:287
  32.0 0.0 collective-permute-done.6
  32.0 0.8 %collective-permute-done.5 = f32[104,128]{1,0:T(8,128)S(1)} collective-permute-done((f32[104,128]{1,0:T(8,128)S(1)}, f32[104,128]{1,0:T(8,128)S(1)}, u32[]{:S(2)}, u32[]{:S(2)}) %collective-permute-start.5) | collective-permute-done | bytes 53280 | tf_op jit(solution)/shard_map/ppermute | solution.py:287
  32.8 0.0 collective-permute-done.13
  32.9 0.3 collective-permute-start.18
  33.2 2.6 %collective-permute-start.19 = (f32[168,128]{1,0:T(8,128)S(1)}, f32[168,128]{1,0:T(8,128)S(1)}, u32[]{:S(2)}, u32[]{:S(2)}) collective-permute-start(f32[168,128]{1,0:T(8,128)S(1)} %get-tuple-element.48.refs_3_), channel_id=1, source_target_pairs={{0,4},{1,5},{2,6},{3,7},{4,0},{5,1},{6,2},{7,3},{8,12},{9,13},{10,... | collective-permute-start | bytes 258056 | tf_op jit(solution)/shard_map/ppermute | solution.py:287
  35.7 1.6 %collective-permute-start.20 = (f32[168,128]{1,0:T(8,128)S(1)}, f32[168,128]{1,0:T(8,128)S(1)}, u32[]{:S(2)}, u32[]{:S(2)}) collective-permute-start(f32[168,128]{1,0:T(8,128)S(1)} %get-tuple-element.49.refs_4_), channel_id=1, source_target_pairs={{0,6},{1,7},{2,4},{3,5},{4,2},{5,3},{6,0},{7,1},{8,14},{9,15},{10,... | collective-permute-start | bytes 258056 | tf_op jit(solution)/shard_map/ppermute | solution.py:287
  37.3 1.2 %collective-permute-start.16 = (f32[136,128]{1,0:T(8,128)S(1)}, f32[136,128]{1,0:T(8,128)S(1)}, u32[]{:S(2)}, u32[]{:S(2)}) collective-permute-start(f32[136,128]{1,0:T(8,128)S(1)} %get-tuple-element.51), channel_id=1, source_target_pairs={{0,17},{1,16},{2,19},{3,18},{4,21},{5,20},{6,23},{7,22},{8,25},{9,... | collective-permute-start | bytes 208904 | tf_op jit(solution)/shard_map/ppermute | solution.py:287
  38.5 0.8 %collective-permute-start.14 = (f32[136,128]{1,0:T(8,128)S(1)}, f32[136,128]{1,0:T(8,128)S(1)}, u32[]{:S(2)}, u32[]{:S(2)}) collective-permute-start(f32[136,128]{1,0:T(8,128)S(1)} %get-tuple-element.51), channel_id=1, source_target_pairs={{0,1},{1,0},{2,3},{3,2},{4,5},{5,4},{6,7},{7,6},{8,9},{9,8},{10,11... | collective-permute-start | bytes 208904 | tf_op jit(solution)/shard_map/ppermute | solution.py:287
  39.4 0.0 collective-permute-done.18.refs_0_
  39.4 1.5 %collective-permute-start.15 = (f32[136,128]{1,0:T(8,128)S(1)}, f32[136,128]{1,0:T(8,128)S(1)}, u32[]{:S(2)}, u32[]{:S(2)}) collective-permute-start(f32[136,128]{1,0:T(8,128)S(1)} %get-tuple-element.50.refs_1_), channel_id=1, source_target_pairs={{0,16},{1,17},{2,18},{3,19},{4,20},{5,21},{6,22},{7,23},{8,24},{9,... | collective-permute-start | bytes 208904 | tf_op jit(solution)/shard_map/ppermute | solution.py:287
  40.9 1.9 %collective-permute-done.19.refs_1_ = f32[168,128]{1,0:T(8,128)S(1)} collective-permute-done((f32[168,128]{1,0:T(8,128)S(1)}, f32[168,128]{1,0:T(8,128)S(1)}, u32[]{:S(2)}, u32[]{:S(2)}) %collective-permute-start.19) | collective-permute-done | bytes 86048 | tf_op jit(solution)/shard_map/ppermute | solution.py:287
  42.8 0.0 collective-permute-done.20.refs_2_
  42.8 1.2 %collective-permute-start.23 = (f32[408,128]{1,0:T(8,128)S(1)}, f32[408,128]{1,0:T(8,128)S(1)}, u32[]{:S(2)}, u32[]{:S(2)}) collective-permute-start(f32[408,128]{1,0:T(8,128)S(1)} %get-tuple-element.53), channel_id=1, source_target_pairs={{0,17},{1,16},{2,19},{3,18},{4,21},{5,20},{6,23},{7,22},{8,25},{9,... | collective-permute-start | bytes 626696 | tf_op jit(solution)/shard_map/ppermute | solution.py:287
  44.0 0.8 %collective-permute-start.21 = (f32[408,128]{1,0:T(8,128)S(1)}, f32[408,128]{1,0:T(8,128)S(1)}, u32[]{:S(2)}, u32[]{:S(2)}) collective-permute-start(f32[408,128]{1,0:T(8,128)S(1)} %get-tuple-element.53), channel_id=1, source_target_pairs={{0,1},{1,0},{2,3},{3,2},{4,5},{5,4},{6,7},{7,6},{8,9},{9,8},{10,11... | collective-permute-start | bytes 626696 | tf_op jit(solution)/shard_map/ppermute | solution.py:287
  44.8 0.0 collective-permute-done.16.refs_4_
  44.8 1.5 %collective-permute-start.22 = (f32[408,128]{1,0:T(8,128)S(1)}, f32[408,128]{1,0:T(8,128)S(1)}, u32[]{:S(2)}, u32[]{:S(2)}) collective-permute-start(f32[408,128]{1,0:T(8,128)S(1)} %get-tuple-element.52.refs_6_), channel_id=1, source_target_pairs={{0,16},{1,17},{2,18},{3,19},{4,20},{5,21},{6,22},{7,23},{8,24},{9,... | collective-permute-start | bytes 626696 | tf_op jit(solution)/shard_map/ppermute | solution.py:287
  46.3 0.0 collective-permute-done.14.refs_2_
  46.4 0.0 collective-permute-done.15.refs_3_
  46.4 0.1 collective-permute-start.17
  46.5 0.5 collective-permute-start.24
  47.0 4.2 %collective-permute-done.23.refs_9_ = f32[408,128]{1,0:T(8,128)S(1)} collective-permute-done((f32[408,128]{1,0:T(8,128)S(1)}, f32[408,128]{1,0:T(8,128)S(1)}, u32[]{:S(2)}, u32[]{:S(2)}) %collective-permute-start.23) | collective-permute-done | bytes 208928 | tf_op jit(solution)/shard_map/ppermute | solution.py:287
  51.2 0.0 collective-permute-start.27
  51.2 1.2 %collective-permute-done.21.refs_7_ = f32[408,128]{1,0:T(8,128)S(1)} collective-permute-done((f32[408,128]{1,0:T(8,128)S(1)}, f32[408,128]{1,0:T(8,128)S(1)}, u32[]{:S(2)}, u32[]{:S(2)}) %collective-permute-start.21) | collective-permute-done | bytes 208928 | tf_op jit(solution)/shard_map/ppermute | solution.py:287
  52.4 0.0 collective-permute-start.25
  52.4 0.9 %collective-permute-done.22.refs_8_ = f32[408,128]{1,0:T(8,128)S(1)} collective-permute-done((f32[408,128]{1,0:T(8,128)S(1)}, f32[408,128]{1,0:T(8,128)S(1)}, u32[]{:S(2)}, u32[]{:S(2)}) %collective-permute-start.22) | collective-permute-done | bytes 208928 | tf_op jit(solution)/shard_map/ppermute | solution.py:287
  53.3 0.0 collective-permute-start.26
  53.3 0.0 collective-permute-done.24.refs_10_
  53.3 0.5 collective-permute-done.25.refs_11_
  53.8 0.9 %collective-permute-done.26.refs_12_ = f32[408,128]{1,0:T(8,128)S(1)} collective-permute-done((f32[408,128]{1,0:T(8,128)S(1)}, f32[408,128]{1,0:T(8,128)S(1)}, u32[]{:S(2)}, u32[]{:S(2)}) %collective-permute-start.26) | collective-permute-done | bytes 208928 | tf_op jit(solution)/shard_map/ppermute | solution.py:287
  54.7 2.8 %shard_map.110 = (f32[16,32,288]{2,1,0:T(8,128)}, f32[512,512]{1,0:T(8,128)}, f32[16,32,32]{2,1,0:T(8,128)}, f32[12,24,288]{2,1,0:T(8,128)}) custom-call(s32[4,24]{1,0:T(4,128)S(1)} %copy-done, f32[136,128]{1,0:T(8,128)S(1)} %get-tuple-element.50.refs_1_, f32[136,128]{1,0:T(8,128)S(1)} %collective-permute-done.14.refs_2_, ...), custom_call_target="tpu_custom_call" | custom-call | tf_op jit(solution)/shard_map/pallas_call | solution.py:40
  (22 shorter events, 0.2 us)
Async XLA Ops:
  0.6 1.3 %copy-start.1 = (bf16[512,512]{1,0:T(8,128)(2,1)S(1)}, bf16[512,512]{1,0:T(8,128)(2,1)}, u32[]{:S(2)}) copy-start(bf16[512,512]{1,0:T(8,128)(2,1)} %refs_3_.1) | copy-start | bytes 1572868
  0.6 1.3 %copy-start.2 = (bf16[16,288,32]{1,2,0:T(8,128)(2,1)S(1)}, bf16[16,288,32]{1,2,0:T(8,128)(2,1)}, u32[]{:S(2)}) copy-start(bf16[16,288,32]{1,2,0:T(8,128)(2,1)} %param.9) | copy-start | bytes 884740
  0.7 1.0 %copy-start.3 = (bf16[2,8,8,512]{3,2,1,0:T(8,128)(2,1)S(1)}, bf16[2,8,8,512]{3,2,1,0:T(8,128)(2,1)}, u32[]{:S(2)}) copy-start(bf16[2,8,8,512]{3,2,1,0:T(8,128)(2,1)} %refs_0_.4) | copy-start | bytes 393220
  1.6 1.0 %copy-start.4 = (bf16[2,8,8,512]{3,2,1,0:T(8,128)(2,1)S(1)}, bf16[2,8,8,512]{3,2,1,0:T(8,128)(2,1)}, u32[]{:S(2)}) copy-start(bf16[2,8,8,512]{3,2,1,0:T(8,128)(2,1)} %refs_1_.1) | copy-start | bytes 393220
  1.6 1.0 %copy-start.6 = (f32[512]{0:T(512)S(1)}, f32[512]{0:T(512)}, u32[]{:S(2)}) copy-start(f32[512]{0:T(512)} %param.12) | copy-start | bytes 6148
  2.0 0.7 %copy-start.5 = (f32[512]{0:T(512)S(1)}, f32[512]{0:T(512)}, u32[]{:S(2)}) copy-start(f32[512]{0:T(512)} %param.11) | copy-start | bytes 6148
  4.7 4.6 %collective-permute-start = (f32[16,104,128]{2,1,0:T(8,128)S(1)}, f32[16,104,128]{2,1,0:T(8,128)S(1)}, u32[]{:S(2)}, u32[]{:S(2)}) collective-permute-start(f32[16,104,128]{2,1,0:T(8,128)S(1)} %get-tuple-element.37), channel_id=1, source_target_pairs={{0,8},{1,9},{2,10},{3,11},{4,12},{5,13},{6,14},{7,15},{8,0},{9,1},... | collective-permute-start | bytes 2555912 | tf_op jit(solution)/shard_map/ppermute | solution.py:287
  5.2 7.8 %collective-permute-start.7 = (f32[4,32,128]{2,1,0:T(8,128)S(1)}, f32[4,32,128]{2,1,0:T(8,128)S(1)}, u32[]{:S(2)}, u32[]{:S(2)}) collective-permute-start(f32[4,32,128]{2,1,0:T(8,128)S(1)} %get-tuple-element.39), channel_id=1, source_target_pairs={{0,1},{1,0},{2,3},{3,2},{4,5},{5,4},{6,7},{7,6},{8,9},{9,8},{10,11... | collective-permute-start | bytes 196616 | tf_op jit(solution)/shard_map/ppermute | solution.py:287
  7.7 5.3 %collective-permute-start.8 = (f32[4,32,128]{2,1,0:T(8,128)S(1)}, f32[4,32,128]{2,1,0:T(8,128)S(1)}, u32[]{:S(2)}, u32[]{:S(2)}) collective-permute-start(f32[4,32,128]{2,1,0:T(8,128)S(1)} %get-tuple-element.40), channel_id=1, source_target_pairs={{0,16},{1,17},{2,18},{3,19},{4,20},{5,21},{6,22},{7,23},{8,24},{9,... | collective-permute-start | bytes 196616 | tf_op jit(solution)/shard_map/ppermute | solution.py:287
  9.2 5.9 %collective-permute-start.9 = (f32[4,32,128]{2,1,0:T(8,128)S(1)}, f32[4,32,128]{2,1,0:T(8,128)S(1)}, u32[]{:S(2)}, u32[]{:S(2)}) collective-permute-start(f32[4,32,128]{2,1,0:T(8,128)S(1)} %get-tuple-element.41), channel_id=1, source_target_pairs={{0,17},{1,16},{2,19},{3,18},{4,21},{5,20},{6,23},{7,22},{8,25},{9,... | collective-permute-start | bytes 196616 | tf_op jit(solution)/shard_map/ppermute | solution.py:287
  9.4 9.9 %collective-permute-start.1 = (f32[4,104,128]{2,1,0:T(8,128)S(1)}, f32[4,104,128]{2,1,0:T(8,128)S(1)}, u32[]{:S(2)}, u32[]{:S(2)}) collective-permute-start(f32[4,104,128]{2,1,0:T(8,128)S(1)} %get-tuple-element.58), channel_id=1, source_target_pairs={{0,1},{1,0},{2,3},{3,2},{4,5},{5,4},{6,7},{7,6},{8,9},{9,8},{10,11... | collective-permute-start | bytes 638984 | tf_op jit(solution)/shard_map/ppermute | solution.py:287
  11.5 11.8 %collective-permute-start.3 = (f32[4,104,128]{2,1,0:T(8,128)S(1)}, f32[4,104,128]{2,1,0:T(8,128)S(1)}, u32[]{:S(2)}, u32[]{:S(2)}) collective-permute-start(f32[4,104,128]{2,1,0:T(8,128)S(1)} %get-tuple-element.59), channel_id=1, source_target_pairs={{0,17},{1,16},{2,19},{3,18},{4,21},{5,20},{6,23},{7,22},{8,25},{9,... | collective-permute-start | bytes 638984 | tf_op jit(solution)/shard_map/ppermute | solution.py:287
  12.9 11.0 %collective-permute-start.2 = (f32[4,104,128]{2,1,0:T(8,128)S(1)}, f32[4,104,128]{2,1,0:T(8,128)S(1)}, u32[]{:S(2)}, u32[]{:S(2)}) collective-permute-start(f32[4,104,128]{2,1,0:T(8,128)S(1)} %get-tuple-element.60), channel_id=1, source_target_pairs={{0,16},{1,17},{2,18},{3,19},{4,20},{5,21},{6,22},{7,23},{8,24},{9,... | collective-permute-start | bytes 638984 | tf_op jit(solution)/shard_map/ppermute | solution.py:287
  15.1 12.6 %collective-permute-start.10 = (f32[4,32,128]{2,1,0:T(8,128)S(1)}, f32[4,32,128]{2,1,0:T(8,128)S(1)}, u32[]{:S(2)}, u32[]{:S(2)}) collective-permute-start(f32[4,32,128]{2,1,0:T(8,128)S(1)} %get-tuple-element.42), channel_id=1, source_target_pairs={{0,2},{1,3},{2,0},{3,1},{4,6},{5,7},{6,4},{7,5},{8,10},{9,11},{10,... | collective-permute-start | bytes 196616 | tf_op jit(solution)/shard_map/ppermute | solution.py:287
  16.8 11.8 %collective-permute-start.11 = (f32[4,32,128]{2,1,0:T(8,128)S(1)}, f32[4,32,128]{2,1,0:T(8,128)S(1)}, u32[]{:S(2)}, u32[]{:S(2)}) collective-permute-start(f32[4,32,128]{2,1,0:T(8,128)S(1)} %get-tuple-element.43), channel_id=1, source_target_pairs={{0,4},{1,5},{2,6},{3,7},{4,0},{5,1},{6,2},{7,3},{8,12},{9,13},{10,... | collective-permute-start | bytes 196616 | tf_op jit(solution)/shard_map/ppermute | solution.py:287
  19.4 9.2 %collective-permute-start.12 = (f32[4,32,128]{2,1,0:T(8,128)S(1)}, f32[4,32,128]{2,1,0:T(8,128)S(1)}, u32[]{:S(2)}, u32[]{:S(2)}) collective-permute-start(f32[4,32,128]{2,1,0:T(8,128)S(1)} %get-tuple-element.44), channel_id=1, source_target_pairs={{0,6},{1,7},{2,4},{3,5},{4,2},{5,3},{6,0},{7,1},{8,14},{9,15},{10,... | collective-permute-start | bytes 196616 | tf_op jit(solution)/shard_map/ppermute | solution.py:287
  24.1 7.9 %collective-permute-start.6 = (f32[104,128]{1,0:T(8,128)S(1)}, f32[104,128]{1,0:T(8,128)S(1)}, u32[]{:S(2)}, u32[]{:S(2)}) collective-permute-start(f32[104,128]{1,0:T(8,128)S(1)} %get-tuple-element.62.refs_2_), channel_id=1, source_target_pairs={{0,6},{1,7},{2,4},{3,5},{4,2},{5,3},{6,0},{7,1},{8,14},{9,15},{10,... | collective-permute-start | bytes 159752 | tf_op jit(solution)/shard_map/ppermute | solution.py:287
  27.7 5.0 %collective-permute-start.5 = (f32[104,128]{1,0:T(8,128)S(1)}, f32[104,128]{1,0:T(8,128)S(1)}, u32[]{:S(2)}, u32[]{:S(2)}) collective-permute-start(f32[104,128]{1,0:T(8,128)S(1)} %get-tuple-element.63.refs_1_), channel_id=1, source_target_pairs={{0,4},{1,5},{2,6},{3,7},{4,0},{5,1},{6,2},{7,3},{8,12},{9,13},{10,... | collective-permute-start | bytes 159752 | tf_op jit(solution)/shard_map/ppermute | solution.py:287
  27.8 4.2 %collective-permute-start.4 = (f32[104,128]{1,0:T(8,128)S(1)}, f32[104,128]{1,0:T(8,128)S(1)}, u32[]{:S(2)}, u32[]{:S(2)}) collective-permute-start(f32[104,128]{1,0:T(8,128)S(1)} %shard_map.104), channel_id=1, source_target_pairs={{0,2},{1,3},{2,0},{3,1},{4,6},{5,7},{6,4},{7,5},{8,10},{9,11},{10,... | collective-permute-start | bytes 159752 | tf_op jit(solution)/shard_map/ppermute | solution.py:287
  30.0 2.8 %collective-permute-start.13 = (f32[8,32,128]{2,1,0:T(8,128)S(1)}, f32[8,32,128]{2,1,0:T(8,128)S(1)}, u32[]{:S(2)}, u32[]{:S(2)}) collective-permute-start(f32[8,32,128]{2,1,0:T(8,128)S(1)} %get-tuple-element.46), channel_id=1, source_target_pairs={{0,8},{1,9},{2,10},{3,11},{4,12},{5,13},{6,14},{7,15},{8,0},{9,1},... | collective-permute-start | bytes 393224 | tf_op jit(solution)/shard_map/ppermute | solution.py:287
  32.9 6.5 %collective-permute-start.18 = (f32[168,128]{1,0:T(8,128)S(1)}, f32[168,128]{1,0:T(8,128)S(1)}, u32[]{:S(2)}, u32[]{:S(2)}) collective-permute-start(f32[168,128]{1,0:T(8,128)S(1)} %get-tuple-element.47.refs_2_), channel_id=1, source_target_pairs={{0,2},{1,3},{2,0},{3,1},{4,6},{5,7},{6,4},{7,5},{8,10},{9,11},{10,... | collective-permute-start | bytes 258056 | tf_op jit(solution)/shard_map/ppermute | solution.py:287
  33.2 9.6 %collective-permute-start.19 = (f32[168,128]{1,0:T(8,128)S(1)}, f32[168,128]{1,0:T(8,128)S(1)}, u32[]{:S(2)}, u32[]{:S(2)}) collective-permute-start(f32[168,128]{1,0:T(8,128)S(1)} %get-tuple-element.48.refs_3_), channel_id=1, source_target_pairs={{0,4},{1,5},{2,6},{3,7},{4,0},{5,1},{6,2},{7,3},{8,12},{9,13},{10,... | collective-permute-start | bytes 258056 | tf_op jit(solution)/shard_map/ppermute | solution.py:287
  35.7 7.0 %collective-permute-start.20 = (f32[168,128]{1,0:T(8,128)S(1)}, f32[168,128]{1,0:T(8,128)S(1)}, u32[]{:S(2)}, u32[]{:S(2)}) collective-permute-start(f32[168,128]{1,0:T(8,128)S(1)} %get-tuple-element.49.refs_4_), channel_id=1, source_target_pairs={{0,6},{1,7},{2,4},{3,5},{4,2},{5,3},{6,0},{7,1},{8,14},{9,15},{10,... | collective-permute-start | bytes 258056 | tf_op jit(solution)/shard_map/ppermute | solution.py:287
  37.3 7.5 %collective-permute-start.16 = (f32[136,128]{1,0:T(8,128)S(1)}, f32[136,128]{1,0:T(8,128)S(1)}, u32[]{:S(2)}, u32[]{:S(2)}) collective-permute-start(f32[136,128]{1,0:T(8,128)S(1)} %get-tuple-element.51), channel_id=1, source_target_pairs={{0,17},{1,16},{2,19},{3,18},{4,21},{5,20},{6,23},{7,22},{8,25},{9,... | collective-permute-start | bytes 208904 | tf_op jit(solution)/shard_map/ppermute | solution.py:287
  38.5 7.8 %collective-permute-start.14 = (f32[136,128]{1,0:T(8,128)S(1)}, f32[136,128]{1,0:T(8,128)S(1)}, u32[]{:S(2)}, u32[]{:S(2)}) collective-permute-start(f32[136,128]{1,0:T(8,128)S(1)} %get-tuple-element.51), channel_id=1, source_target_pairs={{0,1},{1,0},{2,3},{3,2},{4,5},{5,4},{6,7},{7,6},{8,9},{9,8},{10,11... | collective-permute-start | bytes 208904 | tf_op jit(solution)/shard_map/ppermute | solution.py:287
  39.4 7.0 %collective-permute-start.15 = (f32[136,128]{1,0:T(8,128)S(1)}, f32[136,128]{1,0:T(8,128)S(1)}, u32[]{:S(2)}, u32[]{:S(2)}) collective-permute-start(f32[136,128]{1,0:T(8,128)S(1)} %get-tuple-element.50.refs_1_), channel_id=1, source_target_pairs={{0,16},{1,17},{2,18},{3,19},{4,20},{5,21},{6,22},{7,23},{8,24},{9,... | collective-permute-start | bytes 208904 | tf_op jit(solution)/shard_map/ppermute | solution.py:287
  42.8 8.4 %collective-permute-start.23 = (f32[408,128]{1,0:T(8,128)S(1)}, f32[408,128]{1,0:T(8,128)S(1)}, u32[]{:S(2)}, u32[]{:S(2)}) collective-permute-start(f32[408,128]{1,0:T(8,128)S(1)} %get-tuple-element.53), channel_id=1, source_target_pairs={{0,17},{1,16},{2,19},{3,18},{4,21},{5,20},{6,23},{7,22},{8,25},{9,... | collective-permute-start | bytes 626696 | tf_op jit(solution)/shard_map/ppermute | solution.py:287
  44.0 8.3 %collective-permute-start.21 = (f32[408,128]{1,0:T(8,128)S(1)}, f32[408,128]{1,0:T(8,128)S(1)}, u32[]{:S(2)}, u32[]{:S(2)}) collective-permute-start(f32[408,128]{1,0:T(8,128)S(1)} %get-tuple-element.53), channel_id=1, source_target_pairs={{0,1},{1,0},{2,3},{3,2},{4,5},{5,4},{6,7},{7,6},{8,9},{9,8},{10,11... | collective-permute-start | bytes 626696 | tf_op jit(solution)/shard_map/ppermute | solution.py:287
  44.8 8.4 %collective-permute-start.22 = (f32[408,128]{1,0:T(8,128)S(1)}, f32[408,128]{1,0:T(8,128)S(1)}, u32[]{:S(2)}, u32[]{:S(2)}) collective-permute-start(f32[408,128]{1,0:T(8,128)S(1)} %get-tuple-element.52.refs_6_), channel_id=1, source_target_pairs={{0,16},{1,17},{2,18},{3,19},{4,20},{5,21},{6,22},{7,23},{8,24},{9,... | collective-permute-start | bytes 626696 | tf_op jit(solution)/shard_map/ppermute | solution.py:287
  46.4 8.4 %copy-start = (s32[4,24]{1,0:T(4,128)S(1)}, s32[4,24]{1,0:T(4,128)}, u32[]{:S(2)}) copy-start(s32[4,24]{1,0:T(4,128)} %refs_0_.5) | copy-start | bytes 1156
  46.4 6.9 %collective-permute-start.17 = (f32[4,136,128]{2,1,0:T(8,128)S(1)}, f32[4,136,128]{2,1,0:T(8,128)S(1)}, u32[]{:S(2)}, u32[]{:S(2)}) collective-permute-start(f32[4,136,128]{2,1,0:T(8,128)S(1)} %pad_maximum_fusion), channel_id=1, source_target_pairs={{0,8},{1,9},{2,10},{3,11},{4,12},{5,13},{6,14},{7,15},{8,0},{9,1},... | collective-permute-start | bytes 835592 | tf_op jit(solution)/shard_map/ppermute | solution.py:287
  46.5 6.8 %collective-permute-start.24 = (f32[408,128]{1,0:T(8,128)S(1)}, f32[408,128]{1,0:T(8,128)S(1)}, u32[]{:S(2)}, u32[]{:S(2)}) collective-permute-start(f32[408,128]{1,0:T(8,128)S(1)} %get-tuple-element.52.refs_6_), channel_id=1, source_target_pairs={{0,8},{1,9},{2,10},{3,11},{4,12},{5,13},{6,14},{7,15},{8,0},{9,1},... | collective-permute-start | bytes 626696 | tf_op jit(solution)/shard_map/ppermute | solution.py:287
  51.2 2.1 %collective-permute-start.27 = (f32[408,128]{1,0:T(8,128)S(1)}, f32[408,128]{1,0:T(8,128)S(1)}, u32[]{:S(2)}, u32[]{:S(2)}) collective-permute-start(f32[408,128]{1,0:T(8,128)S(1)} %collective-permute-done.23.refs_9_), channel_id=1, source_target_pairs={{0,8},{1,9},{2,10},{3,11},{4,12},{5,13},{6,14},{7,15},{8,0},{9,1},... | collective-permute-start | bytes 626696 | tf_op jit(solution)/shard_map/ppermute | solution.py:287
  52.4 1.5 %collective-permute-start.25 = (f32[408,128]{1,0:T(8,128)S(1)}, f32[408,128]{1,0:T(8,128)S(1)}, u32[]{:S(2)}, u32[]{:S(2)}) collective-permute-start(f32[408,128]{1,0:T(8,128)S(1)} %collective-permute-done.21.refs_7_), channel_id=1, source_target_pairs={{0,8},{1,9},{2,10},{3,11},{4,12},{5,13},{6,14},{7,15},{8,0},{9,1},... | collective-permute-start | bytes 626696 | tf_op jit(solution)/shard_map/ppermute | solution.py:287
  53.3 1.5 %collective-permute-start.26 = (f32[408,128]{1,0:T(8,128)S(1)}, f32[408,128]{1,0:T(8,128)S(1)}, u32[]{:S(2)}, u32[]{:S(2)}) collective-permute-start(f32[408,128]{1,0:T(8,128)S(1)} %collective-permute-done.22.refs_8_), channel_id=1, source_target_pairs={{0,8},{1,9},{2,10},{3,11},{4,12},{5,13},{6,14},{7,15},{8,0},{9,1},... | collective-permute-start | bytes 626696 | tf_op jit(solution)/shard_map/ppermute | solution.py:287

commit v6 on v5

--- a/solution.py
+++ b/solution.py
@@ -26,7 +26,7 @@
     return pl.BlockSpec(memory_space=pltpu.VMEM)
 
 
-def call(body, outs, scratch, *args, in_hbm=False, flops=0, after=()):
+def call(body, outs, scratch, *args, in_hbm=False, out_hbm=False, flops=0, after=()):
     count = len(args)
 
     def run(*refs):
@@ -41,7 +41,7 @@
         run,
         out_shape=[jax.ShapeDtypeStruct(shape, kind) for shape, kind in outs],
         in_specs=[place(a) for a in args] + [pl.BlockSpec(memory_space=pl.ANY) for _ in after],
-        out_specs=[whole_vmem() for _ in outs],
+        out_specs=[pl.BlockSpec(memory_space=pltpu.HBM) if out_hbm else whole_vmem() for _ in outs],
         scratch_shapes=scratch,
         compiler_params=pltpu.CompilerParams(vmem_limit_bytes=VMEM_LIMIT),
         cost_estimate=pl.CostEstimate(flops=flops, bytes_accessed=0, transcendentals=0) if flops else None,
@@ -57,12 +57,9 @@
     return plane_id() * 4 + ((lax.axis_index("dp") >> 1) & 3)
 
 
-def send_kernel(x_hbm, *refs):
-    out_refs, (x_ref, held, sem) = refs[:4], refs[4:]
-    copy = pltpu.make_async_copy(x_hbm, x_ref, sem)
-    copy.start()
+def send_kernel(x_ref, *refs):
+    out_refs, held = refs[:4], refs[4]
     me = cell_id()
-    copy.wait()
     x_t = x_ref[...].astype(F32).reshape(128, 512).T
     for group in range(16):
         held[group ^ (me & 15)] = x_t[32 * group : 32 * group + 32]
@@ -95,17 +92,11 @@
 
 
 def local_kernel(*refs):
-    sources, (mine_ref, other_ref), held, sems = refs[:6], refs[6:8], refs[8:14], refs[14]
-    block_w, hid_t, sums = refs[15:]
-    copies = [pltpu.make_async_copy(src, dst, sems.at[i]) for i, (src, dst) in enumerate(zip(sources, held))]
-    for copy in copies:
-        copy.start()
+    held, (mine_ref, other_ref), (block_w, hid_t, sums) = refs[:6], refs[6:8], refs[8:]
     x_ref, og_ref, gw_ref, pw_ref, gain_ref, shift_ref = held
     me = cell_id()
     images = x_ref.shape[0]
     rows = images * 64
-    for copy in copies:
-        copy.wait()
     group_at = lax.broadcasted_iota(jnp.int32, (32, 128), 1) // 32
     for q in range(4):
         stacked = gw_ref[4 * q : 4 * q + 4].astype(F32).reshape(128, 288).T
@@ -225,58 +216,79 @@
         ref[104:, :] = piece_ref[0, at : at + size - 104, :]
 
 
-def merge_kernel(*refs):
-    parts, (own_ref, peer_ref) = refs[:3], refs[3:]
-    size = own_ref.shape[0] // 3
-    for z, ref in enumerate(parts):
-        at = size * z
-        own_ref[at : at + size, :] = ref[:size, :]
-        peer_ref[at : at + 104, :] = ref[:104, :]
-        peer_ref[at + 104 : at + size, :] = ref[size:, :]
+def merge_kernel(z1_ref, z2_ref, z3_ref, own_ref, here_ref, peer_ref):
+    packed = (here_ref.shape[0] - 208) // 3
+    step = 104 + packed
+    for out, at in ((own_ref, 104), (here_ref, 104), (peer_ref, step)):
+        for i, ref in enumerate((z2_ref, z3_ref)):
+            out[step * i : step * i + 104, :] = ref[:104, :]
+            out[step * i + 104 : step * i + step, :] = ref[at : at + packed, :]
+        out[2 * step : 2 * step + packed, :] = z1_ref[at : at + packed, :]
+    own_ref[2 * step + packed :, :] = z1_ref[:104, :]
+
+
+def forward_kernel(*refs):
+    for i, ref in enumerate(refs[:3]):
+        refs[3][104 * i : 104 * i + 104, :] = ref[:104, :]
 
 
 def finish_kernel(grad_scale, mean_scale, slot_ref, *refs):
-    parts, (group_ref, proj_ref, out_ref, owned_ref), (sums, blocks) = refs[:13], refs[13:17], refs[17:]
+    parts, outs, (sums, blocks, *held), sems = refs[:15], refs[15:19], refs[19:25], refs[25]
+    group_ref, proj_ref, out_ref, owned_ref = held
+    copies = [pltpu.make_async_copy(src, dst, sems.at[i]) for i, (src, dst) in enumerate(zip(held, outs))]
     me = cell_id()
     count = owned_ref.shape[0] // 2
-    step = 104 + packed_rows(count)
+    packed = packed_rows(count)
+    step = 104 + packed
+    places = []
     for place in range(8):
+        core, xy = place // 4, place % 4
+        late, forward = parts[5 + 5 * core + xy], parts[9 + 5 * core]
         for z in range(4):
-            j = (4 * place + z) ^ me
-            if z > 0:
-                ref, base = parts[5 + place], step * (z - 1)
-            elif place < 4:
-                ref, base = parts[place], 0
+            if z == 0:
+                ref = parts[4].at[xy] if core else parts[xy]
+                weight, factor = (ref, 0), (ref, 104)
+            elif z == 1:
+                weight = (late, 2 * step + packed) if xy == 0 else (forward, 104 * (xy - 1))
+                factor = (late, 2 * step)
             else:
-                ref, base = parts[4].at[place - 4], 0
-            for w in range(4):
-                at = pl.multiple_of(16 * j, 16)
-                row = base + 16 * w
-                proj_ref[pl.ds(at, 16), 128 * w : 128 * w + 128] = ref[row : row + 16, :] * grad_scale
-            sums[pl.ds(pl.multiple_of(40 * j, 8), 40), :] = ref[base + 64 : base + 104, :]
-            base += 104
-            tiles = [ref[base + count * t : base + count * t + count, :] for t in range(5)]
-            last = []
-            for i in range(count):
-                spot = base + 5 * count + i // 4
-                last.append(ref[spot : spot + 1, 32 * (i % 4) : 32 * (i % 4) + 32])
-            value = jnp.concatenate(tiles + [jnp.concatenate(last, axis=0)], axis=1) * mean_scale
-            for a in range(3):
-                pieces = []
-                for b in range(3):
-                    at = 96 * PAIRS.index(SAME.get((a, b), (a, b)))
-                    pieces.append(value[:, at : at + 96])
-                blocks[j >> 4, 3 * (j & 15) + a] = jnp.concatenate(pieces, axis=1)
+                weight, factor = (late, step * (z - 2)), (late, step * (z - 2) + 104)
+            places.append(((4 * place + z) ^ me, weight, factor))
+    for j, (ref, base), _ in places:
+        for w in range(4):
+            at = pl.multiple_of(16 * j, 16)
+            row = base + 16 * w
+            proj_ref[pl.ds(at, 16), 128 * w : 128 * w + 128] = ref[row : row + 16, :] * grad_scale
+        sums[pl.ds(pl.multiple_of(40 * j, 8), 40), :] = ref[base + 64 : base + 104, :]
+    copies[1].start()
     for q in range(4):
         group_ref[4 * q : 4 * q + 4] = (sums[320 * q : 320 * q + 288, :].T * grad_scale).reshape(4, 32, 288)
         for g in range(4):
             out_ref[4 * q + g] = sums[320 * q + 288 : 320 * q + 320, 32 * g : 32 * g + 32] * mean_scale
+    copies[0].start()
+    copies[2].start()
+    for j, _, (ref, base) in places:
+        tiles = [ref[base + count * t : base + count * t + count, :] for t in range(5)]
+        last = []
+        for i in range(count):
+            spot = base + 5 * count + i // 4
+            last.append(ref[spot : spot + 1, 32 * (i % 4) : 32 * (i % 4) + 32])
+        value = jnp.concatenate(tiles + [jnp.concatenate(last, axis=0)], axis=1) * mean_scale
+        for a in range(3):
+            pieces = []
+            for b in range(3):
+                at = 96 * PAIRS.index(SAME.get((a, b), (a, b)))
+                pieces.append(value[:, at : at + 96])
+            blocks[j >> 4, 3 * (j & 15) + a] = jnp.concatenate(pieces, axis=1)
     owner = lax.axis_index("owner")
     for s in range(owned_ref.shape[1]):
         block = slot_ref[owner, s]
         for core in range(2):
             value = blocks[core, jnp.maximum(block, 0)]
             owned_ref[count * core : count * core + count, s, :] = jnp.where(block >= 0, value, 0.0)
+    copies[3].start()
+    for copy in copies:
+        copy.wait()
 
 
 def per_device(n_owner, n_dp, activations, out_grad, group_weight, proj_weight, bn_gain, bn_shift, slot_block):
@@ -304,9 +316,8 @@
     sent = call(
         send_kernel,
         [((4, 32, 128), F32)] * 4,
-        [pltpu.VMEM(activations.shape, BF16), pltpu.VMEM((16, 32, 128), F32), pltpu.SemaphoreType.DMA],
+        [pltpu.VMEM((16, 32, 128), F32)],
         activations,
-        in_hbm=True,
         flops=SEND_FLOPS,
     )
     inputs = [
@@ -320,15 +331,12 @@
     mine, other = call(
         local_kernel,
         [((16, 104, 128), F32)] * 2,
-        [pltpu.VMEM(a.shape, a.dtype) for a in inputs]
-        + [
-            pltpu.SemaphoreType.DMA((len(inputs),)),
+        [
             pltpu.VMEM((4, 1152, 128), BF16),
             pltpu.VMEM((32, 16, rows), BF16),
             pltpu.VMEM((1280, 128), F32),
         ],
         *inputs,
-        in_hbm=True,
         flops=LOCAL_FLOPS,
     )
     sent, other = lax.optimization_barrier((sent, other))
@@ -363,21 +371,29 @@
     piece = piece.reshape(4, 2 * packed, 128)
 
     line = call(line_kernel, [((104 + 2 * packed, 128), F32)] * 3, [], total, piece)
+    line = [swap(line[z - 1], 0, 2 * z) for z in range(1, 4)]
     first, first_peer = call(
-        first_kernel, [((104 + packed, 128), F32)] * 2, [], total, piece, flops=FIRST_FLOPS, after=line if AFTER_LINE else ()
-    )
-    line = [swap(line[z - 1], 0, 2 * z) for z in range(1, 4)]
+        first_kernel, [((104 + packed, 128), F32)] * 2, [], total, piece, flops=FIRST_FLOPS, after=(line[0],)
+    )
     early = [first, swap(first_peer, 0, 1), swap(first, 2, 0), swap(first_peer, 2, 1)]
-    own, peer = call(merge_kernel, [((3 * (104 + packed), 128), F32)] * 2, [], *line)
-    late = [own, swap(peer, 0, 1), swap(own, 2, 0), swap(peer, 2, 1)]
+    (passed,) = call(forward_kernel, [((312, 128), F32)], [], *early[1:])
+    passed = swap(passed, 0, 2)
+    own, here, peer = call(
+        merge_kernel, [((312 + 3 * packed, 128), F32)] + [((208 + 3 * packed, 128), F32)] * 2, [], *line
+    )
+    late = [own, swap(peer, 0, 1), swap(here, 2, 0), swap(peer, 2, 1), passed]
     parts = early + [swap(jnp.stack(early), 1, 0)] + late + [swap(v, 1, 0) for v in late]
     slots = slot_block.shape[1]
+    outs = [((16, 32, 288), F32), ((512, 512), F32), ((16, 32, 32), F32), ((half, slots, 288), F32)]
     group_grad, proj_grad, out_factor, factor_owned = call(
         functools.partial(finish_kernel, grad_scale, mean_scale),
-        [((16, 32, 288), F32), ((512, 512), F32), ((16, 32, 32), F32), ((half, slots, 288), F32)],
-        [pltpu.VMEM((1280, 128), F32), pltpu.VMEM((2, 48, half // 2, 288), F32)],
+        outs,
+        [pltpu.VMEM((1280, 128), F32), pltpu.VMEM((2, 48, half // 2, 288), F32)]
+        + [pltpu.VMEM(shape, kind) for shape, kind in outs]
+        + [pltpu.SemaphoreType.DMA((4,))],
         slot_block,
         *parts,
+        out_hbm=True,
     )
     return group_grad.transpose(0, 2, 1), proj_grad, out_factor, factor_owned.transpose(1, 0, 2)
 

time: 58.1 us -> 57.4 us (0.988)
  starting transfers between devices: 32.1 us -> 33.7 us
  waiting for transfers between devices: 16.1 us -> 14.8 us
  Pallas kernels: 6.64 us -> 5.87 us
    ppermute x28 -> x30, starting transfers between devices: 32.1 us -> 33.7 us  [swap(): return lax.ppermute(value, AXES, pairs)]
    ppermute x28 -> x30, waiting for transfers between devices: 16.1 us -> 14.8 us  [swap(): return lax.ppermute(value, AXES, pairs)]
    pallas_call x9 -> x10, Pallas kernels: 6.64 us -> 5.87 us  [call(): pl.pallas_call(run, out_shape=[jax.ShapeDtypeStruct(shape, kind) for shap...]
  transfers between devices with their start and end apart: 28 -> 30, of which waited for: 11 -> 13; matrix products, arithmetic and copies ran while one was open for 0% -> 0% of each run, Pallas kernels for 3% -> 3%
where the time goes in v6:
time: 57.4 us; the launch traced here: 57.3 us
  starting transfers between devices  33.7 us (59%)
  waiting for transfers between devices  14.8 us (26%)
  Pallas kernels  5.87 us (10%)
  local copies, waits for them, and re-layouts  1.85 us (3%)
  between operations  0.81 us (1%)
    ppermute x30, starting transfers between devices, swap(): return lax.ppermute(value, AXES, pairs)  33.7 us
    ppermute x30, waiting for transfers between devices, swap(): return lax.ppermute(value, AXES, pairs)  14.8 us
    pallas_call x10, Pallas kernels, call(): pl.pallas_call(run, out_shape=[jax.ShapeDtypeStruct(shape, kind) for shap...  5.87 us
    unnamed x14, local copies, waits for them, and re-layouts  1.79 us
  transfers between devices with their start and end apart: 30, of which 13 were waited for; matrix products, arithmetic and copies ran while one was open for 0% of the time, Pallas kernels for 3%

profile of v6, /device:TPU:0, one launch (start us, length us, event | category | flops | bytes accessed | tf_op | source)
XLA Modules:
  0.0 57.3 jit_solution(8710299819384943857)
XLA Ops:
  0.7 1.0 %copy-done.3 = bf16[2,8,8,512]{3,2,1,0:T(8,128)(2,1)S(1)} copy-done((bf16[2,8,8,512]{3,2,1,0:T(8,128)(2,1)S(1)}, bf16[2,8,8,512]{3,2,1,0:T(8,128)(2,1)}, u32[]{:S(2)}) %copy-start.3) | copy-done | bytes 131096
  1.6 0.1 shard_map.103
  1.8 0.0 copy-start.5
  1.8 0.1 copy-done.2
  1.8 0.7 %copy-done.4 = bf16[2,8,8,512]{3,2,1,0:T(8,128)(2,1)S(1)} copy-done((bf16[2,8,8,512]{3,2,1,0:T(8,128)(2,1)S(1)}, bf16[2,8,8,512]{3,2,1,0:T(8,128)(2,1)}, u32[]{:S(2)}) %copy-start.4) | copy-done | bytes 131096
  2.6 1.4 %shard_map.102 = (f32[16,104,128]{2,1,0:T(8,128)S(1)}, f32[16,104,128]{2,1,0:T(8,128)S(1)}) custom-call(bf16[2,8,8,512]{3,2,1,0:T(8,128)(2,1)S(1)} %copy-done.3, bf16[2,8,8,512]{3,2,1,0:T(8,128)(2,1)S(1)} %copy-done.4, bf16[16,32,288]{2,1,0:T(8,128)(2,1)S(1)} %bitcast.30, bf16[512,512]{1,0:T(8,128)(2,1)S(1)} %copy-done.1, f32[1,512]{1,0:T(1,128)S(1)} %bitcast.31, ...), custom_call_target="tpu_custom_call" | custom-call | flops 4000000000 | tf_op jit(solution)/shard_map/pallas_call | solution.py:40
  4.0 0.5 collective-permute-start
  4.5 2.6 %collective-permute-start.7 = (f32[4,32,128]{2,1,0:T(8,128)S(1)}, f32[4,32,128]{2,1,0:T(8,128)S(1)}, u32[]{:S(2)}, u32[]{:S(2)}) collective-permute-start(f32[4,32,128]{2,1,0:T(8,128)S(1)} %get-tuple-element.40), channel_id=1, source_target_pairs={{0,1},{1,0},{2,3},{3,2},{4,5},{5,4},{6,7},{7,6},{8,9},{9,8},{10,11... | collective-permute-start | bytes 196616 | tf_op jit(solution)/shard_map/ppermute | solution.py:299
  7.1 1.5 %collective-permute-start.8 = (f32[4,32,128]{2,1,0:T(8,128)S(1)}, f32[4,32,128]{2,1,0:T(8,128)S(1)}, u32[]{:S(2)}, u32[]{:S(2)}) collective-permute-start(f32[4,32,128]{2,1,0:T(8,128)S(1)} %get-tuple-element.41), channel_id=1, source_target_pairs={{0,16},{1,17},{2,18},{3,19},{4,20},{5,21},{6,22},{7,23},{8,24},{9,... | collective-permute-start | bytes 196616 | tf_op jit(solution)/shard_map/ppermute | solution.py:299
  8.6 0.0 collective-permute-start.9
  8.6 0.0 collective-permute-done
  8.6 0.1 add.24.refs_4_
  8.8 2.0 %collective-permute-start.1 = (f32[4,104,128]{2,1,0:T(8,128)S(1)}, f32[4,104,128]{2,1,0:T(8,128)S(1)}, u32[]{:S(2)}, u32[]{:S(2)}) collective-permute-start(f32[4,104,128]{2,1,0:T(8,128)S(1)} %get-tuple-element.60), channel_id=1, source_target_pairs={{0,1},{1,0},{2,3},{3,2},{4,5},{5,4},{6,7},{7,6},{8,9},{9,8},{10,11... | collective-permute-start | bytes 638984 | tf_op jit(solution)/shard_map/ppermute | solution.py:299
  10.8 1.5 %collective-permute-start.3 = (f32[4,104,128]{2,1,0:T(8,128)S(1)}, f32[4,104,128]{2,1,0:T(8,128)S(1)}, u32[]{:S(2)}, u32[]{:S(2)}) collective-permute-start(f32[4,104,128]{2,1,0:T(8,128)S(1)} %get-tuple-element.61), channel_id=1, source_target_pairs={{0,17},{1,16},{2,19},{3,18},{4,21},{5,20},{6,23},{7,22},{8,25},{9,... | collective-permute-start | bytes 638984 | tf_op jit(solution)/shard_map/ppermute | solution.py:299
  12.3 0.0 collective-permute-done.7.refs_1_
  12.3 0.0 collective-permute-start.2
  12.3 0.0 collective-permute-done.8.refs_2_
  12.3 2.1 %collective-permute-done.9.refs_3_ = f32[4,32,128]{2,1,0:T(8,128)S(1)} collective-permute-done((f32[4,32,128]{2,1,0:T(8,128)S(1)}, f32[4,32,128]{2,1,0:T(8,128)S(1)}, u32[]{:S(2)}, u32[]{:S(2)}) %collective-permute-start.9) | collective-permute-done | bytes 65568 | tf_op jit(solution)/shard_map/ppermute | solution.py:299
  14.5 1.6 %collective-permute-start.10 = (f32[4,32,128]{2,1,0:T(8,128)S(1)}, f32[4,32,128]{2,1,0:T(8,128)S(1)}, u32[]{:S(2)}, u32[]{:S(2)}) collective-permute-start(f32[4,32,128]{2,1,0:T(8,128)S(1)} %get-tuple-element.43), channel_id=1, source_target_pairs={{0,2},{1,3},{2,0},{3,1},{4,6},{5,7},{6,4},{7,5},{8,10},{9,11},{10,... | collective-permute-start | bytes 196616 | tf_op jit(solution)/shard_map/ppermute | solution.py:299
  16.1 2.6 %collective-permute-start.11 = (f32[4,32,128]{2,1,0:T(8,128)S(1)}, f32[4,32,128]{2,1,0:T(8,128)S(1)}, u32[]{:S(2)}, u32[]{:S(2)}) collective-permute-start(f32[4,32,128]{2,1,0:T(8,128)S(1)} %get-tuple-element.44), channel_id=1, source_target_pairs={{0,4},{1,5},{2,6},{3,7},{4,0},{5,1},{6,2},{7,3},{8,12},{9,13},{10,... | collective-permute-start | bytes 196616 | tf_op jit(solution)/shard_map/ppermute | solution.py:299
  18.7 0.0 collective-permute-done.1
  18.7 3.0 %collective-permute-start.12 = (f32[4,32,128]{2,1,0:T(8,128)S(1)}, f32[4,32,128]{2,1,0:T(8,128)S(1)}, u32[]{:S(2)}, u32[]{:S(2)}) collective-permute-start(f32[4,32,128]{2,1,0:T(8,128)S(1)} %get-tuple-element.45), channel_id=1, source_target_pairs={{0,6},{1,7},{2,4},{3,5},{4,2},{5,3},{6,0},{7,1},{8,14},{9,15},{10,... | collective-permute-start | bytes 196616 | tf_op jit(solution)/shard_map/ppermute | solution.py:299
  21.7 0.9 %collective-permute-done.3 = f32[4,104,128]{2,1,0:T(8,128)S(1)} collective-permute-done((f32[4,104,128]{2,1,0:T(8,128)S(1)}, f32[4,104,128]{2,1,0:T(8,128)S(1)}, u32[]{:S(2)}, u32[]{:S(2)}) %collective-permute-start.3) | collective-permute-done | bytes 213024 | tf_op jit(solution)/shard_map/ppermute | solution.py:299
  22.6 0.7 %collective-permute-done.2 = f32[4,104,128]{2,1,0:T(8,128)S(1)} collective-permute-done((f32[4,104,128]{2,1,0:T(8,128)S(1)}, f32[4,104,128]{2,1,0:T(8,128)S(1)}, u32[]{:S(2)}, u32[]{:S(2)}) %collective-permute-start.2) | collective-permute-done | bytes 213024 | tf_op jit(solution)/shard_map/ppermute | solution.py:299
  23.4 3.7 %collective-permute-start.6 = (f32[104,128]{1,0:T(8,128)S(1)}, f32[104,128]{1,0:T(8,128)S(1)}, u32[]{:S(2)}, u32[]{:S(2)}) collective-permute-start(f32[104,128]{1,0:T(8,128)S(1)} %get-tuple-element.64.refs_2_), channel_id=1, source_target_pairs={{0,6},{1,7},{2,4},{3,5},{4,2},{5,3},{6,0},{7,1},{8,14},{9,15},{10,... | collective-permute-start | bytes 159752 | tf_op jit(solution)/shard_map/ppermute | solution.py:299
  27.1 0.0 collective-permute-start.5
  27.1 0.0 collective-permute-done.10.refs_4_
  27.1 0.8 %collective-permute-start.4 = (f32[104,128]{1,0:T(8,128)S(1)}, f32[104,128]{1,0:T(8,128)S(1)}, u32[]{:S(2)}, u32[]{:S(2)}) collective-permute-start(f32[104,128]{1,0:T(8,128)S(1)} %shard_map.104), channel_id=1, source_target_pairs={{0,2},{1,3},{2,0},{3,1},{4,6},{5,7},{6,4},{7,5},{8,10},{9,11},{10,... | collective-permute-start | bytes 159752 | tf_op jit(solution)/shard_map/ppermute | solution.py:299
  27.9 0.0 collective-permute-done.11.refs_5_
  27.9 0.0 collective-permute-done.12.refs_6_
  27.9 1.4 %shard_map.106 = (f32[8,32,128]{2,1,0:T(8,128)S(1)}, f32[8,32,128]{2,1,0:T(8,128)S(1)}) custom-call(f32[4,32,128]{2,1,0:T(8,128)S(1)} %get-tuple-element.39.refs_0_, f32[4,32,128]{2,1,0:T(8,128)S(1)} %collective-permute-done.7.refs_1_, f32[4,32,128]{2,1,0:T(8,128)S(1)} %collective-permute-done.8.refs_2_, f32[4,32,128]{2,1,0:T(8,128)S(1)} %collective-permute-done.9.refs_3_, ...), custom_call_target="tpu_custom_call" | custom-call | flops 4000000000 | tf_op jit(solution)/shard_map/pallas_call | solution.py:40
  29.4 0.1 collective-permute-start.13
  29.4 1.8 %collective-permute-done.4 = f32[104,128]{1,0:T(8,128)S(1)} collective-permute-done((f32[104,128]{1,0:T(8,128)S(1)}, f32[104,128]{1,0:T(8,128)S(1)}, u32[]{:S(2)}, u32[]{:S(2)}) %collective-permute-start.4) | collective-permute-done | bytes 53280 | tf_op jit(solution)/shard_map/ppermute | solution.py:299
  31.3 0.0 collective-permute-done.6
  31.3 0.8 %collective-permute-done.5 = f32[104,128]{1,0:T(8,128)S(1)} collective-permute-done((f32[104,128]{1,0:T(8,128)S(1)}, f32[104,128]{1,0:T(8,128)S(1)}, u32[]{:S(2)}, u32[]{:S(2)}) %collective-permute-start.5) | collective-permute-done | bytes 53280 | tf_op jit(solution)/shard_map/ppermute | solution.py:299
  32.1 0.0 collective-permute-done.13
  32.2 0.3 collective-permute-start.14
  32.5 2.6 %collective-permute-start.19 = (f32[168,128]{1,0:T(8,128)S(1)}, f32[168,128]{1,0:T(8,128)S(1)}, u32[]{:S(2)}, u32[]{:S(2)}) collective-permute-start(f32[168,128]{1,0:T(8,128)S(1)} %get-tuple-element.51), channel_id=1, source_target_pairs={{0,4},{1,5},{2,6},{3,7},{4,0},{5,1},{6,2},{7,3},{8,12},{9,13},{10,... | collective-permute-start | bytes 258056 | tf_op jit(solution)/shard_map/ppermute | solution.py:299
  35.1 1.6 %collective-permute-start.20 = (f32[168,128]{1,0:T(8,128)S(1)}, f32[168,128]{1,0:T(8,128)S(1)}, u32[]{:S(2)}, u32[]{:S(2)}) collective-permute-start(f32[168,128]{1,0:T(8,128)S(1)} %get-tuple-element.52), channel_id=1, source_target_pairs={{0,6},{1,7},{2,4},{3,5},{4,2},{5,3},{6,0},{7,1},{8,14},{9,15},{10,... | collective-permute-start | bytes 258056 | tf_op jit(solution)/shard_map/ppermute | solution.py:299
  36.6 0.8 %collective-permute-done.14.refs_2_.refs_0_ = f32[168,128]{1,0:T(8,128)S(1)} collective-permute-done((f32[168,128]{1,0:T(8,128)S(1)}, f32[168,128]{1,0:T(8,128)S(1)}, u32[]{:S(2)}, u32[]{:S(2)}) %collective-permute-start.14) | collective-permute-done | bytes 86048 | tf_op jit(solution)/shard_map/ppermute | solution.py:299
  37.5 1.2 %collective-permute-start.17 = (f32[136,128]{1,0:T(8,128)S(1)}, f32[136,128]{1,0:T(8,128)S(1)}, u32[]{:S(2)}, u32[]{:S(2)}) collective-permute-start(f32[136,128]{1,0:T(8,128)S(1)} %get-tuple-element.50), channel_id=1, source_target_pairs={{0,17},{1,16},{2,19},{3,18},{4,21},{5,20},{6,23},{7,22},{8,25},{9,... | collective-permute-start | bytes 208904 | tf_op jit(solution)/shard_map/ppermute | solution.py:299
  38.7 0.8 %collective-permute-start.15 = (f32[136,128]{1,0:T(8,128)S(1)}, f32[136,128]{1,0:T(8,128)S(1)}, u32[]{:S(2)}, u32[]{:S(2)}) collective-permute-start(f32[136,128]{1,0:T(8,128)S(1)} %get-tuple-element.50), channel_id=1, source_target_pairs={{0,1},{1,0},{2,3},{3,2},{4,5},{5,4},{6,7},{7,6},{8,9},{9,8},{10,11... | collective-permute-start | bytes 208904 | tf_op jit(solution)/shard_map/ppermute | solution.py:299
  39.5 1.5 %collective-permute-start.16 = (f32[136,128]{1,0:T(8,128)S(1)}, f32[136,128]{1,0:T(8,128)S(1)}, u32[]{:S(2)}, u32[]{:S(2)}) collective-permute-start(f32[136,128]{1,0:T(8,128)S(1)} %get-tuple-element.49.refs_1_), channel_id=1, source_target_pairs={{0,16},{1,17},{2,18},{3,19},{4,20},{5,21},{6,22},{7,23},{8,24},{9,... | collective-permute-start | bytes 208904 | tf_op jit(solution)/shard_map/ppermute | solution.py:299
  41.0 1.1 %collective-permute-done.19.refs_1_ = f32[168,128]{1,0:T(8,128)S(1)} collective-permute-done((f32[168,128]{1,0:T(8,128)S(1)}, f32[168,128]{1,0:T(8,128)S(1)}, u32[]{:S(2)}, u32[]{:S(2)}) %collective-permute-start.19) | collective-permute-done | bytes 86048 | tf_op jit(solution)/shard_map/ppermute | solution.py:299
  42.1 0.0 collective-permute-done.20.refs_2_
  42.1 0.6 %collective-permute-start.22 = (f32[304,128]{1,0:T(8,128)S(1)}, f32[304,128]{1,0:T(8,128)S(1)}, u32[]{:S(2)}, u32[]{:S(2)}) collective-permute-start(f32[304,128]{1,0:T(8,128)S(1)} %get-tuple-element.55), channel_id=1, source_target_pairs={{0,16},{1,17},{2,18},{3,19},{4,20},{5,21},{6,22},{7,23},{8,24},{9,... | collective-permute-start | bytes 466952 | tf_op jit(solution)/shard_map/ppermute | solution.py:299
  42.7 2.2 %collective-permute-start.23 = (f32[304,128]{1,0:T(8,128)S(1)}, f32[304,128]{1,0:T(8,128)S(1)}, u32[]{:S(2)}, u32[]{:S(2)}) collective-permute-start(f32[304,128]{1,0:T(8,128)S(1)} %get-tuple-element.54), channel_id=1, source_target_pairs={{0,17},{1,16},{2,19},{3,18},{4,21},{5,20},{6,23},{7,22},{8,25},{9,... | collective-permute-start | bytes 466952 | tf_op jit(solution)/shard_map/ppermute | solution.py:299
  44.9 0.0 collective-permute-done.17.refs_2_.refs_4_
  44.9 0.8 %collective-permute-start.21 = (f32[304,128]{1,0:T(8,128)S(1)}, f32[304,128]{1,0:T(8,128)S(1)}, u32[]{:S(2)}, u32[]{:S(2)}) collective-permute-start(f32[304,128]{1,0:T(8,128)S(1)} %get-tuple-element.54), channel_id=1, source_target_pairs={{0,1},{1,0},{2,3},{3,2},{4,5},{5,4},{6,7},{7,6},{8,9},{9,8},{10,11... | collective-permute-start | bytes 466952 | tf_op jit(solution)/shard_map/ppermute | solution.py:299
  45.7 0.0 collective-permute-done.15.refs_0_.refs_2_
  45.7 0.0 collective-permute-start.25
  45.7 0.5 collective-permute-done.16.refs_1_.refs_3_
  46.2 1.2 %collective-permute-start.24 = (f32[312,128]{1,0:T(8,128)S(1)}, f32[312,128]{1,0:T(8,128)S(1)}, u32[]{:S(2)}, u32[]{:S(2)}) collective-permute-start(f32[312,128]{1,0:T(8,128)S(1)} %shard_map.110), channel_id=1, source_target_pairs={{0,2},{1,3},{2,0},{3,1},{4,6},{5,7},{6,4},{7,5},{8,10},{9,11},{10,... | collective-permute-start | bytes 479240 | tf_op jit(solution)/shard_map/ppermute | solution.py:299
  47.4 2.7 %collective-permute-done.22.refs_8_ = f32[304,128]{1,0:T(8,128)S(1)} collective-permute-done((f32[304,128]{1,0:T(8,128)S(1)}, f32[304,128]{1,0:T(8,128)S(1)}, u32[]{:S(2)}, u32[]{:S(2)}) %collective-permute-start.22) | collective-permute-done | bytes 155680 | tf_op jit(solution)/shard_map/ppermute | solution.py:299
  50.2 0.0 collective-permute-start.18
  50.2 2.1 %collective-permute-done.24.refs_10_ = f32[312,128]{1,0:T(8,128)S(1)} collective-permute-done((f32[312,128]{1,0:T(8,128)S(1)}, f32[312,128]{1,0:T(8,128)S(1)}, u32[]{:S(2)}, u32[]{:S(2)}) %collective-permute-start.24) | collective-permute-done | bytes 159776 | tf_op jit(solution)/shard_map/ppermute | solution.py:299
  52.3 0.5 collective-permute-start.27
  52.8 0.1 collective-permute-start.28
  52.9 0.0 collective-permute-done.25.refs_11_
  52.9 0.4 collective-permute-start.26
  53.3 0.6 %collective-permute-done.27.refs_13_ = f32[304,128]{1,0:T(8,128)S(1)} collective-permute-done((f32[304,128]{1,0:T(8,128)S(1)}, f32[304,128]{1,0:T(8,128)S(1)}, u32[]{:S(2)}, u32[]{:S(2)}) %collective-permute-start.27) | collective-permute-done | bytes 155680 | tf_op jit(solution)/shard_map/ppermute | solution.py:299
  53.9 0.3 collective-permute-done.28.refs_14_
  54.2 0.2 collective-permute-done.26.refs_12_
  54.4 2.8 %shard_map.111 = (f32[16,32,288]{2,1,0:T(8,128)}, f32[512,512]{1,0:T(8,128)}, f32[16,32,32]{2,1,0:T(8,128)}, f32[12,24,288]{2,1,0:T(8,128)}) custom-call(s32[4,24]{1,0:T(4,128)S(1)} %copy-done, f32[136,128]{1,0:T(8,128)S(1)} %get-tuple-element.49.refs_1_, f32[136,128]{1,0:T(8,128)S(1)} %collective-permute-done.15.refs_0_.refs_2_, ...), custom_call_target="tpu_custom_call" | custom-call | tf_op jit(solution)/shard_map/pallas_call | solution.py:40
  (27 shorter events, 0.3 us)
Async XLA Ops:
  0.6 1.2 %copy-start.1 = (bf16[512,512]{1,0:T(8,128)(2,1)S(1)}, bf16[512,512]{1,0:T(8,128)(2,1)}, u32[]{:S(2)}) copy-start(bf16[512,512]{1,0:T(8,128)(2,1)} %refs_3_.1) | copy-start | bytes 1572868
  0.6 1.2 %copy-start.2 = (bf16[16,288,32]{1,2,0:T(8,128)(2,1)S(1)}, bf16[16,288,32]{1,2,0:T(8,128)(2,1)}, u32[]{:S(2)}) copy-start(bf16[16,288,32]{1,2,0:T(8,128)(2,1)} %param.9) | copy-start | bytes 884740
  0.7 1.0 %copy-start.3 = (bf16[2,8,8,512]{3,2,1,0:T(8,128)(2,1)S(1)}, bf16[2,8,8,512]{3,2,1,0:T(8,128)(2,1)}, u32[]{:S(2)}) copy-start(bf16[2,8,8,512]{3,2,1,0:T(8,128)(2,1)} %refs_0_.4) | copy-start | bytes 393220
  1.6 1.0 %copy-start.4 = (bf16[2,8,8,512]{3,2,1,0:T(8,128)(2,1)S(1)}, bf16[2,8,8,512]{3,2,1,0:T(8,128)(2,1)}, u32[]{:S(2)}) copy-start(bf16[2,8,8,512]{3,2,1,0:T(8,128)(2,1)} %refs_1_.1) | copy-start | bytes 393220
  1.6 1.0 %copy-start.6 = (f32[512]{0:T(512)S(1)}, f32[512]{0:T(512)}, u32[]{:S(2)}) copy-start(f32[512]{0:T(512)} %param.12) | copy-start | bytes 6148
  1.8 0.8 %copy-start.5 = (f32[512]{0:T(512)S(1)}, f32[512]{0:T(512)}, u32[]{:S(2)}) copy-start(f32[512]{0:T(512)} %param.11) | copy-start | bytes 6148
  4.0 4.6 %collective-permute-start = (f32[16,104,128]{2,1,0:T(8,128)S(1)}, f32[16,104,128]{2,1,0:T(8,128)S(1)}, u32[]{:S(2)}, u32[]{:S(2)}) collective-permute-start(f32[16,104,128]{2,1,0:T(8,128)S(1)} %get-tuple-element.38), channel_id=1, source_target_pairs={{0,8},{1,9},{2,10},{3,11},{4,12},{5,13},{6,14},{7,15},{8,0},{9,1},... | collective-permute-start | bytes 2555912 | tf_op jit(solution)/shard_map/ppermute | solution.py:299
  4.5 7.8 %collective-permute-start.7 = (f32[4,32,128]{2,1,0:T(8,128)S(1)}, f32[4,32,128]{2,1,0:T(8,128)S(1)}, u32[]{:S(2)}, u32[]{:S(2)}) collective-permute-start(f32[4,32,128]{2,1,0:T(8,128)S(1)} %get-tuple-element.40), channel_id=1, source_target_pairs={{0,1},{1,0},{2,3},{3,2},{4,5},{5,4},{6,7},{7,6},{8,9},{9,8},{10,11... | collective-permute-start | bytes 196616 | tf_op jit(solution)/shard_map/ppermute | solution.py:299
  7.1 5.3 %collective-permute-start.8 = (f32[4,32,128]{2,1,0:T(8,128)S(1)}, f32[4,32,128]{2,1,0:T(8,128)S(1)}, u32[]{:S(2)}, u32[]{:S(2)}) collective-permute-start(f32[4,32,128]{2,1,0:T(8,128)S(1)} %get-tuple-element.41), channel_id=1, source_target_pairs={{0,16},{1,17},{2,18},{3,19},{4,20},{5,21},{6,22},{7,23},{8,24},{9,... | collective-permute-start | bytes 196616 | tf_op jit(solution)/shard_map/ppermute | solution.py:299
  8.6 5.9 %collective-permute-start.9 = (f32[4,32,128]{2,1,0:T(8,128)S(1)}, f32[4,32,128]{2,1,0:T(8,128)S(1)}, u32[]{:S(2)}, u32[]{:S(2)}) collective-permute-start(f32[4,32,128]{2,1,0:T(8,128)S(1)} %get-tuple-element.42), channel_id=1, source_target_pairs={{0,17},{1,16},{2,19},{3,18},{4,21},{5,20},{6,23},{7,22},{8,25},{9,... | collective-permute-start | bytes 196616 | tf_op jit(solution)/shard_map/ppermute | solution.py:299
  8.8 9.9 %collective-permute-start.1 = (f32[4,104,128]{2,1,0:T(8,128)S(1)}, f32[4,104,128]{2,1,0:T(8,128)S(1)}, u32[]{:S(2)}, u32[]{:S(2)}) collective-permute-start(f32[4,104,128]{2,1,0:T(8,128)S(1)} %get-tuple-element.60), channel_id=1, source_target_pairs={{0,1},{1,0},{2,3},{3,2},{4,5},{5,4},{6,7},{7,6},{8,9},{9,8},{10,11... | collective-permute-start | bytes 638984 | tf_op jit(solution)/shard_map/ppermute | solution.py:299
  10.8 11.8 %collective-permute-start.3 = (f32[4,104,128]{2,1,0:T(8,128)S(1)}, f32[4,104,128]{2,1,0:T(8,128)S(1)}, u32[]{:S(2)}, u32[]{:S(2)}) collective-permute-start(f32[4,104,128]{2,1,0:T(8,128)S(1)} %get-tuple-element.61), channel_id=1, source_target_pairs={{0,17},{1,16},{2,19},{3,18},{4,21},{5,20},{6,23},{7,22},{8,25},{9,... | collective-permute-start | bytes 638984 | tf_op jit(solution)/shard_map/ppermute | solution.py:299
  12.3 11.0 %collective-permute-start.2 = (f32[4,104,128]{2,1,0:T(8,128)S(1)}, f32[4,104,128]{2,1,0:T(8,128)S(1)}, u32[]{:S(2)}, u32[]{:S(2)}) collective-permute-start(f32[4,104,128]{2,1,0:T(8,128)S(1)} %get-tuple-element.62), channel_id=1, source_target_pairs={{0,16},{1,17},{2,18},{3,19},{4,20},{5,21},{6,22},{7,23},{8,24},{9,... | collective-permute-start | bytes 638984 | tf_op jit(solution)/shard_map/ppermute | solution.py:299
  14.5 12.6 %collective-permute-start.10 = (f32[4,32,128]{2,1,0:T(8,128)S(1)}, f32[4,32,128]{2,1,0:T(8,128)S(1)}, u32[]{:S(2)}, u32[]{:S(2)}) collective-permute-start(f32[4,32,128]{2,1,0:T(8,128)S(1)} %get-tuple-element.43), channel_id=1, source_target_pairs={{0,2},{1,3},{2,0},{3,1},{4,6},{5,7},{6,4},{7,5},{8,10},{9,11},{10,... | collective-permute-start | bytes 196616 | tf_op jit(solution)/shard_map/ppermute | solution.py:299
  16.1 11.8 %collective-permute-start.11 = (f32[4,32,128]{2,1,0:T(8,128)S(1)}, f32[4,32,128]{2,1,0:T(8,128)S(1)}, u32[]{:S(2)}, u32[]{:S(2)}) collective-permute-start(f32[4,32,128]{2,1,0:T(8,128)S(1)} %get-tuple-element.44), channel_id=1, source_target_pairs={{0,4},{1,5},{2,6},{3,7},{4,0},{5,1},{6,2},{7,3},{8,12},{9,13},{10,... | collective-permute-start | bytes 196616 | tf_op jit(solution)/shard_map/ppermute | solution.py:299
  18.7 9.2 %collective-permute-start.12 = (f32[4,32,128]{2,1,0:T(8,128)S(1)}, f32[4,32,128]{2,1,0:T(8,128)S(1)}, u32[]{:S(2)}, u32[]{:S(2)}) collective-permute-start(f32[4,32,128]{2,1,0:T(8,128)S(1)} %get-tuple-element.45), channel_id=1, source_target_pairs={{0,6},{1,7},{2,4},{3,5},{4,2},{5,3},{6,0},{7,1},{8,14},{9,15},{10,... | collective-permute-start | bytes 196616 | tf_op jit(solution)/shard_map/ppermute | solution.py:299
  23.4 7.9 %collective-permute-start.6 = (f32[104,128]{1,0:T(8,128)S(1)}, f32[104,128]{1,0:T(8,128)S(1)}, u32[]{:S(2)}, u32[]{:S(2)}) collective-permute-start(f32[104,128]{1,0:T(8,128)S(1)} %get-tuple-element.64.refs_2_), channel_id=1, source_target_pairs={{0,6},{1,7},{2,4},{3,5},{4,2},{5,3},{6,0},{7,1},{8,14},{9,15},{10,... | collective-permute-start | bytes 159752 | tf_op jit(solution)/shard_map/ppermute | solution.py:299
  27.1 5.0 %collective-permute-start.5 = (f32[104,128]{1,0:T(8,128)S(1)}, f32[104,128]{1,0:T(8,128)S(1)}, u32[]{:S(2)}, u32[]{:S(2)}) collective-permute-start(f32[104,128]{1,0:T(8,128)S(1)} %get-tuple-element.65.refs_1_), channel_id=1, source_target_pairs={{0,4},{1,5},{2,6},{3,7},{4,0},{5,1},{6,2},{7,3},{8,12},{9,13},{10,... | collective-permute-start | bytes 159752 | tf_op jit(solution)/shard_map/ppermute | solution.py:299
  27.1 4.2 %collective-permute-start.4 = (f32[104,128]{1,0:T(8,128)S(1)}, f32[104,128]{1,0:T(8,128)S(1)}, u32[]{:S(2)}, u32[]{:S(2)}) collective-permute-start(f32[104,128]{1,0:T(8,128)S(1)} %shard_map.104), channel_id=1, source_target_pairs={{0,2},{1,3},{2,0},{3,1},{4,6},{5,7},{6,4},{7,5},{8,10},{9,11},{10,... | collective-permute-start | bytes 159752 | tf_op jit(solution)/shard_map/ppermute | solution.py:299
  29.4 2.7 %collective-permute-start.13 = (f32[8,32,128]{2,1,0:T(8,128)S(1)}, f32[8,32,128]{2,1,0:T(8,128)S(1)}, u32[]{:S(2)}, u32[]{:S(2)}) collective-permute-start(f32[8,32,128]{2,1,0:T(8,128)S(1)} %get-tuple-element.47), channel_id=1, source_target_pairs={{0,8},{1,9},{2,10},{3,11},{4,12},{5,13},{6,14},{7,15},{8,0},{9,1},... | collective-permute-start | bytes 393224 | tf_op jit(solution)/shard_map/ppermute | solution.py:299
  32.2 5.3 %collective-permute-start.14 = (f32[168,128]{1,0:T(8,128)S(1)}, f32[168,128]{1,0:T(8,128)S(1)}, u32[]{:S(2)}, u32[]{:S(2)}) collective-permute-start(f32[168,128]{1,0:T(8,128)S(1)} %get-tuple-element.48), channel_id=1, source_target_pairs={{0,2},{1,3},{2,0},{3,1},{4,6},{5,7},{6,4},{7,5},{8,10},{9,11},{10,... | collective-permute-start | bytes 258056 | tf_op jit(solution)/shard_map/ppermute | solution.py:299
  32.5 9.6 %collective-permute-start.19 = (f32[168,128]{1,0:T(8,128)S(1)}, f32[168,128]{1,0:T(8,128)S(1)}, u32[]{:S(2)}, u32[]{:S(2)}) collective-permute-start(f32[168,128]{1,0:T(8,128)S(1)} %get-tuple-element.51), channel_id=1, source_target_pairs={{0,4},{1,5},{2,6},{3,7},{4,0},{5,1},{6,2},{7,3},{8,12},{9,13},{10,... | collective-permute-start | bytes 258056 | tf_op jit(solution)/shard_map/ppermute | solution.py:299
  35.1 7.0 %collective-permute-start.20 = (f32[168,128]{1,0:T(8,128)S(1)}, f32[168,128]{1,0:T(8,128)S(1)}, u32[]{:S(2)}, u32[]{:S(2)}) collective-permute-start(f32[168,128]{1,0:T(8,128)S(1)} %get-tuple-element.52), channel_id=1, source_target_pairs={{0,6},{1,7},{2,4},{3,5},{4,2},{5,3},{6,0},{7,1},{8,14},{9,15},{10,... | collective-permute-start | bytes 258056 | tf_op jit(solution)/shard_map/ppermute | solution.py:299
  37.5 7.4 %collective-permute-start.17 = (f32[136,128]{1,0:T(8,128)S(1)}, f32[136,128]{1,0:T(8,128)S(1)}, u32[]{:S(2)}, u32[]{:S(2)}) collective-permute-start(f32[136,128]{1,0:T(8,128)S(1)} %get-tuple-element.50), channel_id=1, source_target_pairs={{0,17},{1,16},{2,19},{3,18},{4,21},{5,20},{6,23},{7,22},{8,25},{9,... | collective-permute-start | bytes 208904 | tf_op jit(solution)/shard_map/ppermute | solution.py:299
  38.7 7.0 %collective-permute-start.15 = (f32[136,128]{1,0:T(8,128)S(1)}, f32[136,128]{1,0:T(8,128)S(1)}, u32[]{:S(2)}, u32[]{:S(2)}) collective-permute-start(f32[136,128]{1,0:T(8,128)S(1)} %get-tuple-element.50), channel_id=1, source_target_pairs={{0,1},{1,0},{2,3},{3,2},{4,5},{5,4},{6,7},{7,6},{8,9},{9,8},{10,11... | collective-permute-start | bytes 208904 | tf_op jit(solution)/shard_map/ppermute | solution.py:299
  39.5 6.7 %collective-permute-start.16 = (f32[136,128]{1,0:T(8,128)S(1)}, f32[136,128]{1,0:T(8,128)S(1)}, u32[]{:S(2)}, u32[]{:S(2)}) collective-permute-start(f32[136,128]{1,0:T(8,128)S(1)} %get-tuple-element.49.refs_1_), channel_id=1, source_target_pairs={{0,16},{1,17},{2,18},{3,19},{4,20},{5,21},{6,22},{7,23},{8,24},{9,... | collective-permute-start | bytes 208904 | tf_op jit(solution)/shard_map/ppermute | solution.py:299
  42.1 8.0 %collective-permute-start.22 = (f32[304,128]{1,0:T(8,128)S(1)}, f32[304,128]{1,0:T(8,128)S(1)}, u32[]{:S(2)}, u32[]{:S(2)}) collective-permute-start(f32[304,128]{1,0:T(8,128)S(1)} %get-tuple-element.55), channel_id=1, source_target_pairs={{0,16},{1,17},{2,18},{3,19},{4,20},{5,21},{6,22},{7,23},{8,24},{9,... | collective-permute-start | bytes 466952 | tf_op jit(solution)/shard_map/ppermute | solution.py:299
  42.7 9.6 %collective-permute-start.23 = (f32[304,128]{1,0:T(8,128)S(1)}, f32[304,128]{1,0:T(8,128)S(1)}, u32[]{:S(2)}, u32[]{:S(2)}) collective-permute-start(f32[304,128]{1,0:T(8,128)S(1)} %get-tuple-element.54), channel_id=1, source_target_pairs={{0,17},{1,16},{2,19},{3,18},{4,21},{5,20},{6,23},{7,22},{8,25},{9,... | collective-permute-start | bytes 466952 | tf_op jit(solution)/shard_map/ppermute | solution.py:299
  44.9 7.9 %collective-permute-start.21 = (f32[304,128]{1,0:T(8,128)S(1)}, f32[304,128]{1,0:T(8,128)S(1)}, u32[]{:S(2)}, u32[]{:S(2)}) collective-permute-start(f32[304,128]{1,0:T(8,128)S(1)} %get-tuple-element.54), channel_id=1, source_target_pairs={{0,1},{1,0},{2,3},{3,2},{4,5},{5,4},{6,7},{7,6},{8,9},{9,8},{10,11... | collective-permute-start | bytes 466952 | tf_op jit(solution)/shard_map/ppermute | solution.py:299
  45.7 7.2 %collective-permute-start.25 = (f32[408,128]{1,0:T(8,128)S(1)}, f32[408,128]{1,0:T(8,128)S(1)}, u32[]{:S(2)}, u32[]{:S(2)}) collective-permute-start(f32[408,128]{1,0:T(8,128)S(1)} %get-tuple-element.53.refs_6_), channel_id=1, source_target_pairs={{0,8},{1,9},{2,10},{3,11},{4,12},{5,13},{6,14},{7,15},{8,0},{9,1},... | collective-permute-start | bytes 626696 | tf_op jit(solution)/shard_map/ppermute | solution.py:299
  46.2 6.0 %collective-permute-start.24 = (f32[312,128]{1,0:T(8,128)S(1)}, f32[312,128]{1,0:T(8,128)S(1)}, u32[]{:S(2)}, u32[]{:S(2)}) collective-permute-start(f32[312,128]{1,0:T(8,128)S(1)} %shard_map.110), channel_id=1, source_target_pairs={{0,2},{1,3},{2,0},{3,1},{4,6},{5,7},{6,4},{7,5},{8,10},{9,11},{10,... | collective-permute-start | bytes 479240 | tf_op jit(solution)/shard_map/ppermute | solution.py:299
  47.4 7.0 %copy-start = (s32[4,24]{1,0:T(4,128)S(1)}, s32[4,24]{1,0:T(4,128)}, u32[]{:S(2)}) copy-start(s32[4,24]{1,0:T(4,128)} %refs_0_.5) | copy-start | bytes 1156
  50.2 4.3 %collective-permute-start.18 = (f32[4,136,128]{2,1,0:T(8,128)S(1)}, f32[4,136,128]{2,1,0:T(8,128)S(1)}, u32[]{:S(2)}, u32[]{:S(2)}) collective-permute-start(f32[4,136,128]{2,1,0:T(8,128)S(1)} %pad_maximum_fusion), channel_id=1, source_target_pairs={{0,8},{1,9},{2,10},{3,11},{4,12},{5,13},{6,14},{7,15},{8,0},{9,1},... | collective-permute-start | bytes 835592 | tf_op jit(solution)/shard_map/ppermute | solution.py:299
  52.3 2.1 %collective-permute-start.29 = (f32[312,128]{1,0:T(8,128)S(1)}, f32[312,128]{1,0:T(8,128)S(1)}, u32[]{:S(2)}, u32[]{:S(2)}) collective-permute-start(f32[312,128]{1,0:T(8,128)S(1)} %collective-permute-done.24.refs_10_), channel_id=1, source_target_pairs={{0,8},{1,9},{2,10},{3,11},{4,12},{5,13},{6,14},{7,15},{8,0},{9,1},... | collective-permute-start | bytes 479240 | tf_op jit(solution)/shard_map/ppermute | solution.py:299
  52.3 1.6 %collective-permute-start.27 = (f32[304,128]{1,0:T(8,128)S(1)}, f32[304,128]{1,0:T(8,128)S(1)}, u32[]{:S(2)}, u32[]{:S(2)}) collective-permute-start(f32[304,128]{1,0:T(8,128)S(1)} %collective-permute-done.22.refs_8_), channel_id=1, source_target_pairs={{0,8},{1,9},{2,10},{3,11},{4,12},{5,13},{6,14},{7,15},{8,0},{9,1},... | collective-permute-start | bytes 466952 | tf_op jit(solution)/shard_map/ppermute | solution.py:299
  52.8 1.4 %collective-permute-start.28 = (f32[304,128]{1,0:T(8,128)S(1)}, f32[304,128]{1,0:T(8,128)S(1)}, u32[]{:S(2)}, u32[]{:S(2)}) collective-permute-start(f32[304,128]{1,0:T(8,128)S(1)} %collective-permute-done.23.refs_9_), channel_id=1, source_target_pairs={{0,8},{1,9},{2,10},{3,11},{4,12},{5,13},{6,14},{7,15},{8,0},{9,1},... | collective-permute-start | bytes 466952 | tf_op jit(solution)/shard_map/ppermute | solution.py:299
  52.9 1.5 %collective-permute-start.26 = (f32[304,128]{1,0:T(8,128)S(1)}, f32[304,128]{1,0:T(8,128)S(1)}, u32[]{:S(2)}, u32[]{:S(2)}) collective-permute-start(f32[304,128]{1,0:T(8,128)S(1)} %collective-permute-done.21.refs_7_), channel_id=1, source_target_pairs={{0,8},{1,9},{2,10},{3,11},{4,12},{5,13},{6,14},{7,15},{8,0},{9,1},... | collective-permute-start | bytes 466952 | tf_op jit(solution)/shard_map/ppermute | solution.py:299

commit v7 on v5

--- a/solution.py
+++ b/solution.py
@@ -57,12 +57,9 @@
     return plane_id() * 4 + ((lax.axis_index("dp") >> 1) & 3)
 
 
-def send_kernel(x_hbm, *refs):
-    out_refs, (x_ref, held, sem) = refs[:4], refs[4:]
-    copy = pltpu.make_async_copy(x_hbm, x_ref, sem)
-    copy.start()
+def send_kernel(x_ref, *refs):
+    out_refs, held = refs[:4], refs[4]
     me = cell_id()
-    copy.wait()
     x_t = x_ref[...].astype(F32).reshape(128, 512).T
     for group in range(16):
         held[group ^ (me & 15)] = x_t[32 * group : 32 * group + 32]
@@ -95,17 +92,11 @@
 
 
 def local_kernel(*refs):
-    sources, (mine_ref, other_ref), held, sems = refs[:6], refs[6:8], refs[8:14], refs[14]
-    block_w, hid_t, sums = refs[15:]
-    copies = [pltpu.make_async_copy(src, dst, sems.at[i]) for i, (src, dst) in enumerate(zip(sources, held))]
-    for copy in copies:
-        copy.start()
+    held, (mine_ref, other_ref), (block_w, hid_t, sums) = refs[:6], refs[6:8], refs[8:]
     x_ref, og_ref, gw_ref, pw_ref, gain_ref, shift_ref = held
     me = cell_id()
     images = x_ref.shape[0]
     rows = images * 64
-    for copy in copies:
-        copy.wait()
     group_at = lax.broadcasted_iota(jnp.int32, (32, 128), 1) // 32
     for q in range(4):
         stacked = gw_ref[4 * q : 4 * q + 4].astype(F32).reshape(128, 288).T
@@ -304,9 +295,8 @@
     sent = call(
         send_kernel,
         [((4, 32, 128), F32)] * 4,
-        [pltpu.VMEM(activations.shape, BF16), pltpu.VMEM((16, 32, 128), F32), pltpu.SemaphoreType.DMA],
+        [pltpu.VMEM((16, 32, 128), F32)],
         activations,
-        in_hbm=True,
         flops=SEND_FLOPS,
     )
     inputs = [
@@ -320,15 +310,12 @@
     mine, other = call(
         local_kernel,
         [((16, 104, 128), F32)] * 2,
-        [pltpu.VMEM(a.shape, a.dtype) for a in inputs]
-        + [
-            pltpu.SemaphoreType.DMA((len(inputs),)),
+        [
             pltpu.VMEM((4, 1152, 128), BF16),
             pltpu.VMEM((32, 16, rows), BF16),
             pltpu.VMEM((1280, 128), F32),
         ],
         *inputs,
-        in_hbm=True,
         flops=LOCAL_FLOPS,
     )
     sent, other = lax.optimization_barrier((sent, other))
@@ -338,7 +325,8 @@
         stack_kernel, [((4, 32, 128), F32)] * 3, [], *got, flops=STACK_FLOPS, after=(total,) if AFTER_CORE else ()
     )
     far = [swap(blocks[z - 1], 0, 2 * z) for z in range(1, 4)]
-    total = total[0:4] + swap(total[4:8], 0, 1) + swap(total[8:12], 2, 0) + swap(total[12:16], 2, 1)
+    by_y, by_both, by_x = swap(total[8:12], 2, 0), swap(total[12:16], 2, 1), swap(total[4:8], 0, 1)
+    total = total[0:4] + by_y + by_both + by_x
     plane_sum = total
     z2, z3 = swap(total[2], 0, 4), swap(total[3], 0, 6)
     (last,) = call(copy_kernel, [((104, 128), F32)], [], total[1], flops=4000000000, after=(total[2], total[3]))

time: 58.1 us -> 56.5 us (0.972)
  waiting for transfers between devices: 16.1 us -> 15.2 us
  Pallas kernels: 6.64 us -> 5.85 us
    ppermute x28, waiting for transfers between devices: 16.1 us -> 15.2 us  [swap(): return lax.ppermute(value, AXES, pairs)]
    pallas_call x9, Pallas kernels: 6.64 us -> 5.85 us  [call(): pl.pallas_call(run, out_shape=[jax.ShapeDtypeStruct(shape, kind) for shap...]
  transfers between devices with their start and end apart: 28 -> 28, of which waited for: 11 -> 10; matrix products, arithmetic and copies ran while one was open for 0% -> 0% of each run, Pallas kernels for 3% -> 3%
where the time goes in v7:
time: 56.5 us; the launch traced here: 56.1 us
  starting transfers between devices  32.1 us (57%)
  waiting for transfers between devices  15.2 us (27%)
  Pallas kernels  5.85 us (10%)
  local copies, waits for them, and re-layouts  1.85 us (3%)
  between operations  0.82 us (1%)
    ppermute x28, starting transfers between devices, swap(): return lax.ppermute(value, AXES, pairs)  32.1 us
    ppermute x28, waiting for transfers between devices, swap(): return lax.ppermute(value, AXES, pairs)  15.2 us
    pallas_call x9, Pallas kernels, call(): pl.pallas_call(run, out_shape=[jax.ShapeDtypeStruct(shape, kind) for shap...  5.85 us
    unnamed x14, local copies, waits for them, and re-layouts  1.79 us
  transfers between devices with their start and end apart: 28, of which 10 were waited for; matrix products, arithmetic and copies ran while one was open for 0% of the time, Pallas kernels for 3%

profile of v7, /device:TPU:0, one launch (start us, length us, event | category | flops | bytes accessed | tf_op | source)
XLA Modules:
  0.0 56.1 jit_solution(16742992583871922366)
XLA Ops:
  0.7 1.0 %copy-done.3 = bf16[2,8,8,512]{3,2,1,0:T(8,128)(2,1)S(1)} copy-done((bf16[2,8,8,512]{3,2,1,0:T(8,128)(2,1)S(1)}, bf16[2,8,8,512]{3,2,1,0:T(8,128)(2,1)}, u32[]{:S(2)}) %copy-start.3) | copy-done | bytes 131096
  1.6 0.1 shard_map.103
  1.8 0.0 copy-start.5
  1.8 0.1 copy-done.2
  1.8 0.7 %copy-done.4 = bf16[2,8,8,512]{3,2,1,0:T(8,128)(2,1)S(1)} copy-done((bf16[2,8,8,512]{3,2,1,0:T(8,128)(2,1)S(1)}, bf16[2,8,8,512]{3,2,1,0:T(8,128)(2,1)}, u32[]{:S(2)}) %copy-start.4) | copy-done | bytes 131096
  2.6 1.4 %shard_map.102 = (f32[16,104,128]{2,1,0:T(8,128)S(1)}, f32[16,104,128]{2,1,0:T(8,128)S(1)}) custom-call(bf16[2,8,8,512]{3,2,1,0:T(8,128)(2,1)S(1)} %copy-done.3, bf16[2,8,8,512]{3,2,1,0:T(8,128)(2,1)S(1)} %copy-done.4, bf16[16,32,288]{2,1,0:T(8,128)(2,1)S(1)} %bitcast.30, bf16[512,512]{1,0:T(8,128)(2,1)S(1)} %copy-done.1, f32[1,512]{1,0:T(1,128)S(1)} %bitcast.31, ...), custom_call_target="tpu_custom_call" | custom-call | flops 4000000000 | tf_op jit(solution)/shard_map/pallas_call | solution.py:40
  4.0 0.5 collective-permute-start
  4.5 2.6 %collective-permute-start.7 = (f32[4,32,128]{2,1,0:T(8,128)S(1)}, f32[4,32,128]{2,1,0:T(8,128)S(1)}, u32[]{:S(2)}, u32[]{:S(2)}) collective-permute-start(f32[4,32,128]{2,1,0:T(8,128)S(1)} %get-tuple-element.39), channel_id=1, source_target_pairs={{0,1},{1,0},{2,3},{3,2},{4,5},{5,4},{6,7},{7,6},{8,9},{9,8},{10,11... | collective-permute-start | bytes 196616 | tf_op jit(solution)/shard_map/ppermute | solution.py:278
  7.1 1.5 %collective-permute-start.8 = (f32[4,32,128]{2,1,0:T(8,128)S(1)}, f32[4,32,128]{2,1,0:T(8,128)S(1)}, u32[]{:S(2)}, u32[]{:S(2)}) collective-permute-start(f32[4,32,128]{2,1,0:T(8,128)S(1)} %get-tuple-element.40), channel_id=1, source_target_pairs={{0,16},{1,17},{2,18},{3,19},{4,20},{5,21},{6,22},{7,23},{8,24},{9,... | collective-permute-start | bytes 196616 | tf_op jit(solution)/shard_map/ppermute | solution.py:278
  8.6 0.0 collective-permute-start.9
  8.6 0.0 collective-permute-done
  8.6 0.1 add.24.refs_4_
  8.8 2.1 %collective-permute-start.1 = (f32[4,104,128]{2,1,0:T(8,128)S(1)}, f32[4,104,128]{2,1,0:T(8,128)S(1)}, u32[]{:S(2)}, u32[]{:S(2)}) collective-permute-start(f32[4,104,128]{2,1,0:T(8,128)S(1)} %get-tuple-element.58), channel_id=1, source_target_pairs={{0,16},{1,17},{2,18},{3,19},{4,20},{5,21},{6,22},{7,23},{8,24},{9,... | collective-permute-start | bytes 638984 | tf_op jit(solution)/shard_map/ppermute | solution.py:278
  10.8 1.5 %collective-permute-start.3 = (f32[4,104,128]{2,1,0:T(8,128)S(1)}, f32[4,104,128]{2,1,0:T(8,128)S(1)}, u32[]{:S(2)}, u32[]{:S(2)}) collective-permute-start(f32[4,104,128]{2,1,0:T(8,128)S(1)} %get-tuple-element.59), channel_id=1, source_target_pairs={{0,1},{1,0},{2,3},{3,2},{4,5},{5,4},{6,7},{7,6},{8,9},{9,8},{10,11... | collective-permute-start | bytes 638984 | tf_op jit(solution)/shard_map/ppermute | solution.py:278
  12.3 0.0 collective-permute-done.7.refs_1_
  12.3 0.2 collective-permute-start.2
  12.5 0.0 collective-permute-done.8.refs_2_
  12.5 2.0 %collective-permute-done.9.refs_3_ = f32[4,32,128]{2,1,0:T(8,128)S(1)} collective-permute-done((f32[4,32,128]{2,1,0:T(8,128)S(1)}, f32[4,32,128]{2,1,0:T(8,128)S(1)}, u32[]{:S(2)}, u32[]{:S(2)}) %collective-permute-start.9) | collective-permute-done | bytes 65568 | tf_op jit(solution)/shard_map/ppermute | solution.py:278
  14.5 1.5 %collective-permute-start.10 = (f32[4,32,128]{2,1,0:T(8,128)S(1)}, f32[4,32,128]{2,1,0:T(8,128)S(1)}, u32[]{:S(2)}, u32[]{:S(2)}) collective-permute-start(f32[4,32,128]{2,1,0:T(8,128)S(1)} %get-tuple-element.42), channel_id=1, source_target_pairs={{0,2},{1,3},{2,0},{3,1},{4,6},{5,7},{6,4},{7,5},{8,10},{9,11},{10,... | collective-permute-start | bytes 196616 | tf_op jit(solution)/shard_map/ppermute | solution.py:278
  16.0 2.6 %collective-permute-start.11 = (f32[4,32,128]{2,1,0:T(8,128)S(1)}, f32[4,32,128]{2,1,0:T(8,128)S(1)}, u32[]{:S(2)}, u32[]{:S(2)}) collective-permute-start(f32[4,32,128]{2,1,0:T(8,128)S(1)} %get-tuple-element.43), channel_id=1, source_target_pairs={{0,4},{1,5},{2,6},{3,7},{4,0},{5,1},{6,2},{7,3},{8,12},{9,13},{10,... | collective-permute-start | bytes 196616 | tf_op jit(solution)/shard_map/ppermute | solution.py:278
  18.6 0.0 collective-permute-done.1
  18.6 2.9 %collective-permute-start.12 = (f32[4,32,128]{2,1,0:T(8,128)S(1)}, f32[4,32,128]{2,1,0:T(8,128)S(1)}, u32[]{:S(2)}, u32[]{:S(2)}) collective-permute-start(f32[4,32,128]{2,1,0:T(8,128)S(1)} %get-tuple-element.44), channel_id=1, source_target_pairs={{0,6},{1,7},{2,4},{3,5},{4,2},{5,3},{6,0},{7,1},{8,14},{9,15},{10,... | collective-permute-start | bytes 196616 | tf_op jit(solution)/shard_map/ppermute | solution.py:278
  21.6 0.0 collective-permute-done.3
  21.6 0.9 %collective-permute-done.2 = f32[4,104,128]{2,1,0:T(8,128)S(1)} collective-permute-done((f32[4,104,128]{2,1,0:T(8,128)S(1)}, f32[4,104,128]{2,1,0:T(8,128)S(1)}, u32[]{:S(2)}, u32[]{:S(2)}) %collective-permute-start.2) | collective-permute-done | bytes 213024 | tf_op jit(solution)/shard_map/ppermute | solution.py:278
  22.5 0.1 fusion.1.refs_7_
  22.6 3.7 %collective-permute-start.6 = (f32[104,128]{1,0:T(8,128)S(1)}, f32[104,128]{1,0:T(8,128)S(1)}, u32[]{:S(2)}, u32[]{:S(2)}) collective-permute-start(f32[104,128]{1,0:T(8,128)S(1)} %get-tuple-element.62.refs_2_), channel_id=1, source_target_pairs={{0,6},{1,7},{2,4},{3,5},{4,2},{5,3},{6,0},{7,1},{8,14},{9,15},{10,... | collective-permute-start | bytes 159752 | tf_op jit(solution)/shard_map/ppermute | solution.py:278
  26.3 0.0 collective-permute-start.5
  26.3 0.0 collective-permute-done.10.refs_4_
  26.3 0.8 %collective-permute-start.4 = (f32[104,128]{1,0:T(8,128)S(1)}, f32[104,128]{1,0:T(8,128)S(1)}, u32[]{:S(2)}, u32[]{:S(2)}) collective-permute-start(f32[104,128]{1,0:T(8,128)S(1)} %shard_map.104), channel_id=1, source_target_pairs={{0,2},{1,3},{2,0},{3,1},{4,6},{5,7},{6,4},{7,5},{8,10},{9,11},{10,... | collective-permute-start | bytes 159752 | tf_op jit(solution)/shard_map/ppermute | solution.py:278
  27.1 0.0 collective-permute-done.11.refs_5_
  27.1 0.0 collective-permute-done.12.refs_6_
  27.1 1.4 %shard_map.106 = (f32[8,32,128]{2,1,0:T(8,128)S(1)}, f32[8,32,128]{2,1,0:T(8,128)S(1)}) custom-call(f32[4,32,128]{2,1,0:T(8,128)S(1)} %get-tuple-element.38.refs_0_, f32[4,32,128]{2,1,0:T(8,128)S(1)} %collective-permute-done.7.refs_1_, f32[4,32,128]{2,1,0:T(8,128)S(1)} %collective-permute-done.8.refs_2_, f32[4,32,128]{2,1,0:T(8,128)S(1)} %collective-permute-done.9.refs_3_, ...), custom_call_target="tpu_custom_call" | custom-call | flops 4000000000 | tf_op jit(solution)/shard_map/pallas_call | solution.py:40
  28.6 0.1 collective-permute-start.13
  28.6 1.8 %collective-permute-done.4 = f32[104,128]{1,0:T(8,128)S(1)} collective-permute-done((f32[104,128]{1,0:T(8,128)S(1)}, f32[104,128]{1,0:T(8,128)S(1)}, u32[]{:S(2)}, u32[]{:S(2)}) %collective-permute-start.4) | collective-permute-done | bytes 53280 | tf_op jit(solution)/shard_map/ppermute | solution.py:278
  30.5 0.0 collective-permute-done.6
  30.5 0.8 %collective-permute-done.5 = f32[104,128]{1,0:T(8,128)S(1)} collective-permute-done((f32[104,128]{1,0:T(8,128)S(1)}, f32[104,128]{1,0:T(8,128)S(1)}, u32[]{:S(2)}, u32[]{:S(2)}) %collective-permute-start.5) | collective-permute-done | bytes 53280 | tf_op jit(solution)/shard_map/ppermute | solution.py:278
  31.3 0.0 collective-permute-done.13
  31.4 0.4 collective-permute-start.18
  31.7 2.5 %collective-permute-start.19 = (f32[168,128]{1,0:T(8,128)S(1)}, f32[168,128]{1,0:T(8,128)S(1)}, u32[]{:S(2)}, u32[]{:S(2)}) collective-permute-start(f32[168,128]{1,0:T(8,128)S(1)} %get-tuple-element.48.refs_3_), channel_id=1, source_target_pairs={{0,4},{1,5},{2,6},{3,7},{4,0},{5,1},{6,2},{7,3},{8,12},{9,13},{10,... | collective-permute-start | bytes 258056 | tf_op jit(solution)/shard_map/ppermute | solution.py:278
  34.3 1.6 %collective-permute-start.20 = (f32[168,128]{1,0:T(8,128)S(1)}, f32[168,128]{1,0:T(8,128)S(1)}, u32[]{:S(2)}, u32[]{:S(2)}) collective-permute-start(f32[168,128]{1,0:T(8,128)S(1)} %get-tuple-element.49.refs_4_), channel_id=1, source_target_pairs={{0,6},{1,7},{2,4},{3,5},{4,2},{5,3},{6,0},{7,1},{8,14},{9,15},{10,... | collective-permute-start | bytes 258056 | tf_op jit(solution)/shard_map/ppermute | solution.py:278
  35.8 1.8 %collective-permute-start.16 = (f32[136,128]{1,0:T(8,128)S(1)}, f32[136,128]{1,0:T(8,128)S(1)}, u32[]{:S(2)}, u32[]{:S(2)}) collective-permute-start(f32[136,128]{1,0:T(8,128)S(1)} %get-tuple-element.51), channel_id=1, source_target_pairs={{0,17},{1,16},{2,19},{3,18},{4,21},{5,20},{6,23},{7,22},{8,25},{9,... | collective-permute-start | bytes 208904 | tf_op jit(solution)/shard_map/ppermute | solution.py:278
  37.6 0.6 %collective-permute-start.14 = (f32[136,128]{1,0:T(8,128)S(1)}, f32[136,128]{1,0:T(8,128)S(1)}, u32[]{:S(2)}, u32[]{:S(2)}) collective-permute-start(f32[136,128]{1,0:T(8,128)S(1)} %get-tuple-element.51), channel_id=1, source_target_pairs={{0,1},{1,0},{2,3},{3,2},{4,5},{5,4},{6,7},{7,6},{8,9},{9,8},{10,11... | collective-permute-start | bytes 208904 | tf_op jit(solution)/shard_map/ppermute | solution.py:278
  38.3 0.0 collective-permute-done.18.refs_0_
  38.3 1.1 %collective-permute-start.15 = (f32[136,128]{1,0:T(8,128)S(1)}, f32[136,128]{1,0:T(8,128)S(1)}, u32[]{:S(2)}, u32[]{:S(2)}) collective-permute-start(f32[136,128]{1,0:T(8,128)S(1)} %get-tuple-element.50.refs_1_), channel_id=1, source_target_pairs={{0,16},{1,17},{2,18},{3,19},{4,20},{5,21},{6,22},{7,23},{8,24},{9,... | collective-permute-start | bytes 208904 | tf_op jit(solution)/shard_map/ppermute | solution.py:278
  39.4 1.9 %collective-permute-done.19.refs_1_ = f32[168,128]{1,0:T(8,128)S(1)} collective-permute-done((f32[168,128]{1,0:T(8,128)S(1)}, f32[168,128]{1,0:T(8,128)S(1)}, u32[]{:S(2)}, u32[]{:S(2)}) %collective-permute-start.19) | collective-permute-done | bytes 86048 | tf_op jit(solution)/shard_map/ppermute | solution.py:278
  41.3 0.0 collective-permute-done.20.refs_2_
  41.3 1.8 %collective-permute-start.23 = (f32[408,128]{1,0:T(8,128)S(1)}, f32[408,128]{1,0:T(8,128)S(1)}, u32[]{:S(2)}, u32[]{:S(2)}) collective-permute-start(f32[408,128]{1,0:T(8,128)S(1)} %get-tuple-element.53), channel_id=1, source_target_pairs={{0,17},{1,16},{2,19},{3,18},{4,21},{5,20},{6,23},{7,22},{8,25},{9,... | collective-permute-start | bytes 626696 | tf_op jit(solution)/shard_map/ppermute | solution.py:278
  43.1 0.7 %collective-permute-start.21 = (f32[408,128]{1,0:T(8,128)S(1)}, f32[408,128]{1,0:T(8,128)S(1)}, u32[]{:S(2)}, u32[]{:S(2)}) collective-permute-start(f32[408,128]{1,0:T(8,128)S(1)} %get-tuple-element.53), channel_id=1, source_target_pairs={{0,1},{1,0},{2,3},{3,2},{4,5},{5,4},{6,7},{7,6},{8,9},{9,8},{10,11... | collective-permute-start | bytes 626696 | tf_op jit(solution)/shard_map/ppermute | solution.py:278
  43.8 0.0 collective-permute-done.16.refs_4_
  43.8 1.1 %collective-permute-start.22 = (f32[408,128]{1,0:T(8,128)S(1)}, f32[408,128]{1,0:T(8,128)S(1)}, u32[]{:S(2)}, u32[]{:S(2)}) collective-permute-start(f32[408,128]{1,0:T(8,128)S(1)} %get-tuple-element.52.refs_6_), channel_id=1, source_target_pairs={{0,16},{1,17},{2,18},{3,19},{4,20},{5,21},{6,22},{7,23},{8,24},{9,... | collective-permute-start | bytes 626696 | tf_op jit(solution)/shard_map/ppermute | solution.py:278
  44.9 0.0 collective-permute-done.14.refs_2_
  44.9 0.1 collective-permute-start.17
  45.0 0.5 collective-permute-start.24
  45.5 4.2 %collective-permute-done.23.refs_9_ = f32[408,128]{1,0:T(8,128)S(1)} collective-permute-done((f32[408,128]{1,0:T(8,128)S(1)}, f32[408,128]{1,0:T(8,128)S(1)}, u32[]{:S(2)}, u32[]{:S(2)}) %collective-permute-start.23) | collective-permute-done | bytes 208928 | tf_op jit(solution)/shard_map/ppermute | solution.py:278
  49.7 0.0 collective-permute-start.27
  49.7 1.6 %collective-permute-done.21.refs_7_ = f32[408,128]{1,0:T(8,128)S(1)} collective-permute-done((f32[408,128]{1,0:T(8,128)S(1)}, f32[408,128]{1,0:T(8,128)S(1)}, u32[]{:S(2)}, u32[]{:S(2)}) %collective-permute-start.21) | collective-permute-done | bytes 208928 | tf_op jit(solution)/shard_map/ppermute | solution.py:278
  51.2 0.0 collective-permute-start.25
  51.2 0.6 %collective-permute-done.22.refs_8_ = f32[408,128]{1,0:T(8,128)S(1)} collective-permute-done((f32[408,128]{1,0:T(8,128)S(1)}, f32[408,128]{1,0:T(8,128)S(1)}, u32[]{:S(2)}, u32[]{:S(2)}) %collective-permute-start.22) | collective-permute-done | bytes 208928 | tf_op jit(solution)/shard_map/ppermute | solution.py:278
  51.8 0.0 collective-permute-done.24.refs_10_
  51.8 0.0 collective-permute-done.17.refs_5_
  51.8 0.0 collective-permute-done.27.refs_13_
  51.8 0.9 %collective-permute-done.25.refs_11_ = f32[408,128]{1,0:T(8,128)S(1)} collective-permute-done((f32[408,128]{1,0:T(8,128)S(1)}, f32[408,128]{1,0:T(8,128)S(1)}, u32[]{:S(2)}, u32[]{:S(2)}) %collective-permute-start.25) | collective-permute-done | bytes 208928 | tf_op jit(solution)/shard_map/ppermute | solution.py:278
  52.7 0.6 %collective-permute-done.26.refs_12_ = f32[408,128]{1,0:T(8,128)S(1)} collective-permute-done((f32[408,128]{1,0:T(8,128)S(1)}, f32[408,128]{1,0:T(8,128)S(1)}, u32[]{:S(2)}, u32[]{:S(2)}) %collective-permute-start.26) | collective-permute-done | bytes 208928 | tf_op jit(solution)/shard_map/ppermute | solution.py:278
  53.2 2.8 %shard_map.110 = (f32[16,32,288]{2,1,0:T(8,128)}, f32[512,512]{1,0:T(8,128)}, f32[16,32,32]{2,1,0:T(8,128)}, f32[12,24,288]{2,1,0:T(8,128)}) custom-call(s32[4,24]{1,0:T(4,128)S(1)} %copy-done, f32[136,128]{1,0:T(8,128)S(1)} %get-tuple-element.50.refs_1_, f32[136,128]{1,0:T(8,128)S(1)} %collective-permute-done.14.refs_2_, ...), custom_call_target="tpu_custom_call" | custom-call | tf_op jit(solution)/shard_map/pallas_call | solution.py:40
  (22 shorter events, 0.2 us)
Async XLA Ops:
  0.6 1.2 %copy-start.1 = (bf16[512,512]{1,0:T(8,128)(2,1)S(1)}, bf16[512,512]{1,0:T(8,128)(2,1)}, u32[]{:S(2)}) copy-start(bf16[512,512]{1,0:T(8,128)(2,1)} %refs_3_.1) | copy-start | bytes 1572868
  0.6 1.2 %copy-start.2 = (bf16[16,288,32]{1,2,0:T(8,128)(2,1)S(1)}, bf16[16,288,32]{1,2,0:T(8,128)(2,1)}, u32[]{:S(2)}) copy-start(bf16[16,288,32]{1,2,0:T(8,128)(2,1)} %param.9) | copy-start | bytes 884740
  0.7 1.0 %copy-start.3 = (bf16[2,8,8,512]{3,2,1,0:T(8,128)(2,1)S(1)}, bf16[2,8,8,512]{3,2,1,0:T(8,128)(2,1)}, u32[]{:S(2)}) copy-start(bf16[2,8,8,512]{3,2,1,0:T(8,128)(2,1)} %refs_0_.4) | copy-start | bytes 393220
  1.6 1.0 %copy-start.4 = (bf16[2,8,8,512]{3,2,1,0:T(8,128)(2,1)S(1)}, bf16[2,8,8,512]{3,2,1,0:T(8,128)(2,1)}, u32[]{:S(2)}) copy-start(bf16[2,8,8,512]{3,2,1,0:T(8,128)(2,1)} %refs_1_.1) | copy-start | bytes 393220
  1.6 1.0 %copy-start.6 = (f32[512]{0:T(512)S(1)}, f32[512]{0:T(512)}, u32[]{:S(2)}) copy-start(f32[512]{0:T(512)} %param.12) | copy-start | bytes 6148
  1.8 0.8 %copy-start.5 = (f32[512]{0:T(512)S(1)}, f32[512]{0:T(512)}, u32[]{:S(2)}) copy-start(f32[512]{0:T(512)} %param.11) | copy-start | bytes 6148
  4.0 4.6 %collective-permute-start = (f32[16,104,128]{2,1,0:T(8,128)S(1)}, f32[16,104,128]{2,1,0:T(8,128)S(1)}, u32[]{:S(2)}, u32[]{:S(2)}) collective-permute-start(f32[16,104,128]{2,1,0:T(8,128)S(1)} %get-tuple-element.37), channel_id=1, source_target_pairs={{0,8},{1,9},{2,10},{3,11},{4,12},{5,13},{6,14},{7,15},{8,0},{9,1},... | collective-permute-start | bytes 2555912 | tf_op jit(solution)/shard_map/ppermute | solution.py:278
  4.5 7.8 %collective-permute-start.7 = (f32[4,32,128]{2,1,0:T(8,128)S(1)}, f32[4,32,128]{2,1,0:T(8,128)S(1)}, u32[]{:S(2)}, u32[]{:S(2)}) collective-permute-start(f32[4,32,128]{2,1,0:T(8,128)S(1)} %get-tuple-element.39), channel_id=1, source_target_pairs={{0,1},{1,0},{2,3},{3,2},{4,5},{5,4},{6,7},{7,6},{8,9},{9,8},{10,11... | collective-permute-start | bytes 196616 | tf_op jit(solution)/shard_map/ppermute | solution.py:278
  7.1 5.4 %collective-permute-start.8 = (f32[4,32,128]{2,1,0:T(8,128)S(1)}, f32[4,32,128]{2,1,0:T(8,128)S(1)}, u32[]{:S(2)}, u32[]{:S(2)}) collective-permute-start(f32[4,32,128]{2,1,0:T(8,128)S(1)} %get-tuple-element.40), channel_id=1, source_target_pairs={{0,16},{1,17},{2,18},{3,19},{4,20},{5,21},{6,22},{7,23},{8,24},{9,... | collective-permute-start | bytes 196616 | tf_op jit(solution)/shard_map/ppermute | solution.py:278
  8.6 5.9 %collective-permute-start.9 = (f32[4,32,128]{2,1,0:T(8,128)S(1)}, f32[4,32,128]{2,1,0:T(8,128)S(1)}, u32[]{:S(2)}, u32[]{:S(2)}) collective-permute-start(f32[4,32,128]{2,1,0:T(8,128)S(1)} %get-tuple-element.41), channel_id=1, source_target_pairs={{0,17},{1,16},{2,19},{3,18},{4,21},{5,20},{6,23},{7,22},{8,25},{9,... | collective-permute-start | bytes 196616 | tf_op jit(solution)/shard_map/ppermute | solution.py:278
  8.8 9.8 %collective-permute-start.1 = (f32[4,104,128]{2,1,0:T(8,128)S(1)}, f32[4,104,128]{2,1,0:T(8,128)S(1)}, u32[]{:S(2)}, u32[]{:S(2)}) collective-permute-start(f32[4,104,128]{2,1,0:T(8,128)S(1)} %get-tuple-element.58), channel_id=1, source_target_pairs={{0,16},{1,17},{2,18},{3,19},{4,20},{5,21},{6,22},{7,23},{8,24},{9,... | collective-permute-start | bytes 638984 | tf_op jit(solution)/shard_map/ppermute | solution.py:278
  10.8 10.7 %collective-permute-start.3 = (f32[4,104,128]{2,1,0:T(8,128)S(1)}, f32[4,104,128]{2,1,0:T(8,128)S(1)}, u32[]{:S(2)}, u32[]{:S(2)}) collective-permute-start(f32[4,104,128]{2,1,0:T(8,128)S(1)} %get-tuple-element.59), channel_id=1, source_target_pairs={{0,1},{1,0},{2,3},{3,2},{4,5},{5,4},{6,7},{7,6},{8,9},{9,8},{10,11... | collective-permute-start | bytes 638984 | tf_op jit(solution)/shard_map/ppermute | solution.py:278
  12.3 10.2 %collective-permute-start.2 = (f32[4,104,128]{2,1,0:T(8,128)S(1)}, f32[4,104,128]{2,1,0:T(8,128)S(1)}, u32[]{:S(2)}, u32[]{:S(2)}) collective-permute-start(f32[4,104,128]{2,1,0:T(8,128)S(1)} %get-tuple-element.60), channel_id=1, source_target_pairs={{0,17},{1,16},{2,19},{3,18},{4,21},{5,20},{6,23},{7,22},{8,25},{9,... | collective-permute-start | bytes 638984 | tf_op jit(solution)/shard_map/ppermute | solution.py:278
  14.5 11.8 %collective-permute-start.10 = (f32[4,32,128]{2,1,0:T(8,128)S(1)}, f32[4,32,128]{2,1,0:T(8,128)S(1)}, u32[]{:S(2)}, u32[]{:S(2)}) collective-permute-start(f32[4,32,128]{2,1,0:T(8,128)S(1)} %get-tuple-element.42), channel_id=1, source_target_pairs={{0,2},{1,3},{2,0},{3,1},{4,6},{5,7},{6,4},{7,5},{8,10},{9,11},{10,... | collective-permute-start | bytes 196616 | tf_op jit(solution)/shard_map/ppermute | solution.py:278
  16.0 11.1 %collective-permute-start.11 = (f32[4,32,128]{2,1,0:T(8,128)S(1)}, f32[4,32,128]{2,1,0:T(8,128)S(1)}, u32[]{:S(2)}, u32[]{:S(2)}) collective-permute-start(f32[4,32,128]{2,1,0:T(8,128)S(1)} %get-tuple-element.43), channel_id=1, source_target_pairs={{0,4},{1,5},{2,6},{3,7},{4,0},{5,1},{6,2},{7,3},{8,12},{9,13},{10,... | collective-permute-start | bytes 196616 | tf_op jit(solution)/shard_map/ppermute | solution.py:278
  18.6 8.5 %collective-permute-start.12 = (f32[4,32,128]{2,1,0:T(8,128)S(1)}, f32[4,32,128]{2,1,0:T(8,128)S(1)}, u32[]{:S(2)}, u32[]{:S(2)}) collective-permute-start(f32[4,32,128]{2,1,0:T(8,128)S(1)} %get-tuple-element.44), channel_id=1, source_target_pairs={{0,6},{1,7},{2,4},{3,5},{4,2},{5,3},{6,0},{7,1},{8,14},{9,15},{10,... | collective-permute-start | bytes 196616 | tf_op jit(solution)/shard_map/ppermute | solution.py:278
  22.6 7.9 %collective-permute-start.6 = (f32[104,128]{1,0:T(8,128)S(1)}, f32[104,128]{1,0:T(8,128)S(1)}, u32[]{:S(2)}, u32[]{:S(2)}) collective-permute-start(f32[104,128]{1,0:T(8,128)S(1)} %get-tuple-element.62.refs_2_), channel_id=1, source_target_pairs={{0,6},{1,7},{2,4},{3,5},{4,2},{5,3},{6,0},{7,1},{8,14},{9,15},{10,... | collective-permute-start | bytes 159752 | tf_op jit(solution)/shard_map/ppermute | solution.py:278
  26.3 5.0 %collective-permute-start.5 = (f32[104,128]{1,0:T(8,128)S(1)}, f32[104,128]{1,0:T(8,128)S(1)}, u32[]{:S(2)}, u32[]{:S(2)}) collective-permute-start(f32[104,128]{1,0:T(8,128)S(1)} %get-tuple-element.63.refs_1_), channel_id=1, source_target_pairs={{0,4},{1,5},{2,6},{3,7},{4,0},{5,1},{6,2},{7,3},{8,12},{9,13},{10,... | collective-permute-start | bytes 159752 | tf_op jit(solution)/shard_map/ppermute | solution.py:278
  26.3 4.2 %collective-permute-start.4 = (f32[104,128]{1,0:T(8,128)S(1)}, f32[104,128]{1,0:T(8,128)S(1)}, u32[]{:S(2)}, u32[]{:S(2)}) collective-permute-start(f32[104,128]{1,0:T(8,128)S(1)} %shard_map.104), channel_id=1, source_target_pairs={{0,2},{1,3},{2,0},{3,1},{4,6},{5,7},{6,4},{7,5},{8,10},{9,11},{10,... | collective-permute-start | bytes 159752 | tf_op jit(solution)/shard_map/ppermute | solution.py:278
  28.6 2.8 %collective-permute-start.13 = (f32[8,32,128]{2,1,0:T(8,128)S(1)}, f32[8,32,128]{2,1,0:T(8,128)S(1)}, u32[]{:S(2)}, u32[]{:S(2)}) collective-permute-start(f32[8,32,128]{2,1,0:T(8,128)S(1)} %get-tuple-element.46), channel_id=1, source_target_pairs={{0,8},{1,9},{2,10},{3,11},{4,12},{5,13},{6,14},{7,15},{8,0},{9,1},... | collective-permute-start | bytes 393224 | tf_op jit(solution)/shard_map/ppermute | solution.py:278
  31.4 6.9 %collective-permute-start.18 = (f32[168,128]{1,0:T(8,128)S(1)}, f32[168,128]{1,0:T(8,128)S(1)}, u32[]{:S(2)}, u32[]{:S(2)}) collective-permute-start(f32[168,128]{1,0:T(8,128)S(1)} %get-tuple-element.47.refs_2_), channel_id=1, source_target_pairs={{0,2},{1,3},{2,0},{3,1},{4,6},{5,7},{6,4},{7,5},{8,10},{9,11},{10,... | collective-permute-start | bytes 258056 | tf_op jit(solution)/shard_map/ppermute | solution.py:278
  31.7 9.5 %collective-permute-start.19 = (f32[168,128]{1,0:T(8,128)S(1)}, f32[168,128]{1,0:T(8,128)S(1)}, u32[]{:S(2)}, u32[]{:S(2)}) collective-permute-start(f32[168,128]{1,0:T(8,128)S(1)} %get-tuple-element.48.refs_3_), channel_id=1, source_target_pairs={{0,4},{1,5},{2,6},{3,7},{4,0},{5,1},{6,2},{7,3},{8,12},{9,13},{10,... | collective-permute-start | bytes 258056 | tf_op jit(solution)/shard_map/ppermute | solution.py:278
  34.3 7.0 %collective-permute-start.20 = (f32[168,128]{1,0:T(8,128)S(1)}, f32[168,128]{1,0:T(8,128)S(1)}, u32[]{:S(2)}, u32[]{:S(2)}) collective-permute-start(f32[168,128]{1,0:T(8,128)S(1)} %get-tuple-element.49.refs_4_), channel_id=1, source_target_pairs={{0,6},{1,7},{2,4},{3,5},{4,2},{5,3},{6,0},{7,1},{8,14},{9,15},{10,... | collective-permute-start | bytes 258056 | tf_op jit(solution)/shard_map/ppermute | solution.py:278
  35.8 7.9 %collective-permute-start.16 = (f32[136,128]{1,0:T(8,128)S(1)}, f32[136,128]{1,0:T(8,128)S(1)}, u32[]{:S(2)}, u32[]{:S(2)}) collective-permute-start(f32[136,128]{1,0:T(8,128)S(1)} %get-tuple-element.51), channel_id=1, source_target_pairs={{0,17},{1,16},{2,19},{3,18},{4,21},{5,20},{6,23},{7,22},{8,25},{9,... | collective-permute-start | bytes 208904 | tf_op jit(solution)/shard_map/ppermute | solution.py:278
  37.6 7.2 %collective-permute-start.14 = (f32[136,128]{1,0:T(8,128)S(1)}, f32[136,128]{1,0:T(8,128)S(1)}, u32[]{:S(2)}, u32[]{:S(2)}) collective-permute-start(f32[136,128]{1,0:T(8,128)S(1)} %get-tuple-element.51), channel_id=1, source_target_pairs={{0,1},{1,0},{2,3},{3,2},{4,5},{5,4},{6,7},{7,6},{8,9},{9,8},{10,11... | collective-permute-start | bytes 208904 | tf_op jit(solution)/shard_map/ppermute | solution.py:278
  38.3 6.6 %collective-permute-start.15 = (f32[136,128]{1,0:T(8,128)S(1)}, f32[136,128]{1,0:T(8,128)S(1)}, u32[]{:S(2)}, u32[]{:S(2)}) collective-permute-start(f32[136,128]{1,0:T(8,128)S(1)} %get-tuple-element.50.refs_1_), channel_id=1, source_target_pairs={{0,16},{1,17},{2,18},{3,19},{4,20},{5,21},{6,22},{7,23},{8,24},{9,... | collective-permute-start | bytes 208904 | tf_op jit(solution)/shard_map/ppermute | solution.py:278
  41.3 8.3 %collective-permute-start.23 = (f32[408,128]{1,0:T(8,128)S(1)}, f32[408,128]{1,0:T(8,128)S(1)}, u32[]{:S(2)}, u32[]{:S(2)}) collective-permute-start(f32[408,128]{1,0:T(8,128)S(1)} %get-tuple-element.53), channel_id=1, source_target_pairs={{0,17},{1,16},{2,19},{3,18},{4,21},{5,20},{6,23},{7,22},{8,25},{9,... | collective-permute-start | bytes 626696 | tf_op jit(solution)/shard_map/ppermute | solution.py:278
  43.1 8.1 %collective-permute-start.21 = (f32[408,128]{1,0:T(8,128)S(1)}, f32[408,128]{1,0:T(8,128)S(1)}, u32[]{:S(2)}, u32[]{:S(2)}) collective-permute-start(f32[408,128]{1,0:T(8,128)S(1)} %get-tuple-element.53), channel_id=1, source_target_pairs={{0,1},{1,0},{2,3},{3,2},{4,5},{5,4},{6,7},{7,6},{8,9},{9,8},{10,11... | collective-permute-start | bytes 626696 | tf_op jit(solution)/shard_map/ppermute | solution.py:278
  43.8 8.0 %collective-permute-start.22 = (f32[408,128]{1,0:T(8,128)S(1)}, f32[408,128]{1,0:T(8,128)S(1)}, u32[]{:S(2)}, u32[]{:S(2)}) collective-permute-start(f32[408,128]{1,0:T(8,128)S(1)} %get-tuple-element.52.refs_6_), channel_id=1, source_target_pairs={{0,16},{1,17},{2,18},{3,19},{4,20},{5,21},{6,22},{7,23},{8,24},{9,... | collective-permute-start | bytes 626696 | tf_op jit(solution)/shard_map/ppermute | solution.py:278
  44.9 8.4 %copy-start = (s32[4,24]{1,0:T(4,128)S(1)}, s32[4,24]{1,0:T(4,128)}, u32[]{:S(2)}) copy-start(s32[4,24]{1,0:T(4,128)} %refs_0_.5) | copy-start | bytes 1156
  44.9 6.9 %collective-permute-start.17 = (f32[4,136,128]{2,1,0:T(8,128)S(1)}, f32[4,136,128]{2,1,0:T(8,128)S(1)}, u32[]{:S(2)}, u32[]{:S(2)}) collective-permute-start(f32[4,136,128]{2,1,0:T(8,128)S(1)} %pad_maximum_fusion), channel_id=1, source_target_pairs={{0,8},{1,9},{2,10},{3,11},{4,12},{5,13},{6,14},{7,15},{8,0},{9,1},... | collective-permute-start | bytes 835592 | tf_op jit(solution)/shard_map/ppermute | solution.py:278
  45.0 6.8 %collective-permute-start.24 = (f32[408,128]{1,0:T(8,128)S(1)}, f32[408,128]{1,0:T(8,128)S(1)}, u32[]{:S(2)}, u32[]{:S(2)}) collective-permute-start(f32[408,128]{1,0:T(8,128)S(1)} %get-tuple-element.52.refs_6_), channel_id=1, source_target_pairs={{0,8},{1,9},{2,10},{3,11},{4,12},{5,13},{6,14},{7,15},{8,0},{9,1},... | collective-permute-start | bytes 626696 | tf_op jit(solution)/shard_map/ppermute | solution.py:278
  49.7 2.1 %collective-permute-start.27 = (f32[408,128]{1,0:T(8,128)S(1)}, f32[408,128]{1,0:T(8,128)S(1)}, u32[]{:S(2)}, u32[]{:S(2)}) collective-permute-start(f32[408,128]{1,0:T(8,128)S(1)} %collective-permute-done.23.refs_9_), channel_id=1, source_target_pairs={{0,8},{1,9},{2,10},{3,11},{4,12},{5,13},{6,14},{7,15},{8,0},{9,1},... | collective-permute-start | bytes 626696 | tf_op jit(solution)/shard_map/ppermute | solution.py:278
  51.2 1.5 %collective-permute-start.25 = (f32[408,128]{1,0:T(8,128)S(1)}, f32[408,128]{1,0:T(8,128)S(1)}, u32[]{:S(2)}, u32[]{:S(2)}) collective-permute-start(f32[408,128]{1,0:T(8,128)S(1)} %collective-permute-done.21.refs_7_), channel_id=1, source_target_pairs={{0,8},{1,9},{2,10},{3,11},{4,12},{5,13},{6,14},{7,15},{8,0},{9,1},... | collective-permute-start | bytes 626696 | tf_op jit(solution)/shard_map/ppermute | solution.py:278
  51.8 1.5 %collective-permute-start.26 = (f32[408,128]{1,0:T(8,128)S(1)}, f32[408,128]{1,0:T(8,128)S(1)}, u32[]{:S(2)}, u32[]{:S(2)}) collective-permute-start(f32[408,128]{1,0:T(8,128)S(1)} %collective-permute-done.22.refs_8_), channel_id=1, source_target_pairs={{0,8},{1,9},{2,10},{3,11},{4,12},{5,13},{6,14},{7,15},{8,0},{9,1},... | collective-permute-start | bytes 626696 | tf_op jit(solution)/shard_map/ppermute | solution.py:278

commit v8 on v7

--- a/solution.py
+++ b/solution.py
@@ -15,6 +15,7 @@
 FACTOR_FLOPS = 4000000000
 FIRST_FLOPS = 4000000000
 AFTER_CORE = AFTER_PLANE = AFTER_LINE = True
+HALF_FLOPS = 1000000000
 SEND_FLOPS = 6000000000
 LOCAL_FLOPS = 4000000000
 VMEM_LIMIT = 48 * 1024 * 1024
@@ -26,7 +27,7 @@
     return pl.BlockSpec(memory_space=pltpu.VMEM)
 
 
-def call(body, outs, scratch, *args, in_hbm=False, flops=0, after=()):
+def call(body, outs, scratch, *args, in_hbm=False, out_hbm=False, flops=0, after=()):
     count = len(args)
 
     def run(*refs):
@@ -41,7 +42,7 @@
         run,
         out_shape=[jax.ShapeDtypeStruct(shape, kind) for shape, kind in outs],
         in_specs=[place(a) for a in args] + [pl.BlockSpec(memory_space=pl.ANY) for _ in after],
-        out_specs=[whole_vmem() for _ in outs],
+        out_specs=[pl.BlockSpec(memory_space=pltpu.HBM) if out_hbm else whole_vmem() for _ in outs],
         scratch_shapes=scratch,
         compiler_params=pltpu.CompilerParams(vmem_limit_bytes=VMEM_LIMIT),
         cost_estimate=pl.CostEstimate(flops=flops, bytes_accessed=0, transcendentals=0) if flops else None,
@@ -226,48 +227,74 @@
         peer_ref[at + 104 : at + size, :] = ref[size:, :]
 
 
-def finish_kernel(grad_scale, mean_scale, slot_ref, *refs):
-    parts, (group_ref, proj_ref, out_ref, owned_ref), (sums, blocks) = refs[:13], refs[13:17], refs[17:]
-    me = cell_id()
-    count = owned_ref.shape[0] // 2
+def unpack(scales, slot_ref, parts, outs, sums, blocks):
+    group_ref, proj_ref, out_ref, owned_ref = outs
+    grad_scale, mean_scale = scales
+    me = cell_id() & 15
+    count = owned_ref.shape[0]
     step = 104 + packed_rows(count)
-    for place in range(8):
+    spots = []
+    for place in range(4):
+        early, late = parts[place], parts[4 + place]
         for z in range(4):
-            j = (4 * place + z) ^ me
-            if z > 0:
-                ref, base = parts[5 + place], step * (z - 1)
-            elif place < 4:
-                ref, base = parts[place], 0
-            else:
-                ref, base = parts[4].at[place - 4], 0
-            for w in range(4):
-                at = pl.multiple_of(16 * j, 16)
-                row = base + 16 * w
-                proj_ref[pl.ds(at, 16), 128 * w : 128 * w + 128] = ref[row : row + 16, :] * grad_scale
-            sums[pl.ds(pl.multiple_of(40 * j, 8), 40), :] = ref[base + 64 : base + 104, :]
-            base += 104
-            tiles = [ref[base + count * t : base + count * t + count, :] for t in range(5)]
-            last = []
-            for i in range(count):
-                spot = base + 5 * count + i // 4
-                last.append(ref[spot : spot + 1, 32 * (i % 4) : 32 * (i % 4) + 32])
-            value = jnp.concatenate(tiles + [jnp.concatenate(last, axis=0)], axis=1) * mean_scale
-            for a in range(3):
-                pieces = []
-                for b in range(3):
-                    at = 96 * PAIRS.index(SAME.get((a, b), (a, b)))
-                    pieces.append(value[:, at : at + 96])
-                blocks[j >> 4, 3 * (j & 15) + a] = jnp.concatenate(pieces, axis=1)
-    for q in range(4):
+            ref, base = (early, 0) if z == 0 else (late, step * (z - 1))
+            spots.append(((4 * place + z) ^ me, ref, base))
+    for j, ref, base in spots:
+        for w in range(4):
+            at = pl.multiple_of(16 * j, 16)
+            row = base + 16 * w
+            proj_ref[pl.ds(at, 16), 128 * w : 128 * w + 128] = ref[row : row + 16, :] * grad_scale
+        sums[pl.ds(pl.multiple_of(40 * j, 8), 40), :] = ref[base + 64 : base + 104, :]
+    for q in range(2):
         group_ref[4 * q : 4 * q + 4] = (sums[320 * q : 320 * q + 288, :].T * grad_scale).reshape(4, 32, 288)
         for g in range(4):
             out_ref[4 * q + g] = sums[320 * q + 288 : 320 * q + 320, 32 * g : 32 * g + 32] * mean_scale
+    for j, ref, base in spots:
+        base += 104
+        tiles = [ref[base + count * t : base + count * t + count, :] for t in range(5)]
+        last = []
+        for i in range(count):
+            spot = base + 5 * count + i // 4
+            last.append(ref[spot : spot + 1, 32 * (i % 4) : 32 * (i % 4) + 32])
+        value = jnp.concatenate(tiles + [jnp.concatenate(last, axis=0)], axis=1) * mean_scale
+        for a in range(3):
+            pieces = []
+            for b in range(3):
+                at = 96 * PAIRS.index(SAME.get((a, b), (a, b)))
+                pieces.append(value[:, at : at + 96])
+            blocks[3 * j + a] = jnp.concatenate(pieces, axis=1)
     owner = lax.axis_index("owner")
     for s in range(owned_ref.shape[1]):
         block = slot_ref[owner, s]
-        for core in range(2):
-            value = blocks[core, jnp.maximum(block, 0)]
-            owned_ref[count * core : count * core + count, s, :] = jnp.where(block >= 0, value, 0.0)
+        value = blocks[jnp.maximum(block, 0)]
+        owned_ref[:, s, :] = jnp.where(block >= 0, value, 0.0)
+
+
+def half_kernel(scales, slot_ref, *refs):
+    parts, outs, (sums, blocks) = refs[:8], refs[8:12], refs[12:]
+    unpack(scales, slot_ref, parts, outs, sums, blocks)
+
+
+def finish_kernel(scales, slot_ref, *refs):
+    mine, (early, *late), outs = refs[:4], refs[4:9], refs[9:13]
+    (sums, blocks, *held), sems = refs[13:19], refs[19]
+    core = lax.axis_index("owner") & 1
+
+    def send(at, source, which):
+        copies = []
+        for i, (src, dst) in enumerate(zip(source, outs)):
+            size = src.shape[0]
+            copies.append(pltpu.make_async_copy(src, dst.at[pl.ds(which * size, size)], sems.at[at + i]))
+        return copies
+
+    copies = send(0, mine, core) + send(4, held, 1 - core)
+    for copy in copies[:4]:
+        copy.start()
+    unpack(scales, slot_ref, [early.at[i] for i in range(4)] + late, held, sums, blocks)
+    for copy in copies[4:]:
+        copy.start()
+    for copy in copies:
+        copy.wait()
 
 
 def per_device(n_owner, n_dp, activations, out_grad, group_weight, proj_weight, bn_gain, bn_shift, slot_block):
@@ -358,14 +385,23 @@
     early = [first, swap(first_peer, 0, 1), swap(first, 2, 0), swap(first_peer, 2, 1)]
     own, peer = call(merge_kernel, [((3 * (104 + packed), 128), F32)] * 2, [], *line)
     late = [own, swap(peer, 0, 1), swap(own, 2, 0), swap(peer, 2, 1)]
-    parts = early + [swap(jnp.stack(early), 1, 0)] + late + [swap(v, 1, 0) for v in late]
     slots = slot_block.shape[1]
+    scales = (grad_scale, mean_scale)
+    outs = [((16, 32, 288), F32), ((512, 512), F32), ((16, 32, 32), F32), ((half, slots, 288), F32)]
+    halves = [((shape[0] // 2, *shape[1:]), kind) for shape, kind in outs]
+    scratch = [pltpu.VMEM((640, 128), F32), pltpu.VMEM((48, half // 2, 288), F32)]
+    crossed = [swap(jnp.stack(early), 1, 0)] + [swap(v, 1, 0) for v in late]
+    mine = call(
+        functools.partial(half_kernel, scales), halves, scratch, slot_block, *early, *late, flops=HALF_FLOPS
+    )
     group_grad, proj_grad, out_factor, factor_owned = call(
-        functools.partial(finish_kernel, grad_scale, mean_scale),
-        [((16, 32, 288), F32), ((512, 512), F32), ((16, 32, 32), F32), ((half, slots, 288), F32)],
-        [pltpu.VMEM((1280, 128), F32), pltpu.VMEM((2, 48, half // 2, 288), F32)],
+        functools.partial(finish_kernel, scales),
+        outs,
+        scratch + [pltpu.VMEM(shape, kind) for shape, kind in halves] + [pltpu.SemaphoreType.DMA((8,))],
         slot_block,
-        *parts,
+        *mine,
+        *crossed,
+        out_hbm=True,
     )
     return group_grad.transpose(0, 2, 1), proj_grad, out_factor, factor_owned.transpose(1, 0, 2)
 

time: 56.5 us -> 56.3 us (level)
  waiting for transfers between devices: 15.2 us -> 14.1 us
  Pallas kernels: 5.85 us -> 6.59 us
    ppermute x28, waiting for transfers between devices: 15.2 us -> 14.1 us  [swap(): return lax.ppermute(value, AXES, pairs)]
    pallas_call x9 -> x10, Pallas kernels: 5.85 us -> 6.59 us  [call(): pl.pallas_call(run, out_shape=[jax.ShapeDtypeStruct(shape, kind) for shap...]
  transfers between devices with their start and end apart: 28 -> 28, of which waited for: 10 -> 9; matrix products, arithmetic and copies ran while one was open for 0% -> 0% of each run, Pallas kernels for 3% -> 5%
where the time goes in v8:
time: 56.3 us; the launch traced here: 55.7 us
  starting transfers between devices  32.1 us (57%)
  waiting for transfers between devices  14.1 us (25%)
  Pallas kernels  6.59 us (12%)
  local copies, waits for them, and re-layouts  1.85 us (3%)
  between operations  0.85 us (2%)
    ppermute x28, starting transfers between devices, swap(): return lax.ppermute(value, AXES, pairs)  32.1 us
    ppermute x28, waiting for transfers between devices, swap(): return lax.ppermute(value, AXES, pairs)  14.1 us
    pallas_call x10, Pallas kernels, call(): pl.pallas_call(run, out_shape=[jax.ShapeDtypeStruct(shape, kind) for shap...  6.59 us
    unnamed x14, local copies, waits for them, and re-layouts  1.79 us
  transfers between devices with their start and end apart: 28, of which 9 were waited for; matrix products, arithmetic and copies ran while one was open for 0% of the time, Pallas kernels for 5%

profile of v8, /device:TPU:0, one launch (start us, length us, event | category | flops | bytes accessed | tf_op | source)
XLA Modules:
  0.0 55.7 jit_solution(10367847172329457375)
XLA Ops:
  0.7 1.0 %copy-done.3 = bf16[2,8,8,512]{3,2,1,0:T(8,128)(2,1)S(1)} copy-done((bf16[2,8,8,512]{3,2,1,0:T(8,128)(2,1)S(1)}, bf16[2,8,8,512]{3,2,1,0:T(8,128)(2,1)}, u32[]{:S(2)}) %copy-start.3) | copy-done | bytes 131096
  1.6 0.1 shard_map.103
  1.8 0.0 copy-start.5
  1.8 0.1 copy-done.2
  1.8 0.7 %copy-done.4 = bf16[2,8,8,512]{3,2,1,0:T(8,128)(2,1)S(1)} copy-done((bf16[2,8,8,512]{3,2,1,0:T(8,128)(2,1)S(1)}, bf16[2,8,8,512]{3,2,1,0:T(8,128)(2,1)}, u32[]{:S(2)}) %copy-start.4) | copy-done | bytes 131096
  2.6 1.4 %shard_map.102 = (f32[16,104,128]{2,1,0:T(8,128)S(1)}, f32[16,104,128]{2,1,0:T(8,128)S(1)}) custom-call(bf16[2,8,8,512]{3,2,1,0:T(8,128)(2,1)S(1)} %copy-done.3, bf16[2,8,8,512]{3,2,1,0:T(8,128)(2,1)S(1)} %copy-done.4, bf16[16,32,288]{2,1,0:T(8,128)(2,1)S(1)} %bitcast.30, bf16[512,512]{1,0:T(8,128)(2,1)S(1)} %copy-done.1, f32[1,512]{1,0:T(1,128)S(1)} %bitcast.31, ...), custom_call_target="tpu_custom_call" | custom-call | flops 4000000000 | tf_op jit(solution)/shard_map/pallas_call | solution.py:41
  4.0 0.5 collective-permute-start
  4.5 2.6 %collective-permute-start.7 = (f32[4,32,128]{2,1,0:T(8,128)S(1)}, f32[4,32,128]{2,1,0:T(8,128)S(1)}, u32[]{:S(2)}, u32[]{:S(2)}) collective-permute-start(f32[4,32,128]{2,1,0:T(8,128)S(1)} %get-tuple-element.43), channel_id=1, source_target_pairs={{0,1},{1,0},{2,3},{3,2},{4,5},{5,4},{6,7},{7,6},{8,9},{9,8},{10,11... | collective-permute-start | bytes 196616 | tf_op jit(solution)/shard_map/ppermute | solution.py:305
  7.1 1.5 %collective-permute-start.8 = (f32[4,32,128]{2,1,0:T(8,128)S(1)}, f32[4,32,128]{2,1,0:T(8,128)S(1)}, u32[]{:S(2)}, u32[]{:S(2)}) collective-permute-start(f32[4,32,128]{2,1,0:T(8,128)S(1)} %get-tuple-element.44), channel_id=1, source_target_pairs={{0,16},{1,17},{2,18},{3,19},{4,20},{5,21},{6,22},{7,23},{8,24},{9,... | collective-permute-start | bytes 196616 | tf_op jit(solution)/shard_map/ppermute | solution.py:305
  8.6 0.0 collective-permute-start.9
  8.6 0.0 collective-permute-done
  8.6 0.1 add.24.refs_4_
  8.8 2.1 %collective-permute-start.1 = (f32[4,104,128]{2,1,0:T(8,128)S(1)}, f32[4,104,128]{2,1,0:T(8,128)S(1)}, u32[]{:S(2)}, u32[]{:S(2)}) collective-permute-start(f32[4,104,128]{2,1,0:T(8,128)S(1)} %get-tuple-element.66), channel_id=1, source_target_pairs={{0,16},{1,17},{2,18},{3,19},{4,20},{5,21},{6,22},{7,23},{8,24},{9,... | collective-permute-start | bytes 638984 | tf_op jit(solution)/shard_map/ppermute | solution.py:305
  10.8 1.5 %collective-permute-start.3 = (f32[4,104,128]{2,1,0:T(8,128)S(1)}, f32[4,104,128]{2,1,0:T(8,128)S(1)}, u32[]{:S(2)}, u32[]{:S(2)}) collective-permute-start(f32[4,104,128]{2,1,0:T(8,128)S(1)} %get-tuple-element.67), channel_id=1, source_target_pairs={{0,1},{1,0},{2,3},{3,2},{4,5},{5,4},{6,7},{7,6},{8,9},{9,8},{10,11... | collective-permute-start | bytes 638984 | tf_op jit(solution)/shard_map/ppermute | solution.py:305
  12.3 0.0 collective-permute-done.7.refs_1_
  12.3 0.2 collective-permute-start.2
  12.5 0.0 collective-permute-done.8.refs_2_
  12.5 2.0 %collective-permute-done.9.refs_3_ = f32[4,32,128]{2,1,0:T(8,128)S(1)} collective-permute-done((f32[4,32,128]{2,1,0:T(8,128)S(1)}, f32[4,32,128]{2,1,0:T(8,128)S(1)}, u32[]{:S(2)}, u32[]{:S(2)}) %collective-permute-start.9) | collective-permute-done | bytes 65568 | tf_op jit(solution)/shard_map/ppermute | solution.py:305
  14.5 1.5 %collective-permute-start.10 = (f32[4,32,128]{2,1,0:T(8,128)S(1)}, f32[4,32,128]{2,1,0:T(8,128)S(1)}, u32[]{:S(2)}, u32[]{:S(2)}) collective-permute-start(f32[4,32,128]{2,1,0:T(8,128)S(1)} %get-tuple-element.46), channel_id=1, source_target_pairs={{0,2},{1,3},{2,0},{3,1},{4,6},{5,7},{6,4},{7,5},{8,10},{9,11},{10,... | collective-permute-start | bytes 196616 | tf_op jit(solution)/shard_map/ppermute | solution.py:305
  16.0 2.6 %collective-permute-start.11 = (f32[4,32,128]{2,1,0:T(8,128)S(1)}, f32[4,32,128]{2,1,0:T(8,128)S(1)}, u32[]{:S(2)}, u32[]{:S(2)}) collective-permute-start(f32[4,32,128]{2,1,0:T(8,128)S(1)} %get-tuple-element.47), channel_id=1, source_target_pairs={{0,4},{1,5},{2,6},{3,7},{4,0},{5,1},{6,2},{7,3},{8,12},{9,13},{10,... | collective-permute-start | bytes 196616 | tf_op jit(solution)/shard_map/ppermute | solution.py:305
  18.6 0.0 collective-permute-done.1
  18.6 2.9 %collective-permute-start.12 = (f32[4,32,128]{2,1,0:T(8,128)S(1)}, f32[4,32,128]{2,1,0:T(8,128)S(1)}, u32[]{:S(2)}, u32[]{:S(2)}) collective-permute-start(f32[4,32,128]{2,1,0:T(8,128)S(1)} %get-tuple-element.48), channel_id=1, source_target_pairs={{0,6},{1,7},{2,4},{3,5},{4,2},{5,3},{6,0},{7,1},{8,14},{9,15},{10,... | collective-permute-start | bytes 196616 | tf_op jit(solution)/shard_map/ppermute | solution.py:305
  21.6 0.0 collective-permute-done.3
  21.6 0.9 %collective-permute-done.2 = f32[4,104,128]{2,1,0:T(8,128)S(1)} collective-permute-done((f32[4,104,128]{2,1,0:T(8,128)S(1)}, f32[4,104,128]{2,1,0:T(8,128)S(1)}, u32[]{:S(2)}, u32[]{:S(2)}) %collective-permute-start.2) | collective-permute-done | bytes 213024 | tf_op jit(solution)/shard_map/ppermute | solution.py:305
  22.5 0.1 fusion.1.refs_7_
  22.6 3.7 %collective-permute-start.6 = (f32[104,128]{1,0:T(8,128)S(1)}, f32[104,128]{1,0:T(8,128)S(1)}, u32[]{:S(2)}, u32[]{:S(2)}) collective-permute-start(f32[104,128]{1,0:T(8,128)S(1)} %get-tuple-element.70.refs_2_), channel_id=1, source_target_pairs={{0,6},{1,7},{2,4},{3,5},{4,2},{5,3},{6,0},{7,1},{8,14},{9,15},{10,... | collective-permute-start | bytes 159752 | tf_op jit(solution)/shard_map/ppermute | solution.py:305
  26.3 0.0 collective-permute-start.5
  26.3 0.0 collective-permute-done.10.refs_4_
  26.3 0.8 %collective-permute-start.4 = (f32[104,128]{1,0:T(8,128)S(1)}, f32[104,128]{1,0:T(8,128)S(1)}, u32[]{:S(2)}, u32[]{:S(2)}) collective-permute-start(f32[104,128]{1,0:T(8,128)S(1)} %shard_map.104), channel_id=1, source_target_pairs={{0,2},{1,3},{2,0},{3,1},{4,6},{5,7},{6,4},{7,5},{8,10},{9,11},{10,... | collective-permute-start | bytes 159752 | tf_op jit(solution)/shard_map/ppermute | solution.py:305
  27.1 0.0 collective-permute-done.11.refs_5_
  27.1 0.0 collective-permute-done.12.refs_6_
  27.1 1.4 %shard_map.106 = (f32[8,32,128]{2,1,0:T(8,128)S(1)}, f32[8,32,128]{2,1,0:T(8,128)S(1)}) custom-call(f32[4,32,128]{2,1,0:T(8,128)S(1)} %get-tuple-element.42.refs_0_, f32[4,32,128]{2,1,0:T(8,128)S(1)} %collective-permute-done.7.refs_1_, f32[4,32,128]{2,1,0:T(8,128)S(1)} %collective-permute-done.8.refs_2_, f32[4,32,128]{2,1,0:T(8,128)S(1)} %collective-permute-done.9.refs_3_, ...), custom_call_target="tpu_custom_call" | custom-call | flops 4000000000 | tf_op jit(solution)/shard_map/pallas_call | solution.py:41
  28.6 0.1 collective-permute-start.13
  28.6 1.8 %collective-permute-done.4 = f32[104,128]{1,0:T(8,128)S(1)} collective-permute-done((f32[104,128]{1,0:T(8,128)S(1)}, f32[104,128]{1,0:T(8,128)S(1)}, u32[]{:S(2)}, u32[]{:S(2)}) %collective-permute-start.4) | collective-permute-done | bytes 53280 | tf_op jit(solution)/shard_map/ppermute | solution.py:305
  30.5 0.0 collective-permute-done.6
  30.5 0.8 %collective-permute-done.5 = f32[104,128]{1,0:T(8,128)S(1)} collective-permute-done((f32[104,128]{1,0:T(8,128)S(1)}, f32[104,128]{1,0:T(8,128)S(1)}, u32[]{:S(2)}, u32[]{:S(2)}) %collective-permute-start.5) | collective-permute-done | bytes 53280 | tf_op jit(solution)/shard_map/ppermute | solution.py:305
  31.3 0.0 collective-permute-done.13
  31.4 0.4 collective-permute-start.17
  31.7 2.5 %collective-permute-start.18 = (f32[168,128]{1,0:T(8,128)S(1)}, f32[168,128]{1,0:T(8,128)S(1)}, u32[]{:S(2)}, u32[]{:S(2)}) collective-permute-start(f32[168,128]{1,0:T(8,128)S(1)} %get-tuple-element.52.refs_3_), channel_id=1, source_target_pairs={{0,4},{1,5},{2,6},{3,7},{4,0},{5,1},{6,2},{7,3},{8,12},{9,13},{10,... | collective-permute-start | bytes 258056 | tf_op jit(solution)/shard_map/ppermute | solution.py:305
  34.3 1.6 %collective-permute-start.19 = (f32[168,128]{1,0:T(8,128)S(1)}, f32[168,128]{1,0:T(8,128)S(1)}, u32[]{:S(2)}, u32[]{:S(2)}) collective-permute-start(f32[168,128]{1,0:T(8,128)S(1)} %get-tuple-element.53.refs_4_), channel_id=1, source_target_pairs={{0,6},{1,7},{2,4},{3,5},{4,2},{5,3},{6,0},{7,1},{8,14},{9,15},{10,... | collective-permute-start | bytes 258056 | tf_op jit(solution)/shard_map/ppermute | solution.py:305
  35.8 1.8 %collective-permute-start.16 = (f32[136,128]{1,0:T(8,128)S(1)}, f32[136,128]{1,0:T(8,128)S(1)}, u32[]{:S(2)}, u32[]{:S(2)}) collective-permute-start(f32[136,128]{1,0:T(8,128)S(1)} %get-tuple-element.55), channel_id=1, source_target_pairs={{0,17},{1,16},{2,19},{3,18},{4,21},{5,20},{6,23},{7,22},{8,25},{9,... | collective-permute-start | bytes 208904 | tf_op jit(solution)/shard_map/ppermute | solution.py:305
  37.6 0.6 %collective-permute-start.14 = (f32[136,128]{1,0:T(8,128)S(1)}, f32[136,128]{1,0:T(8,128)S(1)}, u32[]{:S(2)}, u32[]{:S(2)}) collective-permute-start(f32[136,128]{1,0:T(8,128)S(1)} %get-tuple-element.55), channel_id=1, source_target_pairs={{0,1},{1,0},{2,3},{3,2},{4,5},{5,4},{6,7},{7,6},{8,9},{9,8},{10,11... | collective-permute-start | bytes 208904 | tf_op jit(solution)/shard_map/ppermute | solution.py:305
  38.3 0.0 collective-permute-done.17.refs_0_
  38.3 1.1 %collective-permute-start.15 = (f32[136,128]{1,0:T(8,128)S(1)}, f32[136,128]{1,0:T(8,128)S(1)}, u32[]{:S(2)}, u32[]{:S(2)}) collective-permute-start(f32[136,128]{1,0:T(8,128)S(1)} %get-tuple-element.54.refs_1_), channel_id=1, source_target_pairs={{0,16},{1,17},{2,18},{3,19},{4,20},{5,21},{6,22},{7,23},{8,24},{9,... | collective-permute-start | bytes 208904 | tf_op jit(solution)/shard_map/ppermute | solution.py:305
  39.4 1.9 %collective-permute-done.18.refs_1_ = f32[168,128]{1,0:T(8,128)S(1)} collective-permute-done((f32[168,128]{1,0:T(8,128)S(1)}, f32[168,128]{1,0:T(8,128)S(1)}, u32[]{:S(2)}, u32[]{:S(2)}) %collective-permute-start.18) | collective-permute-done | bytes 86048 | tf_op jit(solution)/shard_map/ppermute | solution.py:305
  41.3 0.0 collective-permute-done.19.refs_2_
  41.3 1.8 %collective-permute-start.22 = (f32[408,128]{1,0:T(8,128)S(1)}, f32[408,128]{1,0:T(8,128)S(1)}, u32[]{:S(2)}, u32[]{:S(2)}) collective-permute-start(f32[408,128]{1,0:T(8,128)S(1)} %get-tuple-element.57), channel_id=1, source_target_pairs={{0,17},{1,16},{2,19},{3,18},{4,21},{5,20},{6,23},{7,22},{8,25},{9,... | collective-permute-start | bytes 626696 | tf_op jit(solution)/shard_map/ppermute | solution.py:305
  43.1 0.7 %collective-permute-start.20 = (f32[408,128]{1,0:T(8,128)S(1)}, f32[408,128]{1,0:T(8,128)S(1)}, u32[]{:S(2)}, u32[]{:S(2)}) collective-permute-start(f32[408,128]{1,0:T(8,128)S(1)} %get-tuple-element.57), channel_id=1, source_target_pairs={{0,1},{1,0},{2,3},{3,2},{4,5},{5,4},{6,7},{7,6},{8,9},{9,8},{10,11... | collective-permute-start | bytes 626696 | tf_op jit(solution)/shard_map/ppermute | solution.py:305
  43.8 0.0 collective-permute-done.16.refs_4_
  43.8 1.1 %collective-permute-start.21 = (f32[408,128]{1,0:T(8,128)S(1)}, f32[408,128]{1,0:T(8,128)S(1)}, u32[]{:S(2)}, u32[]{:S(2)}) collective-permute-start(f32[408,128]{1,0:T(8,128)S(1)} %get-tuple-element.56.refs_5_), channel_id=1, source_target_pairs={{0,16},{1,17},{2,18},{3,19},{4,20},{5,21},{6,22},{7,23},{8,24},{9,... | collective-permute-start | bytes 626696 | tf_op jit(solution)/shard_map/ppermute | solution.py:305
  44.9 0.0 collective-permute-done.14.refs_2_
  44.9 0.0 collective-permute-done.15.refs_3_
  44.9 0.1 collective-permute-start.23
  45.0 0.5 collective-permute-start.24
  45.5 4.2 %collective-permute-done.22.refs_8_ = f32[408,128]{1,0:T(8,128)S(1)} collective-permute-done((f32[408,128]{1,0:T(8,128)S(1)}, f32[408,128]{1,0:T(8,128)S(1)}, u32[]{:S(2)}, u32[]{:S(2)}) %collective-permute-start.22) | collective-permute-done | bytes 208928 | tf_op jit(solution)/shard_map/ppermute | solution.py:305
  49.7 1.6 %collective-permute-done.20.refs_6_ = f32[408,128]{1,0:T(8,128)S(1)} collective-permute-done((f32[408,128]{1,0:T(8,128)S(1)}, f32[408,128]{1,0:T(8,128)S(1)}, u32[]{:S(2)}, u32[]{:S(2)}) %collective-permute-start.20) | collective-permute-done | bytes 208928 | tf_op jit(solution)/shard_map/ppermute | solution.py:305
  51.2 0.6 %collective-permute-done.21.refs_7_ = f32[408,128]{1,0:T(8,128)S(1)} collective-permute-done((f32[408,128]{1,0:T(8,128)S(1)}, f32[408,128]{1,0:T(8,128)S(1)}, u32[]{:S(2)}, u32[]{:S(2)}) %collective-permute-start.21) | collective-permute-done | bytes 208928 | tf_op jit(solution)/shard_map/ppermute | solution.py:305
  51.8 0.0 collective-permute-start.26
  51.8 1.1 %shard_map.110 = (f32[8,32,288]{2,1,0:T(8,128)S(1)}, f32[256,512]{1,0:T(8,128)S(1)}, f32[8,32,32]{2,1,0:T(8,128)S(1)}, f32[6,24,288]{2,1,0:T(8,128)S(1)}) custom-call(s32[4,24]{1,0:T(4,128)S(1)} %copy-done, f32[136,128]{1,0:T(8,128)S(1)} %get-tuple-element.54.refs_1_, f32[136,128]{1,0:T(8,128)S(1)} %collective-permute-done.14.refs_2_, ...), custom_call_target="tpu_custom_call" | custom-call | flops 1000000000 | tf_op jit(solution)/shard_map/pallas_call | solution.py:41
  52.9 0.0 collective-permute-done.24.refs_6_
  52.9 0.0 collective-permute-done.23.refs_5_
  52.9 0.0 collective-permute-done.25.refs_7_
  52.9 0.3 collective-permute-done.26.refs_8_
  53.2 2.5 %shard_map.111 = (f32[16,32,288]{2,1,0:T(8,128)}, f32[512,512]{1,0:T(8,128)}, f32[16,32,32]{2,1,0:T(8,128)}, f32[12,24,288]{2,1,0:T(8,128)}) custom-call(s32[4,24]{1,0:T(4,128)S(1)} %copy-done, f32[8,32,288]{2,1,0:T(8,128)S(1)} %get-tuple-element.58.refs_1_, f32[256,512]{1,0:T(8,128)S(1)} %get-tuple-element.59.refs_2_, ...), custom_call_target="tpu_custom_call" | custom-call | tf_op jit(solution)/shard_map/pallas_call | solution.py:41
  (23 shorter events, 0.2 us)
Async XLA Ops:
  0.6 1.2 %copy-start.1 = (bf16[512,512]{1,0:T(8,128)(2,1)S(1)}, bf16[512,512]{1,0:T(8,128)(2,1)}, u32[]{:S(2)}) copy-start(bf16[512,512]{1,0:T(8,128)(2,1)} %refs_3_.1) | copy-start | bytes 1572868
  0.6 1.2 %copy-start.2 = (bf16[16,288,32]{1,2,0:T(8,128)(2,1)S(1)}, bf16[16,288,32]{1,2,0:T(8,128)(2,1)}, u32[]{:S(2)}) copy-start(bf16[16,288,32]{1,2,0:T(8,128)(2,1)} %param.9) | copy-start | bytes 884740
  0.7 1.0 %copy-start.3 = (bf16[2,8,8,512]{3,2,1,0:T(8,128)(2,1)S(1)}, bf16[2,8,8,512]{3,2,1,0:T(8,128)(2,1)}, u32[]{:S(2)}) copy-start(bf16[2,8,8,512]{3,2,1,0:T(8,128)(2,1)} %refs_0_.5) | copy-start | bytes 393220
  1.6 1.0 %copy-start.4 = (bf16[2,8,8,512]{3,2,1,0:T(8,128)(2,1)S(1)}, bf16[2,8,8,512]{3,2,1,0:T(8,128)(2,1)}, u32[]{:S(2)}) copy-start(bf16[2,8,8,512]{3,2,1,0:T(8,128)(2,1)} %refs_1_.1) | copy-start | bytes 393220
  1.6 1.0 %copy-start.6 = (f32[512]{0:T(512)S(1)}, f32[512]{0:T(512)}, u32[]{:S(2)}) copy-start(f32[512]{0:T(512)} %param.12) | copy-start | bytes 6148
  1.8 0.8 %copy-start.5 = (f32[512]{0:T(512)S(1)}, f32[512]{0:T(512)}, u32[]{:S(2)}) copy-start(f32[512]{0:T(512)} %param.11) | copy-start | bytes 6148
  4.0 4.6 %collective-permute-start = (f32[16,104,128]{2,1,0:T(8,128)S(1)}, f32[16,104,128]{2,1,0:T(8,128)S(1)}, u32[]{:S(2)}, u32[]{:S(2)}) collective-permute-start(f32[16,104,128]{2,1,0:T(8,128)S(1)} %get-tuple-element.41), channel_id=1, source_target_pairs={{0,8},{1,9},{2,10},{3,11},{4,12},{5,13},{6,14},{7,15},{8,0},{9,1},... | collective-permute-start | bytes 2555912 | tf_op jit(solution)/shard_map/ppermute | solution.py:305
  4.5 7.8 %collective-permute-start.7 = (f32[4,32,128]{2,1,0:T(8,128)S(1)}, f32[4,32,128]{2,1,0:T(8,128)S(1)}, u32[]{:S(2)}, u32[]{:S(2)}) collective-permute-start(f32[4,32,128]{2,1,0:T(8,128)S(1)} %get-tuple-element.43), channel_id=1, source_target_pairs={{0,1},{1,0},{2,3},{3,2},{4,5},{5,4},{6,7},{7,6},{8,9},{9,8},{10,11... | collective-permute-start | bytes 196616 | tf_op jit(solution)/shard_map/ppermute | solution.py:305
  7.1 5.4 %collective-permute-start.8 = (f32[4,32,128]{2,1,0:T(8,128)S(1)}, f32[4,32,128]{2,1,0:T(8,128)S(1)}, u32[]{:S(2)}, u32[]{:S(2)}) collective-permute-start(f32[4,32,128]{2,1,0:T(8,128)S(1)} %get-tuple-element.44), channel_id=1, source_target_pairs={{0,16},{1,17},{2,18},{3,19},{4,20},{5,21},{6,22},{7,23},{8,24},{9,... | collective-permute-start | bytes 196616 | tf_op jit(solution)/shard_map/ppermute | solution.py:305
  8.6 5.9 %collective-permute-start.9 = (f32[4,32,128]{2,1,0:T(8,128)S(1)}, f32[4,32,128]{2,1,0:T(8,128)S(1)}, u32[]{:S(2)}, u32[]{:S(2)}) collective-permute-start(f32[4,32,128]{2,1,0:T(8,128)S(1)} %get-tuple-element.45), channel_id=1, source_target_pairs={{0,17},{1,16},{2,19},{3,18},{4,21},{5,20},{6,23},{7,22},{8,25},{9,... | collective-permute-start | bytes 196616 | tf_op jit(solution)/shard_map/ppermute | solution.py:305
  8.8 9.8 %collective-permute-start.1 = (f32[4,104,128]{2,1,0:T(8,128)S(1)}, f32[4,104,128]{2,1,0:T(8,128)S(1)}, u32[]{:S(2)}, u32[]{:S(2)}) collective-permute-start(f32[4,104,128]{2,1,0:T(8,128)S(1)} %get-tuple-element.66), channel_id=1, source_target_pairs={{0,16},{1,17},{2,18},{3,19},{4,20},{5,21},{6,22},{7,23},{8,24},{9,... | collective-permute-start | bytes 638984 | tf_op jit(solution)/shard_map/ppermute | solution.py:305
  10.8 10.7 %collective-permute-start.3 = (f32[4,104,128]{2,1,0:T(8,128)S(1)}, f32[4,104,128]{2,1,0:T(8,128)S(1)}, u32[]{:S(2)}, u32[]{:S(2)}) collective-permute-start(f32[4,104,128]{2,1,0:T(8,128)S(1)} %get-tuple-element.67), channel_id=1, source_target_pairs={{0,1},{1,0},{2,3},{3,2},{4,5},{5,4},{6,7},{7,6},{8,9},{9,8},{10,11... | collective-permute-start | bytes 638984 | tf_op jit(solution)/shard_map/ppermute | solution.py:305
  12.3 10.2 %collective-permute-start.2 = (f32[4,104,128]{2,1,0:T(8,128)S(1)}, f32[4,104,128]{2,1,0:T(8,128)S(1)}, u32[]{:S(2)}, u32[]{:S(2)}) collective-permute-start(f32[4,104,128]{2,1,0:T(8,128)S(1)} %get-tuple-element.68), channel_id=1, source_target_pairs={{0,17},{1,16},{2,19},{3,18},{4,21},{5,20},{6,23},{7,22},{8,25},{9,... | collective-permute-start | bytes 638984 | tf_op jit(solution)/shard_map/ppermute | solution.py:305
  14.5 11.8 %collective-permute-start.10 = (f32[4,32,128]{2,1,0:T(8,128)S(1)}, f32[4,32,128]{2,1,0:T(8,128)S(1)}, u32[]{:S(2)}, u32[]{:S(2)}) collective-permute-start(f32[4,32,128]{2,1,0:T(8,128)S(1)} %get-tuple-element.46), channel_id=1, source_target_pairs={{0,2},{1,3},{2,0},{3,1},{4,6},{5,7},{6,4},{7,5},{8,10},{9,11},{10,... | collective-permute-start | bytes 196616 | tf_op jit(solution)/shard_map/ppermute | solution.py:305
  16.0 11.1 %collective-permute-start.11 = (f32[4,32,128]{2,1,0:T(8,128)S(1)}, f32[4,32,128]{2,1,0:T(8,128)S(1)}, u32[]{:S(2)}, u32[]{:S(2)}) collective-permute-start(f32[4,32,128]{2,1,0:T(8,128)S(1)} %get-tuple-element.47), channel_id=1, source_target_pairs={{0,4},{1,5},{2,6},{3,7},{4,0},{5,1},{6,2},{7,3},{8,12},{9,13},{10,... | collective-permute-start | bytes 196616 | tf_op jit(solution)/shard_map/ppermute | solution.py:305
  18.6 8.5 %collective-permute-start.12 = (f32[4,32,128]{2,1,0:T(8,128)S(1)}, f32[4,32,128]{2,1,0:T(8,128)S(1)}, u32[]{:S(2)}, u32[]{:S(2)}) collective-permute-start(f32[4,32,128]{2,1,0:T(8,128)S(1)} %get-tuple-element.48), channel_id=1, source_target_pairs={{0,6},{1,7},{2,4},{3,5},{4,2},{5,3},{6,0},{7,1},{8,14},{9,15},{10,... | collective-permute-start | bytes 196616 | tf_op jit(solution)/shard_map/ppermute | solution.py:305
  22.6 7.9 %collective-permute-start.6 = (f32[104,128]{1,0:T(8,128)S(1)}, f32[104,128]{1,0:T(8,128)S(1)}, u32[]{:S(2)}, u32[]{:S(2)}) collective-permute-start(f32[104,128]{1,0:T(8,128)S(1)} %get-tuple-element.70.refs_2_), channel_id=1, source_target_pairs={{0,6},{1,7},{2,4},{3,5},{4,2},{5,3},{6,0},{7,1},{8,14},{9,15},{10,... | collective-permute-start | bytes 159752 | tf_op jit(solution)/shard_map/ppermute | solution.py:305
  26.3 5.0 %collective-permute-start.5 = (f32[104,128]{1,0:T(8,128)S(1)}, f32[104,128]{1,0:T(8,128)S(1)}, u32[]{:S(2)}, u32[]{:S(2)}) collective-permute-start(f32[104,128]{1,0:T(8,128)S(1)} %get-tuple-element.71.refs_1_), channel_id=1, source_target_pairs={{0,4},{1,5},{2,6},{3,7},{4,0},{5,1},{6,2},{7,3},{8,12},{9,13},{10,... | collective-permute-start | bytes 159752 | tf_op jit(solution)/shard_map/ppermute | solution.py:305
  26.3 4.2 %collective-permute-start.4 = (f32[104,128]{1,0:T(8,128)S(1)}, f32[104,128]{1,0:T(8,128)S(1)}, u32[]{:S(2)}, u32[]{:S(2)}) collective-permute-start(f32[104,128]{1,0:T(8,128)S(1)} %shard_map.104), channel_id=1, source_target_pairs={{0,2},{1,3},{2,0},{3,1},{4,6},{5,7},{6,4},{7,5},{8,10},{9,11},{10,... | collective-permute-start | bytes 159752 | tf_op jit(solution)/shard_map/ppermute | solution.py:305
  28.6 2.8 %collective-permute-start.13 = (f32[8,32,128]{2,1,0:T(8,128)S(1)}, f32[8,32,128]{2,1,0:T(8,128)S(1)}, u32[]{:S(2)}, u32[]{:S(2)}) collective-permute-start(f32[8,32,128]{2,1,0:T(8,128)S(1)} %get-tuple-element.50), channel_id=1, source_target_pairs={{0,8},{1,9},{2,10},{3,11},{4,12},{5,13},{6,14},{7,15},{8,0},{9,1},... | collective-permute-start | bytes 393224 | tf_op jit(solution)/shard_map/ppermute | solution.py:305
  31.4 6.9 %collective-permute-start.17 = (f32[168,128]{1,0:T(8,128)S(1)}, f32[168,128]{1,0:T(8,128)S(1)}, u32[]{:S(2)}, u32[]{:S(2)}) collective-permute-start(f32[168,128]{1,0:T(8,128)S(1)} %get-tuple-element.51.refs_2_), channel_id=1, source_target_pairs={{0,2},{1,3},{2,0},{3,1},{4,6},{5,7},{6,4},{7,5},{8,10},{9,11},{10,... | collective-permute-start | bytes 258056 | tf_op jit(solution)/shard_map/ppermute | solution.py:305
  31.7 9.5 %collective-permute-start.18 = (f32[168,128]{1,0:T(8,128)S(1)}, f32[168,128]{1,0:T(8,128)S(1)}, u32[]{:S(2)}, u32[]{:S(2)}) collective-permute-start(f32[168,128]{1,0:T(8,128)S(1)} %get-tuple-element.52.refs_3_), channel_id=1, source_target_pairs={{0,4},{1,5},{2,6},{3,7},{4,0},{5,1},{6,2},{7,3},{8,12},{9,13},{10,... | collective-permute-start | bytes 258056 | tf_op jit(solution)/shard_map/ppermute | solution.py:305
  34.3 7.0 %collective-permute-start.19 = (f32[168,128]{1,0:T(8,128)S(1)}, f32[168,128]{1,0:T(8,128)S(1)}, u32[]{:S(2)}, u32[]{:S(2)}) collective-permute-start(f32[168,128]{1,0:T(8,128)S(1)} %get-tuple-element.53.refs_4_), channel_id=1, source_target_pairs={{0,6},{1,7},{2,4},{3,5},{4,2},{5,3},{6,0},{7,1},{8,14},{9,15},{10,... | collective-permute-start | bytes 258056 | tf_op jit(solution)/shard_map/ppermute | solution.py:305
  35.8 7.9 %collective-permute-start.16 = (f32[136,128]{1,0:T(8,128)S(1)}, f32[136,128]{1,0:T(8,128)S(1)}, u32[]{:S(2)}, u32[]{:S(2)}) collective-permute-start(f32[136,128]{1,0:T(8,128)S(1)} %get-tuple-element.55), channel_id=1, source_target_pairs={{0,17},{1,16},{2,19},{3,18},{4,21},{5,20},{6,23},{7,22},{8,25},{9,... | collective-permute-start | bytes 208904 | tf_op jit(solution)/shard_map/ppermute | solution.py:305
  37.6 7.2 %collective-permute-start.14 = (f32[136,128]{1,0:T(8,128)S(1)}, f32[136,128]{1,0:T(8,128)S(1)}, u32[]{:S(2)}, u32[]{:S(2)}) collective-permute-start(f32[136,128]{1,0:T(8,128)S(1)} %get-tuple-element.55), channel_id=1, source_target_pairs={{0,1},{1,0},{2,3},{3,2},{4,5},{5,4},{6,7},{7,6},{8,9},{9,8},{10,11... | collective-permute-start | bytes 208904 | tf_op jit(solution)/shard_map/ppermute | solution.py:305
  38.3 6.6 %collective-permute-start.15 = (f32[136,128]{1,0:T(8,128)S(1)}, f32[136,128]{1,0:T(8,128)S(1)}, u32[]{:S(2)}, u32[]{:S(2)}) collective-permute-start(f32[136,128]{1,0:T(8,128)S(1)} %get-tuple-element.54.refs_1_), channel_id=1, source_target_pairs={{0,16},{1,17},{2,18},{3,19},{4,20},{5,21},{6,22},{7,23},{8,24},{9,... | collective-permute-start | bytes 208904 | tf_op jit(solution)/shard_map/ppermute | solution.py:305
  41.3 8.3 %collective-permute-start.22 = (f32[408,128]{1,0:T(8,128)S(1)}, f32[408,128]{1,0:T(8,128)S(1)}, u32[]{:S(2)}, u32[]{:S(2)}) collective-permute-start(f32[408,128]{1,0:T(8,128)S(1)} %get-tuple-element.57), channel_id=1, source_target_pairs={{0,17},{1,16},{2,19},{3,18},{4,21},{5,20},{6,23},{7,22},{8,25},{9,... | collective-permute-start | bytes 626696 | tf_op jit(solution)/shard_map/ppermute | solution.py:305
  43.1 8.1 %collective-permute-start.20 = (f32[408,128]{1,0:T(8,128)S(1)}, f32[408,128]{1,0:T(8,128)S(1)}, u32[]{:S(2)}, u32[]{:S(2)}) collective-permute-start(f32[408,128]{1,0:T(8,128)S(1)} %get-tuple-element.57), channel_id=1, source_target_pairs={{0,1},{1,0},{2,3},{3,2},{4,5},{5,4},{6,7},{7,6},{8,9},{9,8},{10,11... | collective-permute-start | bytes 626696 | tf_op jit(solution)/shard_map/ppermute | solution.py:305
  43.8 8.0 %collective-permute-start.21 = (f32[408,128]{1,0:T(8,128)S(1)}, f32[408,128]{1,0:T(8,128)S(1)}, u32[]{:S(2)}, u32[]{:S(2)}) collective-permute-start(f32[408,128]{1,0:T(8,128)S(1)} %get-tuple-element.56.refs_5_), channel_id=1, source_target_pairs={{0,16},{1,17},{2,18},{3,19},{4,20},{5,21},{6,22},{7,23},{8,24},{9,... | collective-permute-start | bytes 626696 | tf_op jit(solution)/shard_map/ppermute | solution.py:305
  44.9 6.9 %copy-start = (s32[4,24]{1,0:T(4,128)S(1)}, s32[4,24]{1,0:T(4,128)}, u32[]{:S(2)}) copy-start(s32[4,24]{1,0:T(4,128)} %refs_0_.7) | copy-start | bytes 1156
  44.9 8.0 %collective-permute-start.23 = (f32[4,136,128]{2,1,0:T(8,128)S(1)}, f32[4,136,128]{2,1,0:T(8,128)S(1)}, u32[]{:S(2)}, u32[]{:S(2)}) collective-permute-start(f32[4,136,128]{2,1,0:T(8,128)S(1)} %pad_maximum_fusion), channel_id=1, source_target_pairs={{0,8},{1,9},{2,10},{3,11},{4,12},{5,13},{6,14},{7,15},{8,0},{9,1},... | collective-permute-start | bytes 835592 | tf_op jit(solution)/shard_map/ppermute | solution.py:305
  45.0 7.9 %collective-permute-start.24 = (f32[408,128]{1,0:T(8,128)S(1)}, f32[408,128]{1,0:T(8,128)S(1)}, u32[]{:S(2)}, u32[]{:S(2)}) collective-permute-start(f32[408,128]{1,0:T(8,128)S(1)} %get-tuple-element.56.refs_5_), channel_id=1, source_target_pairs={{0,8},{1,9},{2,10},{3,11},{4,12},{5,13},{6,14},{7,15},{8,0},{9,1},... | collective-permute-start | bytes 626696 | tf_op jit(solution)/shard_map/ppermute | solution.py:305
  49.7 3.3 %collective-permute-start.27 = (f32[408,128]{1,0:T(8,128)S(1)}, f32[408,128]{1,0:T(8,128)S(1)}, u32[]{:S(2)}, u32[]{:S(2)}) collective-permute-start(f32[408,128]{1,0:T(8,128)S(1)} %collective-permute-done.22.refs_8_), channel_id=1, source_target_pairs={{0,8},{1,9},{2,10},{3,11},{4,12},{5,13},{6,14},{7,15},{8,0},{9,1},... | collective-permute-start | bytes 626696 | tf_op jit(solution)/shard_map/ppermute | solution.py:305
  51.2 1.7 %collective-permute-start.25 = (f32[408,128]{1,0:T(8,128)S(1)}, f32[408,128]{1,0:T(8,128)S(1)}, u32[]{:S(2)}, u32[]{:S(2)}) collective-permute-start(f32[408,128]{1,0:T(8,128)S(1)} %collective-permute-done.20.refs_6_), channel_id=1, source_target_pairs={{0,8},{1,9},{2,10},{3,11},{4,12},{5,13},{6,14},{7,15},{8,0},{9,1},... | collective-permute-start | bytes 626696 | tf_op jit(solution)/shard_map/ppermute | solution.py:305
  51.8 1.5 %collective-permute-start.26 = (f32[408,128]{1,0:T(8,128)S(1)}, f32[408,128]{1,0:T(8,128)S(1)}, u32[]{:S(2)}, u32[]{:S(2)}) collective-permute-start(f32[408,128]{1,0:T(8,128)S(1)} %collective-permute-done.21.refs_7_), channel_id=1, source_target_pairs={{0,8},{1,9},{2,10},{3,11},{4,12},{5,13},{6,14},{7,15},{8,0},{9,1},... | collective-permute-start | bytes 626696 | tf_op jit(solution)/shard_map/ppermute | solution.py:305

commit v9 on v8

--- a/solution.py
+++ b/solution.py
@@ -56,16 +56,6 @@
 
 def cell_id():
     return plane_id() * 4 + ((lax.axis_index("dp") >> 1) & 3)
-
-
-def send_kernel(x_ref, *refs):
-    out_refs, held = refs[:4], refs[4]
-    me = cell_id()
-    x_t = x_ref[...].astype(F32).reshape(128, 512).T
-    for group in range(16):
-        held[group ^ (me & 15)] = x_t[32 * group : 32 * group + 32]
-    for place, out in enumerate(out_refs):
-        out[...] = held[4 * place : 4 * place + 4]
 
 
 def shift_rows(value, row_step, col_step):
@@ -84,6 +74,21 @@
     return value
 
 
+def send_kernel(x_ref, *refs):
+    out_refs, (moved_ref, turned_ref, held) = refs[:4], refs[4:]
+    me = cell_id()
+    x = x_ref[...].astype(F32)
+    x_t = x.reshape(128, 512).T
+    turned_ref[...] = x_t.astype(BF16)
+    for a in range(3):
+        for b in range(3):
+            moved_ref[3 * a + b] = shift_rows(x, a - 1, b - 1).reshape(128, 512).astype(BF16)
+    for group in range(16):
+        held[group ^ (me & 15)] = x_t[32 * group : 32 * group + 32]
+    for place, out in enumerate(out_refs):
+        out[...] = held[4 * place : 4 * place + 4]
+
+
 def diagonal(square):
     lane = lax.broadcasted_iota(jnp.int32, (32, 128), 1)
     out = square[96:128]
@@ -93,10 +98,10 @@
 
 
 def local_kernel(*refs):
-    held, (mine_ref, other_ref), (block_w, hid_t, sums) = refs[:6], refs[6:8], refs[8:]
-    x_ref, og_ref, gw_ref, pw_ref, gain_ref, shift_ref = held
+    held, (mine_ref, other_ref), (block_w, hid_t, sums) = refs[:7], refs[7:9], refs[9:]
+    moved_ref, turned_ref, og_ref, gw_ref, pw_ref, gain_ref, shift_ref = held
     me = cell_id()
-    images = x_ref.shape[0]
+    images = og_ref.shape[0]
     rows = images * 64
     group_at = lax.broadcasted_iota(jnp.int32, (32, 128), 1) // 32
     for q in range(4):
@@ -105,13 +110,9 @@
             for g in range(4):
                 at = s * 128 + 32 * g
                 block_w[q, at : at + 32, :] = jnp.where(group_at == g, stacked[32 * s : 32 * s + 32], 0.0).astype(BF16)
-    x = x_ref[...].astype(F32)
-    moved = [
-        shift_rows(x, a - 1, b - 1).reshape(rows, 512).astype(BF16) for a in range(3) for b in range(3)
-    ]
     conv = []
     for q in range(4):
-        lhs = jnp.concatenate([m[:, 128 * q : 128 * q + 128] for m in moved], axis=1)
+        lhs = jnp.concatenate([moved_ref[s, :, 128 * q : 128 * q + 128] for s in range(9)], axis=1)
         conv.append(jnp.dot(lhs, block_w[q], preferred_element_type=F32))
     conv = jnp.concatenate(conv, axis=1)
     gain = gain_ref[...]
@@ -129,7 +130,6 @@
         for k in range(16):
             for w in range(4):
                 out[k, 16 * w : 16 * w + 16, :] = part[16 * k : 16 * k + 16, 128 * w : 128 * w + 128]
-    x_t = x.reshape(rows, 512).T.astype(BF16)
     g_t = grad.reshape(rows, 512).T.astype(BF16)
     grad4 = grad.reshape(images, 8, 8, 512)
     back_moved = [
@@ -138,7 +138,7 @@
     for q in range(4):
         cut = slice(128 * q, 128 * q + 128)
         rhs = jnp.concatenate([m[:, cut] for m in back_moved], axis=1)
-        part = jnp.dot(x_t[cut], rhs, preferred_element_type=F32)
+        part = jnp.dot(turned_ref[cut, :], rhs, preferred_element_type=F32)
         for s in range(9):
             at = 320 * q + 32 * s
             sums[at : at + 32, :] = diagonal(part[:, 128 * s : 128 * s + 128])
@@ -319,15 +319,16 @@
     grad_scale = 1.0 / math.sqrt(total_rows)
     mean_scale = 1.0 / total_rows
 
-    sent = call(
+    *sent, moved, turned = call(
         send_kernel,
-        [((4, 32, 128), F32)] * 4,
+        [((4, 32, 128), F32)] * 4 + [((9, rows, 512), BF16), ((512, rows), BF16)],
         [pltpu.VMEM((16, 32, 128), F32)],
         activations,
         flops=SEND_FLOPS,
     )
     inputs = [
-        activations,
+        moved,
+        turned,
         out_grad,
         group_weight.transpose(0, 2, 1),
         proj_weight,

time: 56.3 us -> 56.3 us (level)
  no operation moved by 1% of the time
where the time goes in v9:
time: 56.3 us; the launch traced here: 55.7 us
  starting transfers between devices  32.1 us (57%)
  waiting for transfers between devices  14.1 us (25%)
  Pallas kernels  6.63 us (12%)
  local copies, waits for them, and re-layouts  1.82 us (3%)
  between operations  0.84 us (1%)
    ppermute x28, starting transfers between devices, swap(): return lax.ppermute(value, AXES, pairs)  32.1 us
    ppermute x28, waiting for transfers between devices, swap(): return lax.ppermute(value, AXES, pairs)  14.1 us
    pallas_call x10, Pallas kernels, call(): pl.pallas_call(run, out_shape=[jax.ShapeDtypeStruct(shape, kind) for shap...  6.63 us
    unnamed x14, local copies, waits for them, and re-layouts  1.76 us
  transfers between devices with their start and end apart: 28, of which 9 were waited for; matrix products, arithmetic and copies ran while one was open for 0% of the time, Pallas kernels for 5%

profile of v9, /device:TPU:0, one launch (start us, length us, event | category | flops | bytes accessed | tf_op | source)
XLA Modules:
  0.0 55.7 jit_solution(5615385953392163191)
XLA Ops:
  0.7 1.0 %copy-done.3 = bf16[2,8,8,512]{3,2,1,0:T(8,128)(2,1)S(1)} copy-done((bf16[2,8,8,512]{3,2,1,0:T(8,128)(2,1)S(1)}, bf16[2,8,8,512]{3,2,1,0:T(8,128)(2,1)}, u32[]{:S(2)}) %copy-start.3) | copy-done | bytes 131096
  1.6 0.2 shard_map.102
  1.8 0.0 copy-done.2
  1.9 0.7 %copy-done.4 = bf16[2,8,8,512]{3,2,1,0:T(8,128)(2,1)S(1)} copy-done((bf16[2,8,8,512]{3,2,1,0:T(8,128)(2,1)S(1)}, bf16[2,8,8,512]{3,2,1,0:T(8,128)(2,1)}, u32[]{:S(2)}) %copy-start.4) | copy-done | bytes 131096
  2.6 1.4 %shard_map.103 = (f32[16,104,128]{2,1,0:T(8,128)S(1)}, f32[16,104,128]{2,1,0:T(8,128)S(1)}) custom-call(bf16[9,128,512]{2,1,0:T(8,128)(2,1)S(1)} %get-tuple-element.37.refs_0_, bf16[512,128]{1,0:T(8,128)(2,1)S(1)} %get-tuple-element.38.refs_1_, bf16[2,8,8,512]{3,2,1,0:T(8,128)(2,1)S(1)} %copy-done.4, bf16[16,32,288]{2,1,0:T(8,128)(2,1)S(1)} %bitcast.30, ...), custom_call_target="tpu_custom_call" | custom-call | flops 4000000000 | tf_op jit(solution)/shard_map/pallas_call | solution.py:41
  4.0 0.5 collective-permute-start
  4.5 2.6 %collective-permute-start.7 = (f32[4,32,128]{2,1,0:T(8,128)S(1)}, f32[4,32,128]{2,1,0:T(8,128)S(1)}, u32[]{:S(2)}, u32[]{:S(2)}) collective-permute-start(f32[4,32,128]{2,1,0:T(8,128)S(1)} %get-tuple-element.47), channel_id=1, source_target_pairs={{0,1},{1,0},{2,3},{3,2},{4,5},{5,4},{6,7},{7,6},{8,9},{9,8},{10,11... | collective-permute-start | bytes 196616 | tf_op jit(solution)/shard_map/ppermute | solution.py:305
  7.1 1.5 %collective-permute-start.8 = (f32[4,32,128]{2,1,0:T(8,128)S(1)}, f32[4,32,128]{2,1,0:T(8,128)S(1)}, u32[]{:S(2)}, u32[]{:S(2)}) collective-permute-start(f32[4,32,128]{2,1,0:T(8,128)S(1)} %get-tuple-element.48), channel_id=1, source_target_pairs={{0,16},{1,17},{2,18},{3,19},{4,20},{5,21},{6,22},{7,23},{8,24},{9,... | collective-permute-start | bytes 196616 | tf_op jit(solution)/shard_map/ppermute | solution.py:305
  8.6 0.0 collective-permute-start.9
  8.6 0.0 collective-permute-done
  8.6 0.1 add.24.refs_4_
  8.8 2.0 %collective-permute-start.1 = (f32[4,104,128]{2,1,0:T(8,128)S(1)}, f32[4,104,128]{2,1,0:T(8,128)S(1)}, u32[]{:S(2)}, u32[]{:S(2)}) collective-permute-start(f32[4,104,128]{2,1,0:T(8,128)S(1)} %get-tuple-element.70), channel_id=1, source_target_pairs={{0,16},{1,17},{2,18},{3,19},{4,20},{5,21},{6,22},{7,23},{8,24},{9,... | collective-permute-start | bytes 638984 | tf_op jit(solution)/shard_map/ppermute | solution.py:305
  10.8 1.5 %collective-permute-start.3 = (f32[4,104,128]{2,1,0:T(8,128)S(1)}, f32[4,104,128]{2,1,0:T(8,128)S(1)}, u32[]{:S(2)}, u32[]{:S(2)}) collective-permute-start(f32[4,104,128]{2,1,0:T(8,128)S(1)} %get-tuple-element.71), channel_id=1, source_target_pairs={{0,1},{1,0},{2,3},{3,2},{4,5},{5,4},{6,7},{7,6},{8,9},{9,8},{10,11... | collective-permute-start | bytes 638984 | tf_op jit(solution)/shard_map/ppermute | solution.py:305
  12.3 0.0 collective-permute-done.7.refs_1_
  12.3 0.2 collective-permute-start.2
  12.5 0.0 collective-permute-done.8.refs_2_
  12.5 2.0 %collective-permute-done.9.refs_3_ = f32[4,32,128]{2,1,0:T(8,128)S(1)} collective-permute-done((f32[4,32,128]{2,1,0:T(8,128)S(1)}, f32[4,32,128]{2,1,0:T(8,128)S(1)}, u32[]{:S(2)}, u32[]{:S(2)}) %collective-permute-start.9) | collective-permute-done | bytes 65568 | tf_op jit(solution)/shard_map/ppermute | solution.py:305
  14.5 1.6 %collective-permute-start.10 = (f32[4,32,128]{2,1,0:T(8,128)S(1)}, f32[4,32,128]{2,1,0:T(8,128)S(1)}, u32[]{:S(2)}, u32[]{:S(2)}) collective-permute-start(f32[4,32,128]{2,1,0:T(8,128)S(1)} %get-tuple-element.50), channel_id=1, source_target_pairs={{0,2},{1,3},{2,0},{3,1},{4,6},{5,7},{6,4},{7,5},{8,10},{9,11},{10,... | collective-permute-start | bytes 196616 | tf_op jit(solution)/shard_map/ppermute | solution.py:305
  16.0 2.6 %collective-permute-start.11 = (f32[4,32,128]{2,1,0:T(8,128)S(1)}, f32[4,32,128]{2,1,0:T(8,128)S(1)}, u32[]{:S(2)}, u32[]{:S(2)}) collective-permute-start(f32[4,32,128]{2,1,0:T(8,128)S(1)} %get-tuple-element.51), channel_id=1, source_target_pairs={{0,4},{1,5},{2,6},{3,7},{4,0},{5,1},{6,2},{7,3},{8,12},{9,13},{10,... | collective-permute-start | bytes 196616 | tf_op jit(solution)/shard_map/ppermute | solution.py:305
  18.6 0.0 collective-permute-done.1
  18.6 2.9 %collective-permute-start.12 = (f32[4,32,128]{2,1,0:T(8,128)S(1)}, f32[4,32,128]{2,1,0:T(8,128)S(1)}, u32[]{:S(2)}, u32[]{:S(2)}) collective-permute-start(f32[4,32,128]{2,1,0:T(8,128)S(1)} %get-tuple-element.52), channel_id=1, source_target_pairs={{0,6},{1,7},{2,4},{3,5},{4,2},{5,3},{6,0},{7,1},{8,14},{9,15},{10,... | collective-permute-start | bytes 196616 | tf_op jit(solution)/shard_map/ppermute | solution.py:305
  21.6 0.0 collective-permute-done.3
  21.6 0.9 %collective-permute-done.2 = f32[4,104,128]{2,1,0:T(8,128)S(1)} collective-permute-done((f32[4,104,128]{2,1,0:T(8,128)S(1)}, f32[4,104,128]{2,1,0:T(8,128)S(1)}, u32[]{:S(2)}, u32[]{:S(2)}) %collective-permute-start.2) | collective-permute-done | bytes 213024 | tf_op jit(solution)/shard_map/ppermute | solution.py:305
  22.6 3.7 %collective-permute-start.6 = (f32[104,128]{1,0:T(8,128)S(1)}, f32[104,128]{1,0:T(8,128)S(1)}, u32[]{:S(2)}, u32[]{:S(2)}) collective-permute-start(f32[104,128]{1,0:T(8,128)S(1)} %get-tuple-element.74.refs_2_), channel_id=1, source_target_pairs={{0,6},{1,7},{2,4},{3,5},{4,2},{5,3},{6,0},{7,1},{8,14},{9,15},{10,... | collective-permute-start | bytes 159752 | tf_op jit(solution)/shard_map/ppermute | solution.py:305
  26.2 0.0 collective-permute-start.5
  26.3 0.0 collective-permute-done.10.refs_4_
  26.3 0.8 %collective-permute-start.4 = (f32[104,128]{1,0:T(8,128)S(1)}, f32[104,128]{1,0:T(8,128)S(1)}, u32[]{:S(2)}, u32[]{:S(2)}) collective-permute-start(f32[104,128]{1,0:T(8,128)S(1)} %shard_map.104), channel_id=1, source_target_pairs={{0,2},{1,3},{2,0},{3,1},{4,6},{5,7},{6,4},{7,5},{8,10},{9,11},{10,... | collective-permute-start | bytes 159752 | tf_op jit(solution)/shard_map/ppermute | solution.py:305
  27.1 0.0 collective-permute-done.11.refs_5_
  27.1 0.0 collective-permute-done.12.refs_6_
  27.1 1.4 %shard_map.106 = (f32[8,32,128]{2,1,0:T(8,128)S(1)}, f32[8,32,128]{2,1,0:T(8,128)S(1)}) custom-call(f32[4,32,128]{2,1,0:T(8,128)S(1)} %get-tuple-element.46.refs_0_, f32[4,32,128]{2,1,0:T(8,128)S(1)} %collective-permute-done.7.refs_1_, f32[4,32,128]{2,1,0:T(8,128)S(1)} %collective-permute-done.8.refs_2_, f32[4,32,128]{2,1,0:T(8,128)S(1)} %collective-permute-done.9.refs_3_, ...), custom_call_target="tpu_custom_call" | custom-call | flops 4000000000 | tf_op jit(solution)/shard_map/pallas_call | solution.py:41
  28.5 0.1 collective-permute-start.13
  28.6 1.8 %collective-permute-done.4 = f32[104,128]{1,0:T(8,128)S(1)} collective-permute-done((f32[104,128]{1,0:T(8,128)S(1)}, f32[104,128]{1,0:T(8,128)S(1)}, u32[]{:S(2)}, u32[]{:S(2)}) %collective-permute-start.4) | collective-permute-done | bytes 53280 | tf_op jit(solution)/shard_map/ppermute | solution.py:305
  30.5 0.0 collective-permute-done.6
  30.5 0.8 %collective-permute-done.5 = f32[104,128]{1,0:T(8,128)S(1)} collective-permute-done((f32[104,128]{1,0:T(8,128)S(1)}, f32[104,128]{1,0:T(8,128)S(1)}, u32[]{:S(2)}, u32[]{:S(2)}) %collective-permute-start.5) | collective-permute-done | bytes 53280 | tf_op jit(solution)/shard_map/ppermute | solution.py:305
  31.3 0.0 collective-permute-done.13
  31.4 0.4 collective-permute-start.17
  31.7 2.5 %collective-permute-start.18 = (f32[168,128]{1,0:T(8,128)S(1)}, f32[168,128]{1,0:T(8,128)S(1)}, u32[]{:S(2)}, u32[]{:S(2)}) collective-permute-start(f32[168,128]{1,0:T(8,128)S(1)} %get-tuple-element.56.refs_3_), channel_id=1, source_target_pairs={{0,4},{1,5},{2,6},{3,7},{4,0},{5,1},{6,2},{7,3},{8,12},{9,13},{10,... | collective-permute-start | bytes 258056 | tf_op jit(solution)/shard_map/ppermute | solution.py:305
  34.3 1.6 %collective-permute-start.19 = (f32[168,128]{1,0:T(8,128)S(1)}, f32[168,128]{1,0:T(8,128)S(1)}, u32[]{:S(2)}, u32[]{:S(2)}) collective-permute-start(f32[168,128]{1,0:T(8,128)S(1)} %get-tuple-element.57.refs_4_), channel_id=1, source_target_pairs={{0,6},{1,7},{2,4},{3,5},{4,2},{5,3},{6,0},{7,1},{8,14},{9,15},{10,... | collective-permute-start | bytes 258056 | tf_op jit(solution)/shard_map/ppermute | solution.py:305
  35.8 1.8 %collective-permute-start.16 = (f32[136,128]{1,0:T(8,128)S(1)}, f32[136,128]{1,0:T(8,128)S(1)}, u32[]{:S(2)}, u32[]{:S(2)}) collective-permute-start(f32[136,128]{1,0:T(8,128)S(1)} %get-tuple-element.59), channel_id=1, source_target_pairs={{0,17},{1,16},{2,19},{3,18},{4,21},{5,20},{6,23},{7,22},{8,25},{9,... | collective-permute-start | bytes 208904 | tf_op jit(solution)/shard_map/ppermute | solution.py:305
  37.6 0.6 %collective-permute-start.14 = (f32[136,128]{1,0:T(8,128)S(1)}, f32[136,128]{1,0:T(8,128)S(1)}, u32[]{:S(2)}, u32[]{:S(2)}) collective-permute-start(f32[136,128]{1,0:T(8,128)S(1)} %get-tuple-element.59), channel_id=1, source_target_pairs={{0,1},{1,0},{2,3},{3,2},{4,5},{5,4},{6,7},{7,6},{8,9},{9,8},{10,11... | collective-permute-start | bytes 208904 | tf_op jit(solution)/shard_map/ppermute | solution.py:305
  38.2 0.0 collective-permute-done.17.refs_0_
  38.2 1.1 %collective-permute-start.15 = (f32[136,128]{1,0:T(8,128)S(1)}, f32[136,128]{1,0:T(8,128)S(1)}, u32[]{:S(2)}, u32[]{:S(2)}) collective-permute-start(f32[136,128]{1,0:T(8,128)S(1)} %get-tuple-element.58.refs_1_), channel_id=1, source_target_pairs={{0,16},{1,17},{2,18},{3,19},{4,20},{5,21},{6,22},{7,23},{8,24},{9,... | collective-permute-start | bytes 208904 | tf_op jit(solution)/shard_map/ppermute | solution.py:305
  39.4 1.9 %collective-permute-done.18.refs_1_ = f32[168,128]{1,0:T(8,128)S(1)} collective-permute-done((f32[168,128]{1,0:T(8,128)S(1)}, f32[168,128]{1,0:T(8,128)S(1)}, u32[]{:S(2)}, u32[]{:S(2)}) %collective-permute-start.18) | collective-permute-done | bytes 86048 | tf_op jit(solution)/shard_map/ppermute | solution.py:305
  41.3 0.0 collective-permute-done.19.refs_2_
  41.3 1.8 %collective-permute-start.22 = (f32[408,128]{1,0:T(8,128)S(1)}, f32[408,128]{1,0:T(8,128)S(1)}, u32[]{:S(2)}, u32[]{:S(2)}) collective-permute-start(f32[408,128]{1,0:T(8,128)S(1)} %get-tuple-element.61), channel_id=1, source_target_pairs={{0,17},{1,16},{2,19},{3,18},{4,21},{5,20},{6,23},{7,22},{8,25},{9,... | collective-permute-start | bytes 626696 | tf_op jit(solution)/shard_map/ppermute | solution.py:305
  43.1 0.6 %collective-permute-start.20 = (f32[408,128]{1,0:T(8,128)S(1)}, f32[408,128]{1,0:T(8,128)S(1)}, u32[]{:S(2)}, u32[]{:S(2)}) collective-permute-start(f32[408,128]{1,0:T(8,128)S(1)} %get-tuple-element.61), channel_id=1, source_target_pairs={{0,1},{1,0},{2,3},{3,2},{4,5},{5,4},{6,7},{7,6},{8,9},{9,8},{10,11... | collective-permute-start | bytes 626696 | tf_op jit(solution)/shard_map/ppermute | solution.py:305
  43.7 0.0 collective-permute-done.16.refs_4_
  43.7 1.1 %collective-permute-start.21 = (f32[408,128]{1,0:T(8,128)S(1)}, f32[408,128]{1,0:T(8,128)S(1)}, u32[]{:S(2)}, u32[]{:S(2)}) collective-permute-start(f32[408,128]{1,0:T(8,128)S(1)} %get-tuple-element.60.refs_5_), channel_id=1, source_target_pairs={{0,16},{1,17},{2,18},{3,19},{4,20},{5,21},{6,22},{7,23},{8,24},{9,... | collective-permute-start | bytes 626696 | tf_op jit(solution)/shard_map/ppermute | solution.py:305
  44.9 0.0 collective-permute-done.14.refs_2_
  44.9 0.0 collective-permute-done.15.refs_3_
  44.9 0.1 collective-permute-start.23
  45.0 0.5 collective-permute-start.24
  45.5 4.2 %collective-permute-done.22.refs_8_ = f32[408,128]{1,0:T(8,128)S(1)} collective-permute-done((f32[408,128]{1,0:T(8,128)S(1)}, f32[408,128]{1,0:T(8,128)S(1)}, u32[]{:S(2)}, u32[]{:S(2)}) %collective-permute-start.22) | collective-permute-done | bytes 208928 | tf_op jit(solution)/shard_map/ppermute | solution.py:305
  49.6 0.0 collective-permute-start.27
  49.6 1.5 %collective-permute-done.20.refs_6_ = f32[408,128]{1,0:T(8,128)S(1)} collective-permute-done((f32[408,128]{1,0:T(8,128)S(1)}, f32[408,128]{1,0:T(8,128)S(1)}, u32[]{:S(2)}, u32[]{:S(2)}) %collective-permute-start.20) | collective-permute-done | bytes 208928 | tf_op jit(solution)/shard_map/ppermute | solution.py:305
  51.2 0.0 collective-permute-start.25
  51.2 0.6 %collective-permute-done.21.refs_7_ = f32[408,128]{1,0:T(8,128)S(1)} collective-permute-done((f32[408,128]{1,0:T(8,128)S(1)}, f32[408,128]{1,0:T(8,128)S(1)}, u32[]{:S(2)}, u32[]{:S(2)}) %collective-permute-start.21) | collective-permute-done | bytes 208928 | tf_op jit(solution)/shard_map/ppermute | solution.py:305
  51.8 0.0 collective-permute-start.26
  51.8 1.1 %shard_map.110 = (f32[8,32,288]{2,1,0:T(8,128)S(1)}, f32[256,512]{1,0:T(8,128)S(1)}, f32[8,32,32]{2,1,0:T(8,128)S(1)}, f32[6,24,288]{2,1,0:T(8,128)S(1)}) custom-call(s32[4,24]{1,0:T(4,128)S(1)} %copy-done, f32[136,128]{1,0:T(8,128)S(1)} %get-tuple-element.58.refs_1_, f32[136,128]{1,0:T(8,128)S(1)} %collective-permute-done.14.refs_2_, ...), custom_call_target="tpu_custom_call" | custom-call | flops 1000000000 | tf_op jit(solution)/shard_map/pallas_call | solution.py:41
  52.9 0.0 collective-permute-done.24.refs_6_
  52.9 0.0 collective-permute-done.23.refs_5_
  52.9 0.0 collective-permute-done.25.refs_7_
  52.9 0.3 collective-permute-done.26.refs_8_
  53.2 2.5 %shard_map.111 = (f32[16,32,288]{2,1,0:T(8,128)}, f32[512,512]{1,0:T(8,128)}, f32[16,32,32]{2,1,0:T(8,128)}, f32[12,24,288]{2,1,0:T(8,128)}) custom-call(s32[4,24]{1,0:T(4,128)S(1)} %copy-done, f32[8,32,288]{2,1,0:T(8,128)S(1)} %get-tuple-element.62.refs_1_, f32[256,512]{1,0:T(8,128)S(1)} %get-tuple-element.63.refs_2_, ...), custom_call_target="tpu_custom_call" | custom-call | tf_op jit(solution)/shard_map/pallas_call | solution.py:41
  (23 shorter events, 0.3 us)
Async XLA Ops:
  0.6 1.2 %copy-start.1 = (bf16[512,512]{1,0:T(8,128)(2,1)S(1)}, bf16[512,512]{1,0:T(8,128)(2,1)}, u32[]{:S(2)}) copy-start(bf16[512,512]{1,0:T(8,128)(2,1)} %refs_4_.1) | copy-start | bytes 1572868
  0.6 1.2 %copy-start.2 = (bf16[16,288,32]{1,2,0:T(8,128)(2,1)S(1)}, bf16[16,288,32]{1,2,0:T(8,128)(2,1)}, u32[]{:S(2)}) copy-start(bf16[16,288,32]{1,2,0:T(8,128)(2,1)} %param.9) | copy-start | bytes 884740
  0.7 1.0 %copy-start.3 = (bf16[2,8,8,512]{3,2,1,0:T(8,128)(2,1)S(1)}, bf16[2,8,8,512]{3,2,1,0:T(8,128)(2,1)}, u32[]{:S(2)}) copy-start(bf16[2,8,8,512]{3,2,1,0:T(8,128)(2,1)} %refs_0_.3) | copy-start | bytes 393220
  1.6 1.0 %copy-start.4 = (bf16[2,8,8,512]{3,2,1,0:T(8,128)(2,1)S(1)}, bf16[2,8,8,512]{3,2,1,0:T(8,128)(2,1)}, u32[]{:S(2)}) copy-start(bf16[2,8,8,512]{3,2,1,0:T(8,128)(2,1)} %refs_2_.1) | copy-start | bytes 393220
  1.6 1.0 %copy-start.5 = (f32[512]{0:T(512)S(1)}, f32[512]{0:T(512)}, u32[]{:S(2)}) copy-start(f32[512]{0:T(512)} %param.11) | copy-start | bytes 6148
  1.6 1.0 %copy-start.6 = (f32[512]{0:T(512)S(1)}, f32[512]{0:T(512)}, u32[]{:S(2)}) copy-start(f32[512]{0:T(512)} %param.12) | copy-start | bytes 6148
  4.0 4.6 %collective-permute-start = (f32[16,104,128]{2,1,0:T(8,128)S(1)}, f32[16,104,128]{2,1,0:T(8,128)S(1)}, u32[]{:S(2)}, u32[]{:S(2)}) collective-permute-start(f32[16,104,128]{2,1,0:T(8,128)S(1)} %get-tuple-element.45), channel_id=1, source_target_pairs={{0,8},{1,9},{2,10},{3,11},{4,12},{5,13},{6,14},{7,15},{8,0},{9,1},... | collective-permute-start | bytes 2555912 | tf_op jit(solution)/shard_map/ppermute | solution.py:305
  4.5 7.8 %collective-permute-start.7 = (f32[4,32,128]{2,1,0:T(8,128)S(1)}, f32[4,32,128]{2,1,0:T(8,128)S(1)}, u32[]{:S(2)}, u32[]{:S(2)}) collective-permute-start(f32[4,32,128]{2,1,0:T(8,128)S(1)} %get-tuple-element.47), channel_id=1, source_target_pairs={{0,1},{1,0},{2,3},{3,2},{4,5},{5,4},{6,7},{7,6},{8,9},{9,8},{10,11... | collective-permute-start | bytes 196616 | tf_op jit(solution)/shard_map/ppermute | solution.py:305
  7.1 5.4 %collective-permute-start.8 = (f32[4,32,128]{2,1,0:T(8,128)S(1)}, f32[4,32,128]{2,1,0:T(8,128)S(1)}, u32[]{:S(2)}, u32[]{:S(2)}) collective-permute-start(f32[4,32,128]{2,1,0:T(8,128)S(1)} %get-tuple-element.48), channel_id=1, source_target_pairs={{0,16},{1,17},{2,18},{3,19},{4,20},{5,21},{6,22},{7,23},{8,24},{9,... | collective-permute-start | bytes 196616 | tf_op jit(solution)/shard_map/ppermute | solution.py:305
  8.6 5.9 %collective-permute-start.9 = (f32[4,32,128]{2,1,0:T(8,128)S(1)}, f32[4,32,128]{2,1,0:T(8,128)S(1)}, u32[]{:S(2)}, u32[]{:S(2)}) collective-permute-start(f32[4,32,128]{2,1,0:T(8,128)S(1)} %get-tuple-element.49), channel_id=1, source_target_pairs={{0,17},{1,16},{2,19},{3,18},{4,21},{5,20},{6,23},{7,22},{8,25},{9,... | collective-permute-start | bytes 196616 | tf_op jit(solution)/shard_map/ppermute | solution.py:305
  8.8 9.8 %collective-permute-start.1 = (f32[4,104,128]{2,1,0:T(8,128)S(1)}, f32[4,104,128]{2,1,0:T(8,128)S(1)}, u32[]{:S(2)}, u32[]{:S(2)}) collective-permute-start(f32[4,104,128]{2,1,0:T(8,128)S(1)} %get-tuple-element.70), channel_id=1, source_target_pairs={{0,16},{1,17},{2,18},{3,19},{4,20},{5,21},{6,22},{7,23},{8,24},{9,... | collective-permute-start | bytes 638984 | tf_op jit(solution)/shard_map/ppermute | solution.py:305
  10.8 10.8 %collective-permute-start.3 = (f32[4,104,128]{2,1,0:T(8,128)S(1)}, f32[4,104,128]{2,1,0:T(8,128)S(1)}, u32[]{:S(2)}, u32[]{:S(2)}) collective-permute-start(f32[4,104,128]{2,1,0:T(8,128)S(1)} %get-tuple-element.71), channel_id=1, source_target_pairs={{0,1},{1,0},{2,3},{3,2},{4,5},{5,4},{6,7},{7,6},{8,9},{9,8},{10,11... | collective-permute-start | bytes 638984 | tf_op jit(solution)/shard_map/ppermute | solution.py:305
  12.3 10.2 %collective-permute-start.2 = (f32[4,104,128]{2,1,0:T(8,128)S(1)}, f32[4,104,128]{2,1,0:T(8,128)S(1)}, u32[]{:S(2)}, u32[]{:S(2)}) collective-permute-start(f32[4,104,128]{2,1,0:T(8,128)S(1)} %get-tuple-element.72), channel_id=1, source_target_pairs={{0,17},{1,16},{2,19},{3,18},{4,21},{5,20},{6,23},{7,22},{8,25},{9,... | collective-permute-start | bytes 638984 | tf_op jit(solution)/shard_map/ppermute | solution.py:305
  14.5 11.8 %collective-permute-start.10 = (f32[4,32,128]{2,1,0:T(8,128)S(1)}, f32[4,32,128]{2,1,0:T(8,128)S(1)}, u32[]{:S(2)}, u32[]{:S(2)}) collective-permute-start(f32[4,32,128]{2,1,0:T(8,128)S(1)} %get-tuple-element.50), channel_id=1, source_target_pairs={{0,2},{1,3},{2,0},{3,1},{4,6},{5,7},{6,4},{7,5},{8,10},{9,11},{10,... | collective-permute-start | bytes 196616 | tf_op jit(solution)/shard_map/ppermute | solution.py:305
  16.0 11.1 %collective-permute-start.11 = (f32[4,32,128]{2,1,0:T(8,128)S(1)}, f32[4,32,128]{2,1,0:T(8,128)S(1)}, u32[]{:S(2)}, u32[]{:S(2)}) collective-permute-start(f32[4,32,128]{2,1,0:T(8,128)S(1)} %get-tuple-element.51), channel_id=1, source_target_pairs={{0,4},{1,5},{2,6},{3,7},{4,0},{5,1},{6,2},{7,3},{8,12},{9,13},{10,... | collective-permute-start | bytes 196616 | tf_op jit(solution)/shard_map/ppermute | solution.py:305
  18.6 8.5 %collective-permute-start.12 = (f32[4,32,128]{2,1,0:T(8,128)S(1)}, f32[4,32,128]{2,1,0:T(8,128)S(1)}, u32[]{:S(2)}, u32[]{:S(2)}) collective-permute-start(f32[4,32,128]{2,1,0:T(8,128)S(1)} %get-tuple-element.52), channel_id=1, source_target_pairs={{0,6},{1,7},{2,4},{3,5},{4,2},{5,3},{6,0},{7,1},{8,14},{9,15},{10,... | collective-permute-start | bytes 196616 | tf_op jit(solution)/shard_map/ppermute | solution.py:305
  22.6 7.9 %collective-permute-start.6 = (f32[104,128]{1,0:T(8,128)S(1)}, f32[104,128]{1,0:T(8,128)S(1)}, u32[]{:S(2)}, u32[]{:S(2)}) collective-permute-start(f32[104,128]{1,0:T(8,128)S(1)} %get-tuple-element.74.refs_2_), channel_id=1, source_target_pairs={{0,6},{1,7},{2,4},{3,5},{4,2},{5,3},{6,0},{7,1},{8,14},{9,15},{10,... | collective-permute-start | bytes 159752 | tf_op jit(solution)/shard_map/ppermute | solution.py:305
  26.2 5.0 %collective-permute-start.5 = (f32[104,128]{1,0:T(8,128)S(1)}, f32[104,128]{1,0:T(8,128)S(1)}, u32[]{:S(2)}, u32[]{:S(2)}) collective-permute-start(f32[104,128]{1,0:T(8,128)S(1)} %get-tuple-element.75.refs_1_), channel_id=1, source_target_pairs={{0,4},{1,5},{2,6},{3,7},{4,0},{5,1},{6,2},{7,3},{8,12},{9,13},{10,... | collective-permute-start | bytes 159752 | tf_op jit(solution)/shard_map/ppermute | solution.py:305
  26.3 4.2 %collective-permute-start.4 = (f32[104,128]{1,0:T(8,128)S(1)}, f32[104,128]{1,0:T(8,128)S(1)}, u32[]{:S(2)}, u32[]{:S(2)}) collective-permute-start(f32[104,128]{1,0:T(8,128)S(1)} %shard_map.104), channel_id=1, source_target_pairs={{0,2},{1,3},{2,0},{3,1},{4,6},{5,7},{6,4},{7,5},{8,10},{9,11},{10,... | collective-permute-start | bytes 159752 | tf_op jit(solution)/shard_map/ppermute | solution.py:305
  28.5 2.8 %collective-permute-start.13 = (f32[8,32,128]{2,1,0:T(8,128)S(1)}, f32[8,32,128]{2,1,0:T(8,128)S(1)}, u32[]{:S(2)}, u32[]{:S(2)}) collective-permute-start(f32[8,32,128]{2,1,0:T(8,128)S(1)} %get-tuple-element.54), channel_id=1, source_target_pairs={{0,8},{1,9},{2,10},{3,11},{4,12},{5,13},{6,14},{7,15},{8,0},{9,1},... | collective-permute-start | bytes 393224 | tf_op jit(solution)/shard_map/ppermute | solution.py:305
  31.4 6.9 %collective-permute-start.17 = (f32[168,128]{1,0:T(8,128)S(1)}, f32[168,128]{1,0:T(8,128)S(1)}, u32[]{:S(2)}, u32[]{:S(2)}) collective-permute-start(f32[168,128]{1,0:T(8,128)S(1)} %get-tuple-element.55.refs_2_), channel_id=1, source_target_pairs={{0,2},{1,3},{2,0},{3,1},{4,6},{5,7},{6,4},{7,5},{8,10},{9,11},{10,... | collective-permute-start | bytes 258056 | tf_op jit(solution)/shard_map/ppermute | solution.py:305
  31.7 9.5 %collective-permute-start.18 = (f32[168,128]{1,0:T(8,128)S(1)}, f32[168,128]{1,0:T(8,128)S(1)}, u32[]{:S(2)}, u32[]{:S(2)}) collective-permute-start(f32[168,128]{1,0:T(8,128)S(1)} %get-tuple-element.56.refs_3_), channel_id=1, source_target_pairs={{0,4},{1,5},{2,6},{3,7},{4,0},{5,1},{6,2},{7,3},{8,12},{9,13},{10,... | collective-permute-start | bytes 258056 | tf_op jit(solution)/shard_map/ppermute | solution.py:305
  34.3 17.5 %copy-start = (s32[4,24]{1,0:T(4,128)S(1)}, s32[4,24]{1,0:T(4,128)}, u32[]{:S(2)}) copy-start(s32[4,24]{1,0:T(4,128)} %refs_0_.5) | copy-start | bytes 1156
  34.3 7.0 %collective-permute-start.19 = (f32[168,128]{1,0:T(8,128)S(1)}, f32[168,128]{1,0:T(8,128)S(1)}, u32[]{:S(2)}, u32[]{:S(2)}) collective-permute-start(f32[168,128]{1,0:T(8,128)S(1)} %get-tuple-element.57.refs_4_), channel_id=1, source_target_pairs={{0,6},{1,7},{2,4},{3,5},{4,2},{5,3},{6,0},{7,1},{8,14},{9,15},{10,... | collective-permute-start | bytes 258056 | tf_op jit(solution)/shard_map/ppermute | solution.py:305
  35.8 7.9 %collective-permute-start.16 = (f32[136,128]{1,0:T(8,128)S(1)}, f32[136,128]{1,0:T(8,128)S(1)}, u32[]{:S(2)}, u32[]{:S(2)}) collective-permute-start(f32[136,128]{1,0:T(8,128)S(1)} %get-tuple-element.59), channel_id=1, source_target_pairs={{0,17},{1,16},{2,19},{3,18},{4,21},{5,20},{6,23},{7,22},{8,25},{9,... | collective-permute-start | bytes 208904 | tf_op jit(solution)/shard_map/ppermute | solution.py:305
  37.6 7.2 %collective-permute-start.14 = (f32[136,128]{1,0:T(8,128)S(1)}, f32[136,128]{1,0:T(8,128)S(1)}, u32[]{:S(2)}, u32[]{:S(2)}) collective-permute-start(f32[136,128]{1,0:T(8,128)S(1)} %get-tuple-element.59), channel_id=1, source_target_pairs={{0,1},{1,0},{2,3},{3,2},{4,5},{5,4},{6,7},{7,6},{8,9},{9,8},{10,11... | collective-permute-start | bytes 208904 | tf_op jit(solution)/shard_map/ppermute | solution.py:305
  38.2 6.6 %collective-permute-start.15 = (f32[136,128]{1,0:T(8,128)S(1)}, f32[136,128]{1,0:T(8,128)S(1)}, u32[]{:S(2)}, u32[]{:S(2)}) collective-permute-start(f32[136,128]{1,0:T(8,128)S(1)} %get-tuple-element.58.refs_1_), channel_id=1, source_target_pairs={{0,16},{1,17},{2,18},{3,19},{4,20},{5,21},{6,22},{7,23},{8,24},{9,... | collective-permute-start | bytes 208904 | tf_op jit(solution)/shard_map/ppermute | solution.py:305
  41.3 8.3 %collective-permute-start.22 = (f32[408,128]{1,0:T(8,128)S(1)}, f32[408,128]{1,0:T(8,128)S(1)}, u32[]{:S(2)}, u32[]{:S(2)}) collective-permute-start(f32[408,128]{1,0:T(8,128)S(1)} %get-tuple-element.61), channel_id=1, source_target_pairs={{0,17},{1,16},{2,19},{3,18},{4,21},{5,20},{6,23},{7,22},{8,25},{9,... | collective-permute-start | bytes 626696 | tf_op jit(solution)/shard_map/ppermute | solution.py:305
  43.1 8.1 %collective-permute-start.20 = (f32[408,128]{1,0:T(8,128)S(1)}, f32[408,128]{1,0:T(8,128)S(1)}, u32[]{:S(2)}, u32[]{:S(2)}) collective-permute-start(f32[408,128]{1,0:T(8,128)S(1)} %get-tuple-element.61), channel_id=1, source_target_pairs={{0,1},{1,0},{2,3},{3,2},{4,5},{5,4},{6,7},{7,6},{8,9},{9,8},{10,11... | collective-permute-start | bytes 626696 | tf_op jit(solution)/shard_map/ppermute | solution.py:305
  43.7 8.0 %collective-permute-start.21 = (f32[408,128]{1,0:T(8,128)S(1)}, f32[408,128]{1,0:T(8,128)S(1)}, u32[]{:S(2)}, u32[]{:S(2)}) collective-permute-start(f32[408,128]{1,0:T(8,128)S(1)} %get-tuple-element.60.refs_5_), channel_id=1, source_target_pairs={{0,16},{1,17},{2,18},{3,19},{4,20},{5,21},{6,22},{7,23},{8,24},{9,... | collective-permute-start | bytes 626696 | tf_op jit(solution)/shard_map/ppermute | solution.py:305
  44.9 8.0 %collective-permute-start.23 = (f32[4,136,128]{2,1,0:T(8,128)S(1)}, f32[4,136,128]{2,1,0:T(8,128)S(1)}, u32[]{:S(2)}, u32[]{:S(2)}) collective-permute-start(f32[4,136,128]{2,1,0:T(8,128)S(1)} %pad_maximum_fusion), channel_id=1, source_target_pairs={{0,8},{1,9},{2,10},{3,11},{4,12},{5,13},{6,14},{7,15},{8,0},{9,1},... | collective-permute-start | bytes 835592 | tf_op jit(solution)/shard_map/ppermute | solution.py:305
  45.0 7.9 %collective-permute-start.24 = (f32[408,128]{1,0:T(8,128)S(1)}, f32[408,128]{1,0:T(8,128)S(1)}, u32[]{:S(2)}, u32[]{:S(2)}) collective-permute-start(f32[408,128]{1,0:T(8,128)S(1)} %get-tuple-element.60.refs_5_), channel_id=1, source_target_pairs={{0,8},{1,9},{2,10},{3,11},{4,12},{5,13},{6,14},{7,15},{8,0},{9,1},... | collective-permute-start | bytes 626696 | tf_op jit(solution)/shard_map/ppermute | solution.py:305
  49.6 3.3 %collective-permute-start.27 = (f32[408,128]{1,0:T(8,128)S(1)}, f32[408,128]{1,0:T(8,128)S(1)}, u32[]{:S(2)}, u32[]{:S(2)}) collective-permute-start(f32[408,128]{1,0:T(8,128)S(1)} %collective-permute-done.22.refs_8_), channel_id=1, source_target_pairs={{0,8},{1,9},{2,10},{3,11},{4,12},{5,13},{6,14},{7,15},{8,0},{9,1},... | collective-permute-start | bytes 626696 | tf_op jit(solution)/shard_map/ppermute | solution.py:305
  51.2 1.7 %collective-permute-start.25 = (f32[408,128]{1,0:T(8,128)S(1)}, f32[408,128]{1,0:T(8,128)S(1)}, u32[]{:S(2)}, u32[]{:S(2)}) collective-permute-start(f32[408,128]{1,0:T(8,128)S(1)} %collective-permute-done.20.refs_6_), channel_id=1, source_target_pairs={{0,8},{1,9},{2,10},{3,11},{4,12},{5,13},{6,14},{7,15},{8,0},{9,1},... | collective-permute-start | bytes 626696 | tf_op jit(solution)/shard_map/ppermute | solution.py:305
  51.8 1.5 %collective-permute-start.26 = (f32[408,128]{1,0:T(8,128)S(1)}, f32[408,128]{1,0:T(8,128)S(1)}, u32[]{:S(2)}, u32[]{:S(2)}) collective-permute-start(f32[408,128]{1,0:T(8,128)S(1)} %collective-permute-done.21.refs_7_), channel_id=1, source_target_pairs={{0,8},{1,9},{2,10},{3,11},{4,12},{5,13},{6,14},{7,15},{8,0},{9,1},... | collective-permute-start | bytes 626696 | tf_op jit(solution)/shard_map/ppermute | solution.py:305

commit v10 on v8

--- a/solution.py
+++ b/solution.py
@@ -227,7 +227,7 @@
         peer_ref[at + 104 : at + size, :] = ref[size:, :]
 
 
-def unpack(scales, slot_ref, parts, outs, sums, blocks):
+def unpack(scales, slot_ref, parts, outs, sums, blocks, ready=lambda which: None):
     group_ref, proj_ref, out_ref, owned_ref = outs
     grad_scale, mean_scale = scales
     me = cell_id() & 15
@@ -245,10 +245,13 @@
             row = base + 16 * w
             proj_ref[pl.ds(at, 16), 128 * w : 128 * w + 128] = ref[row : row + 16, :] * grad_scale
         sums[pl.ds(pl.multiple_of(40 * j, 8), 40), :] = ref[base + 64 : base + 104, :]
+    ready(1)
     for q in range(2):
         group_ref[4 * q : 4 * q + 4] = (sums[320 * q : 320 * q + 288, :].T * grad_scale).reshape(4, 32, 288)
         for g in range(4):
             out_ref[4 * q + g] = sums[320 * q + 288 : 320 * q + 320, 32 * g : 32 * g + 32] * mean_scale
+    ready(0)
+    ready(2)
     for j, ref, base in spots:
         base += 104
         tiles = [ref[base + count * t : base + count * t + count, :] for t in range(5)]
@@ -268,6 +271,7 @@
         block = slot_ref[owner, s]
         value = blocks[jnp.maximum(block, 0)]
         owned_ref[:, s, :] = jnp.where(block >= 0, value, 0.0)
+    ready(3)
 
 
 def half_kernel(scales, slot_ref, *refs):
@@ -290,9 +294,7 @@
     copies = send(0, mine, core) + send(4, held, 1 - core)
     for copy in copies[:4]:
         copy.start()
-    unpack(scales, slot_ref, [early.at[i] for i in range(4)] + late, held, sums, blocks)
-    for copy in copies[4:]:
-        copy.start()
+    unpack(scales, slot_ref, [early.at[i] for i in range(4)] + late, held, sums, blocks, lambda which: copies[4 + which].start())
     for copy in copies:
         copy.wait()
 

time: 56.3 us -> 56.3 us (level)
  no operation moved by 1% of the time
where the time goes in v10:
time: 56.3 us; the launch traced here: 55.7 us
  starting transfers between devices  32.1 us (57%)
  waiting for transfers between devices  14.1 us (25%)
  Pallas kernels  6.59 us (12%)
  local copies, waits for them, and re-layouts  1.85 us (3%)
  between operations  0.85 us (2%)
    ppermute x28, starting transfers between devices, swap(): return lax.ppermute(value, AXES, pairs)  32.1 us
    ppermute x28, waiting for transfers between devices, swap(): return lax.ppermute(value, AXES, pairs)  14.1 us
    pallas_call x10, Pallas kernels, call(): pl.pallas_call(run, out_shape=[jax.ShapeDtypeStruct(shape, kind) for shap...  6.59 us
    unnamed x14, local copies, waits for them, and re-layouts  1.79 us
  transfers between devices with their start and end apart: 28, of which 9 were waited for; matrix products, arithmetic and copies ran while one was open for 0% of the time, Pallas kernels for 5%

profile of v10, /device:TPU:0, one launch (start us, length us, event | category | flops | bytes accessed | tf_op | source)
XLA Modules:
  0.0 55.7 jit_solution(17481695080168991211)
XLA Ops:
  0.7 1.0 %copy-done.3 = bf16[2,8,8,512]{3,2,1,0:T(8,128)(2,1)S(1)} copy-done((bf16[2,8,8,512]{3,2,1,0:T(8,128)(2,1)S(1)}, bf16[2,8,8,512]{3,2,1,0:T(8,128)(2,1)}, u32[]{:S(2)}) %copy-start.3) | copy-done | bytes 131096
  1.6 0.1 shard_map.103
  1.8 0.0 copy-start.5
  1.8 0.1 copy-done.2
  1.8 0.7 %copy-done.4 = bf16[2,8,8,512]{3,2,1,0:T(8,128)(2,1)S(1)} copy-done((bf16[2,8,8,512]{3,2,1,0:T(8,128)(2,1)S(1)}, bf16[2,8,8,512]{3,2,1,0:T(8,128)(2,1)}, u32[]{:S(2)}) %copy-start.4) | copy-done | bytes 131096
  2.6 1.4 %shard_map.102 = (f32[16,104,128]{2,1,0:T(8,128)S(1)}, f32[16,104,128]{2,1,0:T(8,128)S(1)}) custom-call(bf16[2,8,8,512]{3,2,1,0:T(8,128)(2,1)S(1)} %copy-done.3, bf16[2,8,8,512]{3,2,1,0:T(8,128)(2,1)S(1)} %copy-done.4, bf16[16,32,288]{2,1,0:T(8,128)(2,1)S(1)} %bitcast.30, bf16[512,512]{1,0:T(8,128)(2,1)S(1)} %copy-done.1, f32[1,512]{1,0:T(1,128)S(1)} %bitcast.31, ...), custom_call_target="tpu_custom_call" | custom-call | flops 4000000000 | tf_op jit(solution)/shard_map/pallas_call | solution.py:41
  4.0 0.5 collective-permute-start
  4.5 2.6 %collective-permute-start.7 = (f32[4,32,128]{2,1,0:T(8,128)S(1)}, f32[4,32,128]{2,1,0:T(8,128)S(1)}, u32[]{:S(2)}, u32[]{:S(2)}) collective-permute-start(f32[4,32,128]{2,1,0:T(8,128)S(1)} %get-tuple-element.43), channel_id=1, source_target_pairs={{0,1},{1,0},{2,3},{3,2},{4,5},{5,4},{6,7},{7,6},{8,9},{9,8},{10,11... | collective-permute-start | bytes 196616 | tf_op jit(solution)/shard_map/ppermute | solution.py:307
  7.1 1.5 %collective-permute-start.8 = (f32[4,32,128]{2,1,0:T(8,128)S(1)}, f32[4,32,128]{2,1,0:T(8,128)S(1)}, u32[]{:S(2)}, u32[]{:S(2)}) collective-permute-start(f32[4,32,128]{2,1,0:T(8,128)S(1)} %get-tuple-element.44), channel_id=1, source_target_pairs={{0,16},{1,17},{2,18},{3,19},{4,20},{5,21},{6,22},{7,23},{8,24},{9,... | collective-permute-start | bytes 196616 | tf_op jit(solution)/shard_map/ppermute | solution.py:307
  8.6 0.0 collective-permute-start.9
  8.6 0.0 collective-permute-done
  8.6 0.1 add.24.refs_4_
  8.8 2.1 %collective-permute-start.1 = (f32[4,104,128]{2,1,0:T(8,128)S(1)}, f32[4,104,128]{2,1,0:T(8,128)S(1)}, u32[]{:S(2)}, u32[]{:S(2)}) collective-permute-start(f32[4,104,128]{2,1,0:T(8,128)S(1)} %get-tuple-element.66), channel_id=1, source_target_pairs={{0,16},{1,17},{2,18},{3,19},{4,20},{5,21},{6,22},{7,23},{8,24},{9,... | collective-permute-start | bytes 638984 | tf_op jit(solution)/shard_map/ppermute | solution.py:307
  10.8 1.5 %collective-permute-start.3 = (f32[4,104,128]{2,1,0:T(8,128)S(1)}, f32[4,104,128]{2,1,0:T(8,128)S(1)}, u32[]{:S(2)}, u32[]{:S(2)}) collective-permute-start(f32[4,104,128]{2,1,0:T(8,128)S(1)} %get-tuple-element.67), channel_id=1, source_target_pairs={{0,1},{1,0},{2,3},{3,2},{4,5},{5,4},{6,7},{7,6},{8,9},{9,8},{10,11... | collective-permute-start | bytes 638984 | tf_op jit(solution)/shard_map/ppermute | solution.py:307
  12.3 0.0 collective-permute-done.7.refs_1_
  12.3 0.2 collective-permute-start.2
  12.5 0.0 collective-permute-done.8.refs_2_
  12.5 2.0 %collective-permute-done.9.refs_3_ = f32[4,32,128]{2,1,0:T(8,128)S(1)} collective-permute-done((f32[4,32,128]{2,1,0:T(8,128)S(1)}, f32[4,32,128]{2,1,0:T(8,128)S(1)}, u32[]{:S(2)}, u32[]{:S(2)}) %collective-permute-start.9) | collective-permute-done | bytes 65568 | tf_op jit(solution)/shard_map/ppermute | solution.py:307
  14.5 1.5 %collective-permute-start.10 = (f32[4,32,128]{2,1,0:T(8,128)S(1)}, f32[4,32,128]{2,1,0:T(8,128)S(1)}, u32[]{:S(2)}, u32[]{:S(2)}) collective-permute-start(f32[4,32,128]{2,1,0:T(8,128)S(1)} %get-tuple-element.46), channel_id=1, source_target_pairs={{0,2},{1,3},{2,0},{3,1},{4,6},{5,7},{6,4},{7,5},{8,10},{9,11},{10,... | collective-permute-start | bytes 196616 | tf_op jit(solution)/shard_map/ppermute | solution.py:307
  16.0 2.6 %collective-permute-start.11 = (f32[4,32,128]{2,1,0:T(8,128)S(1)}, f32[4,32,128]{2,1,0:T(8,128)S(1)}, u32[]{:S(2)}, u32[]{:S(2)}) collective-permute-start(f32[4,32,128]{2,1,0:T(8,128)S(1)} %get-tuple-element.47), channel_id=1, source_target_pairs={{0,4},{1,5},{2,6},{3,7},{4,0},{5,1},{6,2},{7,3},{8,12},{9,13},{10,... | collective-permute-start | bytes 196616 | tf_op jit(solution)/shard_map/ppermute | solution.py:307
  18.6 0.0 collective-permute-done.1
  18.6 2.9 %collective-permute-start.12 = (f32[4,32,128]{2,1,0:T(8,128)S(1)}, f32[4,32,128]{2,1,0:T(8,128)S(1)}, u32[]{:S(2)}, u32[]{:S(2)}) collective-permute-start(f32[4,32,128]{2,1,0:T(8,128)S(1)} %get-tuple-element.48), channel_id=1, source_target_pairs={{0,6},{1,7},{2,4},{3,5},{4,2},{5,3},{6,0},{7,1},{8,14},{9,15},{10,... | collective-permute-start | bytes 196616 | tf_op jit(solution)/shard_map/ppermute | solution.py:307
  21.6 0.0 collective-permute-done.3
  21.6 0.9 %collective-permute-done.2 = f32[4,104,128]{2,1,0:T(8,128)S(1)} collective-permute-done((f32[4,104,128]{2,1,0:T(8,128)S(1)}, f32[4,104,128]{2,1,0:T(8,128)S(1)}, u32[]{:S(2)}, u32[]{:S(2)}) %collective-permute-start.2) | collective-permute-done | bytes 213024 | tf_op jit(solution)/shard_map/ppermute | solution.py:307
  22.5 0.1 fusion.1.refs_7_
  22.6 3.7 %collective-permute-start.6 = (f32[104,128]{1,0:T(8,128)S(1)}, f32[104,128]{1,0:T(8,128)S(1)}, u32[]{:S(2)}, u32[]{:S(2)}) collective-permute-start(f32[104,128]{1,0:T(8,128)S(1)} %get-tuple-element.70.refs_2_), channel_id=1, source_target_pairs={{0,6},{1,7},{2,4},{3,5},{4,2},{5,3},{6,0},{7,1},{8,14},{9,15},{10,... | collective-permute-start | bytes 159752 | tf_op jit(solution)/shard_map/ppermute | solution.py:307
  26.3 0.0 collective-permute-start.5
  26.3 0.0 collective-permute-done.10.refs_4_
  26.3 0.8 %collective-permute-start.4 = (f32[104,128]{1,0:T(8,128)S(1)}, f32[104,128]{1,0:T(8,128)S(1)}, u32[]{:S(2)}, u32[]{:S(2)}) collective-permute-start(f32[104,128]{1,0:T(8,128)S(1)} %shard_map.104), channel_id=1, source_target_pairs={{0,2},{1,3},{2,0},{3,1},{4,6},{5,7},{6,4},{7,5},{8,10},{9,11},{10,... | collective-permute-start | bytes 159752 | tf_op jit(solution)/shard_map/ppermute | solution.py:307
  27.1 0.0 collective-permute-done.11.refs_5_
  27.1 0.0 collective-permute-done.12.refs_6_
  27.1 1.4 %shard_map.106 = (f32[8,32,128]{2,1,0:T(8,128)S(1)}, f32[8,32,128]{2,1,0:T(8,128)S(1)}) custom-call(f32[4,32,128]{2,1,0:T(8,128)S(1)} %get-tuple-element.42.refs_0_, f32[4,32,128]{2,1,0:T(8,128)S(1)} %collective-permute-done.7.refs_1_, f32[4,32,128]{2,1,0:T(8,128)S(1)} %collective-permute-done.8.refs_2_, f32[4,32,128]{2,1,0:T(8,128)S(1)} %collective-permute-done.9.refs_3_, ...), custom_call_target="tpu_custom_call" | custom-call | flops 4000000000 | tf_op jit(solution)/shard_map/pallas_call | solution.py:41
  28.6 0.1 collective-permute-start.13
  28.6 1.8 %collective-permute-done.4 = f32[104,128]{1,0:T(8,128)S(1)} collective-permute-done((f32[104,128]{1,0:T(8,128)S(1)}, f32[104,128]{1,0:T(8,128)S(1)}, u32[]{:S(2)}, u32[]{:S(2)}) %collective-permute-start.4) | collective-permute-done | bytes 53280 | tf_op jit(solution)/shard_map/ppermute | solution.py:307
  30.5 0.0 collective-permute-done.6
  30.5 0.8 %collective-permute-done.5 = f32[104,128]{1,0:T(8,128)S(1)} collective-permute-done((f32[104,128]{1,0:T(8,128)S(1)}, f32[104,128]{1,0:T(8,128)S(1)}, u32[]{:S(2)}, u32[]{:S(2)}) %collective-permute-start.5) | collective-permute-done | bytes 53280 | tf_op jit(solution)/shard_map/ppermute | solution.py:307
  31.3 0.0 collective-permute-done.13
  31.4 0.4 collective-permute-start.17
  31.7 2.5 %collective-permute-start.18 = (f32[168,128]{1,0:T(8,128)S(1)}, f32[168,128]{1,0:T(8,128)S(1)}, u32[]{:S(2)}, u32[]{:S(2)}) collective-permute-start(f32[168,128]{1,0:T(8,128)S(1)} %get-tuple-element.52.refs_3_), channel_id=1, source_target_pairs={{0,4},{1,5},{2,6},{3,7},{4,0},{5,1},{6,2},{7,3},{8,12},{9,13},{10,... | collective-permute-start | bytes 258056 | tf_op jit(solution)/shard_map/ppermute | solution.py:307
  34.3 1.6 %collective-permute-start.19 = (f32[168,128]{1,0:T(8,128)S(1)}, f32[168,128]{1,0:T(8,128)S(1)}, u32[]{:S(2)}, u32[]{:S(2)}) collective-permute-start(f32[168,128]{1,0:T(8,128)S(1)} %get-tuple-element.53.refs_4_), channel_id=1, source_target_pairs={{0,6},{1,7},{2,4},{3,5},{4,2},{5,3},{6,0},{7,1},{8,14},{9,15},{10,... | collective-permute-start | bytes 258056 | tf_op jit(solution)/shard_map/ppermute | solution.py:307
  35.8 1.8 %collective-permute-start.16 = (f32[136,128]{1,0:T(8,128)S(1)}, f32[136,128]{1,0:T(8,128)S(1)}, u32[]{:S(2)}, u32[]{:S(2)}) collective-permute-start(f32[136,128]{1,0:T(8,128)S(1)} %get-tuple-element.55), channel_id=1, source_target_pairs={{0,17},{1,16},{2,19},{3,18},{4,21},{5,20},{6,23},{7,22},{8,25},{9,... | collective-permute-start | bytes 208904 | tf_op jit(solution)/shard_map/ppermute | solution.py:307
  37.6 0.6 %collective-permute-start.14 = (f32[136,128]{1,0:T(8,128)S(1)}, f32[136,128]{1,0:T(8,128)S(1)}, u32[]{:S(2)}, u32[]{:S(2)}) collective-permute-start(f32[136,128]{1,0:T(8,128)S(1)} %get-tuple-element.55), channel_id=1, source_target_pairs={{0,1},{1,0},{2,3},{3,2},{4,5},{5,4},{6,7},{7,6},{8,9},{9,8},{10,11... | collective-permute-start | bytes 208904 | tf_op jit(solution)/shard_map/ppermute | solution.py:307
  38.3 0.0 collective-permute-done.17.refs_0_
  38.3 1.1 %collective-permute-start.15 = (f32[136,128]{1,0:T(8,128)S(1)}, f32[136,128]{1,0:T(8,128)S(1)}, u32[]{:S(2)}, u32[]{:S(2)}) collective-permute-start(f32[136,128]{1,0:T(8,128)S(1)} %get-tuple-element.54.refs_1_), channel_id=1, source_target_pairs={{0,16},{1,17},{2,18},{3,19},{4,20},{5,21},{6,22},{7,23},{8,24},{9,... | collective-permute-start | bytes 208904 | tf_op jit(solution)/shard_map/ppermute | solution.py:307
  39.4 1.9 %collective-permute-done.18.refs_1_ = f32[168,128]{1,0:T(8,128)S(1)} collective-permute-done((f32[168,128]{1,0:T(8,128)S(1)}, f32[168,128]{1,0:T(8,128)S(1)}, u32[]{:S(2)}, u32[]{:S(2)}) %collective-permute-start.18) | collective-permute-done | bytes 86048 | tf_op jit(solution)/shard_map/ppermute | solution.py:307
  41.3 0.0 collective-permute-done.19.refs_2_
  41.3 1.8 %collective-permute-start.22 = (f32[408,128]{1,0:T(8,128)S(1)}, f32[408,128]{1,0:T(8,128)S(1)}, u32[]{:S(2)}, u32[]{:S(2)}) collective-permute-start(f32[408,128]{1,0:T(8,128)S(1)} %get-tuple-element.57), channel_id=1, source_target_pairs={{0,17},{1,16},{2,19},{3,18},{4,21},{5,20},{6,23},{7,22},{8,25},{9,... | collective-permute-start | bytes 626696 | tf_op jit(solution)/shard_map/ppermute | solution.py:307
  43.1 0.7 %collective-permute-start.20 = (f32[408,128]{1,0:T(8,128)S(1)}, f32[408,128]{1,0:T(8,128)S(1)}, u32[]{:S(2)}, u32[]{:S(2)}) collective-permute-start(f32[408,128]{1,0:T(8,128)S(1)} %get-tuple-element.57), channel_id=1, source_target_pairs={{0,1},{1,0},{2,3},{3,2},{4,5},{5,4},{6,7},{7,6},{8,9},{9,8},{10,11... | collective-permute-start | bytes 626696 | tf_op jit(solution)/shard_map/ppermute | solution.py:307
  43.8 0.0 collective-permute-done.16.refs_4_
  43.8 1.1 %collective-permute-start.21 = (f32[408,128]{1,0:T(8,128)S(1)}, f32[408,128]{1,0:T(8,128)S(1)}, u32[]{:S(2)}, u32[]{:S(2)}) collective-permute-start(f32[408,128]{1,0:T(8,128)S(1)} %get-tuple-element.56.refs_5_), channel_id=1, source_target_pairs={{0,16},{1,17},{2,18},{3,19},{4,20},{5,21},{6,22},{7,23},{8,24},{9,... | collective-permute-start | bytes 626696 | tf_op jit(solution)/shard_map/ppermute | solution.py:307
  44.9 0.0 collective-permute-done.14.refs_2_
  44.9 0.0 collective-permute-done.15.refs_3_
  44.9 0.1 collective-permute-start.23
  45.0 0.5 collective-permute-start.24
  45.5 4.2 %collective-permute-done.22.refs_8_ = f32[408,128]{1,0:T(8,128)S(1)} collective-permute-done((f32[408,128]{1,0:T(8,128)S(1)}, f32[408,128]{1,0:T(8,128)S(1)}, u32[]{:S(2)}, u32[]{:S(2)}) %collective-permute-start.22) | collective-permute-done | bytes 208928 | tf_op jit(solution)/shard_map/ppermute | solution.py:307
  49.7 1.6 %collective-permute-done.20.refs_6_ = f32[408,128]{1,0:T(8,128)S(1)} collective-permute-done((f32[408,128]{1,0:T(8,128)S(1)}, f32[408,128]{1,0:T(8,128)S(1)}, u32[]{:S(2)}, u32[]{:S(2)}) %collective-permute-start.20) | collective-permute-done | bytes 208928 | tf_op jit(solution)/shard_map/ppermute | solution.py:307
  51.2 0.6 %collective-permute-done.21.refs_7_ = f32[408,128]{1,0:T(8,128)S(1)} collective-permute-done((f32[408,128]{1,0:T(8,128)S(1)}, f32[408,128]{1,0:T(8,128)S(1)}, u32[]{:S(2)}, u32[]{:S(2)}) %collective-permute-start.21) | collective-permute-done | bytes 208928 | tf_op jit(solution)/shard_map/ppermute | solution.py:307
  51.8 0.0 collective-permute-start.26
  51.8 1.1 %shard_map.110 = (f32[8,32,288]{2,1,0:T(8,128)S(1)}, f32[256,512]{1,0:T(8,128)S(1)}, f32[8,32,32]{2,1,0:T(8,128)S(1)}, f32[6,24,288]{2,1,0:T(8,128)S(1)}) custom-call(s32[4,24]{1,0:T(4,128)S(1)} %copy-done, f32[136,128]{1,0:T(8,128)S(1)} %get-tuple-element.54.refs_1_, f32[136,128]{1,0:T(8,128)S(1)} %collective-permute-done.14.refs_2_, ...), custom_call_target="tpu_custom_call" | custom-call | flops 1000000000 | tf_op jit(solution)/shard_map/pallas_call | solution.py:41
  52.9 0.0 collective-permute-done.24.refs_6_
  52.9 0.0 collective-permute-done.23.refs_5_
  52.9 0.0 collective-permute-done.25.refs_7_
  52.9 0.3 collective-permute-done.26.refs_8_
  53.2 2.5 %shard_map.111 = (f32[16,32,288]{2,1,0:T(8,128)}, f32[512,512]{1,0:T(8,128)}, f32[16,32,32]{2,1,0:T(8,128)}, f32[12,24,288]{2,1,0:T(8,128)}) custom-call(s32[4,24]{1,0:T(4,128)S(1)} %copy-done, f32[8,32,288]{2,1,0:T(8,128)S(1)} %get-tuple-element.58.refs_1_, f32[256,512]{1,0:T(8,128)S(1)} %get-tuple-element.59.refs_2_, ...), custom_call_target="tpu_custom_call" | custom-call | tf_op jit(solution)/shard_map/pallas_call | solution.py:41
  (23 shorter events, 0.2 us)
Async XLA Ops:
  0.6 1.2 %copy-start.1 = (bf16[512,512]{1,0:T(8,128)(2,1)S(1)}, bf16[512,512]{1,0:T(8,128)(2,1)}, u32[]{:S(2)}) copy-start(bf16[512,512]{1,0:T(8,128)(2,1)} %refs_3_.1) | copy-start | bytes 1572868
  0.6 1.2 %copy-start.2 = (bf16[16,288,32]{1,2,0:T(8,128)(2,1)S(1)}, bf16[16,288,32]{1,2,0:T(8,128)(2,1)}, u32[]{:S(2)}) copy-start(bf16[16,288,32]{1,2,0:T(8,128)(2,1)} %param.9) | copy-start | bytes 884740
  0.7 1.0 %copy-start.3 = (bf16[2,8,8,512]{3,2,1,0:T(8,128)(2,1)S(1)}, bf16[2,8,8,512]{3,2,1,0:T(8,128)(2,1)}, u32[]{:S(2)}) copy-start(bf16[2,8,8,512]{3,2,1,0:T(8,128)(2,1)} %refs_0_.5) | copy-start | bytes 393220
  1.6 1.0 %copy-start.4 = (bf16[2,8,8,512]{3,2,1,0:T(8,128)(2,1)S(1)}, bf16[2,8,8,512]{3,2,1,0:T(8,128)(2,1)}, u32[]{:S(2)}) copy-start(bf16[2,8,8,512]{3,2,1,0:T(8,128)(2,1)} %refs_1_.1) | copy-start | bytes 393220
  1.6 1.0 %copy-start.6 = (f32[512]{0:T(512)S(1)}, f32[512]{0:T(512)}, u32[]{:S(2)}) copy-start(f32[512]{0:T(512)} %param.12) | copy-start | bytes 6148
  1.8 0.8 %copy-start.5 = (f32[512]{0:T(512)S(1)}, f32[512]{0:T(512)}, u32[]{:S(2)}) copy-start(f32[512]{0:T(512)} %param.11) | copy-start | bytes 6148
  4.0 4.6 %collective-permute-start = (f32[16,104,128]{2,1,0:T(8,128)S(1)}, f32[16,104,128]{2,1,0:T(8,128)S(1)}, u32[]{:S(2)}, u32[]{:S(2)}) collective-permute-start(f32[16,104,128]{2,1,0:T(8,128)S(1)} %get-tuple-element.41), channel_id=1, source_target_pairs={{0,8},{1,9},{2,10},{3,11},{4,12},{5,13},{6,14},{7,15},{8,0},{9,1},... | collective-permute-start | bytes 2555912 | tf_op jit(solution)/shard_map/ppermute | solution.py:307
  4.5 7.8 %collective-permute-start.7 = (f32[4,32,128]{2,1,0:T(8,128)S(1)}, f32[4,32,128]{2,1,0:T(8,128)S(1)}, u32[]{:S(2)}, u32[]{:S(2)}) collective-permute-start(f32[4,32,128]{2,1,0:T(8,128)S(1)} %get-tuple-element.43), channel_id=1, source_target_pairs={{0,1},{1,0},{2,3},{3,2},{4,5},{5,4},{6,7},{7,6},{8,9},{9,8},{10,11... | collective-permute-start | bytes 196616 | tf_op jit(solution)/shard_map/ppermute | solution.py:307
  7.1 5.4 %collective-permute-start.8 = (f32[4,32,128]{2,1,0:T(8,128)S(1)}, f32[4,32,128]{2,1,0:T(8,128)S(1)}, u32[]{:S(2)}, u32[]{:S(2)}) collective-permute-start(f32[4,32,128]{2,1,0:T(8,128)S(1)} %get-tuple-element.44), channel_id=1, source_target_pairs={{0,16},{1,17},{2,18},{3,19},{4,20},{5,21},{6,22},{7,23},{8,24},{9,... | collective-permute-start | bytes 196616 | tf_op jit(solution)/shard_map/ppermute | solution.py:307
  8.6 5.9 %collective-permute-start.9 = (f32[4,32,128]{2,1,0:T(8,128)S(1)}, f32[4,32,128]{2,1,0:T(8,128)S(1)}, u32[]{:S(2)}, u32[]{:S(2)}) collective-permute-start(f32[4,32,128]{2,1,0:T(8,128)S(1)} %get-tuple-element.45), channel_id=1, source_target_pairs={{0,17},{1,16},{2,19},{3,18},{4,21},{5,20},{6,23},{7,22},{8,25},{9,... | collective-permute-start | bytes 196616 | tf_op jit(solution)/shard_map/ppermute | solution.py:307
  8.8 9.8 %collective-permute-start.1 = (f32[4,104,128]{2,1,0:T(8,128)S(1)}, f32[4,104,128]{2,1,0:T(8,128)S(1)}, u32[]{:S(2)}, u32[]{:S(2)}) collective-permute-start(f32[4,104,128]{2,1,0:T(8,128)S(1)} %get-tuple-element.66), channel_id=1, source_target_pairs={{0,16},{1,17},{2,18},{3,19},{4,20},{5,21},{6,22},{7,23},{8,24},{9,... | collective-permute-start | bytes 638984 | tf_op jit(solution)/shard_map/ppermute | solution.py:307
  10.8 10.7 %collective-permute-start.3 = (f32[4,104,128]{2,1,0:T(8,128)S(1)}, f32[4,104,128]{2,1,0:T(8,128)S(1)}, u32[]{:S(2)}, u32[]{:S(2)}) collective-permute-start(f32[4,104,128]{2,1,0:T(8,128)S(1)} %get-tuple-element.67), channel_id=1, source_target_pairs={{0,1},{1,0},{2,3},{3,2},{4,5},{5,4},{6,7},{7,6},{8,9},{9,8},{10,11... | collective-permute-start | bytes 638984 | tf_op jit(solution)/shard_map/ppermute | solution.py:307
  12.3 10.2 %collective-permute-start.2 = (f32[4,104,128]{2,1,0:T(8,128)S(1)}, f32[4,104,128]{2,1,0:T(8,128)S(1)}, u32[]{:S(2)}, u32[]{:S(2)}) collective-permute-start(f32[4,104,128]{2,1,0:T(8,128)S(1)} %get-tuple-element.68), channel_id=1, source_target_pairs={{0,17},{1,16},{2,19},{3,18},{4,21},{5,20},{6,23},{7,22},{8,25},{9,... | collective-permute-start | bytes 638984 | tf_op jit(solution)/shard_map/ppermute | solution.py:307
  14.5 11.8 %collective-permute-start.10 = (f32[4,32,128]{2,1,0:T(8,128)S(1)}, f32[4,32,128]{2,1,0:T(8,128)S(1)}, u32[]{:S(2)}, u32[]{:S(2)}) collective-permute-start(f32[4,32,128]{2,1,0:T(8,128)S(1)} %get-tuple-element.46), channel_id=1, source_target_pairs={{0,2},{1,3},{2,0},{3,1},{4,6},{5,7},{6,4},{7,5},{8,10},{9,11},{10,... | collective-permute-start | bytes 196616 | tf_op jit(solution)/shard_map/ppermute | solution.py:307
  16.0 11.1 %collective-permute-start.11 = (f32[4,32,128]{2,1,0:T(8,128)S(1)}, f32[4,32,128]{2,1,0:T(8,128)S(1)}, u32[]{:S(2)}, u32[]{:S(2)}) collective-permute-start(f32[4,32,128]{2,1,0:T(8,128)S(1)} %get-tuple-element.47), channel_id=1, source_target_pairs={{0,4},{1,5},{2,6},{3,7},{4,0},{5,1},{6,2},{7,3},{8,12},{9,13},{10,... | collective-permute-start | bytes 196616 | tf_op jit(solution)/shard_map/ppermute | solution.py:307
  18.6 8.5 %collective-permute-start.12 = (f32[4,32,128]{2,1,0:T(8,128)S(1)}, f32[4,32,128]{2,1,0:T(8,128)S(1)}, u32[]{:S(2)}, u32[]{:S(2)}) collective-permute-start(f32[4,32,128]{2,1,0:T(8,128)S(1)} %get-tuple-element.48), channel_id=1, source_target_pairs={{0,6},{1,7},{2,4},{3,5},{4,2},{5,3},{6,0},{7,1},{8,14},{9,15},{10,... | collective-permute-start | bytes 196616 | tf_op jit(solution)/shard_map/ppermute | solution.py:307
  22.6 7.9 %collective-permute-start.6 = (f32[104,128]{1,0:T(8,128)S(1)}, f32[104,128]{1,0:T(8,128)S(1)}, u32[]{:S(2)}, u32[]{:S(2)}) collective-permute-start(f32[104,128]{1,0:T(8,128)S(1)} %get-tuple-element.70.refs_2_), channel_id=1, source_target_pairs={{0,6},{1,7},{2,4},{3,5},{4,2},{5,3},{6,0},{7,1},{8,14},{9,15},{10,... | collective-permute-start | bytes 159752 | tf_op jit(solution)/shard_map/ppermute | solution.py:307
  26.3 5.0 %collective-permute-start.5 = (f32[104,128]{1,0:T(8,128)S(1)}, f32[104,128]{1,0:T(8,128)S(1)}, u32[]{:S(2)}, u32[]{:S(2)}) collective-permute-start(f32[104,128]{1,0:T(8,128)S(1)} %get-tuple-element.71.refs_1_), channel_id=1, source_target_pairs={{0,4},{1,5},{2,6},{3,7},{4,0},{5,1},{6,2},{7,3},{8,12},{9,13},{10,... | collective-permute-start | bytes 159752 | tf_op jit(solution)/shard_map/ppermute | solution.py:307
  26.3 4.2 %collective-permute-start.4 = (f32[104,128]{1,0:T(8,128)S(1)}, f32[104,128]{1,0:T(8,128)S(1)}, u32[]{:S(2)}, u32[]{:S(2)}) collective-permute-start(f32[104,128]{1,0:T(8,128)S(1)} %shard_map.104), channel_id=1, source_target_pairs={{0,2},{1,3},{2,0},{3,1},{4,6},{5,7},{6,4},{7,5},{8,10},{9,11},{10,... | collective-permute-start | bytes 159752 | tf_op jit(solution)/shard_map/ppermute | solution.py:307
  28.6 2.8 %collective-permute-start.13 = (f32[8,32,128]{2,1,0:T(8,128)S(1)}, f32[8,32,128]{2,1,0:T(8,128)S(1)}, u32[]{:S(2)}, u32[]{:S(2)}) collective-permute-start(f32[8,32,128]{2,1,0:T(8,128)S(1)} %get-tuple-element.50), channel_id=1, source_target_pairs={{0,8},{1,9},{2,10},{3,11},{4,12},{5,13},{6,14},{7,15},{8,0},{9,1},... | collective-permute-start | bytes 393224 | tf_op jit(solution)/shard_map/ppermute | solution.py:307
  31.4 6.9 %collective-permute-start.17 = (f32[168,128]{1,0:T(8,128)S(1)}, f32[168,128]{1,0:T(8,128)S(1)}, u32[]{:S(2)}, u32[]{:S(2)}) collective-permute-start(f32[168,128]{1,0:T(8,128)S(1)} %get-tuple-element.51.refs_2_), channel_id=1, source_target_pairs={{0,2},{1,3},{2,0},{3,1},{4,6},{5,7},{6,4},{7,5},{8,10},{9,11},{10,... | collective-permute-start | bytes 258056 | tf_op jit(solution)/shard_map/ppermute | solution.py:307
  31.7 9.5 %collective-permute-start.18 = (f32[168,128]{1,0:T(8,128)S(1)}, f32[168,128]{1,0:T(8,128)S(1)}, u32[]{:S(2)}, u32[]{:S(2)}) collective-permute-start(f32[168,128]{1,0:T(8,128)S(1)} %get-tuple-element.52.refs_3_), channel_id=1, source_target_pairs={{0,4},{1,5},{2,6},{3,7},{4,0},{5,1},{6,2},{7,3},{8,12},{9,13},{10,... | collective-permute-start | bytes 258056 | tf_op jit(solution)/shard_map/ppermute | solution.py:307
  34.3 7.0 %collective-permute-start.19 = (f32[168,128]{1,0:T(8,128)S(1)}, f32[168,128]{1,0:T(8,128)S(1)}, u32[]{:S(2)}, u32[]{:S(2)}) collective-permute-start(f32[168,128]{1,0:T(8,128)S(1)} %get-tuple-element.53.refs_4_), channel_id=1, source_target_pairs={{0,6},{1,7},{2,4},{3,5},{4,2},{5,3},{6,0},{7,1},{8,14},{9,15},{10,... | collective-permute-start | bytes 258056 | tf_op jit(solution)/shard_map/ppermute | solution.py:307
  35.8 7.9 %collective-permute-start.16 = (f32[136,128]{1,0:T(8,128)S(1)}, f32[136,128]{1,0:T(8,128)S(1)}, u32[]{:S(2)}, u32[]{:S(2)}) collective-permute-start(f32[136,128]{1,0:T(8,128)S(1)} %get-tuple-element.55), channel_id=1, source_target_pairs={{0,17},{1,16},{2,19},{3,18},{4,21},{5,20},{6,23},{7,22},{8,25},{9,... | collective-permute-start | bytes 208904 | tf_op jit(solution)/shard_map/ppermute | solution.py:307
  37.6 7.2 %collective-permute-start.14 = (f32[136,128]{1,0:T(8,128)S(1)}, f32[136,128]{1,0:T(8,128)S(1)}, u32[]{:S(2)}, u32[]{:S(2)}) collective-permute-start(f32[136,128]{1,0:T(8,128)S(1)} %get-tuple-element.55), channel_id=1, source_target_pairs={{0,1},{1,0},{2,3},{3,2},{4,5},{5,4},{6,7},{7,6},{8,9},{9,8},{10,11... | collective-permute-start | bytes 208904 | tf_op jit(solution)/shard_map/ppermute | solution.py:307
  38.3 6.6 %collective-permute-start.15 = (f32[136,128]{1,0:T(8,128)S(1)}, f32[136,128]{1,0:T(8,128)S(1)}, u32[]{:S(2)}, u32[]{:S(2)}) collective-permute-start(f32[136,128]{1,0:T(8,128)S(1)} %get-tuple-element.54.refs_1_), channel_id=1, source_target_pairs={{0,16},{1,17},{2,18},{3,19},{4,20},{5,21},{6,22},{7,23},{8,24},{9,... | collective-permute-start | bytes 208904 | tf_op jit(solution)/shard_map/ppermute | solution.py:307
  41.3 8.3 %collective-permute-start.22 = (f32[408,128]{1,0:T(8,128)S(1)}, f32[408,128]{1,0:T(8,128)S(1)}, u32[]{:S(2)}, u32[]{:S(2)}) collective-permute-start(f32[408,128]{1,0:T(8,128)S(1)} %get-tuple-element.57), channel_id=1, source_target_pairs={{0,17},{1,16},{2,19},{3,18},{4,21},{5,20},{6,23},{7,22},{8,25},{9,... | collective-permute-start | bytes 626696 | tf_op jit(solution)/shard_map/ppermute | solution.py:307
  43.1 8.1 %collective-permute-start.20 = (f32[408,128]{1,0:T(8,128)S(1)}, f32[408,128]{1,0:T(8,128)S(1)}, u32[]{:S(2)}, u32[]{:S(2)}) collective-permute-start(f32[408,128]{1,0:T(8,128)S(1)} %get-tuple-element.57), channel_id=1, source_target_pairs={{0,1},{1,0},{2,3},{3,2},{4,5},{5,4},{6,7},{7,6},{8,9},{9,8},{10,11... | collective-permute-start | bytes 626696 | tf_op jit(solution)/shard_map/ppermute | solution.py:307
  43.8 8.0 %collective-permute-start.21 = (f32[408,128]{1,0:T(8,128)S(1)}, f32[408,128]{1,0:T(8,128)S(1)}, u32[]{:S(2)}, u32[]{:S(2)}) collective-permute-start(f32[408,128]{1,0:T(8,128)S(1)} %get-tuple-element.56.refs_5_), channel_id=1, source_target_pairs={{0,16},{1,17},{2,18},{3,19},{4,20},{5,21},{6,22},{7,23},{8,24},{9,... | collective-permute-start | bytes 626696 | tf_op jit(solution)/shard_map/ppermute | solution.py:307
  44.9 6.9 %copy-start = (s32[4,24]{1,0:T(4,128)S(1)}, s32[4,24]{1,0:T(4,128)}, u32[]{:S(2)}) copy-start(s32[4,24]{1,0:T(4,128)} %refs_0_.7) | copy-start | bytes 1156
  44.9 8.0 %collective-permute-start.23 = (f32[4,136,128]{2,1,0:T(8,128)S(1)}, f32[4,136,128]{2,1,0:T(8,128)S(1)}, u32[]{:S(2)}, u32[]{:S(2)}) collective-permute-start(f32[4,136,128]{2,1,0:T(8,128)S(1)} %pad_maximum_fusion), channel_id=1, source_target_pairs={{0,8},{1,9},{2,10},{3,11},{4,12},{5,13},{6,14},{7,15},{8,0},{9,1},... | collective-permute-start | bytes 835592 | tf_op jit(solution)/shard_map/ppermute | solution.py:307
  45.0 7.9 %collective-permute-start.24 = (f32[408,128]{1,0:T(8,128)S(1)}, f32[408,128]{1,0:T(8,128)S(1)}, u32[]{:S(2)}, u32[]{:S(2)}) collective-permute-start(f32[408,128]{1,0:T(8,128)S(1)} %get-tuple-element.56.refs_5_), channel_id=1, source_target_pairs={{0,8},{1,9},{2,10},{3,11},{4,12},{5,13},{6,14},{7,15},{8,0},{9,1},... | collective-permute-start | bytes 626696 | tf_op jit(solution)/shard_map/ppermute | solution.py:307
  49.7 3.3 %collective-permute-start.27 = (f32[408,128]{1,0:T(8,128)S(1)}, f32[408,128]{1,0:T(8,128)S(1)}, u32[]{:S(2)}, u32[]{:S(2)}) collective-permute-start(f32[408,128]{1,0:T(8,128)S(1)} %collective-permute-done.22.refs_8_), channel_id=1, source_target_pairs={{0,8},{1,9},{2,10},{3,11},{4,12},{5,13},{6,14},{7,15},{8,0},{9,1},... | collective-permute-start | bytes 626696 | tf_op jit(solution)/shard_map/ppermute | solution.py:307
  51.2 1.7 %collective-permute-start.25 = (f32[408,128]{1,0:T(8,128)S(1)}, f32[408,128]{1,0:T(8,128)S(1)}, u32[]{:S(2)}, u32[]{:S(2)}) collective-permute-start(f32[408,128]{1,0:T(8,128)S(1)} %collective-permute-done.20.refs_6_), channel_id=1, source_target_pairs={{0,8},{1,9},{2,10},{3,11},{4,12},{5,13},{6,14},{7,15},{8,0},{9,1},... | collective-permute-start | bytes 626696 | tf_op jit(solution)/shard_map/ppermute | solution.py:307
  51.8 1.5 %collective-permute-start.26 = (f32[408,128]{1,0:T(8,128)S(1)}, f32[408,128]{1,0:T(8,128)S(1)}, u32[]{:S(2)}, u32[]{:S(2)}) collective-permute-start(f32[408,128]{1,0:T(8,128)S(1)} %collective-permute-done.21.refs_7_), channel_id=1, source_target_pairs={{0,8},{1,9},{2,10},{3,11},{4,12},{5,13},{6,14},{7,15},{8,0},{9,1},... | collective-permute-start | bytes 626696 | tf_op jit(solution)/shard_map/ppermute | solution.py:307

commit v11 on v10

--- a/solution.py
+++ b/solution.py
@@ -353,8 +353,8 @@
     blocks = call(
         stack_kernel, [((4, 32, 128), F32)] * 3, [], *got, flops=STACK_FLOPS, after=(total,) if AFTER_CORE else ()
     )
-    far = [swap(blocks[z - 1], 0, 2 * z) for z in range(1, 4)]
-    by_y, by_both, by_x = swap(total[8:12], 2, 0), swap(total[12:16], 2, 1), swap(total[4:8], 0, 1)
+    far = [swap(blocks[z - 1], 0, 2 * z) for z in (3, 2, 1)][::-1]
+    by_x, by_both, by_y = swap(total[4:8], 0, 1), swap(total[12:16], 2, 1), swap(total[8:12], 2, 0)
     total = total[0:4] + by_y + by_both + by_x
     plane_sum = total
     z2, z3 = swap(total[2], 0, 4), swap(total[3], 0, 6)

time: 56.3 us -> 56.3 us (level)
  no operation moved by 1% of the time
where the time goes in v11:
time: 56.3 us; the launch traced here: 55.7 us
  starting transfers between devices  32.1 us (57%)
  waiting for transfers between devices  14.1 us (25%)
  Pallas kernels  6.59 us (12%)
  local copies, waits for them, and re-layouts  1.85 us (3%)
  between operations  0.85 us (2%)
    ppermute x28, starting transfers between devices, swap(): return lax.ppermute(value, AXES, pairs)  32.1 us
    ppermute x28, waiting for transfers between devices, swap(): return lax.ppermute(value, AXES, pairs)  14.1 us
    pallas_call x10, Pallas kernels, call(): pl.pallas_call(run, out_shape=[jax.ShapeDtypeStruct(shape, kind) for shap...  6.59 us
    unnamed x14, local copies, waits for them, and re-layouts  1.79 us
  transfers between devices with their start and end apart: 28, of which 9 were waited for; matrix products, arithmetic and copies ran while one was open for 0% of the time, Pallas kernels for 5%

profile of v11, /device:TPU:0, one launch (start us, length us, event | category | flops | bytes accessed | tf_op | source)
XLA Modules:
  0.0 55.7 jit_solution(17481695080168991211)
XLA Ops:
  0.7 1.0 %copy-done.3 = bf16[2,8,8,512]{3,2,1,0:T(8,128)(2,1)S(1)} copy-done((bf16[2,8,8,512]{3,2,1,0:T(8,128)(2,1)S(1)}, bf16[2,8,8,512]{3,2,1,0:T(8,128)(2,1)}, u32[]{:S(2)}) %copy-start.3) | copy-done | bytes 131096
  1.6 0.1 shard_map.103
  1.8 0.0 copy-start.5
  1.8 0.1 copy-done.2
  1.8 0.7 %copy-done.4 = bf16[2,8,8,512]{3,2,1,0:T(8,128)(2,1)S(1)} copy-done((bf16[2,8,8,512]{3,2,1,0:T(8,128)(2,1)S(1)}, bf16[2,8,8,512]{3,2,1,0:T(8,128)(2,1)}, u32[]{:S(2)}) %copy-start.4) | copy-done | bytes 131096
  2.6 1.4 %shard_map.102 = (f32[16,104,128]{2,1,0:T(8,128)S(1)}, f32[16,104,128]{2,1,0:T(8,128)S(1)}) custom-call(bf16[2,8,8,512]{3,2,1,0:T(8,128)(2,1)S(1)} %copy-done.3, bf16[2,8,8,512]{3,2,1,0:T(8,128)(2,1)S(1)} %copy-done.4, bf16[16,32,288]{2,1,0:T(8,128)(2,1)S(1)} %bitcast.30, bf16[512,512]{1,0:T(8,128)(2,1)S(1)} %copy-done.1, f32[1,512]{1,0:T(1,128)S(1)} %bitcast.31, ...), custom_call_target="tpu_custom_call" | custom-call | flops 4000000000 | tf_op jit(solution)/shard_map/pallas_call | solution.py:41
  4.0 0.5 collective-permute-start
  4.5 2.6 %collective-permute-start.7 = (f32[4,32,128]{2,1,0:T(8,128)S(1)}, f32[4,32,128]{2,1,0:T(8,128)S(1)}, u32[]{:S(2)}, u32[]{:S(2)}) collective-permute-start(f32[4,32,128]{2,1,0:T(8,128)S(1)} %get-tuple-element.43), channel_id=1, source_target_pairs={{0,1},{1,0},{2,3},{3,2},{4,5},{5,4},{6,7},{7,6},{8,9},{9,8},{10,11... | collective-permute-start | bytes 196616 | tf_op jit(solution)/shard_map/ppermute | solution.py:307
  7.1 1.5 %collective-permute-start.8 = (f32[4,32,128]{2,1,0:T(8,128)S(1)}, f32[4,32,128]{2,1,0:T(8,128)S(1)}, u32[]{:S(2)}, u32[]{:S(2)}) collective-permute-start(f32[4,32,128]{2,1,0:T(8,128)S(1)} %get-tuple-element.44), channel_id=1, source_target_pairs={{0,16},{1,17},{2,18},{3,19},{4,20},{5,21},{6,22},{7,23},{8,24},{9,... | collective-permute-start | bytes 196616 | tf_op jit(solution)/shard_map/ppermute | solution.py:307
  8.6 0.0 collective-permute-start.9
  8.6 0.0 collective-permute-done
  8.6 0.1 add.24.refs_4_
  8.8 2.1 %collective-permute-start.1 = (f32[4,104,128]{2,1,0:T(8,128)S(1)}, f32[4,104,128]{2,1,0:T(8,128)S(1)}, u32[]{:S(2)}, u32[]{:S(2)}) collective-permute-start(f32[4,104,128]{2,1,0:T(8,128)S(1)} %get-tuple-element.66), channel_id=1, source_target_pairs={{0,16},{1,17},{2,18},{3,19},{4,20},{5,21},{6,22},{7,23},{8,24},{9,... | collective-permute-start | bytes 638984 | tf_op jit(solution)/shard_map/ppermute | solution.py:307
  10.8 1.5 %collective-permute-start.3 = (f32[4,104,128]{2,1,0:T(8,128)S(1)}, f32[4,104,128]{2,1,0:T(8,128)S(1)}, u32[]{:S(2)}, u32[]{:S(2)}) collective-permute-start(f32[4,104,128]{2,1,0:T(8,128)S(1)} %get-tuple-element.67), channel_id=1, source_target_pairs={{0,1},{1,0},{2,3},{3,2},{4,5},{5,4},{6,7},{7,6},{8,9},{9,8},{10,11... | collective-permute-start | bytes 638984 | tf_op jit(solution)/shard_map/ppermute | solution.py:307
  12.3 0.0 collective-permute-done.7.refs_1_
  12.3 0.2 collective-permute-start.2
  12.5 0.0 collective-permute-done.8.refs_2_
  12.5 2.0 %collective-permute-done.9.refs_3_ = f32[4,32,128]{2,1,0:T(8,128)S(1)} collective-permute-done((f32[4,32,128]{2,1,0:T(8,128)S(1)}, f32[4,32,128]{2,1,0:T(8,128)S(1)}, u32[]{:S(2)}, u32[]{:S(2)}) %collective-permute-start.9) | collective-permute-done | bytes 65568 | tf_op jit(solution)/shard_map/ppermute | solution.py:307
  14.5 1.5 %collective-permute-start.10 = (f32[4,32,128]{2,1,0:T(8,128)S(1)}, f32[4,32,128]{2,1,0:T(8,128)S(1)}, u32[]{:S(2)}, u32[]{:S(2)}) collective-permute-start(f32[4,32,128]{2,1,0:T(8,128)S(1)} %get-tuple-element.46), channel_id=1, source_target_pairs={{0,2},{1,3},{2,0},{3,1},{4,6},{5,7},{6,4},{7,5},{8,10},{9,11},{10,... | collective-permute-start | bytes 196616 | tf_op jit(solution)/shard_map/ppermute | solution.py:307
  16.0 2.6 %collective-permute-start.11 = (f32[4,32,128]{2,1,0:T(8,128)S(1)}, f32[4,32,128]{2,1,0:T(8,128)S(1)}, u32[]{:S(2)}, u32[]{:S(2)}) collective-permute-start(f32[4,32,128]{2,1,0:T(8,128)S(1)} %get-tuple-element.47), channel_id=1, source_target_pairs={{0,4},{1,5},{2,6},{3,7},{4,0},{5,1},{6,2},{7,3},{8,12},{9,13},{10,... | collective-permute-start | bytes 196616 | tf_op jit(solution)/shard_map/ppermute | solution.py:307
  18.6 0.0 collective-permute-done.1
  18.6 2.9 %collective-permute-start.12 = (f32[4,32,128]{2,1,0:T(8,128)S(1)}, f32[4,32,128]{2,1,0:T(8,128)S(1)}, u32[]{:S(2)}, u32[]{:S(2)}) collective-permute-start(f32[4,32,128]{2,1,0:T(8,128)S(1)} %get-tuple-element.48), channel_id=1, source_target_pairs={{0,6},{1,7},{2,4},{3,5},{4,2},{5,3},{6,0},{7,1},{8,14},{9,15},{10,... | collective-permute-start | bytes 196616 | tf_op jit(solution)/shard_map/ppermute | solution.py:307
  21.6 0.0 collective-permute-done.3
  21.6 0.9 %collective-permute-done.2 = f32[4,104,128]{2,1,0:T(8,128)S(1)} collective-permute-done((f32[4,104,128]{2,1,0:T(8,128)S(1)}, f32[4,104,128]{2,1,0:T(8,128)S(1)}, u32[]{:S(2)}, u32[]{:S(2)}) %collective-permute-start.2) | collective-permute-done | bytes 213024 | tf_op jit(solution)/shard_map/ppermute | solution.py:307
  22.5 0.1 fusion.1.refs_7_
  22.6 3.7 %collective-permute-start.6 = (f32[104,128]{1,0:T(8,128)S(1)}, f32[104,128]{1,0:T(8,128)S(1)}, u32[]{:S(2)}, u32[]{:S(2)}) collective-permute-start(f32[104,128]{1,0:T(8,128)S(1)} %get-tuple-element.70.refs_2_), channel_id=1, source_target_pairs={{0,6},{1,7},{2,4},{3,5},{4,2},{5,3},{6,0},{7,1},{8,14},{9,15},{10,... | collective-permute-start | bytes 159752 | tf_op jit(solution)/shard_map/ppermute | solution.py:307
  26.3 0.0 collective-permute-start.5
  26.3 0.0 collective-permute-done.10.refs_4_
  26.3 0.8 %collective-permute-start.4 = (f32[104,128]{1,0:T(8,128)S(1)}, f32[104,128]{1,0:T(8,128)S(1)}, u32[]{:S(2)}, u32[]{:S(2)}) collective-permute-start(f32[104,128]{1,0:T(8,128)S(1)} %shard_map.104), channel_id=1, source_target_pairs={{0,2},{1,3},{2,0},{3,1},{4,6},{5,7},{6,4},{7,5},{8,10},{9,11},{10,... | collective-permute-start | bytes 159752 | tf_op jit(solution)/shard_map/ppermute | solution.py:307
  27.1 0.0 collective-permute-done.11.refs_5_
  27.1 0.0 collective-permute-done.12.refs_6_
  27.1 1.4 %shard_map.106 = (f32[8,32,128]{2,1,0:T(8,128)S(1)}, f32[8,32,128]{2,1,0:T(8,128)S(1)}) custom-call(f32[4,32,128]{2,1,0:T(8,128)S(1)} %get-tuple-element.42.refs_0_, f32[4,32,128]{2,1,0:T(8,128)S(1)} %collective-permute-done.7.refs_1_, f32[4,32,128]{2,1,0:T(8,128)S(1)} %collective-permute-done.8.refs_2_, f32[4,32,128]{2,1,0:T(8,128)S(1)} %collective-permute-done.9.refs_3_, ...), custom_call_target="tpu_custom_call" | custom-call | flops 4000000000 | tf_op jit(solution)/shard_map/pallas_call | solution.py:41
  28.6 0.1 collective-permute-start.13
  28.6 1.8 %collective-permute-done.4 = f32[104,128]{1,0:T(8,128)S(1)} collective-permute-done((f32[104,128]{1,0:T(8,128)S(1)}, f32[104,128]{1,0:T(8,128)S(1)}, u32[]{:S(2)}, u32[]{:S(2)}) %collective-permute-start.4) | collective-permute-done | bytes 53280 | tf_op jit(solution)/shard_map/ppermute | solution.py:307
  30.5 0.0 collective-permute-done.6
  30.5 0.8 %collective-permute-done.5 = f32[104,128]{1,0:T(8,128)S(1)} collective-permute-done((f32[104,128]{1,0:T(8,128)S(1)}, f32[104,128]{1,0:T(8,128)S(1)}, u32[]{:S(2)}, u32[]{:S(2)}) %collective-permute-start.5) | collective-permute-done | bytes 53280 | tf_op jit(solution)/shard_map/ppermute | solution.py:307
  31.3 0.0 collective-permute-done.13
  31.4 0.4 collective-permute-start.17
  31.7 2.5 %collective-permute-start.18 = (f32[168,128]{1,0:T(8,128)S(1)}, f32[168,128]{1,0:T(8,128)S(1)}, u32[]{:S(2)}, u32[]{:S(2)}) collective-permute-start(f32[168,128]{1,0:T(8,128)S(1)} %get-tuple-element.52.refs_3_), channel_id=1, source_target_pairs={{0,4},{1,5},{2,6},{3,7},{4,0},{5,1},{6,2},{7,3},{8,12},{9,13},{10,... | collective-permute-start | bytes 258056 | tf_op jit(solution)/shard_map/ppermute | solution.py:307
  34.3 1.6 %collective-permute-start.19 = (f32[168,128]{1,0:T(8,128)S(1)}, f32[168,128]{1,0:T(8,128)S(1)}, u32[]{:S(2)}, u32[]{:S(2)}) collective-permute-start(f32[168,128]{1,0:T(8,128)S(1)} %get-tuple-element.53.refs_4_), channel_id=1, source_target_pairs={{0,6},{1,7},{2,4},{3,5},{4,2},{5,3},{6,0},{7,1},{8,14},{9,15},{10,... | collective-permute-start | bytes 258056 | tf_op jit(solution)/shard_map/ppermute | solution.py:307
  35.8 1.8 %collective-permute-start.16 = (f32[136,128]{1,0:T(8,128)S(1)}, f32[136,128]{1,0:T(8,128)S(1)}, u32[]{:S(2)}, u32[]{:S(2)}) collective-permute-start(f32[136,128]{1,0:T(8,128)S(1)} %get-tuple-element.55), channel_id=1, source_target_pairs={{0,17},{1,16},{2,19},{3,18},{4,21},{5,20},{6,23},{7,22},{8,25},{9,... | collective-permute-start | bytes 208904 | tf_op jit(solution)/shard_map/ppermute | solution.py:307
  37.6 0.6 %collective-permute-start.14 = (f32[136,128]{1,0:T(8,128)S(1)}, f32[136,128]{1,0:T(8,128)S(1)}, u32[]{:S(2)}, u32[]{:S(2)}) collective-permute-start(f32[136,128]{1,0:T(8,128)S(1)} %get-tuple-element.55), channel_id=1, source_target_pairs={{0,1},{1,0},{2,3},{3,2},{4,5},{5,4},{6,7},{7,6},{8,9},{9,8},{10,11... | collective-permute-start | bytes 208904 | tf_op jit(solution)/shard_map/ppermute | solution.py:307
  38.3 0.0 collective-permute-done.17.refs_0_
  38.3 1.1 %collective-permute-start.15 = (f32[136,128]{1,0:T(8,128)S(1)}, f32[136,128]{1,0:T(8,128)S(1)}, u32[]{:S(2)}, u32[]{:S(2)}) collective-permute-start(f32[136,128]{1,0:T(8,128)S(1)} %get-tuple-element.54.refs_1_), channel_id=1, source_target_pairs={{0,16},{1,17},{2,18},{3,19},{4,20},{5,21},{6,22},{7,23},{8,24},{9,... | collective-permute-start | bytes 208904 | tf_op jit(solution)/shard_map/ppermute | solution.py:307
  39.4 1.9 %collective-permute-done.18.refs_1_ = f32[168,128]{1,0:T(8,128)S(1)} collective-permute-done((f32[168,128]{1,0:T(8,128)S(1)}, f32[168,128]{1,0:T(8,128)S(1)}, u32[]{:S(2)}, u32[]{:S(2)}) %collective-permute-start.18) | collective-permute-done | bytes 86048 | tf_op jit(solution)/shard_map/ppermute | solution.py:307
  41.3 0.0 collective-permute-done.19.refs_2_
  41.3 1.8 %collective-permute-start.22 = (f32[408,128]{1,0:T(8,128)S(1)}, f32[408,128]{1,0:T(8,128)S(1)}, u32[]{:S(2)}, u32[]{:S(2)}) collective-permute-start(f32[408,128]{1,0:T(8,128)S(1)} %get-tuple-element.57), channel_id=1, source_target_pairs={{0,17},{1,16},{2,19},{3,18},{4,21},{5,20},{6,23},{7,22},{8,25},{9,... | collective-permute-start | bytes 626696 | tf_op jit(solution)/shard_map/ppermute | solution.py:307
  43.1 0.7 %collective-permute-start.20 = (f32[408,128]{1,0:T(8,128)S(1)}, f32[408,128]{1,0:T(8,128)S(1)}, u32[]{:S(2)}, u32[]{:S(2)}) collective-permute-start(f32[408,128]{1,0:T(8,128)S(1)} %get-tuple-element.57), channel_id=1, source_target_pairs={{0,1},{1,0},{2,3},{3,2},{4,5},{5,4},{6,7},{7,6},{8,9},{9,8},{10,11... | collective-permute-start | bytes 626696 | tf_op jit(solution)/shard_map/ppermute | solution.py:307
  43.8 0.0 collective-permute-done.16.refs_4_
  43.8 1.1 %collective-permute-start.21 = (f32[408,128]{1,0:T(8,128)S(1)}, f32[408,128]{1,0:T(8,128)S(1)}, u32[]{:S(2)}, u32[]{:S(2)}) collective-permute-start(f32[408,128]{1,0:T(8,128)S(1)} %get-tuple-element.56.refs_5_), channel_id=1, source_target_pairs={{0,16},{1,17},{2,18},{3,19},{4,20},{5,21},{6,22},{7,23},{8,24},{9,... | collective-permute-start | bytes 626696 | tf_op jit(solution)/shard_map/ppermute | solution.py:307
  44.9 0.0 collective-permute-done.14.refs_2_
  44.9 0.0 collective-permute-done.15.refs_3_
  44.9 0.1 collective-permute-start.23
  45.0 0.5 collective-permute-start.24
  45.5 4.2 %collective-permute-done.22.refs_8_ = f32[408,128]{1,0:T(8,128)S(1)} collective-permute-done((f32[408,128]{1,0:T(8,128)S(1)}, f32[408,128]{1,0:T(8,128)S(1)}, u32[]{:S(2)}, u32[]{:S(2)}) %collective-permute-start.22) | collective-permute-done | bytes 208928 | tf_op jit(solution)/shard_map/ppermute | solution.py:307
  49.7 1.6 %collective-permute-done.20.refs_6_ = f32[408,128]{1,0:T(8,128)S(1)} collective-permute-done((f32[408,128]{1,0:T(8,128)S(1)}, f32[408,128]{1,0:T(8,128)S(1)}, u32[]{:S(2)}, u32[]{:S(2)}) %collective-permute-start.20) | collective-permute-done | bytes 208928 | tf_op jit(solution)/shard_map/ppermute | solution.py:307
  51.2 0.6 %collective-permute-done.21.refs_7_ = f32[408,128]{1,0:T(8,128)S(1)} collective-permute-done((f32[408,128]{1,0:T(8,128)S(1)}, f32[408,128]{1,0:T(8,128)S(1)}, u32[]{:S(2)}, u32[]{:S(2)}) %collective-permute-start.21) | collective-permute-done | bytes 208928 | tf_op jit(solution)/shard_map/ppermute | solution.py:307
  51.8 0.0 collective-permute-start.26
  51.8 1.1 %shard_map.110 = (f32[8,32,288]{2,1,0:T(8,128)S(1)}, f32[256,512]{1,0:T(8,128)S(1)}, f32[8,32,32]{2,1,0:T(8,128)S(1)}, f32[6,24,288]{2,1,0:T(8,128)S(1)}) custom-call(s32[4,24]{1,0:T(4,128)S(1)} %copy-done, f32[136,128]{1,0:T(8,128)S(1)} %get-tuple-element.54.refs_1_, f32[136,128]{1,0:T(8,128)S(1)} %collective-permute-done.14.refs_2_, ...), custom_call_target="tpu_custom_call" | custom-call | flops 1000000000 | tf_op jit(solution)/shard_map/pallas_call | solution.py:41
  52.9 0.0 collective-permute-done.24.refs_6_
  52.9 0.0 collective-permute-done.23.refs_5_
  52.9 0.0 collective-permute-done.25.refs_7_
  52.9 0.3 collective-permute-done.26.refs_8_
  53.2 2.5 %shard_map.111 = (f32[16,32,288]{2,1,0:T(8,128)}, f32[512,512]{1,0:T(8,128)}, f32[16,32,32]{2,1,0:T(8,128)}, f32[12,24,288]{2,1,0:T(8,128)}) custom-call(s32[4,24]{1,0:T(4,128)S(1)} %copy-done, f32[8,32,288]{2,1,0:T(8,128)S(1)} %get-tuple-element.58.refs_1_, f32[256,512]{1,0:T(8,128)S(1)} %get-tuple-element.59.refs_2_, ...), custom_call_target="tpu_custom_call" | custom-call | tf_op jit(solution)/shard_map/pallas_call | solution.py:41
  (23 shorter events, 0.2 us)
Async XLA Ops:
  0.6 1.2 %copy-start.1 = (bf16[512,512]{1,0:T(8,128)(2,1)S(1)}, bf16[512,512]{1,0:T(8,128)(2,1)}, u32[]{:S(2)}) copy-start(bf16[512,512]{1,0:T(8,128)(2,1)} %refs_3_.1) | copy-start | bytes 1572868
  0.6 1.2 %copy-start.2 = (bf16[16,288,32]{1,2,0:T(8,128)(2,1)S(1)}, bf16[16,288,32]{1,2,0:T(8,128)(2,1)}, u32[]{:S(2)}) copy-start(bf16[16,288,32]{1,2,0:T(8,128)(2,1)} %param.9) | copy-start | bytes 884740
  0.7 1.0 %copy-start.3 = (bf16[2,8,8,512]{3,2,1,0:T(8,128)(2,1)S(1)}, bf16[2,8,8,512]{3,2,1,0:T(8,128)(2,1)}, u32[]{:S(2)}) copy-start(bf16[2,8,8,512]{3,2,1,0:T(8,128)(2,1)} %refs_0_.5) | copy-start | bytes 393220
  1.6 1.0 %copy-start.4 = (bf16[2,8,8,512]{3,2,1,0:T(8,128)(2,1)S(1)}, bf16[2,8,8,512]{3,2,1,0:T(8,128)(2,1)}, u32[]{:S(2)}) copy-start(bf16[2,8,8,512]{3,2,1,0:T(8,128)(2,1)} %refs_1_.1) | copy-start | bytes 393220
  1.6 1.0 %copy-start.6 = (f32[512]{0:T(512)S(1)}, f32[512]{0:T(512)}, u32[]{:S(2)}) copy-start(f32[512]{0:T(512)} %param.12) | copy-start | bytes 6148
  1.8 0.8 %copy-start.5 = (f32[512]{0:T(512)S(1)}, f32[512]{0:T(512)}, u32[]{:S(2)}) copy-start(f32[512]{0:T(512)} %param.11) | copy-start | bytes 6148
  4.0 4.6 %collective-permute-start = (f32[16,104,128]{2,1,0:T(8,128)S(1)}, f32[16,104,128]{2,1,0:T(8,128)S(1)}, u32[]{:S(2)}, u32[]{:S(2)}) collective-permute-start(f32[16,104,128]{2,1,0:T(8,128)S(1)} %get-tuple-element.41), channel_id=1, source_target_pairs={{0,8},{1,9},{2,10},{3,11},{4,12},{5,13},{6,14},{7,15},{8,0},{9,1},... | collective-permute-start | bytes 2555912 | tf_op jit(solution)/shard_map/ppermute | solution.py:307
  4.5 7.8 %collective-permute-start.7 = (f32[4,32,128]{2,1,0:T(8,128)S(1)}, f32[4,32,128]{2,1,0:T(8,128)S(1)}, u32[]{:S(2)}, u32[]{:S(2)}) collective-permute-start(f32[4,32,128]{2,1,0:T(8,128)S(1)} %get-tuple-element.43), channel_id=1, source_target_pairs={{0,1},{1,0},{2,3},{3,2},{4,5},{5,4},{6,7},{7,6},{8,9},{9,8},{10,11... | collective-permute-start | bytes 196616 | tf_op jit(solution)/shard_map/ppermute | solution.py:307
  7.1 5.4 %collective-permute-start.8 = (f32[4,32,128]{2,1,0:T(8,128)S(1)}, f32[4,32,128]{2,1,0:T(8,128)S(1)}, u32[]{:S(2)}, u32[]{:S(2)}) collective-permute-start(f32[4,32,128]{2,1,0:T(8,128)S(1)} %get-tuple-element.44), channel_id=1, source_target_pairs={{0,16},{1,17},{2,18},{3,19},{4,20},{5,21},{6,22},{7,23},{8,24},{9,... | collective-permute-start | bytes 196616 | tf_op jit(solution)/shard_map/ppermute | solution.py:307
  8.6 5.9 %collective-permute-start.9 = (f32[4,32,128]{2,1,0:T(8,128)S(1)}, f32[4,32,128]{2,1,0:T(8,128)S(1)}, u32[]{:S(2)}, u32[]{:S(2)}) collective-permute-start(f32[4,32,128]{2,1,0:T(8,128)S(1)} %get-tuple-element.45), channel_id=1, source_target_pairs={{0,17},{1,16},{2,19},{3,18},{4,21},{5,20},{6,23},{7,22},{8,25},{9,... | collective-permute-start | bytes 196616 | tf_op jit(solution)/shard_map/ppermute | solution.py:307
  8.8 9.8 %collective-permute-start.1 = (f32[4,104,128]{2,1,0:T(8,128)S(1)}, f32[4,104,128]{2,1,0:T(8,128)S(1)}, u32[]{:S(2)}, u32[]{:S(2)}) collective-permute-start(f32[4,104,128]{2,1,0:T(8,128)S(1)} %get-tuple-element.66), channel_id=1, source_target_pairs={{0,16},{1,17},{2,18},{3,19},{4,20},{5,21},{6,22},{7,23},{8,24},{9,... | collective-permute-start | bytes 638984 | tf_op jit(solution)/shard_map/ppermute | solution.py:307
  10.8 10.7 %collective-permute-start.3 = (f32[4,104,128]{2,1,0:T(8,128)S(1)}, f32[4,104,128]{2,1,0:T(8,128)S(1)}, u32[]{:S(2)}, u32[]{:S(2)}) collective-permute-start(f32[4,104,128]{2,1,0:T(8,128)S(1)} %get-tuple-element.67), channel_id=1, source_target_pairs={{0,1},{1,0},{2,3},{3,2},{4,5},{5,4},{6,7},{7,6},{8,9},{9,8},{10,11... | collective-permute-start | bytes 638984 | tf_op jit(solution)/shard_map/ppermute | solution.py:307
  12.3 10.2 %collective-permute-start.2 = (f32[4,104,128]{2,1,0:T(8,128)S(1)}, f32[4,104,128]{2,1,0:T(8,128)S(1)}, u32[]{:S(2)}, u32[]{:S(2)}) collective-permute-start(f32[4,104,128]{2,1,0:T(8,128)S(1)} %get-tuple-element.68), channel_id=1, source_target_pairs={{0,17},{1,16},{2,19},{3,18},{4,21},{5,20},{6,23},{7,22},{8,25},{9,... | collective-permute-start | bytes 638984 | tf_op jit(solution)/shard_map/ppermute | solution.py:307
  14.5 11.8 %collective-permute-start.10 = (f32[4,32,128]{2,1,0:T(8,128)S(1)}, f32[4,32,128]{2,1,0:T(8,128)S(1)}, u32[]{:S(2)}, u32[]{:S(2)}) collective-permute-start(f32[4,32,128]{2,1,0:T(8,128)S(1)} %get-tuple-element.46), channel_id=1, source_target_pairs={{0,2},{1,3},{2,0},{3,1},{4,6},{5,7},{6,4},{7,5},{8,10},{9,11},{10,... | collective-permute-start | bytes 196616 | tf_op jit(solution)/shard_map/ppermute | solution.py:307
  16.0 11.1 %collective-permute-start.11 = (f32[4,32,128]{2,1,0:T(8,128)S(1)}, f32[4,32,128]{2,1,0:T(8,128)S(1)}, u32[]{:S(2)}, u32[]{:S(2)}) collective-permute-start(f32[4,32,128]{2,1,0:T(8,128)S(1)} %get-tuple-element.47), channel_id=1, source_target_pairs={{0,4},{1,5},{2,6},{3,7},{4,0},{5,1},{6,2},{7,3},{8,12},{9,13},{10,... | collective-permute-start | bytes 196616 | tf_op jit(solution)/shard_map/ppermute | solution.py:307
  18.6 8.5 %collective-permute-start.12 = (f32[4,32,128]{2,1,0:T(8,128)S(1)}, f32[4,32,128]{2,1,0:T(8,128)S(1)}, u32[]{:S(2)}, u32[]{:S(2)}) collective-permute-start(f32[4,32,128]{2,1,0:T(8,128)S(1)} %get-tuple-element.48), channel_id=1, source_target_pairs={{0,6},{1,7},{2,4},{3,5},{4,2},{5,3},{6,0},{7,1},{8,14},{9,15},{10,... | collective-permute-start | bytes 196616 | tf_op jit(solution)/shard_map/ppermute | solution.py:307
  22.6 7.9 %collective-permute-start.6 = (f32[104,128]{1,0:T(8,128)S(1)}, f32[104,128]{1,0:T(8,128)S(1)}, u32[]{:S(2)}, u32[]{:S(2)}) collective-permute-start(f32[104,128]{1,0:T(8,128)S(1)} %get-tuple-element.70.refs_2_), channel_id=1, source_target_pairs={{0,6},{1,7},{2,4},{3,5},{4,2},{5,3},{6,0},{7,1},{8,14},{9,15},{10,... | collective-permute-start | bytes 159752 | tf_op jit(solution)/shard_map/ppermute | solution.py:307
  26.3 5.0 %collective-permute-start.5 = (f32[104,128]{1,0:T(8,128)S(1)}, f32[104,128]{1,0:T(8,128)S(1)}, u32[]{:S(2)}, u32[]{:S(2)}) collective-permute-start(f32[104,128]{1,0:T(8,128)S(1)} %get-tuple-element.71.refs_1_), channel_id=1, source_target_pairs={{0,4},{1,5},{2,6},{3,7},{4,0},{5,1},{6,2},{7,3},{8,12},{9,13},{10,... | collective-permute-start | bytes 159752 | tf_op jit(solution)/shard_map/ppermute | solution.py:307
  26.3 4.2 %collective-permute-start.4 = (f32[104,128]{1,0:T(8,128)S(1)}, f32[104,128]{1,0:T(8,128)S(1)}, u32[]{:S(2)}, u32[]{:S(2)}) collective-permute-start(f32[104,128]{1,0:T(8,128)S(1)} %shard_map.104), channel_id=1, source_target_pairs={{0,2},{1,3},{2,0},{3,1},{4,6},{5,7},{6,4},{7,5},{8,10},{9,11},{10,... | collective-permute-start | bytes 159752 | tf_op jit(solution)/shard_map/ppermute | solution.py:307
  28.6 2.8 %collective-permute-start.13 = (f32[8,32,128]{2,1,0:T(8,128)S(1)}, f32[8,32,128]{2,1,0:T(8,128)S(1)}, u32[]{:S(2)}, u32[]{:S(2)}) collective-permute-start(f32[8,32,128]{2,1,0:T(8,128)S(1)} %get-tuple-element.50), channel_id=1, source_target_pairs={{0,8},{1,9},{2,10},{3,11},{4,12},{5,13},{6,14},{7,15},{8,0},{9,1},... | collective-permute-start | bytes 393224 | tf_op jit(solution)/shard_map/ppermute | solution.py:307
  31.4 6.9 %collective-permute-start.17 = (f32[168,128]{1,0:T(8,128)S(1)}, f32[168,128]{1,0:T(8,128)S(1)}, u32[]{:S(2)}, u32[]{:S(2)}) collective-permute-start(f32[168,128]{1,0:T(8,128)S(1)} %get-tuple-element.51.refs_2_), channel_id=1, source_target_pairs={{0,2},{1,3},{2,0},{3,1},{4,6},{5,7},{6,4},{7,5},{8,10},{9,11},{10,... | collective-permute-start | bytes 258056 | tf_op jit(solution)/shard_map/ppermute | solution.py:307
  31.7 9.5 %collective-permute-start.18 = (f32[168,128]{1,0:T(8,128)S(1)}, f32[168,128]{1,0:T(8,128)S(1)}, u32[]{:S(2)}, u32[]{:S(2)}) collective-permute-start(f32[168,128]{1,0:T(8,128)S(1)} %get-tuple-element.52.refs_3_), channel_id=1, source_target_pairs={{0,4},{1,5},{2,6},{3,7},{4,0},{5,1},{6,2},{7,3},{8,12},{9,13},{10,... | collective-permute-start | bytes 258056 | tf_op jit(solution)/shard_map/ppermute | solution.py:307
  34.3 7.0 %collective-permute-start.19 = (f32[168,128]{1,0:T(8,128)S(1)}, f32[168,128]{1,0:T(8,128)S(1)}, u32[]{:S(2)}, u32[]{:S(2)}) collective-permute-start(f32[168,128]{1,0:T(8,128)S(1)} %get-tuple-element.53.refs_4_), channel_id=1, source_target_pairs={{0,6},{1,7},{2,4},{3,5},{4,2},{5,3},{6,0},{7,1},{8,14},{9,15},{10,... | collective-permute-start | bytes 258056 | tf_op jit(solution)/shard_map/ppermute | solution.py:307
  35.8 7.9 %collective-permute-start.16 = (f32[136,128]{1,0:T(8,128)S(1)}, f32[136,128]{1,0:T(8,128)S(1)}, u32[]{:S(2)}, u32[]{:S(2)}) collective-permute-start(f32[136,128]{1,0:T(8,128)S(1)} %get-tuple-element.55), channel_id=1, source_target_pairs={{0,17},{1,16},{2,19},{3,18},{4,21},{5,20},{6,23},{7,22},{8,25},{9,... | collective-permute-start | bytes 208904 | tf_op jit(solution)/shard_map/ppermute | solution.py:307
  37.6 7.2 %collective-permute-start.14 = (f32[136,128]{1,0:T(8,128)S(1)}, f32[136,128]{1,0:T(8,128)S(1)}, u32[]{:S(2)}, u32[]{:S(2)}) collective-permute-start(f32[136,128]{1,0:T(8,128)S(1)} %get-tuple-element.55), channel_id=1, source_target_pairs={{0,1},{1,0},{2,3},{3,2},{4,5},{5,4},{6,7},{7,6},{8,9},{9,8},{10,11... | collective-permute-start | bytes 208904 | tf_op jit(solution)/shard_map/ppermute | solution.py:307
  38.3 6.6 %collective-permute-start.15 = (f32[136,128]{1,0:T(8,128)S(1)}, f32[136,128]{1,0:T(8,128)S(1)}, u32[]{:S(2)}, u32[]{:S(2)}) collective-permute-start(f32[136,128]{1,0:T(8,128)S(1)} %get-tuple-element.54.refs_1_), channel_id=1, source_target_pairs={{0,16},{1,17},{2,18},{3,19},{4,20},{5,21},{6,22},{7,23},{8,24},{9,... | collective-permute-start | bytes 208904 | tf_op jit(solution)/shard_map/ppermute | solution.py:307
  41.3 8.3 %collective-permute-start.22 = (f32[408,128]{1,0:T(8,128)S(1)}, f32[408,128]{1,0:T(8,128)S(1)}, u32[]{:S(2)}, u32[]{:S(2)}) collective-permute-start(f32[408,128]{1,0:T(8,128)S(1)} %get-tuple-element.57), channel_id=1, source_target_pairs={{0,17},{1,16},{2,19},{3,18},{4,21},{5,20},{6,23},{7,22},{8,25},{9,... | collective-permute-start | bytes 626696 | tf_op jit(solution)/shard_map/ppermute | solution.py:307
  43.1 8.1 %collective-permute-start.20 = (f32[408,128]{1,0:T(8,128)S(1)}, f32[408,128]{1,0:T(8,128)S(1)}, u32[]{:S(2)}, u32[]{:S(2)}) collective-permute-start(f32[408,128]{1,0:T(8,128)S(1)} %get-tuple-element.57), channel_id=1, source_target_pairs={{0,1},{1,0},{2,3},{3,2},{4,5},{5,4},{6,7},{7,6},{8,9},{9,8},{10,11... | collective-permute-start | bytes 626696 | tf_op jit(solution)/shard_map/ppermute | solution.py:307
  43.8 8.0 %collective-permute-start.21 = (f32[408,128]{1,0:T(8,128)S(1)}, f32[408,128]{1,0:T(8,128)S(1)}, u32[]{:S(2)}, u32[]{:S(2)}) collective-permute-start(f32[408,128]{1,0:T(8,128)S(1)} %get-tuple-element.56.refs_5_), channel_id=1, source_target_pairs={{0,16},{1,17},{2,18},{3,19},{4,20},{5,21},{6,22},{7,23},{8,24},{9,... | collective-permute-start | bytes 626696 | tf_op jit(solution)/shard_map/ppermute | solution.py:307
  44.9 6.9 %copy-start = (s32[4,24]{1,0:T(4,128)S(1)}, s32[4,24]{1,0:T(4,128)}, u32[]{:S(2)}) copy-start(s32[4,24]{1,0:T(4,128)} %refs_0_.7) | copy-start | bytes 1156
  44.9 8.0 %collective-permute-start.23 = (f32[4,136,128]{2,1,0:T(8,128)S(1)}, f32[4,136,128]{2,1,0:T(8,128)S(1)}, u32[]{:S(2)}, u32[]{:S(2)}) collective-permute-start(f32[4,136,128]{2,1,0:T(8,128)S(1)} %pad_maximum_fusion), channel_id=1, source_target_pairs={{0,8},{1,9},{2,10},{3,11},{4,12},{5,13},{6,14},{7,15},{8,0},{9,1},... | collective-permute-start | bytes 835592 | tf_op jit(solution)/shard_map/ppermute | solution.py:307
  45.0 7.9 %collective-permute-start.24 = (f32[408,128]{1,0:T(8,128)S(1)}, f32[408,128]{1,0:T(8,128)S(1)}, u32[]{:S(2)}, u32[]{:S(2)}) collective-permute-start(f32[408,128]{1,0:T(8,128)S(1)} %get-tuple-element.56.refs_5_), channel_id=1, source_target_pairs={{0,8},{1,9},{2,10},{3,11},{4,12},{5,13},{6,14},{7,15},{8,0},{9,1},... | collective-permute-start | bytes 626696 | tf_op jit(solution)/shard_map/ppermute | solution.py:307
  49.7 3.3 %collective-permute-start.27 = (f32[408,128]{1,0:T(8,128)S(1)}, f32[408,128]{1,0:T(8,128)S(1)}, u32[]{:S(2)}, u32[]{:S(2)}) collective-permute-start(f32[408,128]{1,0:T(8,128)S(1)} %collective-permute-done.22.refs_8_), channel_id=1, source_target_pairs={{0,8},{1,9},{2,10},{3,11},{4,12},{5,13},{6,14},{7,15},{8,0},{9,1},... | collective-permute-start | bytes 626696 | tf_op jit(solution)/shard_map/ppermute | solution.py:307
  51.2 1.7 %collective-permute-start.25 = (f32[408,128]{1,0:T(8,128)S(1)}, f32[408,128]{1,0:T(8,128)S(1)}, u32[]{:S(2)}, u32[]{:S(2)}) collective-permute-start(f32[408,128]{1,0:T(8,128)S(1)} %collective-permute-done.20.refs_6_), channel_id=1, source_target_pairs={{0,8},{1,9},{2,10},{3,11},{4,12},{5,13},{6,14},{7,15},{8,0},{9,1},... | collective-permute-start | bytes 626696 | tf_op jit(solution)/shard_map/ppermute | solution.py:307
  51.8 1.5 %collective-permute-start.26 = (f32[408,128]{1,0:T(8,128)S(1)}, f32[408,128]{1,0:T(8,128)S(1)}, u32[]{:S(2)}, u32[]{:S(2)}) collective-permute-start(f32[408,128]{1,0:T(8,128)S(1)} %collective-permute-done.21.refs_7_), channel_id=1, source_target_pairs={{0,8},{1,9},{2,10},{3,11},{4,12},{5,13},{6,14},{7,15},{8,0},{9,1},... | collective-permute-start | bytes 626696 | tf_op jit(solution)/shard_map/ppermute | solution.py:307
